TPU v7x, 32 devices: a whole 2x2x4 slice. The times are simulated.
32 devices in a mesh: parts: 2 (over x), dp: 16 (over z, y, core).
Axes of the slice: x: 2, y: 2, z: 4, core: 2. Of those that a mesh axis runs over, the one named last changes fastest.
Arguments:
- acts: bfloat16 [16384, 4096], P(('parts', 'dp')), parts along dimension 0, may hold values from -24 to 24
- grads: bfloat16 [16384, 4096], P(('parts', 'dp')), parts along dimension 0, may hold values from -24 to 24
- proj_act: bfloat16 [4096, 64], replicated, may hold values from -0.09375 to 0.09375
- proj_grad: bfloat16 [4096, 64], replicated, may hold values from -0.09375 to 0.09375
- queries: bfloat16 [128, 4096], P('dp'), may hold values from -6 to 6
Outputs:
- token_scores: float32 [16384, 128], P(('parts', 'dp')), parts along dimension 0
There are 2 independent parts, one for each index of `parts`. A program takes and returns all parts, laid end to end along the dimension named above; an argument that names none is the same for every part. Nothing has to cross between parts.
All inputs are finite; a program needn't handle non-finite values.
Results may differ from a plain program's by a relative error of at most 0.0003.
Values may be sent and summed in bfloat16 or wider, within the bound.
No kernel may reach another device: no remote copies, remote signals or barrier semaphores. Data moves between devices by JAX's collectives and lax.ppermute only.
A program may use at most 128 MiB of HBM per device.

v0:
```python
import jax
import jax.numpy as jnp
from jax import lax
from jax.sharding import PartitionSpec as P

DAMP = 0.1


def inverse_of(cov):
    identity = jnp.eye(cov.shape[0], dtype=jnp.float32)
    lower = jnp.linalg.cholesky(cov)
    solved = lax.linalg.triangular_solve(lower, identity, left_side=True, lower=True)
    return jnp.dot(solved.T, solved, precision=lax.Precision.HIGHEST)


def precondition(block, inverse_grad, inverse_act):
    factor = inverse_act.shape[0]
    shaped = block.astype(jnp.float32).reshape(block.shape[0], factor, factor)
    result = jnp.einsum(
        "ik,qkl,lj->qij", inverse_grad, shaped, inverse_act, precision=lax.Precision.HIGHEST
    )
    return result.reshape(block.shape[0], factor * factor)


def score_piece(outer, piece):
    return lax.dot_general(
        outer,
        piece,
        (((1,), (1,)), ((), ())),
        precision=lax.Precision.HIGHEST,
        preferred_element_type=jnp.float32,
    )


def outer_rows(left, right):
    tok_rows, factor = left.shape
    return (left[:, :, None] * right[:, None, :]).reshape(tok_rows, factor * factor)


def on_device(acts, grads, proj_act, proj_grad, queries):
    tok_rows = acts.shape[0]
    factor = proj_act.shape[1]
    tok_total = tok_rows * lax.axis_size("dp")
    act_proj = jnp.dot(acts, proj_act, preferred_element_type=jnp.float32)
    grad_proj = jnp.dot(grads, proj_grad, preferred_element_type=jnp.float32)
    sum_act, sum_grad = lax.psum(
        (
            jnp.dot(act_proj.T, act_proj, precision=lax.Precision.HIGHEST),
            jnp.dot(grad_proj.T, grad_proj, precision=lax.Precision.HIGHEST),
        ),
        "dp",
    )
    identity = jnp.eye(factor, dtype=jnp.float32)
    inverse_act = inverse_of(sum_act / tok_total + DAMP * identity)
    inverse_grad = inverse_of(sum_grad / tok_total + DAMP * identity)
    outer = outer_rows(grad_proj, act_proj)
    precond = precondition(queries, inverse_grad, inverse_act)
    return score_piece(outer, lax.all_gather(precond, "dp", axis=0, tiled=True))


def solution(mesh):
    in_specs = (P(("parts", "dp"), None), P(("parts", "dp"), None), P(), P(), P("dp", None))
    out_specs = P(("parts", "dp"), None)
    return jax.shard_map(
        on_device, mesh=mesh, in_specs=in_specs, out_specs=out_specs, check_vma=False
    )
```

profile of v0, /device:TPU:0, one launch (start us, length us, event | category | flops | bytes accessed | tf_op | source)
XLA Modules:
  0.0 165.5 jit_solution(7661210176533525531)
XLA Ops:
  6.5 1.0 copy-done
  7.6 3.7 %fusion.11 = f32[512,64]{0,1:T(8,128)S(1)} fusion(bf16[512,4096]{1,0:T(8,128)(2,1)} %param.8, bf16[4096,64]{0,1:T(8,128)(2,1)S(1)} %copy-done), kind=kOutput, calls=%fused_computation.28 | convolution fusion | flops 268435456 | bytes 4849664 | tf_op jit(solution)/shard_map/dot_general | solution.py:44
  11.3 0.3 fusion.13
  11.6 1.4 fusion.10
  13.0 0.3 fusion.12
  13.3 63.1 %all-reduce = (f32[64,64]{0,1:T(8,128)S(1)}, f32[64,64]{0,1:T(8,128)S(1)}) all-reduce(f32[64,64]{0,1:T(8,128)S(1)} %fusion.12, f32[64,64]{0,1:T(8,128)S(1)} %fusion.13), channel_id=1, replica_groups=mesh['parts'=2,'dp'=16] {'dp'}, use_global_device_ids=true, to_apply=%region_0.0 | all-reduce | flops 8192 | bytes 65536 | tf_op jit(solution)/shard_map/psum | solution.py:46
  76.4 5.8 %cholesky.55 = f32[64,64]{1,0:T(8,128)S(1)} custom-call(f32[64,64]{1,0:T(8,128)S(1)} %fusion.7), custom_call_target="Cholesky" | custom-call | tf_op jit(solution)/shard_map/jit(cholesky)/cholesky | solution.py:11
  82.3 0.6 compare_reduce_fusion
  83.0 0.7 fusion.5
  83.6 4.9 %custom-call.7 = f32[1,64,64]{1,2,0:T(8,128)S(1)} custom-call(f32[1,64,64]{2,1,0:T(8,128)S(1)} %fusion.5), custom_call_target="InvertDiagBlocksLowerTriangular" | custom-call | tf_op jit(solution)/shard_map/triangular_solve/custom-call.0 | solution.py:12
  88.5 0.3 fusion
  88.8 0.2 convolution_bitcast_fusion.1
  89.1 5.8 %cholesky.44 = f32[64,64]{1,0:T(8,128)S(1)} custom-call(f32[64,64]{1,0:T(8,128)S(1)} %fusion.9), custom_call_target="Cholesky" | custom-call | tf_op jit(solution)/shard_map/jit(cholesky)/cholesky | solution.py:11
  95.0 0.6 compare_reduce_fusion.1
  95.7 0.7 fusion.4
  96.3 4.9 %custom-call.6 = f32[1,64,64]{1,2,0:T(8,128)S(1)} custom-call(f32[1,64,64]{2,1,0:T(8,128)S(1)} %fusion.4), custom_call_target="InvertDiagBlocksLowerTriangular" | custom-call | tf_op jit(solution)/shard_map/triangular_solve/custom-call.0 | solution.py:12
  101.2 0.2 fusion.2
  101.5 0.2 convolution_bitcast_fusion.2
  101.9 0.3 convolution_bitcast_fusion
  102.2 0.4 fusion.14
  102.5 0.8 reshape.24
  103.3 4.4 %broadcast_multiply_fusion = f32[512,64,64]{0,2,1:T(8,128)} fusion(f32[512,64]{0,1:T(8,128)S(1)} %fusion.11, f32[512,64]{0,1:T(8,128)S(1)} %fusion.10), kind=kLoop, calls=%fused_computation | loop fusion | flops 2097152 | bytes 8650752 | tf_op jit(solution)/shard_map/mul | solution.py:37
  107.7 34.5 %all-gather.2.cloned.1.call-done = f32[128,4096]{1,0:T(8,128)} async-done(((f32[8,4096]{1,0:T(8,128)}), f32[128,4096]{1,0:T(8,128)}) %all-gather.2.cloned.1.call-update) | async-done | bytes 2097168 | tf_op jit(solution)/shard_map/all_gather | solution.py:58
  142.1 16.5 %fusion.15 = f32[512,128]{1,0:T(8,128)} fusion(f32[512,4096]{0,1:T(8,128)} %bitcast.43, f32[128,4096]{1,0:T(8,128)} %all-gather.2.cloned.1.call-done), kind=kOutput, calls=%fused_computation.32 | convolution fusion | flops 3221225472 | bytes 10747904 | tf_op jit(solution)/shard_map/dot_general | solution.py:26
  (17 shorter events, 0.5 us)
Async XLA Ops:
  6.5 1.0 copy-start
  6.5 5.1 %copy-start.2 = (bf16[4096,64]{0,1:T(8,128)(2,1)S(1)}, bf16[4096,64]{0,1:T(8,128)(2,1)}, u32[]{:S(2)}) copy-start(bf16[4096,64]{0,1:T(8,128)(2,1)} %param.11) | copy-start | bytes 1572868
  6.5 135.6 %all-gather.2.cloned.1.call-start = ((), (), s32[]{:S(2)}) async-start(), calls=%async_computation | async-start | bytes 2228224 | tf_op jit(solution)/shard_map/all_gather | solution.py:58
  7.6 4.0 %copy-start.1 = (bf16[512,4096]{1,0:T(8,128)(2,1)S(1)}, bf16[512,4096]{1,0:T(8,128)(2,1)}, u32[]{:S(2)}) copy-start(bf16[512,4096]{1,0:T(8,128)(2,1)} %param.9) | copy-start | bytes 12582916
  11.3 90.4 %copy-start.3 = (bf16[8,4096]{1,0:T(8,128)(2,1)S(1)}, bf16[8,4096]{1,0:T(8,128)(2,1)}, u32[]{:S(2)}) copy-start(bf16[8,4096]{1,0:T(8,128)(2,1)} %param.12) | copy-start | bytes 196612
Sparse Core Ops, SparseCore 0:
  103.4 38.6 all-gather.1
where the time goes:
time: 166 us; the launch traced here: 165 us
  blocking collectives  63.1 us (38%)
  waiting for transfers between devices  34.5 us (21%)
  other arithmetic  28.6 us (17%)
  matrix products  23.7 us (14%)
  between operations  13.5 us (8%)
  local copies, waits for them, and re-layouts  2.14 us (1%)
    psum x1, blocking collectives, on_device(): lax.psum((jnp.dot(act_proj.T, act_proj, precision=lax.Precision.HIGHEST),...  63.1 us
    all_gather x1, waiting for transfers between devices, on_device(): return score_piece(outer, lax.all_gather(precond, 'dp', axis=0, tiled=True))  34.5 us
    dot_general x1, matrix products, score_piece(): lax.dot_general(outer, piece, (((1,), (1,)), ((), ())), precision=lax.Pre...  16.5 us
    another operation x6, other arithmetic, inverse_of(): lower = jnp.linalg.cholesky(cov)  13 us
    another operation x4, other arithmetic, inverse_of(): lax.linalg.triangular_solve(lower, identity, left_side=True, lower=True)  11.1 us
    mul x1, other arithmetic, outer_rows(): left[:, :, None] * right[:, None, :]  4.35 us
    dot_general x1, matrix products, on_device(): act_proj = jnp.dot(acts, proj_act, preferred_element_type=jnp.float32)  3.73 us
  transfers between devices with their start and end apart: 1, of which 1 were waited for; matrix products, arithmetic and copies ran while one was open for 3% of the time, Pallas kernels for 0%

commit v1 on v0

v1 whole, which is shorter than its diff:
```python
import functools

import jax
import jax.numpy as jnp
from jax import lax
from jax.experimental import pallas as pl
from jax.experimental.pallas import tpu as pltpu
from jax.sharding import PartitionSpec as P

DAMP = 0.1
HIGHEST = lax.Precision.HIGHEST
CHUNKS = 4


def dot_nt(left, right, precision=None):
    return lax.dot_general(
        left, right, (((1,), (1,)), ((), ())), precision=precision, preferred_element_type=jnp.float32
    )


def project_kernel(acts, grads, proj_act, proj_grad, proj_t, cov, tok_buf, weight_buf, tok_sems, weight_sems):
    factor, width = proj_act.shape
    step = width // CHUNKS
    weight_copies = [
        pltpu.make_async_copy(src, weight_buf.at[at, pl.ds(at * factor, factor), :], weight_sems.at[at])
        for at, src in enumerate((proj_act, proj_grad))
    ]
    tok_copies = [
        [
            pltpu.make_async_copy(
                src.at[:, pl.ds(part * step, step)], tok_buf.at[at, part], tok_sems.at[at, part]
            )
            for at, src in enumerate((acts, grads))
        ]
        for part in range(CHUNKS)
    ]
    for copy in weight_copies:
        copy.start()
    for pair in tok_copies:
        for copy in pair:
            copy.start()
    blank = jnp.zeros((factor, width), weight_buf.dtype)
    weight_buf[0, factor:, :] = blank
    weight_buf[1, :factor, :] = blank
    for copy in weight_copies:
        copy.wait()
    both = None
    for part in range(CHUNKS):
        for at in range(2):
            tok_copies[part][at].wait()
            term = dot_nt(tok_buf[at, part], weight_buf[at, :, part * step : (part + 1) * step])
            both = term if both is None else both + term
    flipped = both.T
    proj_t[...] = flipped
    gram = jnp.dot(flipped, both, precision=HIGHEST, preferred_element_type=jnp.float32)
    lane = lax.broadcasted_iota(jnp.int32, (factor, 2 * factor), 1)
    cov[...] = jnp.where(lane < factor, gram[:factor, :], gram[factor:, :])


def project(acts, grads, proj_act, proj_grad):
    tok_rows, width = acts.shape
    factor = proj_act.shape[1]
    return pl.pallas_call(
        project_kernel,
        out_shape=(
            jax.ShapeDtypeStruct((2 * factor, tok_rows), jnp.float32),
            jax.ShapeDtypeStruct((factor, 2 * factor), jnp.float32),
        ),
        in_specs=[pl.BlockSpec(memory_space=pl.ANY)] * 4,
        out_specs=[pl.BlockSpec(memory_space=pltpu.VMEM)] * 2,
        scratch_shapes=[
            pltpu.VMEM((2, CHUNKS, tok_rows, width // CHUNKS), acts.dtype),
            pltpu.VMEM((2, 2 * factor, width), proj_act.dtype),
            pltpu.SemaphoreType.DMA((2, CHUNKS)),
            pltpu.SemaphoreType.DMA((2,)),
        ],
        compiler_params=pltpu.CompilerParams(vmem_limit_bytes=40 * 2**20),
        name="project",
    )(acts, grads, proj_act.T, proj_grad.T)


def inverse_pair(both):
    factor = both.shape[0]
    lane = lax.broadcasted_iota(jnp.int32, both.shape, 1)
    row_at = lax.broadcasted_iota(jnp.int32, both.shape, 0)
    left_half = lane < factor
    inner = jnp.where(left_half, lane, lane - factor)
    for k in range(factor):
        column = jnp.where(left_half, both[:, k : k + 1], both[:, factor + k : factor + k + 1])
        on_lane = inner == k
        scale = 1.0 / column[k : k + 1, :]
        pivot_row = jnp.where(on_lane[:1], 1.0, both[k : k + 1, :]) * scale
        rest = jnp.where(on_lane, 0.0, both) - column * pivot_row
        both = jnp.where(row_at == k, pivot_row, rest)
    return both


def score_kernel(tok_total, terms, proj_t, queries, scores, queries_buf, moved, total, sem):
    factor = proj_t.shape[0] // 2
    copy = pltpu.make_async_copy(queries, queries_buf, sem)
    copy.start()
    both = terms[0][...]
    for term in terms[1:]:
        both = both + term[...]
    lane = lax.broadcasted_iota(jnp.int32, both.shape, 1)
    row_at = lax.broadcasted_iota(jnp.int32, both.shape, 0)
    left_half = lane < factor
    inner = jnp.where(left_half, lane, lane - factor)
    both = both / tok_total + jnp.where(inner == row_at, DAMP, 0.0)
    both = inverse_pair(both)
    blocks = jnp.concatenate(
        [jnp.where(left_half, both, 0.0), jnp.where(left_half, 0.0, both)], axis=0
    )
    moved[...] = jnp.dot(blocks, proj_t[...], precision=HIGHEST, preferred_element_type=jnp.float32)
    copy.wait()
    group = 4
    act_side = moved[:factor, :]
    for first in range(0, factor, group):
        outer = jnp.concatenate(
            [act_side * moved[factor + i : factor + i + 1, :] for i in range(first, first + group)], axis=0
        )
        high = outer.astype(jnp.bfloat16)
        low = (outer - high.astype(jnp.float32)).astype(jnp.bfloat16)
        piece = queries_buf[:, first * factor : (first + group) * factor]
        term = jnp.dot(piece, high, preferred_element_type=jnp.float32)
        term = term + jnp.dot(piece, low, preferred_element_type=jnp.float32)
        if first == 0:
            total[...] = term
        else:
            total[...] += term
    scores[...] = total[...].T


def score(tok_total, terms, proj_t, queries):
    tok_rows = proj_t.shape[1]
    n_queries, flat = queries.shape

    def kernel(*refs):
        n = len(terms)
        score_kernel(tok_total, refs[:n], *refs[n:])

    return pl.pallas_call(
        kernel,
        out_shape=jax.ShapeDtypeStruct((tok_rows, n_queries), jnp.float32),
        in_specs=[pl.BlockSpec(memory_space=pltpu.VMEM)] * (len(terms) + 1)
        + [pl.BlockSpec(memory_space=pl.ANY)],
        out_specs=pl.BlockSpec(memory_space=pltpu.VMEM),
        scratch_shapes=[
            pltpu.VMEM((n_queries, flat), queries.dtype),
            pltpu.VMEM(proj_t.shape, jnp.float32),
            pltpu.VMEM((n_queries, tok_rows), jnp.float32),
            pltpu.SemaphoreType.DMA,
        ],
        compiler_params=pltpu.CompilerParams(vmem_limit_bytes=40 * 2**20),
        name="score",
    )(*terms, proj_t, queries)


def stages_of(size):
    low = 1
    while low * low < size:
        low *= 2
    if size % low:
        return [(1, size)]
    return [(1, low), (low, size // low)]


def shifted(value, size, stride, radix, shift):
    perm = []
    for at in range(size):
        digit = at // stride % radix
        perm.append((at, at + ((digit + shift) % radix - digit) * stride))
    return lax.ppermute(value, "dp", perm)


def on_device(acts, grads, proj_act, proj_grad, queries):
    size = lax.axis_size("dp")
    tok_total = acts.shape[0] * size
    all_queries = lax.all_gather(queries, "dp", axis=0, tiled=True)
    proj_t, cov = project(acts, grads, proj_act, proj_grad)
    terms = [cov]
    for stride, radix in stages_of(size):
        own = functools.reduce(jnp.add, terms)
        terms = [own] + [shifted(own, size, stride, radix, shift) for shift in range(1, radix)]
    return score(tok_total, terms, proj_t, all_queries)


def solution(mesh):
    in_specs = (P(("parts", "dp"), None), P(("parts", "dp"), None), P(), P(), P("dp", None))
    out_specs = P(("parts", "dp"), None)
    return jax.shard_map(
        on_device, mesh=mesh, in_specs=in_specs, out_specs=out_specs, check_vma=False
    )
```

time: 166 us -> 67 us (0.40)
  blocking collectives: 63.1 us -> 0 us
  other arithmetic: 28.6 us -> 0.01 us
  matrix products: 23.7 us -> 0 us
  Pallas kernels: 0 us -> 15.4 us
  waiting for transfers between devices: 34.5 us -> 22.3 us
  starting transfers between devices: 0.01 us -> 7.94 us
  local copies, waits for them, and re-layouts: 2.14 us -> 7.67 us
    psum x1 -> x0, blocking collectives: 63.1 us -> none  [on_device(): lax.psum((jnp.dot(act_proj.T, act_proj, precision=lax.Precision.HIGHEST),...]
    another operation x10 -> x0, other arithmetic: 24.2 us -> none  [the longest x6 13 us: inverse_of(): lower = jnp.linalg.cholesky(cov)]
    dot_general x9 -> x0, matrix products: 23.2 us -> none  [the longest x1 16.5 us: score_piece(): lax.dot_general(outer, piece, (((1,), (1,)), ((), ())), precision=lax.Pre...]
    all_gather x1, waiting for transfers between devices: 34.5 us -> 13.4 us  [on_device(): all_queries = lax.all_gather(queries, 'dp', axis=0, tiled=True)]
    pallas_call x0 -> x2, Pallas kernels: none -> 15.4 us  [the longest x1 8.41 us: score(): pl.pallas_call(kernel, out_shape=jax.ShapeDtypeStruct((tok_rows, n_querie...]
    ppermute x0 -> x6, waiting for transfers between devices: none -> 8.15 us  [shifted(): return lax.ppermute(value, 'dp', perm)]
    ppermute x0 -> x6, starting transfers between devices: none -> 7.93 us  [shifted(): return lax.ppermute(value, 'dp', perm)]
    unnamed x8 -> x10, local copies, waits for them, and re-layouts: 1.05 us -> 7.67 us
  transfers between devices with their start and end apart: 1 -> 7, of which waited for: 1 -> 7; matrix products, arithmetic and copies ran while one was open for 3% -> 0% of each run, Pallas kernels for 0% -> 10%
where the time goes in v1:
time: 67 us; the launch traced here: 66.7 us
  waiting for transfers between devices  22.3 us (33%)
  Pallas kernels  15.4 us (23%)
  between operations  13.4 us (20%)
  starting transfers between devices  7.94 us (12%)
  local copies, waits for them, and re-layouts  7.67 us (11%)
    all_gather x1, waiting for transfers between devices, on_device(): all_queries = lax.all_gather(queries, 'dp', axis=0, tiled=True)  13.4 us
    pallas_call x1, Pallas kernels, score(): pl.pallas_call(kernel, out_shape=jax.ShapeDtypeStruct((tok_rows, n_querie...  8.41 us
    ppermute x6, waiting for transfers between devices, shifted(): return lax.ppermute(value, 'dp', perm)  8.15 us
    ppermute x6, starting transfers between devices, shifted(): return lax.ppermute(value, 'dp', perm)  7.93 us
    unnamed x10, local copies, waits for them, and re-layouts  7.67 us
    pallas_call x1, Pallas kernels, project(): pl.pallas_call(project_kernel, out_shape=(jax.ShapeDtypeStruct((2 * facto...  6.95 us
  transfers between devices with their start and end apart: 7, of which 7 were waited for; matrix products, arithmetic and copies ran while one was open for 0% of the time, Pallas kernels for 10%

profile of v1, /device:TPU:0, one launch (start us, length us, event | category | flops | bytes accessed | tf_op | source)
XLA Modules:
  0.0 66.7 jit_solution(14479539036703408964)
XLA Ops:
  6.5 0.0 all-gather.2.cloned.1.call-start
  6.5 0.7 %all-gather.2.cloned.1.call-update = ((bf16[8,4096]{1,0:T(8,128)(2,1)}), bf16[128,4096]{1,0:T(8,128)(2,1)}) async-update(((), (), s32[]{:S(2)}) %all-gather.2.cloned.1.call-start, bf16[8,4096]{1,0:T(8,128)(2,1)} %param.9) | async-update | bytes 1179672
  7.3 0.0 copy-start
  7.3 2.2 %copy-done = bf16[512,4096]{1,0:T(8,128)(2,1)S(1)} copy-done((bf16[512,4096]{1,0:T(8,128)(2,1)S(1)}, bf16[512,4096]{1,0:T(8,128)(2,1)}, u32[]{:S(2)}) %copy-start) | copy-done | bytes 4194328
  9.4 0.0 copy-start.1
  9.4 2.2 %copy-done.1 = bf16[512,4096]{1,0:T(8,128)(2,1)S(1)} copy-done((bf16[512,4096]{1,0:T(8,128)(2,1)S(1)}, bf16[512,4096]{1,0:T(8,128)(2,1)}, u32[]{:S(2)}) %copy-start.1) | copy-done | bytes 4194328
  11.6 1.0 %copy-done.3 = bf16[4096,64]{0,1:T(8,128)(2,1)S(1)} copy-done((bf16[4096,64]{0,1:T(8,128)(2,1)S(1)}, bf16[4096,64]{0,1:T(8,128)(2,1)}, u32[]{:S(2)}) %copy-start.3) | copy-done | bytes 524312
  12.7 1.0 %copy-done.4 = bf16[4096,64]{0,1:T(8,128)(2,1)S(1)} copy-done((bf16[4096,64]{0,1:T(8,128)(2,1)S(1)}, bf16[4096,64]{0,1:T(8,128)(2,1)}, u32[]{:S(2)}) %copy-start.4) | copy-done | bytes 524312
  13.7 7.0 %project.1 = (f32[128,512]{1,0:T(8,128)S(1)}, f32[64,128]{1,0:T(8,128)S(1)}) custom-call(bf16[512,4096]{1,0:T(8,128)(2,1)S(1)} %copy-done, bf16[512,4096]{1,0:T(8,128)(2,1)S(1)} %copy-done.1, bf16[64,4096]{1,0:T(8,128)(2,1)S(1)} %bitcast.2, bf16[64,4096]{1,0:T(8,128)(2,1)S(1)} %bitcast.3), custom_call_target="tpu_custom_call" | custom-call | tf_op jit(solution)/shard_map/project/pallas_call | solution.py:63
  20.7 2.5 %collective-permute-start.2 = (f32[64,128]{1,0:T(8,128)S(1)}, f32[64,128]{1,0:T(8,128)S(1)}, u32[]{:S(2)}, u32[]{:S(2)}) collective-permute-start(f32[64,128]{1,0:T(8,128)S(1)} %get-tuple-element.7), channel_id=1, source_target_pairs={{0,3},{1,0},{2,1},{3,2},{4,7},{5,4},{6,5},{7,6},{8,11},{9,8},{10,9... | collective-permute-start | bytes 98312 | tf_op jit(solution)/shard_map/ppermute | solution.py:173
  23.1 0.6 collective-permute-start.1
  23.8 0.2 collective-permute-start
  23.9 0.9 %collective-permute-done.2 = f32[64,128]{1,0:T(8,128)S(1)} collective-permute-done((f32[64,128]{1,0:T(8,128)S(1)}, f32[64,128]{1,0:T(8,128)S(1)}, u32[]{:S(2)}, u32[]{:S(2)}) %collective-permute-start.2) | collective-permute-done | bytes 32800 | tf_op jit(solution)/shard_map/ppermute | solution.py:173
  24.8 2.5 %collective-permute-done.1 = f32[64,128]{1,0:T(8,128)S(1)} collective-permute-done((f32[64,128]{1,0:T(8,128)S(1)}, f32[64,128]{1,0:T(8,128)S(1)}, u32[]{:S(2)}, u32[]{:S(2)}) %collective-permute-start.1) | collective-permute-done | bytes 32800 | tf_op jit(solution)/shard_map/ppermute | solution.py:173
  27.3 0.1 collective-permute-done
  27.4 3.6 %collective-permute-start.5 = (f32[64,128]{1,0:T(8,128)S(1)}, f32[64,128]{1,0:T(8,128)S(1)}, u32[]{:S(2)}, u32[]{:S(2)}) collective-permute-start(f32[64,128]{1,0:T(8,128)S(1)} %add_add_fusion.refs_0_), channel_id=1, source_target_pairs={{0,12},{1,13},{2,14},{3,15},{4,0},{5,1},{6,2},{7,3},{8,4},{9,5},{1... | collective-permute-start | bytes 98312 | tf_op jit(solution)/shard_map/ppermute | solution.py:173
  31.1 0.0 collective-permute-start.4
  31.1 1.0 %collective-permute-start.3 = (f32[64,128]{1,0:T(8,128)S(1)}, f32[64,128]{1,0:T(8,128)S(1)}, u32[]{:S(2)}, u32[]{:S(2)}) collective-permute-start(f32[64,128]{1,0:T(8,128)S(1)} %add_add_fusion.refs_0_), channel_id=1, source_target_pairs={{0,4},{1,5},{2,6},{3,7},{4,8},{5,9},{6,10},{7,11},{8,12},{9,13},{1... | collective-permute-start | bytes 98312 | tf_op jit(solution)/shard_map/ppermute | solution.py:173
  32.1 0.6 collective-permute-done.5.refs_3_
  32.7 3.2 %collective-permute-done.4.refs_2_ = f32[64,128]{1,0:T(8,128)S(1)} collective-permute-done((f32[64,128]{1,0:T(8,128)S(1)}, f32[64,128]{1,0:T(8,128)S(1)}, u32[]{:S(2)}, u32[]{:S(2)}) %collective-permute-start.4) | collective-permute-done | bytes 32800 | tf_op jit(solution)/shard_map/ppermute | solution.py:173
  35.9 0.9 %collective-permute-done.3.refs_1_ = f32[64,128]{1,0:T(8,128)S(1)} collective-permute-done((f32[64,128]{1,0:T(8,128)S(1)}, f32[64,128]{1,0:T(8,128)S(1)}, u32[]{:S(2)}, u32[]{:S(2)}) %collective-permute-start.3) | collective-permute-done | bytes 32800 | tf_op jit(solution)/shard_map/ppermute | solution.py:173
  36.8 13.4 %all-gather.2.cloned.1.call-done.refs_5_ = bf16[128,4096]{1,0:T(8,128)(2,1)} async-done(((bf16[8,4096]{1,0:T(8,128)(2,1)}), bf16[128,4096]{1,0:T(8,128)(2,1)}) %all-gather.2.cloned.1.call-update) | async-done | bytes 1048592 | tf_op jit(solution)/shard_map/all_gather | solution.py:179
  50.2 1.2 %copy-done.2 = bf16[128,4096]{1,0:T(8,128)(2,1)S(1)} copy-done((bf16[128,4096]{1,0:T(8,128)(2,1)S(1)}, bf16[128,4096]{1,0:T(8,128)(2,1)}, u32[]{:S(2)}) %copy-start.2) | copy-done | bytes 1048600
  51.4 8.4 %score.1 = f32[512,128]{1,0:T(8,128)} custom-call(f32[64,128]{1,0:T(8,128)S(1)} %add_add_fusion.refs_0_, f32[64,128]{1,0:T(8,128)S(1)} %collective-permute-done.3.refs_1_, f32[64,128]{1,0:T(8,128)S(1)} %collective-permute-done.4.refs_2_, f32[64,128]{1,0:T(8,128)S(1)} %collective-permute-done.5.refs_3_, f32[128,512]{1,0:T(8,128)S(1)} %get-tuple-element.8.refs_4_, ...), custom_call_target="tpu_custom_call" | custom-call | tf_op jit(solution)/shard_map/score/pallas_call | solution.py:142
  (4 shorter events, 0.0 us)
Async XLA Ops:
  6.5 43.7 %all-gather.2.cloned.1.call-start = ((), (), s32[]{:S(2)}) async-start(), calls=%async_computation | async-start | bytes 1114112 | tf_op jit(solution)/shard_map/all_gather | solution.py:179
  7.3 2.2 %copy-start = (bf16[512,4096]{1,0:T(8,128)(2,1)S(1)}, bf16[512,4096]{1,0:T(8,128)(2,1)}, u32[]{:S(2)}) copy-start(bf16[512,4096]{1,0:T(8,128)(2,1)} %acts.1) | copy-start | bytes 12582916
  9.4 2.2 %copy-start.1 = (bf16[512,4096]{1,0:T(8,128)(2,1)S(1)}, bf16[512,4096]{1,0:T(8,128)(2,1)}, u32[]{:S(2)}) copy-start(bf16[512,4096]{1,0:T(8,128)(2,1)} %grads.1) | copy-start | bytes 12582916
  11.6 1.0 %copy-start.3 = (bf16[4096,64]{0,1:T(8,128)(2,1)S(1)}, bf16[4096,64]{0,1:T(8,128)(2,1)}, u32[]{:S(2)}) copy-start(bf16[4096,64]{0,1:T(8,128)(2,1)} %param.7) | copy-start | bytes 1572868
  12.7 1.0 %copy-start.4 = (bf16[4096,64]{0,1:T(8,128)(2,1)S(1)}, bf16[4096,64]{0,1:T(8,128)(2,1)}, u32[]{:S(2)}) copy-start(bf16[4096,64]{0,1:T(8,128)(2,1)} %param.8) | copy-start | bytes 1572868
  20.7 4.1 %collective-permute-start.2 = (f32[64,128]{1,0:T(8,128)S(1)}, f32[64,128]{1,0:T(8,128)S(1)}, u32[]{:S(2)}, u32[]{:S(2)}) collective-permute-start(f32[64,128]{1,0:T(8,128)S(1)} %get-tuple-element.7), channel_id=1, source_target_pairs={{0,3},{1,0},{2,1},{3,2},{4,7},{5,4},{6,5},{7,6},{8,11},{9,8},{10,9... | collective-permute-start | bytes 98312 | tf_op jit(solution)/shard_map/ppermute | solution.py:173
  23.1 4.2 %collective-permute-start.1 = (f32[64,128]{1,0:T(8,128)S(1)}, f32[64,128]{1,0:T(8,128)S(1)}, u32[]{:S(2)}, u32[]{:S(2)}) collective-permute-start(f32[64,128]{1,0:T(8,128)S(1)} %get-tuple-element.7), channel_id=1, source_target_pairs={{0,2},{1,3},{2,0},{3,1},{4,6},{5,7},{6,4},{7,5},{8,10},{9,11},{10,... | collective-permute-start | bytes 98312 | tf_op jit(solution)/shard_map/ppermute | solution.py:173
  23.8 3.6 %collective-permute-start = (f32[64,128]{1,0:T(8,128)S(1)}, f32[64,128]{1,0:T(8,128)S(1)}, u32[]{:S(2)}, u32[]{:S(2)}) collective-permute-start(f32[64,128]{1,0:T(8,128)S(1)} %get-tuple-element.7), channel_id=1, source_target_pairs={{0,1},{1,2},{2,3},{3,0},{4,5},{5,6},{6,7},{7,4},{8,9},{9,10},{10,1... | collective-permute-start | bytes 98312 | tf_op jit(solution)/shard_map/ppermute | solution.py:173
  27.4 5.2 %collective-permute-start.5 = (f32[64,128]{1,0:T(8,128)S(1)}, f32[64,128]{1,0:T(8,128)S(1)}, u32[]{:S(2)}, u32[]{:S(2)}) collective-permute-start(f32[64,128]{1,0:T(8,128)S(1)} %add_add_fusion.refs_0_), channel_id=1, source_target_pairs={{0,12},{1,13},{2,14},{3,15},{4,0},{5,1},{6,2},{7,3},{8,4},{9,5},{1... | collective-permute-start | bytes 98312 | tf_op jit(solution)/shard_map/ppermute | solution.py:173
  31.1 4.8 %collective-permute-start.4 = (f32[64,128]{1,0:T(8,128)S(1)}, f32[64,128]{1,0:T(8,128)S(1)}, u32[]{:S(2)}, u32[]{:S(2)}) collective-permute-start(f32[64,128]{1,0:T(8,128)S(1)} %add_add_fusion.refs_0_), channel_id=1, source_target_pairs={{0,8},{1,9},{2,10},{3,11},{4,12},{5,13},{6,14},{7,15},{8,0},{9,1},... | collective-permute-start | bytes 98312 | tf_op jit(solution)/shard_map/ppermute | solution.py:173
  31.1 5.7 %collective-permute-start.3 = (f32[64,128]{1,0:T(8,128)S(1)}, f32[64,128]{1,0:T(8,128)S(1)}, u32[]{:S(2)}, u32[]{:S(2)}) collective-permute-start(f32[64,128]{1,0:T(8,128)S(1)} %add_add_fusion.refs_0_), channel_id=1, source_target_pairs={{0,4},{1,5},{2,6},{3,7},{4,8},{5,9},{6,10},{7,11},{8,12},{9,13},{1... | collective-permute-start | bytes 98312 | tf_op jit(solution)/shard_map/ppermute | solution.py:173
  50.2 1.2 %copy-start.2 = (bf16[128,4096]{1,0:T(8,128)(2,1)S(1)}, bf16[128,4096]{1,0:T(8,128)(2,1)}, u32[]{:S(2)}) copy-start(bf16[128,4096]{1,0:T(8,128)(2,1)} %all-gather.2.cloned.1.call-done.refs_5_) | copy-start | bytes 3145732
Sparse Core Ops, SparseCore 0:
  9.5 40.6 all-gather.1

commit v2 on v1

--- a/solution.py
+++ b/solution.py
@@ -9,7 +9,7 @@
 
 DAMP = 0.1
 HIGHEST = lax.Precision.HIGHEST
-CHUNKS = 4
+CHUNKS = 8
 
 
 def dot_nt(left, right, precision=None):
@@ -66,7 +66,7 @@
             jax.ShapeDtypeStruct((2 * factor, tok_rows), jnp.float32),
             jax.ShapeDtypeStruct((factor, 2 * factor), jnp.float32),
         ),
-        in_specs=[pl.BlockSpec(memory_space=pl.ANY)] * 4,
+        in_specs=[pl.BlockSpec(memory_space=pltpu.HBM)] * 4,
         out_specs=[pl.BlockSpec(memory_space=pltpu.VMEM)] * 2,
         scratch_shapes=[
             pltpu.VMEM((2, CHUNKS, tok_rows, width // CHUNKS), acts.dtype),
@@ -74,7 +74,10 @@
             pltpu.SemaphoreType.DMA((2, CHUNKS)),
             pltpu.SemaphoreType.DMA((2,)),
         ],
-        compiler_params=pltpu.CompilerParams(vmem_limit_bytes=40 * 2**20),
+        compiler_params=pltpu.CompilerParams(vmem_limit_bytes=60 * 2**20),
+        cost_estimate=pl.CostEstimate(
+            flops=4 * tok_rows * width * factor, bytes_accessed=4 * tok_rows * width, transcendentals=0
+        ),
         name="project",
     )(acts, grads, proj_act.T, proj_grad.T)
 
@@ -95,13 +98,12 @@
     return both
 
 
-def score_kernel(tok_total, terms, proj_t, queries, scores, queries_buf, moved, total, sem):
-    factor = proj_t.shape[0] // 2
-    copy = pltpu.make_async_copy(queries, queries_buf, sem)
-    copy.start()
+def precondition_kernel(tok_total, n_terms, *refs):
+    terms, (proj_t, moved) = refs[:n_terms], refs[n_terms:]
     both = terms[0][...]
     for term in terms[1:]:
         both = both + term[...]
+    factor = both.shape[0]
     lane = lax.broadcasted_iota(jnp.int32, both.shape, 1)
     row_at = lax.broadcasted_iota(jnp.int32, both.shape, 0)
     left_half = lane < factor
@@ -112,7 +114,27 @@
         [jnp.where(left_half, both, 0.0), jnp.where(left_half, 0.0, both)], axis=0
     )
     moved[...] = jnp.dot(blocks, proj_t[...], precision=HIGHEST, preferred_element_type=jnp.float32)
-    copy.wait()
+
+
+def precondition(tok_total, terms, proj_t):
+    n_terms = len(terms)
+    rows, tok_rows = proj_t.shape
+    return pl.pallas_call(
+        functools.partial(precondition_kernel, tok_total, n_terms),
+        out_shape=jax.ShapeDtypeStruct(proj_t.shape, jnp.float32),
+        in_specs=[pl.BlockSpec(memory_space=pltpu.VMEM)] * (n_terms + 1),
+        out_specs=pl.BlockSpec(memory_space=pltpu.VMEM),
+        compiler_params=pltpu.CompilerParams(vmem_limit_bytes=24 * 2**20),
+        cost_estimate=pl.CostEstimate(
+            flops=400 * rows * rows * tok_rows, bytes_accessed=8 * rows * tok_rows, transcendentals=0
+        ),
+        name="precondition",
+    )(*terms, proj_t)
+
+
+def score_kernel(size, n_pieces, moved, *refs):
+    queries, (scores, total, ordered) = refs[:n_pieces], refs[n_pieces:]
+    factor = moved.shape[0] // 2
     group = 4
     act_side = moved[:factor, :]
     for first in range(0, factor, group):
@@ -121,39 +143,46 @@
         )
         high = outer.astype(jnp.bfloat16)
         low = (outer - high.astype(jnp.float32)).astype(jnp.bfloat16)
-        piece = queries_buf[:, first * factor : (first + group) * factor]
-        term = jnp.dot(piece, high, preferred_element_type=jnp.float32)
-        term = term + jnp.dot(piece, low, preferred_element_type=jnp.float32)
-        if first == 0:
-            total[...] = term
-        else:
-            total[...] += term
-    scores[...] = total[...].T
-
-
-def score(tok_total, terms, proj_t, queries):
-    tok_rows = proj_t.shape[1]
-    n_queries, flat = queries.shape
-
-    def kernel(*refs):
-        n = len(terms)
-        score_kernel(tok_total, refs[:n], *refs[n:])
-
+        done = 0
+        for piece in queries:
+            rows = piece.shape[0]
+            values = piece[:, first * factor : (first + group) * factor]
+            term = jnp.dot(values, high, preferred_element_type=jnp.float32)
+            term = term + jnp.dot(values, low, preferred_element_type=jnp.float32)
+            if first == 0:
+                total[done : done + rows, :] = term
+            else:
+                total[done : done + rows, :] += term
+            done += rows
+    rows = total.shape[0] // size
+    for at, owner in enumerate(owners_of(lax.axis_index("dp"), size)):
+        ordered[pl.ds(pl.multiple_of(owner * rows, rows), rows), :] = total[at * rows : (at + 1) * rows, :]
+    scores[...] = ordered[...].T
+
+
+def score(size, moved, queries):
+    tok_rows = moved.shape[1]
+    n_queries = sum(piece.shape[0] for piece in queries)
+    n_pieces = len(queries)
     return pl.pallas_call(
-        kernel,
+        functools.partial(score_kernel, size, n_pieces),
         out_shape=jax.ShapeDtypeStruct((tok_rows, n_queries), jnp.float32),
-        in_specs=[pl.BlockSpec(memory_space=pltpu.VMEM)] * (len(terms) + 1)
-        + [pl.BlockSpec(memory_space=pl.ANY)],
+        in_specs=[pl.BlockSpec(memory_space=pltpu.VMEM)] * (1 + n_pieces),
         out_specs=pl.BlockSpec(memory_space=pltpu.VMEM),
         scratch_shapes=[
-            pltpu.VMEM((n_queries, flat), queries.dtype),
-            pltpu.VMEM(proj_t.shape, jnp.float32),
             pltpu.VMEM((n_queries, tok_rows), jnp.float32),
-            pltpu.SemaphoreType.DMA,
+            pltpu.VMEM((n_queries, tok_rows), jnp.float32),
         ],
-        compiler_params=pltpu.CompilerParams(vmem_limit_bytes=40 * 2**20),
+        compiler_params=pltpu.CompilerParams(vmem_limit_bytes=32 * 2**20),
         name="score",
-    )(*terms, proj_t, queries)
+    )(moved, *queries)
+
+
+def gather_stages(size):
+    core = 2 if size % 2 == 0 else 1
+    rest = size // core
+    near = max(d for d in range(1, rest + 1) if rest % d == 0 and d * d <= rest)
+    return [(core * near, rest // near), (core, near), (1, core)]
 
 
 def stages_of(size):
@@ -161,7 +190,7 @@
     while low * low < size:
         low *= 2
     if size % low:
-        return [(1, size)]
+        return [(1, 1), (1, size)]
     return [(1, low), (low, size // low)]
 
 
@@ -173,16 +202,38 @@
     return lax.ppermute(value, "dp", perm)
 
 
+def after(value, other):
+    return lax.optimization_barrier((value, other))[0]
+
+
+def owners_of(me, size):
+    owners = [me]
+    for stride, radix in gather_stages(size):
+        digit = lax.rem(lax.div(me, stride), radix)
+        steps = [(lax.rem(digit + (radix - shift), radix) - digit) * stride for shift in range(radix)]
+        owners = [owner + step for step in steps for owner in owners]
+    return owners
+
+
+def exchanged(held, size, stride, radix):
+    mine = held[0] if len(held) == 1 else jnp.concatenate(held, axis=0)
+    return [mine] + [shifted(mine, size, stride, radix, shift) for shift in range(1, radix)]
+
+
 def on_device(acts, grads, proj_act, proj_grad, queries):
     size = lax.axis_size("dp")
     tok_total = acts.shape[0] * size
-    all_queries = lax.all_gather(queries, "dp", axis=0, tiled=True)
+    far, near, core = gather_stages(size)
+    first, second = stages_of(size)
+    pieces = exchanged([queries], size, *far)
     proj_t, cov = project(acts, grads, proj_act, proj_grad)
-    terms = [cov]
-    for stride, radix in stages_of(size):
-        own = functools.reduce(jnp.add, terms)
-        terms = [own] + [shifted(own, size, stride, radix, shift) for shift in range(1, radix)]
-    return score(tok_total, terms, proj_t, all_queries)
+    *pieces, cov = lax.optimization_barrier((*pieces, cov))
+    terms = exchanged([cov], size, *first)
+    pieces = exchanged(pieces, size, *near)
+    terms = exchanged([functools.reduce(jnp.add, terms)], size, *second)
+    pieces = exchanged([after(piece, terms) for piece in pieces], size, *core)
+    moved = precondition(tok_total, terms, proj_t)
+    return score(size, moved, pieces)
 
 
 def solution(mesh):

time: 67 us -> 43.5 us (0.65)
  between operations: 13.4 us -> 0.11 us
  waiting for transfers between devices: 22.3 us -> 9.04 us
  local copies, waits for them, and re-layouts: 7.67 us -> 1.01 us
  starting transfers between devices: 7.94 us -> 12.7 us
  Pallas kernels: 15.4 us -> 19.5 us
  other arithmetic: 0.01 us -> 0.77 us
    all_gather x1 -> x0, waiting for transfers between devices: 13.4 us -> none  [on_device(): all_queries = lax.all_gather(queries, 'dp', axis=0, tiled=True)]
    unnamed x10 -> x8, local copies, waits for them, and re-layouts: 7.67 us -> 0.99 us
    ppermute x6 -> x11, starting transfers between devices: 7.93 us -> 12.7 us  [shifted(): return lax.ppermute(value, 'dp', perm)]
    pallas_call x1, Pallas kernels: 6.95 us -> 9.69 us  [project(): pl.pallas_call(project_kernel, out_shape=(jax.ShapeDtypeStruct((2 * facto...]
    pallas_call x1 -> x2, Pallas kernels: 8.41 us -> 9.85 us  [the longest x1 5.92 us: precondition(): pl.pallas_call(functools.partial(precondition_kernel, tok_total, n_terms)...]
    ppermute x6 -> x11, waiting for transfers between devices: 8.15 us -> 9.04 us  [shifted(): return lax.ppermute(value, 'dp', perm)]
    add x1, other arithmetic: 0.01 us -> 0.77 us  [on_device(): terms = exchanged([functools.reduce(jnp.add, terms)], size, *second)]
    unnamed x1 -> x0, waiting for transfers between devices: 0.71 us -> none
  transfers between devices with their start and end apart: 7 -> 11, of which waited for: 7 -> 7; matrix products, arithmetic and copies ran while one was open for 0% -> 0% of each run, Pallas kernels for 10% -> 36%
where the time goes in v2:
time: 43.5 us; the launch traced here: 43.2 us
  Pallas kernels  19.5 us (45%)
  starting transfers between devices  12.7 us (29%)
  waiting for transfers between devices  9.04 us (21%)
  local copies, waits for them, and re-layouts  1.01 us (2%)
  other arithmetic  0.77 us (2%)
    ppermute x11, starting transfers between devices, shifted(): return lax.ppermute(value, 'dp', perm)  12.7 us
    pallas_call x1, Pallas kernels, project(): pl.pallas_call(project_kernel, out_shape=(jax.ShapeDtypeStruct((2 * facto...  9.69 us
    ppermute x11, waiting for transfers between devices, shifted(): return lax.ppermute(value, 'dp', perm)  9.04 us
    pallas_call x1, Pallas kernels, precondition(): pl.pallas_call(functools.partial(precondition_kernel, tok_total, n_terms)...  5.92 us
    pallas_call x1, Pallas kernels, score(): pl.pallas_call(functools.partial(score_kernel, size, n_pieces), out_shape...  3.93 us
    unnamed x8, local copies, waits for them, and re-layouts  0.99 us
  transfers between devices with their start and end apart: 11, of which 7 were waited for; matrix products, arithmetic and copies ran while one was open for 0% of the time, Pallas kernels for 36%

profile of v2, /device:TPU:0, one launch (start us, length us, event | category | flops | bytes accessed | tf_op | source)
XLA Modules:
  0.0 43.2 jit_solution(10852385440848446287)
XLA Ops:
  0.0 4.0 %collective-permute-start.1 = (bf16[8,4096]{1,0:T(8,128)(2,1)}, bf16[8,4096]{1,0:T(8,128)(2,1)S(1)}, u32[]{:S(2)}, u32[]{:S(2)}) collective-permute-start(bf16[8,4096]{1,0:T(8,128)(2,1)} %param.9), channel_id=1, source_target_pairs={{0,8},{1,9},{2,10},{3,11},{4,12},{5,13},{6,14},{7,15},{8,0},{9,1},... | collective-permute-start | bytes 196616 | tf_op jit(solution)/shard_map/ppermute | solution.py:202
  4.0 1.6 %collective-permute-start = (bf16[8,4096]{1,0:T(8,128)(2,1)}, bf16[8,4096]{1,0:T(8,128)(2,1)S(1)}, u32[]{:S(2)}, u32[]{:S(2)}) collective-permute-start(bf16[8,4096]{1,0:T(8,128)(2,1)} %param.9), channel_id=1, source_target_pairs={{0,4},{1,5},{2,6},{3,7},{4,8},{5,9},{6,10},{7,11},{8,12},{9,13},{1... | collective-permute-start | bytes 196616 | tf_op jit(solution)/shard_map/ppermute | solution.py:202
  5.6 2.2 %collective-permute-start.2 = (bf16[8,4096]{1,0:T(8,128)(2,1)}, bf16[8,4096]{1,0:T(8,128)(2,1)S(1)}, u32[]{:S(2)}, u32[]{:S(2)}) collective-permute-start(bf16[8,4096]{1,0:T(8,128)(2,1)} %param.9), channel_id=1, source_target_pairs={{0,12},{1,13},{2,14},{3,15},{4,0},{5,1},{6,2},{7,3},{8,4},{9,5},{1... | collective-permute-start | bytes 196616 | tf_op jit(solution)/shard_map/ppermute | solution.py:202
  7.9 9.7 %project.1 = (f32[128,512]{1,0:T(8,128)}, f32[64,128]{1,0:T(8,128)}) custom-call(bf16[512,4096]{1,0:T(8,128)(2,1)} %acts.1, bf16[512,4096]{1,0:T(8,128)(2,1)} %grads.1, bf16[64,4096]{1,0:T(8,128)(2,1)} %bitcast.2, bf16[64,4096]{1,0:T(8,128)(2,1)} %bitcast.3), custom_call_target="tpu_custom_call" | custom-call | flops 536870912 | bytes 8388608 | tf_op jit(solution)/shard_map/project/pallas_call | solution.py:63
  17.6 0.2 collective-permute-start.5
  17.8 1.5 %collective-permute-start.4 = (f32[64,128]{1,0:T(8,128)}, f32[64,128]{1,0:T(8,128)S(1)}, u32[]{:S(2)}, u32[]{:S(2)}) collective-permute-start(f32[64,128]{1,0:T(8,128)} %get-tuple-element.15), channel_id=1, source_target_pairs={{0,2},{1,3},{2,0},{3,1},{4,6},{5,7},{6,4},{7,5},{8,10},{9,11},{10,... | collective-permute-start | bytes 98312 | tf_op jit(solution)/shard_map/ppermute | solution.py:202
  19.2 0.2 collective-permute-start.3
  19.5 0.2 collective-permute-done.5
  19.7 2.3 %collective-permute-done.4 = f32[64,128]{1,0:T(8,128)S(1)} collective-permute-done((f32[64,128]{1,0:T(8,128)}, f32[64,128]{1,0:T(8,128)S(1)}, u32[]{:S(2)}, u32[]{:S(2)}) %collective-permute-start.4) | collective-permute-done | bytes 32800 | tf_op jit(solution)/shard_map/ppermute | solution.py:202
  22.0 0.8 %collective-permute-done.3 = f32[64,128]{1,0:T(8,128)S(1)} collective-permute-done((f32[64,128]{1,0:T(8,128)}, f32[64,128]{1,0:T(8,128)S(1)}, u32[]{:S(2)}, u32[]{:S(2)}) %collective-permute-start.3) | collective-permute-done | bytes 32800 | tf_op jit(solution)/shard_map/ppermute | solution.py:202
  22.8 0.8 %add_add_fusion.refs_0_ = f32[64,128]{1,0:T(8,128)S(1)} fusion(f32[64,128]{1,0:T(8,128)S(1)} %collective-permute-done.5, f32[64,128]{1,0:T(8,128)S(1)} %collective-permute-done.4, f32[64,128]{1,0:T(8,128)} %get-tuple-element.15, f32[64,128]{1,0:T(8,128)S(1)} %collective-permute-done.3), kind=kLoop, calls=%fused_computation | loop fusion | flops 24576 | bytes 163840 | tf_op jit(solution)/shard_map/add | solution.py:233
  23.6 0.1 collective-permute-start.8
  23.6 1.2 %collective-permute-start.7 = (f32[64,128]{1,0:T(8,128)S(1)}, f32[64,128]{1,0:T(8,128)S(1)}, u32[]{:S(2)}, u32[]{:S(2)}) collective-permute-start(f32[64,128]{1,0:T(8,128)S(1)} %add_add_fusion.refs_0_), channel_id=1, source_target_pairs={{0,8},{1,9},{2,10},{3,11},{4,12},{5,13},{6,14},{7,15},{8,0},{9,1},... | collective-permute-start | bytes 98312 | tf_op jit(solution)/shard_map/ppermute | solution.py:202
  24.9 0.8 %collective-permute-start.6 = (f32[64,128]{1,0:T(8,128)S(1)}, f32[64,128]{1,0:T(8,128)S(1)}, u32[]{:S(2)}, u32[]{:S(2)}) collective-permute-start(f32[64,128]{1,0:T(8,128)S(1)} %add_add_fusion.refs_0_), channel_id=1, source_target_pairs={{0,4},{1,5},{2,6},{3,7},{4,8},{5,9},{6,10},{7,11},{8,12},{9,13},{1... | collective-permute-start | bytes 98312 | tf_op jit(solution)/shard_map/ppermute | solution.py:202
  25.7 0.9 %collective-permute-start.9 = (bf16[32,4096]{1,0:T(8,128)(2,1)S(1)}, bf16[32,4096]{1,0:T(8,128)(2,1)S(1)}, u32[]{:S(2)}, u32[]{:S(2)}) collective-permute-start(bf16[32,4096]{1,0:T(8,128)(2,1)S(1)} %constant_dynamic-update-slice_fusion), channel_id=1, source_target_pairs={{0,2},{1,3},{2,0},{3,1},{4,6},{5,7},{6,4},{7,5},{8,10},{9,11},{10,... | collective-permute-start | bytes 786440 | tf_op jit(solution)/shard_map/ppermute | solution.py:202
  26.6 1.0 %collective-permute-done.8.refs_3_ = f32[64,128]{1,0:T(8,128)S(1)} collective-permute-done((f32[64,128]{1,0:T(8,128)S(1)}, f32[64,128]{1,0:T(8,128)S(1)}, u32[]{:S(2)}, u32[]{:S(2)}) %collective-permute-start.8) | collective-permute-done | bytes 32800 | tf_op jit(solution)/shard_map/ppermute | solution.py:202
  27.5 1.0 %collective-permute-done.7.refs_2_ = f32[64,128]{1,0:T(8,128)S(1)} collective-permute-done((f32[64,128]{1,0:T(8,128)S(1)}, f32[64,128]{1,0:T(8,128)S(1)}, u32[]{:S(2)}, u32[]{:S(2)}) %collective-permute-start.7) | collective-permute-done | bytes 32800 | tf_op jit(solution)/shard_map/ppermute | solution.py:202
  28.5 2.1 %collective-permute-done.6.refs_1_ = f32[64,128]{1,0:T(8,128)S(1)} collective-permute-done((f32[64,128]{1,0:T(8,128)S(1)}, f32[64,128]{1,0:T(8,128)S(1)}, u32[]{:S(2)}, u32[]{:S(2)}) %collective-permute-start.6) | collective-permute-done | bytes 32800 | tf_op jit(solution)/shard_map/ppermute | solution.py:202
  30.6 1.7 %collective-permute-done.9 = bf16[32,4096]{1,0:T(8,128)(2,1)S(1)} collective-permute-done((bf16[32,4096]{1,0:T(8,128)(2,1)S(1)}, bf16[32,4096]{1,0:T(8,128)(2,1)S(1)}, u32[]{:S(2)}, u32[]{:S(2)}) %collective-permute-start.9) | collective-permute-done | bytes 262176 | tf_op jit(solution)/shard_map/ppermute | solution.py:202
  32.3 0.1 collective-permute-start.10
  32.4 0.0 copy-start
  32.4 0.9 %copy-done = f32[128,512]{1,0:T(8,128)S(1)} copy-done((f32[128,512]{1,0:T(8,128)S(1)}, f32[128,512]{1,0:T(8,128)}, u32[]{:S(2)}) %copy-start) | copy-done | bytes 262168
  33.3 5.9 %precondition.1.moved = f32[128,512]{1,0:T(8,128)S(1)} custom-call(f32[64,128]{1,0:T(8,128)S(1)} %add_add_fusion.refs_0_, f32[64,128]{1,0:T(8,128)S(1)} %collective-permute-done.6.refs_1_, f32[64,128]{1,0:T(8,128)S(1)} %collective-permute-done.7.refs_2_, f32[64,128]{1,0:T(8,128)S(1)} %collective-permute-done.8.refs_3_, f32[128,512]{1,0:T(8,128)S(1)} %copy-done), custom_call_target="tpu_custom_call" | custom-call | flops 3355443200 | bytes 524288 | tf_op jit(solution)/shard_map/precondition/pallas_call | solution.py:122
  39.3 3.9 %score.1 = f32[512,128]{1,0:T(8,128)} custom-call(f32[128,512]{1,0:T(8,128)S(1)} %precondition.1.moved, bf16[64,4096]{1,0:T(8,128)(2,1)S(1)} %constant_dynamic-update-slice_fusion.4.refs_0_, bf16[64,4096]{1,0:T(8,128)(2,1)S(1)} %collective-permute-done.10.refs_1_), custom_call_target="tpu_custom_call" | custom-call | tf_op jit(solution)/shard_map/score/pallas_call | solution.py:167
  (12 shorter events, 0.1 us)
Async XLA Ops:
  0.0 17.6 %collective-permute-start.1 = (bf16[8,4096]{1,0:T(8,128)(2,1)}, bf16[8,4096]{1,0:T(8,128)(2,1)S(1)}, u32[]{:S(2)}, u32[]{:S(2)}) collective-permute-start(bf16[8,4096]{1,0:T(8,128)(2,1)} %param.9), channel_id=1, source_target_pairs={{0,8},{1,9},{2,10},{3,11},{4,12},{5,13},{6,14},{7,15},{8,0},{9,1},... | collective-permute-start | bytes 196616 | tf_op jit(solution)/shard_map/ppermute | solution.py:202
  4.0 13.5 %collective-permute-start = (bf16[8,4096]{1,0:T(8,128)(2,1)}, bf16[8,4096]{1,0:T(8,128)(2,1)S(1)}, u32[]{:S(2)}, u32[]{:S(2)}) collective-permute-start(bf16[8,4096]{1,0:T(8,128)(2,1)} %param.9), channel_id=1, source_target_pairs={{0,4},{1,5},{2,6},{3,7},{4,8},{5,9},{6,10},{7,11},{8,12},{9,13},{1... | collective-permute-start | bytes 196616 | tf_op jit(solution)/shard_map/ppermute | solution.py:202
  5.6 12.0 %collective-permute-start.2 = (bf16[8,4096]{1,0:T(8,128)(2,1)}, bf16[8,4096]{1,0:T(8,128)(2,1)S(1)}, u32[]{:S(2)}, u32[]{:S(2)}) collective-permute-start(bf16[8,4096]{1,0:T(8,128)(2,1)} %param.9), channel_id=1, source_target_pairs={{0,12},{1,13},{2,14},{3,15},{4,0},{5,1},{6,2},{7,3},{8,4},{9,5},{1... | collective-permute-start | bytes 196616 | tf_op jit(solution)/shard_map/ppermute | solution.py:202
  7.9 11.6 %copy-start.1 = (bf16[8,4096]{1,0:T(8,128)(2,1)S(1)}, bf16[8,4096]{1,0:T(8,128)(2,1)}, u32[]{:S(2)}) copy-start(bf16[8,4096]{1,0:T(8,128)(2,1)} %param.9) | copy-start | bytes 196612
  17.6 2.1 %collective-permute-start.5 = (f32[64,128]{1,0:T(8,128)}, f32[64,128]{1,0:T(8,128)S(1)}, u32[]{:S(2)}, u32[]{:S(2)}) collective-permute-start(f32[64,128]{1,0:T(8,128)} %get-tuple-element.15), channel_id=1, source_target_pairs={{0,3},{1,0},{2,1},{3,2},{4,7},{5,4},{6,5},{7,6},{8,11},{9,8},{10,9... | collective-permute-start | bytes 98312 | tf_op jit(solution)/shard_map/ppermute | solution.py:202
  17.8 4.2 %collective-permute-start.4 = (f32[64,128]{1,0:T(8,128)}, f32[64,128]{1,0:T(8,128)S(1)}, u32[]{:S(2)}, u32[]{:S(2)}) collective-permute-start(f32[64,128]{1,0:T(8,128)} %get-tuple-element.15), channel_id=1, source_target_pairs={{0,2},{1,3},{2,0},{3,1},{4,6},{5,7},{6,4},{7,5},{8,10},{9,11},{10,... | collective-permute-start | bytes 98312 | tf_op jit(solution)/shard_map/ppermute | solution.py:202
  19.2 3.6 %collective-permute-start.3 = (f32[64,128]{1,0:T(8,128)}, f32[64,128]{1,0:T(8,128)S(1)}, u32[]{:S(2)}, u32[]{:S(2)}) collective-permute-start(f32[64,128]{1,0:T(8,128)} %get-tuple-element.15), channel_id=1, source_target_pairs={{0,1},{1,2},{2,3},{3,0},{4,5},{5,6},{6,7},{7,4},{8,9},{9,10},{10,1... | collective-permute-start | bytes 98312 | tf_op jit(solution)/shard_map/ppermute | solution.py:202
  23.6 4.0 %collective-permute-start.8 = (f32[64,128]{1,0:T(8,128)S(1)}, f32[64,128]{1,0:T(8,128)S(1)}, u32[]{:S(2)}, u32[]{:S(2)}) collective-permute-start(f32[64,128]{1,0:T(8,128)S(1)} %add_add_fusion.refs_0_), channel_id=1, source_target_pairs={{0,12},{1,13},{2,14},{3,15},{4,0},{5,1},{6,2},{7,3},{8,4},{9,5},{1... | collective-permute-start | bytes 98312 | tf_op jit(solution)/shard_map/ppermute | solution.py:202
  23.6 4.9 %collective-permute-start.7 = (f32[64,128]{1,0:T(8,128)S(1)}, f32[64,128]{1,0:T(8,128)S(1)}, u32[]{:S(2)}, u32[]{:S(2)}) collective-permute-start(f32[64,128]{1,0:T(8,128)S(1)} %add_add_fusion.refs_0_), channel_id=1, source_target_pairs={{0,8},{1,9},{2,10},{3,11},{4,12},{5,13},{6,14},{7,15},{8,0},{9,1},... | collective-permute-start | bytes 98312 | tf_op jit(solution)/shard_map/ppermute | solution.py:202
  24.9 5.7 %collective-permute-start.6 = (f32[64,128]{1,0:T(8,128)S(1)}, f32[64,128]{1,0:T(8,128)S(1)}, u32[]{:S(2)}, u32[]{:S(2)}) collective-permute-start(f32[64,128]{1,0:T(8,128)S(1)} %add_add_fusion.refs_0_), channel_id=1, source_target_pairs={{0,4},{1,5},{2,6},{3,7},{4,8},{5,9},{6,10},{7,11},{8,12},{9,13},{1... | collective-permute-start | bytes 98312 | tf_op jit(solution)/shard_map/ppermute | solution.py:202
  25.7 6.6 %collective-permute-start.9 = (bf16[32,4096]{1,0:T(8,128)(2,1)S(1)}, bf16[32,4096]{1,0:T(8,128)(2,1)S(1)}, u32[]{:S(2)}, u32[]{:S(2)}) collective-permute-start(bf16[32,4096]{1,0:T(8,128)(2,1)S(1)} %constant_dynamic-update-slice_fusion), channel_id=1, source_target_pairs={{0,2},{1,3},{2,0},{3,1},{4,6},{5,7},{6,4},{7,5},{8,10},{9,11},{10,... | collective-permute-start | bytes 786440 | tf_op jit(solution)/shard_map/ppermute | solution.py:202
  32.3 7.0 %collective-permute-start.10 = (bf16[64,4096]{1,0:T(8,128)(2,1)S(1)}, bf16[64,4096]{1,0:T(8,128)(2,1)S(1)}, u32[]{:S(2)}, u32[]{:S(2)}) collective-permute-start(bf16[64,4096]{1,0:T(8,128)(2,1)S(1)} %constant_dynamic-update-slice_fusion.4.refs_0_), channel_id=1, source_target_pairs={{0,1},{1,0},{2,3},{3,2},{4,5},{5,4},{6,7},{7,6},{8,9},{9,8},{10,11... | collective-permute-start | bytes 1572872 | tf_op jit(solution)/shard_map/ppermute | solution.py:202
  32.4 1.0 %copy-start = (f32[128,512]{1,0:T(8,128)S(1)}, f32[128,512]{1,0:T(8,128)}, u32[]{:S(2)}) copy-start(f32[128,512]{1,0:T(8,128)} %get-tuple-element.16.refs_4_) | copy-start | bytes 786436

commit v3 on v2

--- a/solution.py
+++ b/solution.py
@@ -9,7 +9,8 @@
 
 DAMP = 0.1
 HIGHEST = lax.Precision.HIGHEST
-CHUNKS = 8
+COPY_ROWS = 128
+DOT_ROWS = 256
 
 
 def dot_nt(left, right, precision=None):
@@ -19,67 +20,69 @@
 
 
 def project_kernel(acts, grads, proj_act, proj_grad, proj_t, cov, tok_buf, weight_buf, tok_sems, weight_sems):
-    factor, width = proj_act.shape
-    step = width // CHUNKS
+    factor = proj_act.shape[0]
+    tok_rows = acts.shape[0]
     weight_copies = [
-        pltpu.make_async_copy(src, weight_buf.at[at, pl.ds(at * factor, factor), :], weight_sems.at[at])
-        for at, src in enumerate((proj_act, proj_grad))
+        pltpu.make_async_copy(src, weight_buf.at[at], weight_sems.at[at]) for at, src in enumerate((proj_act, proj_grad))
     ]
     tok_copies = [
         [
             pltpu.make_async_copy(
-                src.at[:, pl.ds(part * step, step)], tok_buf.at[at, part], tok_sems.at[at, part]
+                src.at[pl.ds(part * COPY_ROWS, COPY_ROWS), :],
+                tok_buf.at[at, pl.ds(part * COPY_ROWS, COPY_ROWS), :],
+                tok_sems.at[at, part],
             )
-            for at, src in enumerate((acts, grads))
+            for part in range(tok_rows // COPY_ROWS)
         ]
-        for part in range(CHUNKS)
+        for at, src in enumerate((acts, grads))
     ]
-    for copy in weight_copies:
-        copy.start()
-    for pair in tok_copies:
-        for copy in pair:
+    for at in range(2):
+        weight_copies[at].start()
+        for copy in tok_copies[at]:
             copy.start()
-    blank = jnp.zeros((factor, width), weight_buf.dtype)
-    weight_buf[0, factor:, :] = blank
-    weight_buf[1, :factor, :] = blank
-    for copy in weight_copies:
-        copy.wait()
-    both = None
-    for part in range(CHUNKS):
-        for at in range(2):
-            tok_copies[part][at].wait()
-            term = dot_nt(tok_buf[at, part], weight_buf[at, :, part * step : (part + 1) * step])
-            both = term if both is None else both + term
-    flipped = both.T
-    proj_t[...] = flipped
-    gram = jnp.dot(flipped, both, precision=HIGHEST, preferred_element_type=jnp.float32)
+    for at in range(2):
+        weight_copies[at].wait()
+        for first in range(0, tok_rows, DOT_ROWS):
+            for part in range(first // COPY_ROWS, (first + DOT_ROWS) // COPY_ROWS):
+                tok_copies[at][part].wait()
+            proj_t[at * factor : (at + 1) * factor, first : first + DOT_ROWS] = dot_nt(
+                weight_buf[at], tok_buf[at, first : first + DOT_ROWS, :]
+            )
+    both = proj_t[...]
+    gram = dot_nt(both, both, HIGHEST)
     lane = lax.broadcasted_iota(jnp.int32, (factor, 2 * factor), 1)
-    cov[...] = jnp.where(lane < factor, gram[:factor, :], gram[factor:, :])
-
-
-def project(acts, grads, proj_act, proj_grad):
+    paired = jnp.where(lane < factor, gram[:factor, :], gram[factor:, :])
+    step = cov.shape[1]
+    for at in range(cov.shape[0]):
+        cov[at] = paired[at * step : (at + 1) * step, :]
+
+
+def project(n_slices, acts, grads, proj_act, proj_grad):
     tok_rows, width = acts.shape
     factor = proj_act.shape[1]
+    operands = [
+        pltpu.with_memory_space_constraint(value, pltpu.HBM) for value in (acts, grads, proj_act.T, proj_grad.T)
+    ]
     return pl.pallas_call(
         project_kernel,
         out_shape=(
             jax.ShapeDtypeStruct((2 * factor, tok_rows), jnp.float32),
-            jax.ShapeDtypeStruct((factor, 2 * factor), jnp.float32),
+            jax.ShapeDtypeStruct((n_slices, factor // n_slices, 2 * factor), jnp.float32),
         ),
         in_specs=[pl.BlockSpec(memory_space=pltpu.HBM)] * 4,
         out_specs=[pl.BlockSpec(memory_space=pltpu.VMEM)] * 2,
         scratch_shapes=[
-            pltpu.VMEM((2, CHUNKS, tok_rows, width // CHUNKS), acts.dtype),
-            pltpu.VMEM((2, 2 * factor, width), proj_act.dtype),
-            pltpu.SemaphoreType.DMA((2, CHUNKS)),
+            pltpu.VMEM((2, tok_rows, width), acts.dtype),
+            pltpu.VMEM((2, factor, width), proj_act.dtype),
+            pltpu.SemaphoreType.DMA((2, tok_rows // COPY_ROWS)),
             pltpu.SemaphoreType.DMA((2,)),
         ],
-        compiler_params=pltpu.CompilerParams(vmem_limit_bytes=60 * 2**20),
+        compiler_params=pltpu.CompilerParams(vmem_limit_bytes=24 * 2**20),
         cost_estimate=pl.CostEstimate(
             flops=4 * tok_rows * width * factor, bytes_accessed=4 * tok_rows * width, transcendentals=0
         ),
         name="project",
-    )(acts, grads, proj_act.T, proj_grad.T)
+    )(*operands)
 
 
 def inverse_pair(both):
@@ -98,11 +101,10 @@
     return both
 
 
-def precondition_kernel(tok_total, n_terms, *refs):
-    terms, (proj_t, moved) = refs[:n_terms], refs[n_terms:]
-    both = terms[0][...]
-    for term in terms[1:]:
-        both = both + term[...]
+def precondition_kernel(tok_total, sums, proj_t, moved, proj_buf, sem):
+    copy = pltpu.make_async_copy(proj_t, proj_buf, sem)
+    copy.start()
+    both = jnp.concatenate([sums[at] for at in range(sums.shape[0])], axis=0)
     factor = both.shape[0]
     lane = lax.broadcasted_iota(jnp.int32, both.shape, 1)
     row_at = lax.broadcasted_iota(jnp.int32, both.shape, 0)
@@ -113,23 +115,24 @@
     blocks = jnp.concatenate(
         [jnp.where(left_half, both, 0.0), jnp.where(left_half, 0.0, both)], axis=0
     )
-    moved[...] = jnp.dot(blocks, proj_t[...], precision=HIGHEST, preferred_element_type=jnp.float32)
-
-
-def precondition(tok_total, terms, proj_t):
-    n_terms = len(terms)
+    copy.wait()
+    moved[...] = jnp.dot(blocks, proj_buf[...], precision=HIGHEST, preferred_element_type=jnp.float32)
+
+
+def precondition(tok_total, sums, proj_t):
     rows, tok_rows = proj_t.shape
     return pl.pallas_call(
-        functools.partial(precondition_kernel, tok_total, n_terms),
+        functools.partial(precondition_kernel, tok_total),
         out_shape=jax.ShapeDtypeStruct(proj_t.shape, jnp.float32),
-        in_specs=[pl.BlockSpec(memory_space=pltpu.VMEM)] * (n_terms + 1),
+        in_specs=[pl.BlockSpec(memory_space=pltpu.VMEM), pl.BlockSpec(memory_space=pl.ANY)],
         out_specs=pl.BlockSpec(memory_space=pltpu.VMEM),
+        scratch_shapes=[pltpu.VMEM(proj_t.shape, jnp.float32), pltpu.SemaphoreType.DMA],
         compiler_params=pltpu.CompilerParams(vmem_limit_bytes=24 * 2**20),
         cost_estimate=pl.CostEstimate(
             flops=400 * rows * rows * tok_rows, bytes_accessed=8 * rows * tok_rows, transcendentals=0
         ),
         name="precondition",
-    )(*terms, proj_t)
+    )(sums, proj_t)
 
 
 def score_kernel(size, n_pieces, moved, *refs):
@@ -185,54 +188,51 @@
     return [(core * near, rest // near), (core, near), (1, core)]
 
 
-def stages_of(size):
-    low = 1
-    while low * low < size:
-        low *= 2
-    if size % low:
-        return [(1, 1), (1, size)]
-    return [(1, low), (low, size // low)]
-
-
-def shifted(value, size, stride, radix, shift):
+def partner(digit, radix, shift):
+    return digit ^ shift if radix & (radix - 1) == 0 else (digit + shift) % radix
+
+
+def swapped(value, size, stride, radix, shift):
     perm = []
     for at in range(size):
         digit = at // stride % radix
-        perm.append((at, at + ((digit + shift) % radix - digit) * stride))
+        perm.append((at, at + (partner(digit, radix, shift) - digit) * stride))
     return lax.ppermute(value, "dp", perm)
-
-
-def after(value, other):
-    return lax.optimization_barrier((value, other))[0]
 
 
 def owners_of(me, size):
     owners = [me]
     for stride, radix in gather_stages(size):
         digit = lax.rem(lax.div(me, stride), radix)
-        steps = [(lax.rem(digit + (radix - shift), radix) - digit) * stride for shift in range(radix)]
+        back = [shift if radix & (radix - 1) == 0 else radix - shift for shift in range(radix)]
+        steps = [(partner(digit, radix, shift) - digit) * stride for shift in back]
         owners = [owner + step for step in steps for owner in owners]
     return owners
 
 
 def exchanged(held, size, stride, radix):
     mine = held[0] if len(held) == 1 else jnp.concatenate(held, axis=0)
-    return [mine] + [shifted(mine, size, stride, radix, shift) for shift in range(1, radix)]
+    return [mine] + [swapped(mine, size, stride, radix, shift) for shift in range(1, radix)]
 
 
 def on_device(acts, grads, proj_act, proj_grad, queries):
     size = lax.axis_size("dp")
+    factor = proj_act.shape[1]
     tok_total = acts.shape[0] * size
     far, near, core = gather_stages(size)
-    first, second = stages_of(size)
     pieces = exchanged([queries], size, *far)
-    proj_t, cov = project(acts, grads, proj_act, proj_grad)
+    sliced = factor % size == 0
+    proj_t, cov = project(size if sliced else 1, acts, grads, proj_act, proj_grad)
     *pieces, cov = lax.optimization_barrier((*pieces, cov))
-    terms = exchanged([cov], size, *first)
     pieces = exchanged(pieces, size, *near)
-    terms = exchanged([functools.reduce(jnp.add, terms)], size, *second)
-    pieces = exchanged([after(piece, terms) for piece in pieces], size, *core)
-    moved = precondition(tok_total, terms, proj_t)
+    if sliced:
+        mine = jnp.sum(lax.all_to_all(cov, "dp", 0, 0, tiled=True), axis=0)
+        *pieces, mine = lax.optimization_barrier((*pieces, mine))
+        sums = lax.all_to_all(jnp.broadcast_to(mine, cov.shape), "dp", 0, 0, tiled=True)
+    else:
+        sums = lax.psum(cov, "dp")
+    pieces = exchanged(pieces, size, *core)
+    moved = precondition(tok_total, sums, proj_t)
     return score(size, moved, pieces)
 
 

time: 43.5 us -> 46.8 us (1.076)
  blocking collectives: 0 us -> 20.6 us
  waiting for transfers between devices: 9.04 us -> 0.01 us
  starting transfers between devices: 12.7 us -> 7.49 us
  Pallas kernels: 19.5 us -> 18.2 us
  local copies, waits for them, and re-layouts: 1.01 us -> 0.07 us
  other arithmetic: 0.77 us -> 0.03 us
    all_to_all x0 -> x2, blocking collectives: none -> 20.6 us  [the longest x1 11.4 us: on_device(): mine = jnp.sum(lax.all_to_all(cov, 'dp', 0, 0, tiled=True), axis=0)]
    ppermute x11 -> x5, waiting for transfers between devices: 9.04 us -> 0.01 us  [swapped(): return lax.ppermute(value, 'dp', perm)]
    ppermute x11 -> x5, starting transfers between devices: 12.7 us -> 7.49 us  [swapped(): return lax.ppermute(value, 'dp', perm)]
    pallas_call x1, Pallas kernels: 9.69 us -> 8.05 us  [project(): pl.pallas_call(project_kernel, out_shape=(jax.ShapeDtypeStruct((2 * facto...]
    unnamed x8 -> x6, local copies, waits for them, and re-layouts: 0.99 us -> 0.04 us
    add x1 -> x0, other arithmetic: 0.77 us -> none  [on_device(): terms = exchanged([functools.reduce(jnp.add, terms)], size, *second)]
  transfers between devices with their start and end apart: 11 -> 5, of which waited for: 7 -> 0; matrix products, arithmetic and copies ran while one was open for 0% -> 0% of each run, Pallas kernels for 36% -> 31%
where the time goes in v3:
time: 46.8 us; the launch traced here: 46.5 us
  blocking collectives  20.6 us (44%)
  Pallas kernels  18.2 us (39%)
  starting transfers between devices  7.49 us (16%)
    all_to_all x1, blocking collectives, on_device(): mine = jnp.sum(lax.all_to_all(cov, 'dp', 0, 0, tiled=True), axis=0)  11.4 us
    all_to_all x1, blocking collectives, on_device(): lax.all_to_all(jnp.broadcast_to(mine, cov.shape), 'dp', 0, 0, tiled=True)  9.2 us
    pallas_call x1, Pallas kernels, project(): pl.pallas_call(project_kernel, out_shape=(jax.ShapeDtypeStruct((2 * facto...  8.05 us
    ppermute x5, starting transfers between devices, swapped(): return lax.ppermute(value, 'dp', perm)  7.49 us
    pallas_call x1, Pallas kernels, precondition(): pl.pallas_call(functools.partial(precondition_kernel, tok_total), out_sha...  6.24 us
    pallas_call x1, Pallas kernels, score(): pl.pallas_call(functools.partial(score_kernel, size, n_pieces), out_shape...  3.93 us
  transfers between devices with their start and end apart: 5, of which 0 were waited for; matrix products, arithmetic and copies ran while one was open for 0% of the time, Pallas kernels for 31%

profile of v3, /device:TPU:0, one launch (start us, length us, event | category | flops | bytes accessed | tf_op | source)
XLA Modules:
  0.0 46.5 jit_solution(12275613817489059387)
XLA Ops:
  0.0 4.0 %collective-permute-start.1 = (bf16[8,4096]{1,0:T(8,128)(2,1)}, bf16[8,4096]{1,0:T(8,128)(2,1)S(1)}, u32[]{:S(2)}, u32[]{:S(2)}) collective-permute-start(bf16[8,4096]{1,0:T(8,128)(2,1)} %param.9), channel_id=1, source_target_pairs={{0,8},{1,9},{2,10},{3,11},{4,12},{5,13},{6,14},{7,15},{8,0},{9,1},... | collective-permute-start | bytes 196616 | tf_op jit(solution)/shard_map/ppermute | solution.py:200
  4.0 1.6 %collective-permute-start = (bf16[8,4096]{1,0:T(8,128)(2,1)}, bf16[8,4096]{1,0:T(8,128)(2,1)S(1)}, u32[]{:S(2)}, u32[]{:S(2)}) collective-permute-start(bf16[8,4096]{1,0:T(8,128)(2,1)} %param.9), channel_id=1, source_target_pairs={{0,4},{1,5},{2,6},{3,7},{4,0},{5,1},{6,2},{7,3},{8,12},{9,13},{10,... | collective-permute-start | bytes 196616 | tf_op jit(solution)/shard_map/ppermute | solution.py:200
  5.6 0.0 collective-permute-start.2
  5.6 0.0 copy-start
  5.6 8.0 %project.1 = (f32[128,512]{1,0:T(8,128)S(1)}, f32[16,4,128]{2,1,0:T(4,128)S(1)}) custom-call(bf16[512,4096]{1,0:T(8,128)(2,1)} %acts.1, bf16[512,4096]{1,0:T(8,128)(2,1)} %grads.1, bf16[64,4096]{1,0:T(8,128)(2,1)} %bitcast.2, bf16[64,4096]{1,0:T(8,128)(2,1)} %bitcast.3), custom_call_target="tpu_custom_call" | custom-call | flops 536870912 | bytes 8388608 | tf_op jit(solution)/shard_map/project/pallas_call | solution.py:66
  13.7 0.0 collective-permute-done.1
  13.7 0.0 collective-permute-done
  13.7 0.0 collective-permute-done.2
  13.7 0.0 copy-done
  13.8 1.8 %collective-permute-start.3 = (bf16[32,4096]{1,0:T(8,128)(2,1)S(1)}, bf16[32,4096]{1,0:T(8,128)(2,1)S(1)}, u32[]{:S(2)}, u32[]{:S(2)}) collective-permute-start(bf16[32,4096]{1,0:T(8,128)(2,1)S(1)} %constant_dynamic-update-slice_fusion), channel_id=1, source_target_pairs={{0,2},{1,3},{2,0},{3,1},{4,6},{5,7},{6,4},{7,5},{8,10},{9,11},{10,... | collective-permute-start | bytes 786440 | tf_op jit(solution)/shard_map/ppermute | solution.py:200
  15.6 11.4 %all_to_all.10 = f32[16,4,128]{2,1,0:T(4,128)S(1)} all-to-all(f32[16,4,128]{2,1,0:T(4,128)S(1)} %get-tuple-element.20), channel_id=1, replica_groups=mesh['parts'=2,'dp'=16] {'dp'}, dimensions={0} | all-to-all | bytes 65536 | tf_op jit(solution)/shard_map/all_to_all | solution.py:229
  27.0 0.0 collective-permute-done.3
  27.1 0.1 collective-permute-start.4
  27.2 9.2 %all_to_all.11.sums = f32[16,4,128]{2,1,0:T(4,128)S(1)} all-to-all(f32[16,4,128]{2,1,0:T(4,128)S(1)} %broadcast_in_dim.3), channel_id=1, replica_groups=mesh['parts'=2,'dp'=16] {'dp'}, dimensions={0} | all-to-all | bytes 65536 | tf_op jit(solution)/shard_map/all_to_all | solution.py:231
  36.4 6.2 %precondition.1.moved = f32[128,512]{1,0:T(8,128)S(1)} custom-call(f32[16,4,128]{2,1,0:T(4,128)S(1)} %all_to_all.11.sums, f32[128,512]{1,0:T(8,128)S(1)} %get-tuple-element.22.proj_t), custom_call_target="tpu_custom_call" | custom-call | flops 3355443200 | bytes 524288 | tf_op jit(solution)/shard_map/precondition/pallas_call | solution.py:124
  42.6 0.0 collective-permute-done.4.refs_1_
  42.6 3.9 %score.1 = f32[512,128]{1,0:T(8,128)} custom-call(f32[128,512]{1,0:T(8,128)S(1)} %precondition.1.moved, bf16[64,4096]{1,0:T(8,128)(2,1)S(1)} %constant_dynamic-update-slice_fusion.4.refs_0_, bf16[64,4096]{1,0:T(8,128)(2,1)S(1)} %collective-permute-done.4.refs_1_), custom_call_target="tpu_custom_call" | custom-call | tf_op jit(solution)/shard_map/score/pallas_call | solution.py:170
  (8 shorter events, 0.1 us)
Async XLA Ops:
  0.0 13.7 %collective-permute-start.1 = (bf16[8,4096]{1,0:T(8,128)(2,1)}, bf16[8,4096]{1,0:T(8,128)(2,1)S(1)}, u32[]{:S(2)}, u32[]{:S(2)}) collective-permute-start(bf16[8,4096]{1,0:T(8,128)(2,1)} %param.9), channel_id=1, source_target_pairs={{0,8},{1,9},{2,10},{3,11},{4,12},{5,13},{6,14},{7,15},{8,0},{9,1},... | collective-permute-start | bytes 196616 | tf_op jit(solution)/shard_map/ppermute | solution.py:200
  4.0 9.6 %collective-permute-start = (bf16[8,4096]{1,0:T(8,128)(2,1)}, bf16[8,4096]{1,0:T(8,128)(2,1)S(1)}, u32[]{:S(2)}, u32[]{:S(2)}) collective-permute-start(bf16[8,4096]{1,0:T(8,128)(2,1)} %param.9), channel_id=1, source_target_pairs={{0,4},{1,5},{2,6},{3,7},{4,0},{5,1},{6,2},{7,3},{8,12},{9,13},{10,... | collective-permute-start | bytes 196616 | tf_op jit(solution)/shard_map/ppermute | solution.py:200
  5.6 8.1 %collective-permute-start.2 = (bf16[8,4096]{1,0:T(8,128)(2,1)}, bf16[8,4096]{1,0:T(8,128)(2,1)S(1)}, u32[]{:S(2)}, u32[]{:S(2)}) collective-permute-start(bf16[8,4096]{1,0:T(8,128)(2,1)} %param.9), channel_id=1, source_target_pairs={{0,12},{1,13},{2,14},{3,15},{4,8},{5,9},{6,10},{7,11},{8,4},{9,5},... | collective-permute-start | bytes 196616 | tf_op jit(solution)/shard_map/ppermute | solution.py:200
  5.6 8.1 %copy-start = (bf16[8,4096]{1,0:T(8,128)(2,1)S(1)}, bf16[8,4096]{1,0:T(8,128)(2,1)}, u32[]{:S(2)}) copy-start(bf16[8,4096]{1,0:T(8,128)(2,1)} %param.9) | copy-start | bytes 196612
  13.8 13.2 %collective-permute-start.3 = (bf16[32,4096]{1,0:T(8,128)(2,1)S(1)}, bf16[32,4096]{1,0:T(8,128)(2,1)S(1)}, u32[]{:S(2)}, u32[]{:S(2)}) collective-permute-start(bf16[32,4096]{1,0:T(8,128)(2,1)S(1)} %constant_dynamic-update-slice_fusion), channel_id=1, source_target_pairs={{0,2},{1,3},{2,0},{3,1},{4,6},{5,7},{6,4},{7,5},{8,10},{9,11},{10,... | collective-permute-start | bytes 786440 | tf_op jit(solution)/shard_map/ppermute | solution.py:200
  27.1 15.5 %collective-permute-start.4 = (bf16[64,4096]{1,0:T(8,128)(2,1)S(1)}, bf16[64,4096]{1,0:T(8,128)(2,1)S(1)}, u32[]{:S(2)}, u32[]{:S(2)}) collective-permute-start(bf16[64,4096]{1,0:T(8,128)(2,1)S(1)} %constant_dynamic-update-slice_fusion.4.refs_0_), channel_id=1, source_target_pairs={{0,1},{1,0},{2,3},{3,2},{4,5},{5,4},{6,7},{7,6},{8,9},{9,8},{10,11... | collective-permute-start | bytes 1572872 | tf_op jit(solution)/shard_map/ppermute | solution.py:200

commit v4 on v3

v4 whole, which is shorter than its diff:
```python
import functools

import jax
import jax.numpy as jnp
from jax import lax
from jax.experimental import pallas as pl
from jax.experimental.pallas import tpu as pltpu
from jax.sharding import PartitionSpec as P

DAMP = 0.1
HIGHEST = lax.Precision.HIGHEST
COPY_ROWS = 128
DOT_ROWS = 256
IN_FLIGHT = 2


def dot_nt(left, right, precision=None):
    return lax.dot_general(
        left, right, (((1,), (1,)), ((), ())), precision=precision, preferred_element_type=jnp.float32
    )


def project_kernel(tokens, weight, *refs):
    *before, proj_t, gram, tok_buf, weight_buf, tok_sems, weight_sem = refs
    tok_rows = tokens.shape[0]
    weight_copy = pltpu.make_async_copy(weight, weight_buf, weight_sem)
    copies = [
        pltpu.make_async_copy(
            tokens.at[pl.ds(part * COPY_ROWS, COPY_ROWS), :],
            tok_buf.at[pl.ds(part * COPY_ROWS, COPY_ROWS), :],
            tok_sems.at[part],
        )
        for part in range(tok_rows // COPY_ROWS)
    ]
    weight_copy.start()
    for copy in copies[:IN_FLIGHT]:
        copy.start()
    weight_copy.wait()
    for first in range(0, tok_rows, DOT_ROWS):
        for part in range(first // COPY_ROWS, (first + DOT_ROWS) // COPY_ROWS):
            copies[part].wait()
            if part + IN_FLIGHT < len(copies):
                copies[part + IN_FLIGHT].start()
        proj_t[:, first : first + DOT_ROWS] = dot_nt(weight_buf[...], tok_buf[first : first + DOT_ROWS, :])
    result = dot_nt(proj_t[...], proj_t[...], HIGHEST)
    gram[...] = jnp.concatenate([ref[...] for ref in before] + [result], axis=1)


def project(tokens, weight, *before):
    tok_rows, width = tokens.shape
    factor = weight.shape[1]
    operands = [pltpu.with_memory_space_constraint(value, pltpu.HBM) for value in (tokens, weight.T)]
    return pl.pallas_call(
        project_kernel,
        out_shape=(
            jax.ShapeDtypeStruct((factor, tok_rows), jnp.float32),
            jax.ShapeDtypeStruct((factor, (1 + len(before)) * factor), jnp.float32),
        ),
        in_specs=[pl.BlockSpec(memory_space=pltpu.HBM)] * 2
        + [pl.BlockSpec(memory_space=pltpu.VMEM)] * len(before),
        out_specs=[pl.BlockSpec(memory_space=pltpu.VMEM)] * 2,
        scratch_shapes=[
            pltpu.VMEM((tok_rows, width), tokens.dtype),
            pltpu.VMEM((factor, width), weight.dtype),
            pltpu.SemaphoreType.DMA((tok_rows // COPY_ROWS,)),
            pltpu.SemaphoreType.DMA,
        ],
        compiler_params=pltpu.CompilerParams(vmem_limit_bytes=24 * 2**20),
        cost_estimate=pl.CostEstimate(
            flops=2 * tok_rows * width * factor, bytes_accessed=2 * tok_rows * width, transcendentals=0
        ),
        name="project",
    )(*operands, *before)


def inverse_pair(both):
    factor = both.shape[0]
    tile = (8, both.shape[1])
    lane = lax.broadcasted_iota(jnp.int32, tile, 1)
    row_at = lax.broadcasted_iota(jnp.int32, tile, 0)
    left_half = lane < factor
    inner = jnp.where(left_half, lane, lane - factor)
    parts = [both[at : at + 8, :] for at in range(0, factor, 8)]

    def column(part, at):
        left = jnp.broadcast_to(part[:, at : at + 1], tile)
        right = jnp.broadcast_to(part[:, factor + at : factor + at + 1], tile)
        return jnp.where(left_half, left, right)

    def row(part, at):
        return jnp.broadcast_to(part[at : at + 1, :], tile)

    for k in range(0, factor, 4):
        home, off = divmod(k, 8)
        columns = [[column(part, k + a) for part in parts] for a in range(4)]
        pivot = [[row(columns[b][home], off + a) if a <= b else None for b in range(4)] for a in range(4)]
        p00, p01, p02, p03 = pivot[0]
        _, p11, p12, p13 = pivot[1]
        _, _, p22, p23 = pivot[2]
        p33 = pivot[3][3]
        on_block = (inner >= k) & (inner < k + 4)
        r0, r1, r2, r3 = [
            jnp.where(on_block, jnp.where(inner == k + a, 1.0, 0.0), row(parts[home], off + a)) for a in range(4)
        ]
        scale = 1.0 / (p00 * p11 - p01 * p01)
        e02 = scale * (p11 * p02 - p01 * p12)
        e03 = scale * (p11 * p03 - p01 * p13)
        e12 = scale * (p00 * p12 - p01 * p02)
        e13 = scale * (p00 * p13 - p01 * p03)
        s22 = p22 - (p02 * e02 + p12 * e12)
        s23 = p23 - (p02 * e03 + p12 * e13)
        s33 = p33 - (p03 * e03 + p13 * e13)
        scale_s = 1.0 / (s22 * s33 - s23 * s23)
        y0 = scale * (p11 * r0 - p01 * r1)
        y1 = scale * (p00 * r1 - p01 * r0)
        t2 = r2 - (p02 * y0 + p12 * y1)
        t3 = r3 - (p03 * y0 + p13 * y1)
        w2 = scale_s * (s33 * t2 - s23 * t3)
        w3 = scale_s * (s22 * t3 - s23 * t2)
        w0 = y0 - (e02 * w2 + e03 * w3)
        w1 = y1 - (e12 * w2 + e13 * w3)
        solved = (w0, w1, w2, w3)
        for m, part in enumerate(parts):
            change = (columns[0][m] * w0 + columns[1][m] * w1) + (columns[2][m] * w2 + columns[3][m] * w3)
            part = jnp.where(on_block, 0.0, part) - change
            if m == home:
                for a in range(4):
                    part = jnp.where(row_at == off + a, solved[a], part)
            parts[m] = part
    return jnp.concatenate(parts, axis=0)


def precondition_kernel(tok_total, n_terms, *refs):
    terms, (act_t, grad_t, moved) = refs[:n_terms], refs[n_terms:]
    both = terms[0][...]
    for term in terms[1:]:
        both = both + term[...]
    factor = both.shape[0]
    lane = lax.broadcasted_iota(jnp.int32, both.shape, 1)
    row_at = lax.broadcasted_iota(jnp.int32, both.shape, 0)
    left_half = lane < factor
    inner = jnp.where(left_half, lane, lane - factor)
    both = both / tok_total + jnp.where(inner == row_at, DAMP, 0.0)
    both = inverse_pair(both)
    blocks = jnp.concatenate(
        [jnp.where(left_half, both, 0.0), jnp.where(left_half, 0.0, both)], axis=0
    )
    proj_t = jnp.concatenate([act_t[...], grad_t[...]], axis=0)
    moved[...] = jnp.dot(blocks, proj_t, precision=HIGHEST, preferred_element_type=jnp.float32)


def precondition(tok_total, terms, act_t, grad_t):
    factor, tok_rows = act_t.shape
    n_terms = len(terms)
    return pl.pallas_call(
        functools.partial(precondition_kernel, tok_total, n_terms),
        out_shape=jax.ShapeDtypeStruct((2 * factor, tok_rows), jnp.float32),
        in_specs=[pl.BlockSpec(memory_space=pltpu.VMEM)] * (n_terms + 2),
        out_specs=pl.BlockSpec(memory_space=pltpu.VMEM),
        compiler_params=pltpu.CompilerParams(vmem_limit_bytes=24 * 2**20),
        cost_estimate=pl.CostEstimate(
            flops=1600 * factor * factor * tok_rows, bytes_accessed=16 * factor * tok_rows, transcendentals=0
        ),
        name="precondition",
    )(*terms, act_t, grad_t)


def score_kernel(size, n_pieces, moved, *refs):
    queries, (scores, total, ordered) = refs[:n_pieces], refs[n_pieces:]
    factor = moved.shape[0] // 2
    group = 4
    act_side = moved[:factor, :]
    for first in range(0, factor, group):
        outer = jnp.concatenate(
            [act_side * moved[factor + i : factor + i + 1, :] for i in range(first, first + group)], axis=0
        )
        high = outer.astype(jnp.bfloat16)
        low = (outer - high.astype(jnp.float32)).astype(jnp.bfloat16)
        columns = slice(first * factor, (first + group) * factor)
        values = jnp.concatenate([piece[:, columns] for piece in queries], axis=0)
        term = jnp.dot(
            jnp.concatenate([values, values], axis=1),
            jnp.concatenate([high, low], axis=0),
            preferred_element_type=jnp.float32,
        )
        if first == 0:
            total[...] = term
        else:
            total[...] += term
    rows = total.shape[0] // size
    for at, owner in enumerate(owners_of(lax.axis_index("dp"), size)):
        ordered[pl.ds(pl.multiple_of(owner * rows, rows), rows), :] = total[at * rows : (at + 1) * rows, :]
    scores[...] = ordered[...].T


def score(size, moved, queries):
    tok_rows = moved.shape[1]
    n_queries = sum(piece.shape[0] for piece in queries)
    n_pieces = len(queries)
    return pl.pallas_call(
        functools.partial(score_kernel, size, n_pieces),
        out_shape=jax.ShapeDtypeStruct((tok_rows, n_queries), jnp.float32),
        in_specs=[pl.BlockSpec(memory_space=pltpu.VMEM)] * (1 + n_pieces),
        out_specs=pl.BlockSpec(memory_space=pltpu.VMEM),
        scratch_shapes=[
            pltpu.VMEM((n_queries, tok_rows), jnp.float32),
            pltpu.VMEM((n_queries, tok_rows), jnp.float32),
        ],
        compiler_params=pltpu.CompilerParams(vmem_limit_bytes=32 * 2**20),
        name="score",
    )(moved, *queries)


def stages_of(size):
    if size & (size - 1):
        return [(1, size)]
    return [(size >> level, 2) for level in range(1, size.bit_length())]


def after(value, other):
    return lax.optimization_barrier((value, other))[0]


def partner(digit, radix, shift):
    return digit ^ shift if radix & (radix - 1) == 0 else (digit + shift) % radix


def swapped(value, size, stride, radix, shift):
    perm = []
    for at in range(size):
        digit = at // stride % radix
        perm.append((at, at + (partner(digit, radix, shift) - digit) * stride))
    return lax.ppermute(value, "dp", perm)


def owners_of(me, size):
    owners = [me]
    for stride, radix in stages_of(size):
        digit = lax.rem(lax.div(me, stride), radix)
        back = [shift if radix & (radix - 1) == 0 else radix - shift for shift in range(radix)]
        steps = [(partner(digit, radix, shift) - digit) * stride for shift in back]
        owners = [owner + step for step in steps for owner in owners]
    return owners


def exchanged(held, size, stride, radix):
    mine = held[0] if len(held) == 1 else jnp.concatenate(held, axis=0)
    return [mine] + [swapped(mine, size, stride, radix, shift) for shift in range(1, radix)]


def on_device(acts, grads, proj_act, proj_grad, queries):
    size = lax.axis_size("dp")
    tok_total = acts.shape[0] * size
    stages = stages_of(size)
    last = len(stages) - 1
    waiting = list(stages)
    pieces = exchanged([queries], size, *waiting.pop(0))
    act_t, gram = project(acts, proj_act)
    pieces = [after(piece, gram) for piece in pieces]
    if waiting:
        pieces = exchanged(pieces, size, *waiting.pop(0))
    grad_t, own = project(grads, proj_grad, gram)
    begins = [at * last // max(1, len(waiting) - 1) for at in range(len(waiting))]
    for level, stage in enumerate(stages):
        if level in begins:
            *pieces, own = lax.optimization_barrier((*pieces, own))
            pieces = exchanged(pieces, size, *waiting.pop(0))
        terms = exchanged([own], size, *stage)
        own = functools.reduce(jnp.add, terms)
    moved = precondition(tok_total, terms, act_t, grad_t)
    return score(size, moved, pieces)


def solution(mesh):
    in_specs = (P(("parts", "dp"), None), P(("parts", "dp"), None), P(), P(), P("dp", None))
    out_specs = P(("parts", "dp"), None)
    return jax.shard_map(
        on_device, mesh=mesh, in_specs=in_specs, out_specs=out_specs, check_vma=False
    )
```

time: 46.8 us -> 37.2 us (0.79)
  blocking collectives: 20.6 us -> 0 us
  waiting for transfers between devices: 0.01 us -> 11.9 us
  Pallas kernels: 18.2 us -> 14.6 us
  starting transfers between devices: 7.49 us -> 10.2 us
    all_to_all x2 -> x0, blocking collectives: 20.6 us -> none  [the longest x1 11.4 us: on_device(): mine = jnp.sum(lax.all_to_all(cov, 'dp', 0, 0, tiled=True), axis=0)]
    ppermute x5 -> x8, waiting for transfers between devices: 0.01 us -> 11.9 us  [swapped(): return lax.ppermute(value, 'dp', perm)]
    ppermute x5 -> x8, starting transfers between devices: 7.49 us -> 10.2 us  [swapped(): return lax.ppermute(value, 'dp', perm)]
    pallas_call x2 -> x3, Pallas kernels: 14.3 us -> 12.1 us  [the longest x2 9.01 us: project(): pl.pallas_call(project_kernel, out_shape=(jax.ShapeDtypeStruct((factor, t...]
    pallas_call x1, Pallas kernels: 3.93 us -> 2.46 us  [score(): pl.pallas_call(functools.partial(score_kernel, size, n_pieces), out_shape...]
  transfers between devices with their start and end apart: 5 -> 8, of which waited for: 0 -> 4; matrix products, arithmetic and copies ran while one was open for 0% -> 0% of each run, Pallas kernels for 31% -> 33%
where the time goes in v4:
time: 37.2 us; the launch traced here: 36.9 us
  Pallas kernels  14.6 us (39%)
  waiting for transfers between devices  11.9 us (32%)
  starting transfers between devices  10.2 us (27%)
    ppermute x8, waiting for transfers between devices, swapped(): return lax.ppermute(value, 'dp', perm)  11.9 us
    ppermute x8, starting transfers between devices, swapped(): return lax.ppermute(value, 'dp', perm)  10.2 us
    pallas_call x2, Pallas kernels, project(): pl.pallas_call(project_kernel, out_shape=(jax.ShapeDtypeStruct((factor, t...  9.01 us
    pallas_call x1, Pallas kernels, precondition(): pl.pallas_call(functools.partial(precondition_kernel, tok_total, n_terms)...  3.09 us
    pallas_call x1, Pallas kernels, score(): pl.pallas_call(functools.partial(score_kernel, size, n_pieces), out_shape...  2.46 us
  transfers between devices with their start and end apart: 8, of which 4 were waited for; matrix products, arithmetic and copies ran while one was open for 0% of the time, Pallas kernels for 33%

profile of v4, /device:TPU:0, one launch (start us, length us, event | category | flops | bytes accessed | tf_op | source)
XLA Modules:
  0.0 36.9 jit_solution(13648641889703156875)
XLA Ops:
  0.0 0.0 copy-start
  0.0 4.0 %collective-permute-start = (bf16[8,4096]{1,0:T(8,128)(2,1)}, bf16[8,4096]{1,0:T(8,128)(2,1)S(1)}, u32[]{:S(2)}, u32[]{:S(2)}) collective-permute-start(bf16[8,4096]{1,0:T(8,128)(2,1)} %param.9), channel_id=1, source_target_pairs={{0,8},{1,9},{2,10},{3,11},{4,12},{5,13},{6,14},{7,15},{8,0},{9,1},... | collective-permute-start | bytes 196616 | tf_op jit(solution)/shard_map/ppermute | solution.py:233
  4.0 4.5 %project.2 = (f32[64,512]{1,0:T(8,128)S(1)}, f32[64,64]{1,0:T(8,128)S(1)}) custom-call(bf16[512,4096]{1,0:T(8,128)(2,1)} %tokens.2, bf16[64,4096]{1,0:T(8,128)(2,1)} %bitcast.2), custom_call_target="tpu_custom_call" | custom-call | flops 268435456 | bytes 4194304 | tf_op jit(solution)/shard_map/project/pallas_call | solution.py:53
  8.5 0.0 copy-done
  8.5 0.0 collective-permute-done
  8.6 1.6 %collective-permute-start.1 = (bf16[16,4096]{1,0:T(8,128)(2,1)S(1)}, bf16[16,4096]{1,0:T(8,128)(2,1)S(1)}, u32[]{:S(2)}, u32[]{:S(2)}) collective-permute-start(bf16[16,4096]{1,0:T(8,128)(2,1)S(1)} %constant_dynamic-update-slice_fusion), channel_id=1, source_target_pairs={{0,4},{1,5},{2,6},{3,7},{4,0},{5,1},{6,2},{7,3},{8,12},{9,13},{10,... | collective-permute-start | bytes 393224 | tf_op jit(solution)/shard_map/ppermute | solution.py:233
  10.2 4.5 %project.3 = (f32[64,512]{1,0:T(8,128)S(1)}, f32[64,128]{1,0:T(8,128)S(1)}) custom-call(bf16[512,4096]{1,0:T(8,128)(2,1)} %tokens.3, bf16[64,4096]{1,0:T(8,128)(2,1)} %bitcast.3, f32[64,64]{1,0:T(8,128)S(1)} %get-tuple-element.17.refs_0_), custom_call_target="tpu_custom_call" | custom-call | flops 268435456 | bytes 4194304 | tf_op jit(solution)/shard_map/project/pallas_call | solution.py:53
  14.8 0.0 collective-permute-done.1
  14.8 1.6 %collective-permute-start.2 = (bf16[32,4096]{1,0:T(8,128)(2,1)S(1)}, bf16[32,4096]{1,0:T(8,128)(2,1)S(1)}, u32[]{:S(2)}, u32[]{:S(2)}) collective-permute-start(bf16[32,4096]{1,0:T(8,128)(2,1)S(1)} %constant_dynamic-update-slice_fusion.2), channel_id=1, source_target_pairs={{0,2},{1,3},{2,0},{3,1},{4,6},{5,7},{6,4},{7,5},{8,10},{9,11},{10,... | collective-permute-start | bytes 786440 | tf_op jit(solution)/shard_map/ppermute | solution.py:233
  16.4 1.6 %collective-permute-start.3 = (f32[64,128]{1,0:T(8,128)S(1)}, f32[64,128]{1,0:T(8,128)S(1)}, u32[]{:S(2)}, u32[]{:S(2)}) collective-permute-start(f32[64,128]{1,0:T(8,128)S(1)} %get-tuple-element.23), channel_id=1, source_target_pairs={{0,8},{1,9},{2,10},{3,11},{4,12},{5,13},{6,14},{7,15},{8,0},{9,1},... | collective-permute-start | bytes 98312 | tf_op jit(solution)/shard_map/ppermute | solution.py:233
  18.0 3.4 %collective-permute-done.3 = f32[64,128]{1,0:T(8,128)S(1)} collective-permute-done((f32[64,128]{1,0:T(8,128)S(1)}, f32[64,128]{1,0:T(8,128)S(1)}, u32[]{:S(2)}, u32[]{:S(2)}) %collective-permute-start.3) | collective-permute-done | bytes 32800 | tf_op jit(solution)/shard_map/ppermute | solution.py:233
  21.4 0.2 collective-permute-start.4
  21.7 3.7 %collective-permute-done.4 = f32[64,128]{1,0:T(8,128)S(1)} collective-permute-done((f32[64,128]{1,0:T(8,128)S(1)}, f32[64,128]{1,0:T(8,128)S(1)}, u32[]{:S(2)}, u32[]{:S(2)}) %collective-permute-start.4) | collective-permute-done | bytes 32800 | tf_op jit(solution)/shard_map/ppermute | solution.py:233
  25.4 0.5 %collective-permute-start.5 = (f32[64,128]{1,0:T(8,128)S(1)}, f32[64,128]{1,0:T(8,128)S(1)}, u32[]{:S(2)}, u32[]{:S(2)}) collective-permute-start(f32[64,128]{1,0:T(8,128)S(1)} %add.10), channel_id=1, source_target_pairs={{0,2},{1,3},{2,0},{3,1},{4,6},{5,7},{6,4},{7,5},{8,10},{9,11},{10,... | collective-permute-start | bytes 98312 | tf_op jit(solution)/shard_map/ppermute | solution.py:233
  25.9 3.4 %collective-permute-done.5 = f32[64,128]{1,0:T(8,128)S(1)} collective-permute-done((f32[64,128]{1,0:T(8,128)S(1)}, f32[64,128]{1,0:T(8,128)S(1)}, u32[]{:S(2)}, u32[]{:S(2)}) %collective-permute-start.5) | collective-permute-done | bytes 32800 | tf_op jit(solution)/shard_map/ppermute | solution.py:233
  29.3 0.0 collective-permute-done.2
  29.3 0.1 collective-permute-start.7
  29.4 0.5 %collective-permute-start.6 = (f32[64,128]{1,0:T(8,128)S(1)}, f32[64,128]{1,0:T(8,128)S(1)}, u32[]{:S(2)}, u32[]{:S(2)}) collective-permute-start(f32[64,128]{1,0:T(8,128)S(1)} %add.11.refs_0_), channel_id=1, source_target_pairs={{0,1},{1,0},{2,3},{3,2},{4,5},{5,4},{6,7},{7,6},{8,9},{9,8},{10,11... | collective-permute-start | bytes 98312 | tf_op jit(solution)/shard_map/ppermute | solution.py:233
  29.9 1.4 %collective-permute-done.6.refs_1_ = f32[64,128]{1,0:T(8,128)S(1)} collective-permute-done((f32[64,128]{1,0:T(8,128)S(1)}, f32[64,128]{1,0:T(8,128)S(1)}, u32[]{:S(2)}, u32[]{:S(2)}) %collective-permute-start.6) | collective-permute-done | bytes 32800 | tf_op jit(solution)/shard_map/ppermute | solution.py:233
  31.4 3.1 %precondition.1.moved = f32[128,512]{1,0:T(8,128)S(1)} custom-call(f32[64,128]{1,0:T(8,128)S(1)} %add.11.refs_0_, f32[64,128]{1,0:T(8,128)S(1)} %collective-permute-done.6.refs_1_, f32[64,512]{1,0:T(8,128)S(1)} %get-tuple-element.25.refs_2_, f32[64,512]{1,0:T(8,128)S(1)} %get-tuple-element.26.refs_3_), custom_call_target="tpu_custom_call" | custom-call | flops 3355443200 | bytes 524288 | tf_op jit(solution)/shard_map/precondition/pallas_call | solution.py:155
  34.5 0.0 collective-permute-done.7.refs_1_
  34.5 2.5 %score.1 = f32[512,128]{1,0:T(8,128)} custom-call(f32[128,512]{1,0:T(8,128)S(1)} %precondition.1.moved, bf16[64,4096]{1,0:T(8,128)(2,1)S(1)} %constant_dynamic-update-slice_fusion.4.refs_0_, bf16[64,4096]{1,0:T(8,128)(2,1)S(1)} %collective-permute-done.7.refs_1_), custom_call_target="tpu_custom_call" | custom-call | tf_op jit(solution)/shard_map/score/pallas_call | solution.py:200
  (9 shorter events, 0.1 us)
Async XLA Ops:
  0.0 8.5 %copy-start = (bf16[8,4096]{1,0:T(8,128)(2,1)S(1)}, bf16[8,4096]{1,0:T(8,128)(2,1)}, u32[]{:S(2)}) copy-start(bf16[8,4096]{1,0:T(8,128)(2,1)} %param.9) | copy-start | bytes 196612
  0.0 8.5 %collective-permute-start = (bf16[8,4096]{1,0:T(8,128)(2,1)}, bf16[8,4096]{1,0:T(8,128)(2,1)S(1)}, u32[]{:S(2)}, u32[]{:S(2)}) collective-permute-start(bf16[8,4096]{1,0:T(8,128)(2,1)} %param.9), channel_id=1, source_target_pairs={{0,8},{1,9},{2,10},{3,11},{4,12},{5,13},{6,14},{7,15},{8,0},{9,1},... | collective-permute-start | bytes 196616 | tf_op jit(solution)/shard_map/ppermute | solution.py:233
  8.6 6.2 %collective-permute-start.1 = (bf16[16,4096]{1,0:T(8,128)(2,1)S(1)}, bf16[16,4096]{1,0:T(8,128)(2,1)S(1)}, u32[]{:S(2)}, u32[]{:S(2)}) collective-permute-start(bf16[16,4096]{1,0:T(8,128)(2,1)S(1)} %constant_dynamic-update-slice_fusion), channel_id=1, source_target_pairs={{0,4},{1,5},{2,6},{3,7},{4,0},{5,1},{6,2},{7,3},{8,12},{9,13},{10,... | collective-permute-start | bytes 393224 | tf_op jit(solution)/shard_map/ppermute | solution.py:233
  14.8 14.5 %collective-permute-start.2 = (bf16[32,4096]{1,0:T(8,128)(2,1)S(1)}, bf16[32,4096]{1,0:T(8,128)(2,1)S(1)}, u32[]{:S(2)}, u32[]{:S(2)}) collective-permute-start(bf16[32,4096]{1,0:T(8,128)(2,1)S(1)} %constant_dynamic-update-slice_fusion.2), channel_id=1, source_target_pairs={{0,2},{1,3},{2,0},{3,1},{4,6},{5,7},{6,4},{7,5},{8,10},{9,11},{10,... | collective-permute-start | bytes 786440 | tf_op jit(solution)/shard_map/ppermute | solution.py:233
  16.4 5.0 %collective-permute-start.3 = (f32[64,128]{1,0:T(8,128)S(1)}, f32[64,128]{1,0:T(8,128)S(1)}, u32[]{:S(2)}, u32[]{:S(2)}) collective-permute-start(f32[64,128]{1,0:T(8,128)S(1)} %get-tuple-element.23), channel_id=1, source_target_pairs={{0,8},{1,9},{2,10},{3,11},{4,12},{5,13},{6,14},{7,15},{8,0},{9,1},... | collective-permute-start | bytes 98312 | tf_op jit(solution)/shard_map/ppermute | solution.py:233
  21.4 3.9 %collective-permute-start.4 = (f32[64,128]{1,0:T(8,128)S(1)}, f32[64,128]{1,0:T(8,128)S(1)}, u32[]{:S(2)}, u32[]{:S(2)}) collective-permute-start(f32[64,128]{1,0:T(8,128)S(1)} %add.9), channel_id=1, source_target_pairs={{0,4},{1,5},{2,6},{3,7},{4,0},{5,1},{6,2},{7,3},{8,12},{9,13},{10,... | collective-permute-start | bytes 98312 | tf_op jit(solution)/shard_map/ppermute | solution.py:233
  25.4 3.9 %collective-permute-start.5 = (f32[64,128]{1,0:T(8,128)S(1)}, f32[64,128]{1,0:T(8,128)S(1)}, u32[]{:S(2)}, u32[]{:S(2)}) collective-permute-start(f32[64,128]{1,0:T(8,128)S(1)} %add.10), channel_id=1, source_target_pairs={{0,2},{1,3},{2,0},{3,1},{4,6},{5,7},{6,4},{7,5},{8,10},{9,11},{10,... | collective-permute-start | bytes 98312 | tf_op jit(solution)/shard_map/ppermute | solution.py:233
  29.3 5.1 %collective-permute-start.7 = (bf16[64,4096]{1,0:T(8,128)(2,1)S(1)}, bf16[64,4096]{1,0:T(8,128)(2,1)S(1)}, u32[]{:S(2)}, u32[]{:S(2)}) collective-permute-start(bf16[64,4096]{1,0:T(8,128)(2,1)S(1)} %constant_dynamic-update-slice_fusion.4.refs_0_), channel_id=1, source_target_pairs={{0,1},{1,0},{2,3},{3,2},{4,5},{5,4},{6,7},{7,6},{8,9},{9,8},{10,11... | collective-permute-start | bytes 1572872 | tf_op jit(solution)/shard_map/ppermute | solution.py:233
  29.4 1.9 %collective-permute-start.6 = (f32[64,128]{1,0:T(8,128)S(1)}, f32[64,128]{1,0:T(8,128)S(1)}, u32[]{:S(2)}, u32[]{:S(2)}) collective-permute-start(f32[64,128]{1,0:T(8,128)S(1)} %add.11.refs_0_), channel_id=1, source_target_pairs={{0,1},{1,0},{2,3},{3,2},{4,5},{5,4},{6,7},{7,6},{8,9},{9,8},{10,11... | collective-permute-start | bytes 98312 | tf_op jit(solution)/shard_map/ppermute | solution.py:233

commit v5 on v4

--- a/solution.py
+++ b/solution.py
@@ -10,67 +10,82 @@
 DAMP = 0.1
 HIGHEST = lax.Precision.HIGHEST
 COPY_ROWS = 128
-DOT_ROWS = 256
 IN_FLIGHT = 2
 
 
-def dot_nt(left, right, precision=None):
-    return lax.dot_general(
-        left, right, (((1,), (1,)), ((), ())), precision=precision, preferred_element_type=jnp.float32
-    )
-
-
-def project_kernel(tokens, weight, *refs):
-    *before, proj_t, gram, tok_buf, weight_buf, tok_sems, weight_sem = refs
-    tok_rows = tokens.shape[0]
-    weight_copy = pltpu.make_async_copy(weight, weight_buf, weight_sem)
+def project_kernel(
+    acts, grads, weight_act, weight_grad, act_t, grad_t, cov, tok_buf, weight_buf, weight_t, tok_sems, weight_sems
+):
+    factor, width = weight_act.shape
+    n_parts = acts.shape[0] // COPY_ROWS
+    weight_copies = [
+        pltpu.make_async_copy(src, weight_buf.at[at], weight_sems.at[at])
+        for at, src in enumerate((weight_act, weight_grad))
+    ]
     copies = [
         pltpu.make_async_copy(
-            tokens.at[pl.ds(part * COPY_ROWS, COPY_ROWS), :],
-            tok_buf.at[pl.ds(part * COPY_ROWS, COPY_ROWS), :],
-            tok_sems.at[part],
+            src.at[pl.ds(part * COPY_ROWS, COPY_ROWS), :],
+            tok_buf.at[at, pl.ds(part * COPY_ROWS, COPY_ROWS), :],
+            tok_sems.at[at, part],
         )
-        for part in range(tok_rows // COPY_ROWS)
+        for at, src in enumerate((acts, grads))
+        for part in range(n_parts)
     ]
-    weight_copy.start()
-    for copy in copies[:IN_FLIGHT]:
+    for copy in weight_copies + copies[:IN_FLIGHT]:
         copy.start()
-    weight_copy.wait()
-    for first in range(0, tok_rows, DOT_ROWS):
-        for part in range(first // COPY_ROWS, (first + DOT_ROWS) // COPY_ROWS):
-            copies[part].wait()
-            if part + IN_FLIGHT < len(copies):
-                copies[part + IN_FLIGHT].start()
-        proj_t[:, first : first + DOT_ROWS] = dot_nt(weight_buf[...], tok_buf[first : first + DOT_ROWS, :])
-    result = dot_nt(proj_t[...], proj_t[...], HIGHEST)
-    gram[...] = jnp.concatenate([ref[...] for ref in before] + [result], axis=1)
-
-
-def project(tokens, weight, *before):
-    tok_rows, width = tokens.shape
-    factor = weight.shape[1]
-    operands = [pltpu.with_memory_space_constraint(value, pltpu.HBM) for value in (tokens, weight.T)]
+    grams = []
+    for at, out in enumerate((act_t, grad_t)):
+        weight_copies[at].wait()
+        for first in range(0, width, 512):
+            block = weight_buf[at, :, first : first + 512].astype(jnp.float32)
+            weight_t[at, first : first + 512, :] = block.T.astype(weight_t.dtype)
+        gram = None
+        part = 0
+        while part < n_parts:
+            many = 1 if at == 1 and part >= n_parts - 2 else min(2, n_parts - part)
+            for done in range(at * n_parts + part, at * n_parts + part + many):
+                copies[done].wait()
+                if done + IN_FLIGHT < len(copies):
+                    copies[done + IN_FLIGHT].start()
+            rows = slice(part * COPY_ROWS, (part + many) * COPY_ROWS)
+            block = jnp.dot(tok_buf[at, rows, :], weight_t[at], preferred_element_type=jnp.float32)
+            flipped = block.T
+            out[:, rows] = flipped
+            term = jnp.dot(flipped, block, precision=HIGHEST, preferred_element_type=jnp.float32)
+            gram = term if gram is None else gram + term
+            part += many
+        grams.append(gram)
+    cov[...] = jnp.concatenate(grams, axis=1)
+
+
+def project(acts, grads, proj_act, proj_grad):
+    tok_rows, width = acts.shape
+    factor = proj_act.shape[1]
+    operands = [
+        pltpu.with_memory_space_constraint(value, pltpu.HBM) for value in (acts, grads, proj_act.T, proj_grad.T)
+    ]
     return pl.pallas_call(
         project_kernel,
         out_shape=(
             jax.ShapeDtypeStruct((factor, tok_rows), jnp.float32),
-            jax.ShapeDtypeStruct((factor, (1 + len(before)) * factor), jnp.float32),
+            jax.ShapeDtypeStruct((factor, tok_rows), jnp.float32),
+            jax.ShapeDtypeStruct((factor, 2 * factor), jnp.float32),
         ),
-        in_specs=[pl.BlockSpec(memory_space=pltpu.HBM)] * 2
-        + [pl.BlockSpec(memory_space=pltpu.VMEM)] * len(before),
-        out_specs=[pl.BlockSpec(memory_space=pltpu.VMEM)] * 2,
+        in_specs=[pl.BlockSpec(memory_space=pltpu.HBM)] * 4,
+        out_specs=[pl.BlockSpec(memory_space=pltpu.VMEM)] * 3,
         scratch_shapes=[
-            pltpu.VMEM((tok_rows, width), tokens.dtype),
-            pltpu.VMEM((factor, width), weight.dtype),
-            pltpu.SemaphoreType.DMA((tok_rows // COPY_ROWS,)),
-            pltpu.SemaphoreType.DMA,
+            pltpu.VMEM((2, tok_rows, width), acts.dtype),
+            pltpu.VMEM((2, factor, width), proj_act.dtype),
+            pltpu.VMEM((2, width, factor), proj_act.dtype),
+            pltpu.SemaphoreType.DMA((2, tok_rows // COPY_ROWS)),
+            pltpu.SemaphoreType.DMA((2,)),
         ],
         compiler_params=pltpu.CompilerParams(vmem_limit_bytes=24 * 2**20),
         cost_estimate=pl.CostEstimate(
-            flops=2 * tok_rows * width * factor, bytes_accessed=2 * tok_rows * width, transcendentals=0
+            flops=4 * tok_rows * width * factor, bytes_accessed=4 * tok_rows * width, transcendentals=0
         ),
         name="project",
-    )(*operands, *before)
+    )(*operands)
 
 
 def inverse_pair(both):
@@ -211,10 +226,17 @@
     )(moved, *queries)
 
 
-def stages_of(size):
+def gather_stages(size):
     if size & (size - 1):
         return [(1, size)]
     return [(size >> level, 2) for level in range(1, size.bit_length())]
+
+
+def sum_rounds(size):
+    core = 2 if size % 2 == 0 else 1
+    rest = size // core
+    near = max(d for d in range(1, rest + 1) if rest % d == 0 and d * d <= rest)
+    return [(1, core * near), (core * near, rest // near)]
 
 
 def after(value, other):
@@ -235,7 +257,7 @@
 
 def owners_of(me, size):
     owners = [me]
-    for stride, radix in stages_of(size):
+    for stride, radix in gather_stages(size):
         digit = lax.rem(lax.div(me, stride), radix)
         back = [shift if radix & (radix - 1) == 0 else radix - shift for shift in range(radix)]
         steps = [(partner(digit, radix, shift) - digit) * stride for shift in back]
@@ -251,22 +273,22 @@
 def on_device(acts, grads, proj_act, proj_grad, queries):
     size = lax.axis_size("dp")
     tok_total = acts.shape[0] * size
-    stages = stages_of(size)
-    last = len(stages) - 1
-    waiting = list(stages)
-    pieces = exchanged([queries], size, *waiting.pop(0))
-    act_t, gram = project(acts, proj_act)
-    pieces = [after(piece, gram) for piece in pieces]
-    if waiting:
-        pieces = exchanged(pieces, size, *waiting.pop(0))
-    grad_t, own = project(grads, proj_grad, gram)
-    begins = [at * last // max(1, len(waiting) - 1) for at in range(len(waiting))]
-    for level, stage in enumerate(stages):
-        if level in begins:
-            *pieces, own = lax.optimization_barrier((*pieces, own))
-            pieces = exchanged(pieces, size, *waiting.pop(0))
-        terms = exchanged([own], size, *stage)
-        own = functools.reduce(jnp.add, terms)
+    stages = gather_stages(size)
+    first, second = sum_rounds(size)
+
+    def gathered(pieces, some):
+        for stage in some:
+            pieces = exchanged(pieces, size, *stage)
+        return pieces
+
+    pieces = gathered([queries], stages[:1])
+    act_t, grad_t, own = project(acts, grads, proj_act, proj_grad)
+    *pieces, own = lax.optimization_barrier((*pieces, own))
+    pieces = gathered(pieces, stages[1:2])
+    own = functools.reduce(jnp.add, exchanged([own], size, *first))
+    pieces = gathered([after(piece, own) for piece in pieces], stages[2:-1])
+    terms = exchanged([own], size, *second)
+    pieces = gathered([after(piece, terms) for piece in pieces], stages[max(2, len(stages) - 1) :])
     moved = precondition(tok_total, terms, act_t, grad_t)
     return score(size, moved, pieces)
 

time: 37.2 us -> 34.1 us (0.917)
  waiting for transfers between devices: 11.9 us -> 8.13 us
  starting transfers between devices: 10.2 us -> 12.9 us
  Pallas kernels: 14.6 us -> 12.7 us
    ppermute x8 -> x10, waiting for transfers between devices: 11.9 us -> 8.13 us  [swapped(): return lax.ppermute(value, 'dp', perm)]
    ppermute x8 -> x10, starting transfers between devices: 10.2 us -> 12.9 us  [swapped(): return lax.ppermute(value, 'dp', perm)]
    pallas_call x2 -> x1, Pallas kernels: 9.01 us -> 7.13 us  [project(): pl.pallas_call(project_kernel, out_shape=(jax.ShapeDtypeStruct((factor, t...]
  transfers between devices with their start and end apart: 8 -> 10, of which waited for: 4 -> 6; matrix products, arithmetic and copies ran while one was open for 0% -> 0% of each run, Pallas kernels for 33% -> 30%
where the time goes in v5:
time: 34.1 us; the launch traced here: 33.9 us
  starting transfers between devices  12.9 us (38%)
  Pallas kernels  12.7 us (37%)
  waiting for transfers between devices  8.13 us (24%)
    ppermute x10, starting transfers between devices, swapped(): return lax.ppermute(value, 'dp', perm)  12.9 us
    ppermute x10, waiting for transfers between devices, swapped(): return lax.ppermute(value, 'dp', perm)  8.13 us
    pallas_call x1, Pallas kernels, project(): pl.pallas_call(project_kernel, out_shape=(jax.ShapeDtypeStruct((factor, t...  7.13 us
    pallas_call x1, Pallas kernels, precondition(): pl.pallas_call(functools.partial(precondition_kernel, tok_total, n_terms)...  3.09 us
    pallas_call x1, Pallas kernels, score(): pl.pallas_call(functools.partial(score_kernel, size, n_pieces), out_shape...  2.46 us
  transfers between devices with their start and end apart: 10, of which 6 were waited for; matrix products, arithmetic and copies ran while one was open for 0% of the time, Pallas kernels for 30%

profile of v5, /device:TPU:0, one launch (start us, length us, event | category | flops | bytes accessed | tf_op | source)
XLA Modules:
  0.0 33.9 jit_solution(3166287489701917375)
XLA Ops:
  0.0 4.0 %collective-permute-start = (bf16[8,4096]{1,0:T(8,128)(2,1)}, bf16[8,4096]{1,0:T(8,128)(2,1)S(1)}, u32[]{:S(2)}, u32[]{:S(2)}) collective-permute-start(bf16[8,4096]{1,0:T(8,128)(2,1)} %param.9), channel_id=1, source_target_pairs={{0,8},{1,9},{2,10},{3,11},{4,12},{5,13},{6,14},{7,15},{8,0},{9,1},... | collective-permute-start | bytes 196616 | tf_op jit(solution)/shard_map/ppermute | solution.py:255
  4.0 7.1 %project.1 = (f32[64,512]{1,0:T(8,128)S(1)}, f32[64,512]{1,0:T(8,128)S(1)}, f32[64,128]{1,0:T(8,128)S(1)}) custom-call(bf16[512,4096]{1,0:T(8,128)(2,1)} %acts.1, bf16[512,4096]{1,0:T(8,128)(2,1)} %grads.1, bf16[64,4096]{1,0:T(8,128)(2,1)} %bitcast.2, bf16[64,4096]{1,0:T(8,128)(2,1)} %bitcast.3), custom_call_target="tpu_custom_call" | custom-call | flops 536870912 | bytes 8388608 | tf_op jit(solution)/shard_map/project/pallas_call | solution.py:67
  11.2 0.0 collective-permute-done
  11.2 0.7 %collective-permute-start.3 = (f32[64,128]{1,0:T(8,128)S(1)}, f32[64,128]{1,0:T(8,128)S(1)}, u32[]{:S(2)}, u32[]{:S(2)}) collective-permute-start(f32[64,128]{1,0:T(8,128)S(1)} %get-tuple-element.16), channel_id=1, source_target_pairs={{0,3},{1,2},{2,1},{3,0},{4,7},{5,6},{6,5},{7,4},{8,11},{9,10},{10,... | collective-permute-start | bytes 98312 | tf_op jit(solution)/shard_map/ppermute | solution.py:255
  11.9 0.9 %collective-permute-start.2 = (f32[64,128]{1,0:T(8,128)S(1)}, f32[64,128]{1,0:T(8,128)S(1)}, u32[]{:S(2)}, u32[]{:S(2)}) collective-permute-start(f32[64,128]{1,0:T(8,128)S(1)} %get-tuple-element.16), channel_id=1, source_target_pairs={{0,2},{1,3},{2,0},{3,1},{4,6},{5,7},{6,4},{7,5},{8,10},{9,11},{10,... | collective-permute-start | bytes 98312 | tf_op jit(solution)/shard_map/ppermute | solution.py:255
  12.9 0.3 collective-permute-start.1
  13.1 0.0 copy-done
  13.1 1.6 %collective-permute-start.7 = (bf16[16,4096]{1,0:T(8,128)(2,1)S(1)}, bf16[16,4096]{1,0:T(8,128)(2,1)S(1)}, u32[]{:S(2)}, u32[]{:S(2)}) collective-permute-start(bf16[16,4096]{1,0:T(8,128)(2,1)S(1)} %constant_dynamic-update-slice_fusion), channel_id=1, source_target_pairs={{0,4},{1,5},{2,6},{3,7},{4,0},{5,1},{6,2},{7,3},{8,12},{9,13},{10,... | collective-permute-start | bytes 393224 | tf_op jit(solution)/shard_map/ppermute | solution.py:255
  14.8 0.1 collective-permute-done.3
  14.9 1.3 %collective-permute-done.2 = f32[64,128]{1,0:T(8,128)S(1)} collective-permute-done((f32[64,128]{1,0:T(8,128)S(1)}, f32[64,128]{1,0:T(8,128)S(1)}, u32[]{:S(2)}, u32[]{:S(2)}) %collective-permute-start.2) | collective-permute-done | bytes 32800 | tf_op jit(solution)/shard_map/ppermute | solution.py:255
  16.2 0.0 collective-permute-done.1
  16.2 1.4 %collective-permute-start.6 = (f32[64,128]{1,0:T(8,128)S(1)}, f32[64,128]{1,0:T(8,128)S(1)}, u32[]{:S(2)}, u32[]{:S(2)}) collective-permute-start(f32[64,128]{1,0:T(8,128)S(1)} %add_add_fusion.refs_0_), channel_id=1, source_target_pairs={{0,12},{1,13},{2,14},{3,15},{4,8},{5,9},{6,10},{7,11},{8,4},{9,5},... | collective-permute-start | bytes 98312 | tf_op jit(solution)/shard_map/ppermute | solution.py:255
  17.6 1.7 %collective-permute-start.5 = (f32[64,128]{1,0:T(8,128)S(1)}, f32[64,128]{1,0:T(8,128)S(1)}, u32[]{:S(2)}, u32[]{:S(2)}) collective-permute-start(f32[64,128]{1,0:T(8,128)S(1)} %add_add_fusion.refs_0_), channel_id=1, source_target_pairs={{0,8},{1,9},{2,10},{3,11},{4,12},{5,13},{6,14},{7,15},{8,0},{9,1},... | collective-permute-start | bytes 98312 | tf_op jit(solution)/shard_map/ppermute | solution.py:255
  19.3 1.3 %collective-permute-start.4 = (f32[64,128]{1,0:T(8,128)S(1)}, f32[64,128]{1,0:T(8,128)S(1)}, u32[]{:S(2)}, u32[]{:S(2)}) collective-permute-start(f32[64,128]{1,0:T(8,128)S(1)} %add_add_fusion.refs_0_), channel_id=1, source_target_pairs={{0,4},{1,5},{2,6},{3,7},{4,0},{5,1},{6,2},{7,3},{8,12},{9,13},{10,... | collective-permute-start | bytes 98312 | tf_op jit(solution)/shard_map/ppermute | solution.py:255
  20.7 0.0 collective-permute-done.7
  20.7 0.8 %collective-permute-start.8 = (bf16[32,4096]{1,0:T(8,128)(2,1)S(1)}, bf16[32,4096]{1,0:T(8,128)(2,1)S(1)}, u32[]{:S(2)}, u32[]{:S(2)}) collective-permute-start(bf16[32,4096]{1,0:T(8,128)(2,1)S(1)} %constant_dynamic-update-slice_fusion.2), channel_id=1, source_target_pairs={{0,2},{1,3},{2,0},{3,1},{4,6},{5,7},{6,4},{7,5},{8,10},{9,11},{10,... | collective-permute-start | bytes 786440 | tf_op jit(solution)/shard_map/ppermute | solution.py:255
  21.5 0.6 %collective-permute-done.6.refs_3_ = f32[64,128]{1,0:T(8,128)S(1)} collective-permute-done((f32[64,128]{1,0:T(8,128)S(1)}, f32[64,128]{1,0:T(8,128)S(1)}, u32[]{:S(2)}, u32[]{:S(2)}) %collective-permute-start.6) | collective-permute-done | bytes 32800 | tf_op jit(solution)/shard_map/ppermute | solution.py:255
  22.1 1.2 %collective-permute-done.5.refs_2_ = f32[64,128]{1,0:T(8,128)S(1)} collective-permute-done((f32[64,128]{1,0:T(8,128)S(1)}, f32[64,128]{1,0:T(8,128)S(1)}, u32[]{:S(2)}, u32[]{:S(2)}) %collective-permute-start.5) | collective-permute-done | bytes 32800 | tf_op jit(solution)/shard_map/ppermute | solution.py:255
  23.2 0.3 collective-permute-done.4.refs_1_
  23.6 4.6 %collective-permute-done.8 = bf16[32,4096]{1,0:T(8,128)(2,1)S(1)} collective-permute-done((bf16[32,4096]{1,0:T(8,128)(2,1)S(1)}, bf16[32,4096]{1,0:T(8,128)(2,1)S(1)}, u32[]{:S(2)}, u32[]{:S(2)}) %collective-permute-start.8) | collective-permute-done | bytes 262176 | tf_op jit(solution)/shard_map/ppermute | solution.py:255
  28.3 0.1 collective-permute-start.9
  28.3 3.1 %precondition.1.moved = f32[128,512]{1,0:T(8,128)S(1)} custom-call(f32[64,128]{1,0:T(8,128)S(1)} %add_add_fusion.refs_0_, f32[64,128]{1,0:T(8,128)S(1)} %collective-permute-done.4.refs_1_, f32[64,128]{1,0:T(8,128)S(1)} %collective-permute-done.5.refs_2_, f32[64,128]{1,0:T(8,128)S(1)} %collective-permute-done.6.refs_3_, ...), custom_call_target="tpu_custom_call" | custom-call | flops 3355443200 | bytes 524288 | tf_op jit(solution)/shard_map/precondition/pallas_call | solution.py:170
  31.4 0.0 collective-permute-done.9.refs_1_
  31.4 2.5 %score.1 = f32[512,128]{1,0:T(8,128)} custom-call(f32[128,512]{1,0:T(8,128)S(1)} %precondition.1.moved, bf16[64,4096]{1,0:T(8,128)(2,1)S(1)} %constant_dynamic-update-slice_fusion.4.refs_0_, bf16[64,4096]{1,0:T(8,128)(2,1)S(1)} %collective-permute-done.9.refs_1_), custom_call_target="tpu_custom_call" | custom-call | tf_op jit(solution)/shard_map/score/pallas_call | solution.py:215
  (8 shorter events, 0.1 us)
Async XLA Ops:
  0.0 11.2 %collective-permute-start = (bf16[8,4096]{1,0:T(8,128)(2,1)}, bf16[8,4096]{1,0:T(8,128)(2,1)S(1)}, u32[]{:S(2)}, u32[]{:S(2)}) collective-permute-start(bf16[8,4096]{1,0:T(8,128)(2,1)} %param.9), channel_id=1, source_target_pairs={{0,8},{1,9},{2,10},{3,11},{4,12},{5,13},{6,14},{7,15},{8,0},{9,1},... | collective-permute-start | bytes 196616 | tf_op jit(solution)/shard_map/ppermute | solution.py:255
  4.0 9.1 %copy-start = (bf16[8,4096]{1,0:T(8,128)(2,1)S(1)}, bf16[8,4096]{1,0:T(8,128)(2,1)}, u32[]{:S(2)}) copy-start(bf16[8,4096]{1,0:T(8,128)(2,1)} %param.9) | copy-start | bytes 196612
  11.2 3.7 %collective-permute-start.3 = (f32[64,128]{1,0:T(8,128)S(1)}, f32[64,128]{1,0:T(8,128)S(1)}, u32[]{:S(2)}, u32[]{:S(2)}) collective-permute-start(f32[64,128]{1,0:T(8,128)S(1)} %get-tuple-element.16), channel_id=1, source_target_pairs={{0,3},{1,2},{2,1},{3,0},{4,7},{5,6},{6,5},{7,4},{8,11},{9,10},{10,... | collective-permute-start | bytes 98312 | tf_op jit(solution)/shard_map/ppermute | solution.py:255
  11.9 4.2 %collective-permute-start.2 = (f32[64,128]{1,0:T(8,128)S(1)}, f32[64,128]{1,0:T(8,128)S(1)}, u32[]{:S(2)}, u32[]{:S(2)}) collective-permute-start(f32[64,128]{1,0:T(8,128)S(1)} %get-tuple-element.16), channel_id=1, source_target_pairs={{0,2},{1,3},{2,0},{3,1},{4,6},{5,7},{6,4},{7,5},{8,10},{9,11},{10,... | collective-permute-start | bytes 98312 | tf_op jit(solution)/shard_map/ppermute | solution.py:255
  12.9 3.3 %collective-permute-start.1 = (f32[64,128]{1,0:T(8,128)S(1)}, f32[64,128]{1,0:T(8,128)S(1)}, u32[]{:S(2)}, u32[]{:S(2)}) collective-permute-start(f32[64,128]{1,0:T(8,128)S(1)} %get-tuple-element.16), channel_id=1, source_target_pairs={{0,1},{1,0},{2,3},{3,2},{4,5},{5,4},{6,7},{7,6},{8,9},{9,8},{10,11... | collective-permute-start | bytes 98312 | tf_op jit(solution)/shard_map/ppermute | solution.py:255
  13.1 7.5 %collective-permute-start.7 = (bf16[16,4096]{1,0:T(8,128)(2,1)S(1)}, bf16[16,4096]{1,0:T(8,128)(2,1)S(1)}, u32[]{:S(2)}, u32[]{:S(2)}) collective-permute-start(bf16[16,4096]{1,0:T(8,128)(2,1)S(1)} %constant_dynamic-update-slice_fusion), channel_id=1, source_target_pairs={{0,4},{1,5},{2,6},{3,7},{4,0},{5,1},{6,2},{7,3},{8,12},{9,13},{10,... | collective-permute-start | bytes 393224 | tf_op jit(solution)/shard_map/ppermute | solution.py:255
  16.2 5.9 %collective-permute-start.6 = (f32[64,128]{1,0:T(8,128)S(1)}, f32[64,128]{1,0:T(8,128)S(1)}, u32[]{:S(2)}, u32[]{:S(2)}) collective-permute-start(f32[64,128]{1,0:T(8,128)S(1)} %add_add_fusion.refs_0_), channel_id=1, source_target_pairs={{0,12},{1,13},{2,14},{3,15},{4,8},{5,9},{6,10},{7,11},{8,4},{9,5},... | collective-permute-start | bytes 98312 | tf_op jit(solution)/shard_map/ppermute | solution.py:255
  17.6 5.6 %collective-permute-start.5 = (f32[64,128]{1,0:T(8,128)S(1)}, f32[64,128]{1,0:T(8,128)S(1)}, u32[]{:S(2)}, u32[]{:S(2)}) collective-permute-start(f32[64,128]{1,0:T(8,128)S(1)} %add_add_fusion.refs_0_), channel_id=1, source_target_pairs={{0,8},{1,9},{2,10},{3,11},{4,12},{5,13},{6,14},{7,15},{8,0},{9,1},... | collective-permute-start | bytes 98312 | tf_op jit(solution)/shard_map/ppermute | solution.py:255
  19.3 4.3 %collective-permute-start.4 = (f32[64,128]{1,0:T(8,128)S(1)}, f32[64,128]{1,0:T(8,128)S(1)}, u32[]{:S(2)}, u32[]{:S(2)}) collective-permute-start(f32[64,128]{1,0:T(8,128)S(1)} %add_add_fusion.refs_0_), channel_id=1, source_target_pairs={{0,4},{1,5},{2,6},{3,7},{4,0},{5,1},{6,2},{7,3},{8,12},{9,13},{10,... | collective-permute-start | bytes 98312 | tf_op jit(solution)/shard_map/ppermute | solution.py:255
  20.7 7.5 %collective-permute-start.8 = (bf16[32,4096]{1,0:T(8,128)(2,1)S(1)}, bf16[32,4096]{1,0:T(8,128)(2,1)S(1)}, u32[]{:S(2)}, u32[]{:S(2)}) collective-permute-start(bf16[32,4096]{1,0:T(8,128)(2,1)S(1)} %constant_dynamic-update-slice_fusion.2), channel_id=1, source_target_pairs={{0,2},{1,3},{2,0},{3,1},{4,6},{5,7},{6,4},{7,5},{8,10},{9,11},{10,... | collective-permute-start | bytes 786440 | tf_op jit(solution)/shard_map/ppermute | solution.py:255
  28.3 3.2 %collective-permute-start.9 = (bf16[64,4096]{1,0:T(8,128)(2,1)S(1)}, bf16[64,4096]{1,0:T(8,128)(2,1)S(1)}, u32[]{:S(2)}, u32[]{:S(2)}) collective-permute-start(bf16[64,4096]{1,0:T(8,128)(2,1)S(1)} %constant_dynamic-update-slice_fusion.4.refs_0_), channel_id=1, source_target_pairs={{0,1},{1,0},{2,3},{3,2},{4,5},{5,4},{6,7},{7,6},{8,9},{9,8},{10,11... | collective-permute-start | bytes 1572872 | tf_op jit(solution)/shard_map/ppermute | solution.py:255

commit v6 on v5

--- a/solution.py
+++ b/solution.py
@@ -10,51 +10,72 @@
 DAMP = 0.1
 HIGHEST = lax.Precision.HIGHEST
 COPY_ROWS = 128
-IN_FLIGHT = 2
+IN_FLIGHT = 4
 
 
 def project_kernel(
     acts, grads, weight_act, weight_grad, act_t, grad_t, cov, tok_buf, weight_buf, weight_t, tok_sems, weight_sems
 ):
-    factor, width = weight_act.shape
+    width = weight_act.shape[1]
     n_parts = acts.shape[0] // COPY_ROWS
     weight_copies = [
         pltpu.make_async_copy(src, weight_buf.at[at], weight_sems.at[at])
         for at, src in enumerate((weight_act, weight_grad))
     ]
-    copies = [
-        pltpu.make_async_copy(
-            src.at[pl.ds(part * COPY_ROWS, COPY_ROWS), :],
-            tok_buf.at[at, pl.ds(part * COPY_ROWS, COPY_ROWS), :],
-            tok_sems.at[at, part],
-        )
+    tok_copies = [
+        [
+            pltpu.make_async_copy(
+                src.at[pl.ds(part * COPY_ROWS, COPY_ROWS), :],
+                tok_buf.at[at, pl.ds(part * COPY_ROWS, COPY_ROWS), :],
+                tok_sems.at[at, part],
+            )
+            for part in range(n_parts)
+        ]
         for at, src in enumerate((acts, grads))
-        for part in range(n_parts)
     ]
-    for copy in weight_copies + copies[:IN_FLIGHT]:
-        copy.start()
-    grams = []
-    for at, out in enumerate((act_t, grad_t)):
-        weight_copies[at].wait()
+    queue = [weight_copies[0], *tok_copies[0], *tok_copies[1]]
+    queue.insert(3, weight_copies[1])
+
+    def start_next(many):
+        for copy in queue[:many]:
+            copy.start()
+        del queue[:many]
+
+    def turned(at):
         for first in range(0, width, 512):
             block = weight_buf[at, :, first : first + 512].astype(jnp.float32)
             weight_t[at, first : first + 512, :] = block.T.astype(weight_t.dtype)
-        gram = None
-        part = 0
-        while part < n_parts:
-            many = 1 if at == 1 and part >= n_parts - 2 else min(2, n_parts - part)
-            for done in range(at * n_parts + part, at * n_parts + part + many):
-                copies[done].wait()
-                if done + IN_FLIGHT < len(copies):
-                    copies[done + IN_FLIGHT].start()
-            rows = slice(part * COPY_ROWS, (part + many) * COPY_ROWS)
-            block = jnp.dot(tok_buf[at, rows, :], weight_t[at], preferred_element_type=jnp.float32)
-            flipped = block.T
-            out[:, rows] = flipped
-            term = jnp.dot(flipped, block, precision=HIGHEST, preferred_element_type=jnp.float32)
-            gram = term if gram is None else gram + term
-            part += many
-        grams.append(gram)
+
+    steps = [(at, part, min(2, n_parts - part)) for at in range(2) for part in range(0, n_parts, 2)]
+    at, part, many = steps.pop()
+    steps += [(at, part + one, 1) for one in range(many)]
+    grams = [None, None]
+
+    def add_gram(at, flipped, block):
+        term = jnp.dot(flipped, block, precision=HIGHEST, preferred_element_type=jnp.float32)
+        grams[at] = term if grams[at] is None else grams[at] + term
+
+    start_next(1 + IN_FLIGHT)
+    weight_copies[0].wait()
+    turned(0)
+    before = None
+    for step, (at, part, many) in enumerate(steps):
+        for copy in tok_copies[at][part : part + many]:
+            copy.wait()
+            start_next(1)
+        if step == 1:
+            weight_copies[1].wait()
+            start_next(1)
+        rows = slice(part * COPY_ROWS, (part + many) * COPY_ROWS)
+        block = jnp.dot(tok_buf[at, rows, :], weight_t[at], preferred_element_type=jnp.float32)
+        if step == 1:
+            turned(1)
+        if before is not None:
+            add_gram(*before)
+        flipped = block.T
+        (act_t, grad_t)[at][:, rows] = flipped
+        before = (at, flipped, block)
+    add_gram(*before)
     cov[...] = jnp.concatenate(grams, axis=1)
 
 
@@ -286,9 +307,12 @@
     *pieces, own = lax.optimization_barrier((*pieces, own))
     pieces = gathered(pieces, stages[1:2])
     own = functools.reduce(jnp.add, exchanged([own], size, *first))
-    pieces = gathered([after(piece, own) for piece in pieces], stages[2:-1])
+    *pieces, own = lax.optimization_barrier((*pieces, own))
+    pieces = gathered(pieces, stages[2:-1])
     terms = exchanged([own], size, *second)
-    pieces = gathered([after(piece, terms) for piece in pieces], stages[max(2, len(stages) - 1) :])
+    *both, = lax.optimization_barrier((*pieces, *terms))
+    pieces, terms = both[: len(pieces)], both[len(pieces) :]
+    pieces = gathered(pieces, stages[max(2, len(stages) - 1) :])
     moved = precondition(tok_total, terms, act_t, grad_t)
     return score(size, moved, pieces)
 

time: 34.1 us -> 32 us (0.938)
  waiting for transfers between devices: 8.13 us -> 6.63 us
  Pallas kernels: 12.7 us -> 11.6 us
  starting transfers between devices: 12.9 us -> 13.4 us
    ppermute x10, waiting for transfers between devices: 8.13 us -> 6.63 us  [swapped(): return lax.ppermute(value, 'dp', perm)]
    pallas_call x1, Pallas kernels: 7.13 us -> 6.06 us  [project(): pl.pallas_call(project_kernel, out_shape=(jax.ShapeDtypeStruct((factor, t...]
    ppermute x10, starting transfers between devices: 12.9 us -> 13.4 us  [swapped(): return lax.ppermute(value, 'dp', perm)]
  transfers between devices with their start and end apart: 10 -> 10, of which waited for: 6 -> 6; matrix products, arithmetic and copies ran while one was open for 0% -> 0% of each run, Pallas kernels for 30% -> 29%
where the time goes in v6:
time: 32 us; the launch traced here: 31.8 us
  starting transfers between devices  13.4 us (42%)
  Pallas kernels  11.6 us (36%)
  waiting for transfers between devices  6.63 us (21%)
    ppermute x10, starting transfers between devices, swapped(): return lax.ppermute(value, 'dp', perm)  13.4 us
    ppermute x10, waiting for transfers between devices, swapped(): return lax.ppermute(value, 'dp', perm)  6.63 us
    pallas_call x1, Pallas kernels, project(): pl.pallas_call(project_kernel, out_shape=(jax.ShapeDtypeStruct((factor, t...  6.06 us
    pallas_call x1, Pallas kernels, precondition(): pl.pallas_call(functools.partial(precondition_kernel, tok_total, n_terms)...  3.09 us
    pallas_call x1, Pallas kernels, score(): pl.pallas_call(functools.partial(score_kernel, size, n_pieces), out_shape...  2.46 us
  transfers between devices with their start and end apart: 10, of which 6 were waited for; matrix products, arithmetic and copies ran while one was open for 0% of the time, Pallas kernels for 29%

profile of v6, /device:TPU:0, one launch (start us, length us, event | category | flops | bytes accessed | tf_op | source)
XLA Modules:
  0.0 31.8 jit_solution(111100248327405130)
XLA Ops:
  0.0 4.0 %collective-permute-start = (bf16[8,4096]{1,0:T(8,128)(2,1)}, bf16[8,4096]{1,0:T(8,128)(2,1)S(1)}, u32[]{:S(2)}, u32[]{:S(2)}) collective-permute-start(bf16[8,4096]{1,0:T(8,128)(2,1)} %param.9), channel_id=1, source_target_pairs={{0,8},{1,9},{2,10},{3,11},{4,12},{5,13},{6,14},{7,15},{8,0},{9,1},... | collective-permute-start | bytes 196616 | tf_op jit(solution)/shard_map/ppermute | solution.py:276
  4.0 6.1 %project.1 = (f32[64,512]{1,0:T(8,128)S(1)}, f32[64,512]{1,0:T(8,128)S(1)}, f32[64,128]{1,0:T(8,128)S(1)}) custom-call(bf16[512,4096]{1,0:T(8,128)(2,1)} %acts.1, bf16[512,4096]{1,0:T(8,128)(2,1)} %grads.1, bf16[64,4096]{1,0:T(8,128)(2,1)} %bitcast.2, bf16[64,4096]{1,0:T(8,128)(2,1)} %bitcast.3), custom_call_target="tpu_custom_call" | custom-call | flops 536870912 | bytes 8388608 | tf_op jit(solution)/shard_map/project/pallas_call | solution.py:88
  10.1 0.0 collective-permute-done
  10.1 0.7 %collective-permute-start.4 = (f32[64,128]{1,0:T(8,128)S(1)}, f32[64,128]{1,0:T(8,128)S(1)}, u32[]{:S(2)}, u32[]{:S(2)}) collective-permute-start(f32[64,128]{1,0:T(8,128)S(1)} %get-tuple-element.23), channel_id=1, source_target_pairs={{0,3},{1,2},{2,1},{3,0},{4,7},{5,6},{6,5},{7,4},{8,11},{9,10},{10,... | collective-permute-start | bytes 98312 | tf_op jit(solution)/shard_map/ppermute | solution.py:276
  10.9 0.9 %collective-permute-start.3 = (f32[64,128]{1,0:T(8,128)S(1)}, f32[64,128]{1,0:T(8,128)S(1)}, u32[]{:S(2)}, u32[]{:S(2)}) collective-permute-start(f32[64,128]{1,0:T(8,128)S(1)} %get-tuple-element.23), channel_id=1, source_target_pairs={{0,2},{1,3},{2,0},{3,1},{4,6},{5,7},{6,4},{7,5},{8,10},{9,11},{10,... | collective-permute-start | bytes 98312 | tf_op jit(solution)/shard_map/ppermute | solution.py:276
  11.8 0.3 collective-permute-start.2
  12.0 0.0 copy-done
  12.1 1.6 %collective-permute-start.1 = (bf16[16,4096]{1,0:T(8,128)(2,1)S(1)}, bf16[16,4096]{1,0:T(8,128)(2,1)S(1)}, u32[]{:S(2)}, u32[]{:S(2)}) collective-permute-start(bf16[16,4096]{1,0:T(8,128)(2,1)S(1)} %constant_dynamic-update-slice_fusion), channel_id=1, source_target_pairs={{0,4},{1,5},{2,6},{3,7},{4,0},{5,1},{6,2},{7,3},{8,12},{9,13},{10,... | collective-permute-start | bytes 393224 | tf_op jit(solution)/shard_map/ppermute | solution.py:276
  13.7 0.1 collective-permute-done.4
  13.8 1.3 %collective-permute-done.3 = f32[64,128]{1,0:T(8,128)S(1)} collective-permute-done((f32[64,128]{1,0:T(8,128)S(1)}, f32[64,128]{1,0:T(8,128)S(1)}, u32[]{:S(2)}, u32[]{:S(2)}) %collective-permute-start.3) | collective-permute-done | bytes 32800 | tf_op jit(solution)/shard_map/ppermute | solution.py:276
  15.1 0.0 collective-permute-done.2
  15.1 2.7 %collective-permute-done.1 = bf16[16,4096]{1,0:T(8,128)(2,1)S(1)} collective-permute-done((bf16[16,4096]{1,0:T(8,128)(2,1)S(1)}, bf16[16,4096]{1,0:T(8,128)(2,1)S(1)}, u32[]{:S(2)}, u32[]{:S(2)}) %collective-permute-start.1) | collective-permute-done | bytes 131104 | tf_op jit(solution)/shard_map/ppermute | solution.py:276
  17.8 1.3 %collective-permute-start.5 = (bf16[32,4096]{1,0:T(8,128)(2,1)S(1)}, bf16[32,4096]{1,0:T(8,128)(2,1)S(1)}, u32[]{:S(2)}, u32[]{:S(2)}) collective-permute-start(bf16[32,4096]{1,0:T(8,128)(2,1)S(1)} %constant_dynamic-update-slice_fusion.2), channel_id=1, source_target_pairs={{0,2},{1,3},{2,0},{3,1},{4,6},{5,7},{6,4},{7,5},{8,10},{9,11},{10,... | collective-permute-start | bytes 786440 | tf_op jit(solution)/shard_map/ppermute | solution.py:276
  19.2 1.3 %collective-permute-start.8 = (f32[64,128]{1,0:T(8,128)S(1)}, f32[64,128]{1,0:T(8,128)S(1)}, u32[]{:S(2)}, u32[]{:S(2)}) collective-permute-start(f32[64,128]{1,0:T(8,128)S(1)} %add_add_fusion.refs_0_), channel_id=1, source_target_pairs={{0,12},{1,13},{2,14},{3,15},{4,8},{5,9},{6,10},{7,11},{8,4},{9,5},... | collective-permute-start | bytes 98312 | tf_op jit(solution)/shard_map/ppermute | solution.py:276
  20.5 1.7 %collective-permute-start.7 = (f32[64,128]{1,0:T(8,128)S(1)}, f32[64,128]{1,0:T(8,128)S(1)}, u32[]{:S(2)}, u32[]{:S(2)}) collective-permute-start(f32[64,128]{1,0:T(8,128)S(1)} %add_add_fusion.refs_0_), channel_id=1, source_target_pairs={{0,8},{1,9},{2,10},{3,11},{4,12},{5,13},{6,14},{7,15},{8,0},{9,1},... | collective-permute-start | bytes 98312 | tf_op jit(solution)/shard_map/ppermute | solution.py:276
  22.2 1.3 %collective-permute-start.6 = (f32[64,128]{1,0:T(8,128)S(1)}, f32[64,128]{1,0:T(8,128)S(1)}, u32[]{:S(2)}, u32[]{:S(2)}) collective-permute-start(f32[64,128]{1,0:T(8,128)S(1)} %add_add_fusion.refs_0_), channel_id=1, source_target_pairs={{0,4},{1,5},{2,6},{3,7},{4,0},{5,1},{6,2},{7,3},{8,12},{9,13},{10,... | collective-permute-start | bytes 98312 | tf_op jit(solution)/shard_map/ppermute | solution.py:276
  23.5 1.3 %collective-permute-done.8.refs_3_ = f32[64,128]{1,0:T(8,128)S(1)} collective-permute-done((f32[64,128]{1,0:T(8,128)S(1)}, f32[64,128]{1,0:T(8,128)S(1)}, u32[]{:S(2)}, u32[]{:S(2)}) %collective-permute-start.8) | collective-permute-done | bytes 32800 | tf_op jit(solution)/shard_map/ppermute | solution.py:276
  24.9 0.7 %collective-permute-done.7.refs_2_ = f32[64,128]{1,0:T(8,128)S(1)} collective-permute-done((f32[64,128]{1,0:T(8,128)S(1)}, f32[64,128]{1,0:T(8,128)S(1)}, u32[]{:S(2)}, u32[]{:S(2)}) %collective-permute-start.7) | collective-permute-done | bytes 32800 | tf_op jit(solution)/shard_map/ppermute | solution.py:276
  25.6 0.5 %collective-permute-done.6.refs_1_ = f32[64,128]{1,0:T(8,128)S(1)} collective-permute-done((f32[64,128]{1,0:T(8,128)S(1)}, f32[64,128]{1,0:T(8,128)S(1)}, u32[]{:S(2)}, u32[]{:S(2)}) %collective-permute-start.6) | collective-permute-done | bytes 32800 | tf_op jit(solution)/shard_map/ppermute | solution.py:276
  26.1 0.0 collective-permute-done.5
  26.2 0.1 collective-permute-start.9
  26.2 3.1 %precondition.1.moved = f32[128,512]{1,0:T(8,128)S(1)} custom-call(f32[64,128]{1,0:T(8,128)S(1)} %add_add_fusion.refs_0_, f32[64,128]{1,0:T(8,128)S(1)} %collective-permute-done.6.refs_1_, f32[64,128]{1,0:T(8,128)S(1)} %collective-permute-done.7.refs_2_, f32[64,128]{1,0:T(8,128)S(1)} %collective-permute-done.8.refs_3_, ...), custom_call_target="tpu_custom_call" | custom-call | flops 3355443200 | bytes 524288 | tf_op jit(solution)/shard_map/precondition/pallas_call | solution.py:191
  29.3 0.0 collective-permute-done.9.refs_1_
  29.3 2.5 %score.1 = f32[512,128]{1,0:T(8,128)} custom-call(f32[128,512]{1,0:T(8,128)S(1)} %precondition.1.moved, bf16[64,4096]{1,0:T(8,128)(2,1)S(1)} %constant_dynamic-update-slice_fusion.4.refs_0_, bf16[64,4096]{1,0:T(8,128)(2,1)S(1)} %collective-permute-done.9.refs_1_), custom_call_target="tpu_custom_call" | custom-call | tf_op jit(solution)/shard_map/score/pallas_call | solution.py:236
  (8 shorter events, 0.1 us)
Async XLA Ops:
  0.0 10.1 %collective-permute-start = (bf16[8,4096]{1,0:T(8,128)(2,1)}, bf16[8,4096]{1,0:T(8,128)(2,1)S(1)}, u32[]{:S(2)}, u32[]{:S(2)}) collective-permute-start(bf16[8,4096]{1,0:T(8,128)(2,1)} %param.9), channel_id=1, source_target_pairs={{0,8},{1,9},{2,10},{3,11},{4,12},{5,13},{6,14},{7,15},{8,0},{9,1},... | collective-permute-start | bytes 196616 | tf_op jit(solution)/shard_map/ppermute | solution.py:276
  4.0 8.0 %copy-start = (bf16[8,4096]{1,0:T(8,128)(2,1)S(1)}, bf16[8,4096]{1,0:T(8,128)(2,1)}, u32[]{:S(2)}) copy-start(bf16[8,4096]{1,0:T(8,128)(2,1)} %param.9) | copy-start | bytes 196612
  10.1 3.7 %collective-permute-start.4 = (f32[64,128]{1,0:T(8,128)S(1)}, f32[64,128]{1,0:T(8,128)S(1)}, u32[]{:S(2)}, u32[]{:S(2)}) collective-permute-start(f32[64,128]{1,0:T(8,128)S(1)} %get-tuple-element.23), channel_id=1, source_target_pairs={{0,3},{1,2},{2,1},{3,0},{4,7},{5,6},{6,5},{7,4},{8,11},{9,10},{10,... | collective-permute-start | bytes 98312 | tf_op jit(solution)/shard_map/ppermute | solution.py:276
  10.9 4.3 %collective-permute-start.3 = (f32[64,128]{1,0:T(8,128)S(1)}, f32[64,128]{1,0:T(8,128)S(1)}, u32[]{:S(2)}, u32[]{:S(2)}) collective-permute-start(f32[64,128]{1,0:T(8,128)S(1)} %get-tuple-element.23), channel_id=1, source_target_pairs={{0,2},{1,3},{2,0},{3,1},{4,6},{5,7},{6,4},{7,5},{8,10},{9,11},{10,... | collective-permute-start | bytes 98312 | tf_op jit(solution)/shard_map/ppermute | solution.py:276
  11.8 3.3 %collective-permute-start.2 = (f32[64,128]{1,0:T(8,128)S(1)}, f32[64,128]{1,0:T(8,128)S(1)}, u32[]{:S(2)}, u32[]{:S(2)}) collective-permute-start(f32[64,128]{1,0:T(8,128)S(1)} %get-tuple-element.23), channel_id=1, source_target_pairs={{0,1},{1,0},{2,3},{3,2},{4,5},{5,4},{6,7},{7,6},{8,9},{9,8},{10,11... | collective-permute-start | bytes 98312 | tf_op jit(solution)/shard_map/ppermute | solution.py:276
  12.1 5.7 %collective-permute-start.1 = (bf16[16,4096]{1,0:T(8,128)(2,1)S(1)}, bf16[16,4096]{1,0:T(8,128)(2,1)S(1)}, u32[]{:S(2)}, u32[]{:S(2)}) collective-permute-start(bf16[16,4096]{1,0:T(8,128)(2,1)S(1)} %constant_dynamic-update-slice_fusion), channel_id=1, source_target_pairs={{0,4},{1,5},{2,6},{3,7},{4,0},{5,1},{6,2},{7,3},{8,12},{9,13},{10,... | collective-permute-start | bytes 393224 | tf_op jit(solution)/shard_map/ppermute | solution.py:276
  17.8 8.3 %collective-permute-start.5 = (bf16[32,4096]{1,0:T(8,128)(2,1)S(1)}, bf16[32,4096]{1,0:T(8,128)(2,1)S(1)}, u32[]{:S(2)}, u32[]{:S(2)}) collective-permute-start(bf16[32,4096]{1,0:T(8,128)(2,1)S(1)} %constant_dynamic-update-slice_fusion.2), channel_id=1, source_target_pairs={{0,2},{1,3},{2,0},{3,1},{4,6},{5,7},{6,4},{7,5},{8,10},{9,11},{10,... | collective-permute-start | bytes 786440 | tf_op jit(solution)/shard_map/ppermute | solution.py:276
  19.2 5.7 %collective-permute-start.8 = (f32[64,128]{1,0:T(8,128)S(1)}, f32[64,128]{1,0:T(8,128)S(1)}, u32[]{:S(2)}, u32[]{:S(2)}) collective-permute-start(f32[64,128]{1,0:T(8,128)S(1)} %add_add_fusion.refs_0_), channel_id=1, source_target_pairs={{0,12},{1,13},{2,14},{3,15},{4,8},{5,9},{6,10},{7,11},{8,4},{9,5},... | collective-permute-start | bytes 98312 | tf_op jit(solution)/shard_map/ppermute | solution.py:276
  20.5 5.1 %collective-permute-start.7 = (f32[64,128]{1,0:T(8,128)S(1)}, f32[64,128]{1,0:T(8,128)S(1)}, u32[]{:S(2)}, u32[]{:S(2)}) collective-permute-start(f32[64,128]{1,0:T(8,128)S(1)} %add_add_fusion.refs_0_), channel_id=1, source_target_pairs={{0,8},{1,9},{2,10},{3,11},{4,12},{5,13},{6,14},{7,15},{8,0},{9,1},... | collective-permute-start | bytes 98312 | tf_op jit(solution)/shard_map/ppermute | solution.py:276
  22.2 3.9 %collective-permute-start.6 = (f32[64,128]{1,0:T(8,128)S(1)}, f32[64,128]{1,0:T(8,128)S(1)}, u32[]{:S(2)}, u32[]{:S(2)}) collective-permute-start(f32[64,128]{1,0:T(8,128)S(1)} %add_add_fusion.refs_0_), channel_id=1, source_target_pairs={{0,4},{1,5},{2,6},{3,7},{4,0},{5,1},{6,2},{7,3},{8,12},{9,13},{10,... | collective-permute-start | bytes 98312 | tf_op jit(solution)/shard_map/ppermute | solution.py:276
  26.2 3.2 %collective-permute-start.9 = (bf16[64,4096]{1,0:T(8,128)(2,1)S(1)}, bf16[64,4096]{1,0:T(8,128)(2,1)S(1)}, u32[]{:S(2)}, u32[]{:S(2)}) collective-permute-start(bf16[64,4096]{1,0:T(8,128)(2,1)S(1)} %constant_dynamic-update-slice_fusion.4.refs_0_), channel_id=1, source_target_pairs={{0,1},{1,0},{2,3},{3,2},{4,5},{5,4},{6,7},{7,6},{8,9},{9,8},{10,11... | collective-permute-start | bytes 1572872 | tf_op jit(solution)/shard_map/ppermute | solution.py:276

commit v7 on v4

--- a/solution.py
+++ b/solution.py
@@ -10,8 +10,6 @@
 DAMP = 0.1
 HIGHEST = lax.Precision.HIGHEST
 COPY_ROWS = 128
-DOT_ROWS = 256
-IN_FLIGHT = 2
 
 
 def dot_nt(left, right, precision=None):
@@ -21,47 +19,64 @@
 
 
 def project_kernel(tokens, weight, *refs):
-    *before, proj_t, gram, tok_buf, weight_buf, tok_sems, weight_sem = refs
-    tok_rows = tokens.shape[0]
-    weight_copy = pltpu.make_async_copy(weight, weight_buf, weight_sem)
+    *refs, tok_buf, weight_buf, weight_t, tok_sems, weight_sem = refs
+    before, proj_t, cov = refs if len(refs) == 3 else (None, *refs, None)
+    width = weight.shape[1]
+    n_parts = tokens.shape[0] // COPY_ROWS
     copies = [
         pltpu.make_async_copy(
             tokens.at[pl.ds(part * COPY_ROWS, COPY_ROWS), :],
             tok_buf.at[pl.ds(part * COPY_ROWS, COPY_ROWS), :],
             tok_sems.at[part],
         )
-        for part in range(tok_rows // COPY_ROWS)
+        for part in range(n_parts)
     ]
+    weight_copy = pltpu.make_async_copy(weight, weight_buf, weight_sem)
     weight_copy.start()
-    for copy in copies[:IN_FLIGHT]:
+    for copy in copies:
         copy.start()
+    if before is not None:
+        early = dot_nt(before[...], before[...], HIGHEST)
     weight_copy.wait()
-    for first in range(0, tok_rows, DOT_ROWS):
-        for part in range(first // COPY_ROWS, (first + DOT_ROWS) // COPY_ROWS):
-            copies[part].wait()
-            if part + IN_FLIGHT < len(copies):
-                copies[part + IN_FLIGHT].start()
-        proj_t[:, first : first + DOT_ROWS] = dot_nt(weight_buf[...], tok_buf[first : first + DOT_ROWS, :])
-    result = dot_nt(proj_t[...], proj_t[...], HIGHEST)
-    gram[...] = jnp.concatenate([ref[...] for ref in before] + [result], axis=1)
+    for first in range(0, width, 512):
+        block = weight_buf[:, first : first + 512].astype(jnp.float32)
+        weight_t[first : first + 512, :] = block.T.astype(weight_t.dtype)
+    steps = [(part, min(2, n_parts - part)) for part in range(0, n_parts, 2)]
+    part, many = steps.pop()
+    steps += [(part + one, 1) for one in range(many)]
+    gram = late = None
+    for part, many in steps:
+        for copy in copies[part : part + many]:
+            copy.wait()
+        rows = slice(part * COPY_ROWS, (part + many) * COPY_ROWS)
+        block = jnp.dot(tok_buf[rows, :], weight_t[...], preferred_element_type=jnp.float32)
+        if late is not None:
+            term = jnp.dot(*late, precision=HIGHEST, preferred_element_type=jnp.float32)
+            gram = term if gram is None else gram + term
+        flipped = block.T
+        proj_t[:, rows] = flipped
+        late = (flipped, block) if cov is not None else None
+    if cov is not None:
+        term = jnp.dot(*late, precision=HIGHEST, preferred_element_type=jnp.float32)
+        cov[...] = jnp.concatenate([early, term if gram is None else gram + term], axis=1)
 
 
 def project(tokens, weight, *before):
     tok_rows, width = tokens.shape
     factor = weight.shape[1]
     operands = [pltpu.with_memory_space_constraint(value, pltpu.HBM) for value in (tokens, weight.T)]
+    out_shape = [jax.ShapeDtypeStruct((factor, tok_rows), jnp.float32)]
+    out_shape += [jax.ShapeDtypeStruct((factor, 2 * factor), jnp.float32)] * len(before)
     return pl.pallas_call(
         project_kernel,
-        out_shape=(
-            jax.ShapeDtypeStruct((factor, tok_rows), jnp.float32),
-            jax.ShapeDtypeStruct((factor, (1 + len(before)) * factor), jnp.float32),
-        ),
+        out_shape=out_shape,
         in_specs=[pl.BlockSpec(memory_space=pltpu.HBM)] * 2
         + [pl.BlockSpec(memory_space=pltpu.VMEM)] * len(before),
-        out_specs=[pl.BlockSpec(memory_space=pltpu.VMEM)] * 2,
+        out_specs=[pl.BlockSpec(memory_space=pltpu.VMEM)] * len(out_shape),
         scratch_shapes=[
             pltpu.VMEM((tok_rows, width), tokens.dtype),
             pltpu.VMEM((factor, width), weight.dtype),
+            pltpu.VMEM((width, factor), weight.dtype),
             pltpu.SemaphoreType.DMA((tok_rows // COPY_ROWS,)),
             pltpu.SemaphoreType.DMA,
         ],
@@ -130,11 +145,10 @@
     return jnp.concatenate(parts, axis=0)
 
 
-def precondition_kernel(tok_total, n_terms, *refs):
-    terms, (act_t, grad_t, moved) = refs[:n_terms], refs[n_terms:]
-    both = terms[0][...]
-    for term in terms[1:]:
-        both = both + term[...]
+def precondition_kernel(tok_total, terms, act_t, grad_t, moved):
+    both = terms[0]
+    for at in range(1, terms.shape[0]):
+        both = both + terms[at]
     factor = both.shape[0]
     lane = lax.broadcasted_iota(jnp.int32, both.shape, 1)
     row_at = lax.broadcasted_iota(jnp.int32, both.shape, 0)
@@ -151,18 +165,17 @@
 
 def precondition(tok_total, terms, act_t, grad_t):
     factor, tok_rows = act_t.shape
-    n_terms = len(terms)
     return pl.pallas_call(
-        functools.partial(precondition_kernel, tok_total, n_terms),
+        functools.partial(precondition_kernel, tok_total),
         out_shape=jax.ShapeDtypeStruct((2 * factor, tok_rows), jnp.float32),
-        in_specs=[pl.BlockSpec(memory_space=pltpu.VMEM)] * (n_terms + 2),
+        in_specs=[pl.BlockSpec(memory_space=pltpu.VMEM)] * 3,
         out_specs=pl.BlockSpec(memory_space=pltpu.VMEM),
         compiler_params=pltpu.CompilerParams(vmem_limit_bytes=24 * 2**20),
         cost_estimate=pl.CostEstimate(
             flops=1600 * factor * factor * tok_rows, bytes_accessed=16 * factor * tok_rows, transcendentals=0
         ),
         name="precondition",
-    )(*terms, act_t, grad_t)
+    )(terms, act_t, grad_t)
 
 
 def score_kernel(size, n_pieces, moved, *refs):
@@ -211,10 +224,17 @@
     )(moved, *queries)
 
 
-def stages_of(size):
+def gather_stages(size):
     if size & (size - 1):
         return [(1, size)]
     return [(size >> level, 2) for level in range(1, size.bit_length())]
+
+
+def sum_rounds(size):
+    core = 2 if size % 2 == 0 else 1
+    rest = size // core
+    near = max(d for d in range(1, rest + 1) if rest % d == 0 and d * d <= rest)
+    return [(1, core * near), (core * near, rest // near)]
 
 
 def after(value, other):
@@ -235,7 +255,7 @@
 
 def owners_of(me, size):
     owners = [me]
-    for stride, radix in stages_of(size):
+    for stride, radix in gather_stages(size):
         digit = lax.rem(lax.div(me, stride), radix)
         back = [shift if radix & (radix - 1) == 0 else radix - shift for shift in range(radix)]
         steps = [(partner(digit, radix, shift) - digit) * stride for shift in back]
@@ -248,25 +268,36 @@
     return [mine] + [swapped(mine, size, stride, radix, shift) for shift in range(1, radix)]
 
 
+def replicated(own, size, stride, radix):
+    groups = [
+        [at + step * stride for step in range(radix)] for at in range(size) if at // stride % radix == 0
+    ]
+    copies = jnp.broadcast_to(own, (radix, *own.shape))
+    return lax.all_to_all(copies, "dp", 0, 0, axis_index_groups=groups, tiled=True)
+
+
 def on_device(acts, grads, proj_act, proj_grad, queries):
     size = lax.axis_size("dp")
     tok_total = acts.shape[0] * size
-    stages = stages_of(size)
-    last = len(stages) - 1
-    waiting = list(stages)
-    pieces = exchanged([queries], size, *waiting.pop(0))
-    act_t, gram = project(acts, proj_act)
-    pieces = [after(piece, gram) for piece in pieces]
-    if waiting:
-        pieces = exchanged(pieces, size, *waiting.pop(0))
-    grad_t, own = project(grads, proj_grad, gram)
-    begins = [at * last // max(1, len(waiting) - 1) for at in range(len(waiting))]
-    for level, stage in enumerate(stages):
-        if level in begins:
-            *pieces, own = lax.optimization_barrier((*pieces, own))
-            pieces = exchanged(pieces, size, *waiting.pop(0))
-        terms = exchanged([own], size, *stage)
-        own = functools.reduce(jnp.add, terms)
+    stages = gather_stages(size)
+    first, second = sum_rounds(size)
+
+    def gathered(pieces, some):
+        for stage in some:
+            pieces = exchanged(pieces, size, *stage)
+        return pieces
+
+    pieces = gathered([queries], stages[:1])
+    (act_t,) = project(acts, proj_act)
+    *pieces, act_t = lax.optimization_barrier((*pieces, act_t))
+    pieces = gathered(pieces, stages[1:2])
+    grad_t, own = project(grads, proj_grad, act_t)
+    *pieces, own = lax.optimization_barrier((*pieces, own))
+    pieces = gathered(pieces, stages[2:-1])
+    own = functools.reduce(jnp.add, exchanged([own], size, *first))
+    terms = replicated(own, size, *second)
+    *pieces, terms = lax.optimization_barrier((*pieces, terms))
+    pieces = gathered(pieces, stages[max(2, len(stages) - 1) :])
     moved = precondition(tok_total, terms, act_t, grad_t)
     return score(size, moved, pieces)
 

time: 37.2 us -> 33.9 us (0.911)
  waiting for transfers between devices: 11.9 us -> 0.95 us
  blocking collectives: 0 us -> 9.79 us
  Pallas kernels: 14.6 us -> 13.5 us
  starting transfers between devices: 10.2 us -> 9.26 us
    ppermute x8 -> x7, waiting for transfers between devices: 11.9 us -> 0.95 us  [swapped(): return lax.ppermute(value, 'dp', perm)]
    all_to_all x0 -> x1, blocking collectives: none -> 9.79 us  [replicated(): lax.all_to_all(copies, 'dp', 0, 0, axis_index_groups=groups, tiled=True)]
    pallas_call x3, Pallas kernels: 12.1 us -> 11 us  [the longest x2 7.96 us: project(): pl.pallas_call(project_kernel, out_shape=out_shape, in_specs=[pl.BlockSpe...]
    ppermute x8 -> x7, starting transfers between devices: 10.2 us -> 9.26 us  [swapped(): return lax.ppermute(value, 'dp', perm)]
  transfers between devices with their start and end apart: 8 -> 7, of which waited for: 4 -> 2; matrix products, arithmetic and copies ran while one was open for 0% -> 0% of each run, Pallas kernels for 33% -> 33%
where the time goes in v7:
time: 33.9 us; the launch traced here: 33.7 us
  Pallas kernels  13.5 us (40%)
  blocking collectives  9.79 us (29%)
  starting transfers between devices  9.26 us (27%)
  waiting for transfers between devices  0.95 us (3%)
    all_to_all x1, blocking collectives, replicated(): lax.all_to_all(copies, 'dp', 0, 0, axis_index_groups=groups, tiled=True)  9.79 us
    ppermute x7, starting transfers between devices, swapped(): return lax.ppermute(value, 'dp', perm)  9.26 us
    pallas_call x2, Pallas kernels, project(): pl.pallas_call(project_kernel, out_shape=out_shape, in_specs=[pl.BlockSpe...  7.96 us
    pallas_call x1, Pallas kernels, precondition(): pl.pallas_call(functools.partial(precondition_kernel, tok_total), out_sha...  3.09 us
    pallas_call x1, Pallas kernels, score(): pl.pallas_call(functools.partial(score_kernel, size, n_pieces), out_shape...  2.47 us
    ppermute x7, waiting for transfers between devices, swapped(): return lax.ppermute(value, 'dp', perm)  0.95 us
  transfers between devices with their start and end apart: 7, of which 2 were waited for; matrix products, arithmetic and copies ran while one was open for 0% of the time, Pallas kernels for 33%

profile of v7, /device:TPU:0, one launch (start us, length us, event | category | flops | bytes accessed | tf_op | source)
XLA Modules:
  0.0 33.7 jit_solution(661246641064661214)
XLA Ops:
  0.0 0.0 copy-start
  0.0 4.0 %collective-permute-start = (bf16[8,4096]{1,0:T(8,128)(2,1)}, bf16[8,4096]{1,0:T(8,128)(2,1)S(1)}, u32[]{:S(2)}, u32[]{:S(2)}) collective-permute-start(bf16[8,4096]{1,0:T(8,128)(2,1)} %param.9), channel_id=1, source_target_pairs={{0,8},{1,9},{2,10},{3,11},{4,12},{5,13},{6,14},{7,15},{8,0},{9,1},... | collective-permute-start | bytes 196616 | tf_op jit(solution)/shard_map/ppermute | solution.py:253
  4.0 4.1 %project.2.refs_0_.act_t = f32[64,512]{1,0:T(8,128)S(1)} custom-call(bf16[512,4096]{1,0:T(8,128)(2,1)} %tokens.2, bf16[64,4096]{1,0:T(8,128)(2,1)} %bitcast.2), custom_call_target="tpu_custom_call" | custom-call | flops 268435456 | bytes 4194304 | tf_op jit(solution)/shard_map/project/pallas_call | solution.py:70
  8.1 0.0 collective-permute-done
  8.1 0.0 copy-done
  8.2 1.6 %collective-permute-start.1 = (bf16[16,4096]{1,0:T(8,128)(2,1)S(1)}, bf16[16,4096]{1,0:T(8,128)(2,1)S(1)}, u32[]{:S(2)}, u32[]{:S(2)}) collective-permute-start(bf16[16,4096]{1,0:T(8,128)(2,1)S(1)} %constant_dynamic-update-slice_fusion), channel_id=1, source_target_pairs={{0,4},{1,5},{2,6},{3,7},{4,0},{5,1},{6,2},{7,3},{8,12},{9,13},{10,... | collective-permute-start | bytes 393224 | tf_op jit(solution)/shard_map/ppermute | solution.py:253
  9.8 3.9 %project.3 = (f32[64,512]{1,0:T(8,128)S(1)}, f32[64,128]{1,0:T(8,128)S(1)}) custom-call(bf16[512,4096]{1,0:T(8,128)(2,1)} %tokens.3, bf16[64,4096]{1,0:T(8,128)(2,1)} %bitcast.3, f32[64,512]{1,0:T(8,128)S(1)} %project.2.refs_0_.act_t), custom_call_target="tpu_custom_call" | custom-call | flops 268435456 | bytes 4194304 | tf_op jit(solution)/shard_map/project/pallas_call | solution.py:70
  13.7 0.0 collective-permute-done.1
  13.7 0.5 %collective-permute-start.5 = (f32[64,128]{1,0:T(8,128)S(1)}, f32[64,128]{1,0:T(8,128)S(1)}, u32[]{:S(2)}, u32[]{:S(2)}) collective-permute-start(f32[64,128]{1,0:T(8,128)S(1)} %get-tuple-element.22), channel_id=1, source_target_pairs={{0,3},{1,2},{2,1},{3,0},{4,7},{5,6},{6,5},{7,4},{8,11},{9,10},{10,... | collective-permute-start | bytes 98312 | tf_op jit(solution)/shard_map/ppermute | solution.py:253
  14.2 1.2 %collective-permute-start.4 = (f32[64,128]{1,0:T(8,128)S(1)}, f32[64,128]{1,0:T(8,128)S(1)}, u32[]{:S(2)}, u32[]{:S(2)}) collective-permute-start(f32[64,128]{1,0:T(8,128)S(1)} %get-tuple-element.22), channel_id=1, source_target_pairs={{0,2},{1,3},{2,0},{3,1},{4,6},{5,7},{6,4},{7,5},{8,10},{9,11},{10,... | collective-permute-start | bytes 98312 | tf_op jit(solution)/shard_map/ppermute | solution.py:253
  15.4 0.3 collective-permute-start.3
  15.7 1.6 %collective-permute-start.2 = (bf16[32,4096]{1,0:T(8,128)(2,1)S(1)}, bf16[32,4096]{1,0:T(8,128)(2,1)S(1)}, u32[]{:S(2)}, u32[]{:S(2)}) collective-permute-start(bf16[32,4096]{1,0:T(8,128)(2,1)S(1)} %constant_dynamic-update-slice_fusion.2), channel_id=1, source_target_pairs={{0,2},{1,3},{2,0},{3,1},{4,6},{5,7},{6,4},{7,5},{8,10},{9,11},{10,... | collective-permute-start | bytes 786440 | tf_op jit(solution)/shard_map/ppermute | solution.py:253
  17.3 0.1 collective-permute-done.5
  17.4 0.8 %collective-permute-done.4 = f32[64,128]{1,0:T(8,128)S(1)} collective-permute-done((f32[64,128]{1,0:T(8,128)S(1)}, f32[64,128]{1,0:T(8,128)S(1)}, u32[]{:S(2)}, u32[]{:S(2)}) %collective-permute-start.4) | collective-permute-done | bytes 32800 | tf_op jit(solution)/shard_map/ppermute | solution.py:253
  18.2 0.0 collective-permute-done.3
  18.2 9.8 %all_to_all.5.terms = f32[4,64,128]{2,1,0:T(8,128)S(1)} all-to-all(f32[4,64,128]{2,1,0:T(8,128)S(1)} %broadcast_in_dim.3), channel_id=1, replica_groups={{0,4,8,12},{1,5,9,13},{2,6,10,14},{3,7,11,15},{16,20,24,28},{17,21,25,2..., dimensions={0} | all-to-all | bytes 262144 | tf_op jit(solution)/shard_map/all_to_all | solution.py:276
  28.0 0.0 collective-permute-done.2
  28.1 0.1 collective-permute-start.6
  28.2 3.1 %precondition.1.moved = f32[128,512]{1,0:T(8,128)S(1)} custom-call(f32[4,64,128]{2,1,0:T(8,128)S(1)} %all_to_all.5.terms, f32[64,512]{1,0:T(8,128)S(1)} %project.2.refs_0_.act_t, f32[64,512]{1,0:T(8,128)S(1)} %get-tuple-element.24.grad_t), custom_call_target="tpu_custom_call" | custom-call | flops 3355443200 | bytes 524288 | tf_op jit(solution)/shard_map/precondition/pallas_call | solution.py:168
  31.3 0.0 collective-permute-done.6.refs_1_
  31.3 2.5 %score.1 = f32[512,128]{1,0:T(8,128)} custom-call(f32[128,512]{1,0:T(8,128)S(1)} %precondition.1.moved, bf16[64,4096]{1,0:T(8,128)(2,1)S(1)} %constant_dynamic-update-slice_fusion.4.refs_0_, bf16[64,4096]{1,0:T(8,128)(2,1)S(1)} %collective-permute-done.6.refs_1_), custom_call_target="tpu_custom_call" | custom-call | tf_op jit(solution)/shard_map/score/pallas_call | solution.py:213
  (8 shorter events, 0.1 us)
Async XLA Ops:
  0.0 8.1 %copy-start = (bf16[8,4096]{1,0:T(8,128)(2,1)S(1)}, bf16[8,4096]{1,0:T(8,128)(2,1)}, u32[]{:S(2)}) copy-start(bf16[8,4096]{1,0:T(8,128)(2,1)} %param.9) | copy-start | bytes 196612
  0.0 8.1 %collective-permute-start = (bf16[8,4096]{1,0:T(8,128)(2,1)}, bf16[8,4096]{1,0:T(8,128)(2,1)S(1)}, u32[]{:S(2)}, u32[]{:S(2)}) collective-permute-start(bf16[8,4096]{1,0:T(8,128)(2,1)} %param.9), channel_id=1, source_target_pairs={{0,8},{1,9},{2,10},{3,11},{4,12},{5,13},{6,14},{7,15},{8,0},{9,1},... | collective-permute-start | bytes 196616 | tf_op jit(solution)/shard_map/ppermute | solution.py:253
  8.2 5.5 %collective-permute-start.1 = (bf16[16,4096]{1,0:T(8,128)(2,1)S(1)}, bf16[16,4096]{1,0:T(8,128)(2,1)S(1)}, u32[]{:S(2)}, u32[]{:S(2)}) collective-permute-start(bf16[16,4096]{1,0:T(8,128)(2,1)S(1)} %constant_dynamic-update-slice_fusion), channel_id=1, source_target_pairs={{0,4},{1,5},{2,6},{3,7},{4,0},{5,1},{6,2},{7,3},{8,12},{9,13},{10,... | collective-permute-start | bytes 393224 | tf_op jit(solution)/shard_map/ppermute | solution.py:253
  13.7 3.7 %collective-permute-start.5 = (f32[64,128]{1,0:T(8,128)S(1)}, f32[64,128]{1,0:T(8,128)S(1)}, u32[]{:S(2)}, u32[]{:S(2)}) collective-permute-start(f32[64,128]{1,0:T(8,128)S(1)} %get-tuple-element.22), channel_id=1, source_target_pairs={{0,3},{1,2},{2,1},{3,0},{4,7},{5,6},{6,5},{7,4},{8,11},{9,10},{10,... | collective-permute-start | bytes 98312 | tf_op jit(solution)/shard_map/ppermute | solution.py:253
  14.2 4.0 %collective-permute-start.4 = (f32[64,128]{1,0:T(8,128)S(1)}, f32[64,128]{1,0:T(8,128)S(1)}, u32[]{:S(2)}, u32[]{:S(2)}) collective-permute-start(f32[64,128]{1,0:T(8,128)S(1)} %get-tuple-element.22), channel_id=1, source_target_pairs={{0,2},{1,3},{2,0},{3,1},{4,6},{5,7},{6,4},{7,5},{8,10},{9,11},{10,... | collective-permute-start | bytes 98312 | tf_op jit(solution)/shard_map/ppermute | solution.py:253
  15.4 2.8 %collective-permute-start.3 = (f32[64,128]{1,0:T(8,128)S(1)}, f32[64,128]{1,0:T(8,128)S(1)}, u32[]{:S(2)}, u32[]{:S(2)}) collective-permute-start(f32[64,128]{1,0:T(8,128)S(1)} %get-tuple-element.22), channel_id=1, source_target_pairs={{0,1},{1,0},{2,3},{3,2},{4,5},{5,4},{6,7},{7,6},{8,9},{9,8},{10,11... | collective-permute-start | bytes 98312 | tf_op jit(solution)/shard_map/ppermute | solution.py:253
  15.7 12.4 %collective-permute-start.2 = (bf16[32,4096]{1,0:T(8,128)(2,1)S(1)}, bf16[32,4096]{1,0:T(8,128)(2,1)S(1)}, u32[]{:S(2)}, u32[]{:S(2)}) collective-permute-start(bf16[32,4096]{1,0:T(8,128)(2,1)S(1)} %constant_dynamic-update-slice_fusion.2), channel_id=1, source_target_pairs={{0,2},{1,3},{2,0},{3,1},{4,6},{5,7},{6,4},{7,5},{8,10},{9,11},{10,... | collective-permute-start | bytes 786440 | tf_op jit(solution)/shard_map/ppermute | solution.py:253
  28.1 3.2 %collective-permute-start.6 = (bf16[64,4096]{1,0:T(8,128)(2,1)S(1)}, bf16[64,4096]{1,0:T(8,128)(2,1)S(1)}, u32[]{:S(2)}, u32[]{:S(2)}) collective-permute-start(bf16[64,4096]{1,0:T(8,128)(2,1)S(1)} %constant_dynamic-update-slice_fusion.4.refs_0_), channel_id=1, source_target_pairs={{0,1},{1,0},{2,3},{3,2},{4,5},{5,4},{6,7},{7,6},{8,9},{9,8},{10,11... | collective-permute-start | bytes 1572872 | tf_op jit(solution)/shard_map/ppermute | solution.py:253

commit v8 on v6

--- a/solution.py
+++ b/solution.py
@@ -47,6 +47,7 @@
             weight_t[at, first : first + 512, :] = block.T.astype(weight_t.dtype)
 
     steps = [(at, part, min(2, n_parts - part)) for at in range(2) for part in range(0, n_parts, 2)]
+    last_act = len(steps) // 2 - 1
     at, part, many = steps.pop()
     steps += [(at, part + one, 1) for one in range(many)]
     grams = [None, None]
@@ -63,12 +64,12 @@
         for copy in tok_copies[at][part : part + many]:
             copy.wait()
             start_next(1)
-        if step == 1:
+        if step == last_act:
             weight_copies[1].wait()
             start_next(1)
         rows = slice(part * COPY_ROWS, (part + many) * COPY_ROWS)
         block = jnp.dot(tok_buf[at, rows, :], weight_t[at], preferred_element_type=jnp.float32)
-        if step == 1:
+        if step == last_act:
             turned(1)
         if before is not None:
             add_gram(*before)
@@ -166,11 +167,12 @@
     return jnp.concatenate(parts, axis=0)
 
 
-def precondition_kernel(tok_total, n_terms, *refs):
-    terms, (act_t, grad_t, moved) = refs[:n_terms], refs[n_terms:]
-    both = terms[0][...]
-    for term in terms[1:]:
-        both = both + term[...]
+def is_even():
+    return lax.rem(lax.axis_index("dp"), 2) == 0
+
+
+def precondition_kernel(tok_total, own, other, act_t, grad_t, moved):
+    both = jnp.where(is_even(), other[...], own[...])
     factor = both.shape[0]
     lane = lax.broadcasted_iota(jnp.int32, both.shape, 1)
     row_at = lax.broadcasted_iota(jnp.int32, both.shape, 0)
@@ -185,24 +187,23 @@
     moved[...] = jnp.dot(blocks, proj_t, precision=HIGHEST, preferred_element_type=jnp.float32)
 
 
-def precondition(tok_total, terms, act_t, grad_t):
+def precondition(tok_total, own, other, act_t, grad_t):
     factor, tok_rows = act_t.shape
-    n_terms = len(terms)
     return pl.pallas_call(
-        functools.partial(precondition_kernel, tok_total, n_terms),
+        functools.partial(precondition_kernel, tok_total),
         out_shape=jax.ShapeDtypeStruct((2 * factor, tok_rows), jnp.float32),
-        in_specs=[pl.BlockSpec(memory_space=pltpu.VMEM)] * (n_terms + 2),
+        in_specs=[pl.BlockSpec(memory_space=pltpu.VMEM)] * 4,
         out_specs=pl.BlockSpec(memory_space=pltpu.VMEM),
         compiler_params=pltpu.CompilerParams(vmem_limit_bytes=24 * 2**20),
         cost_estimate=pl.CostEstimate(
             flops=1600 * factor * factor * tok_rows, bytes_accessed=16 * factor * tok_rows, transcendentals=0
         ),
         name="precondition",
-    )(*terms, act_t, grad_t)
-
-
-def score_kernel(size, n_pieces, moved, *refs):
-    queries, (scores, total, ordered) = refs[:n_pieces], refs[n_pieces:]
+    )(own, other, act_t, grad_t)
+
+
+def score_kernel(owners, moved, own, other, scores, total, ordered):
+    even = is_even()
     factor = moved.shape[0] // 2
     group = 4
     act_side = moved[:factor, :]
@@ -213,7 +214,7 @@
         high = outer.astype(jnp.bfloat16)
         low = (outer - high.astype(jnp.float32)).astype(jnp.bfloat16)
         columns = slice(first * factor, (first + group) * factor)
-        values = jnp.concatenate([piece[:, columns] for piece in queries], axis=0)
+        values = jnp.where(even, own[:, columns], other[:, columns])
         term = jnp.dot(
             jnp.concatenate([values, values], axis=1),
             jnp.concatenate([high, low], axis=0),
@@ -223,98 +224,96 @@
             total[...] = term
         else:
             total[...] += term
-    rows = total.shape[0] // size
-    for at, owner in enumerate(owners_of(lax.axis_index("dp"), size)):
-        ordered[pl.ds(pl.multiple_of(owner * rows, rows), rows), :] = total[at * rows : (at + 1) * rows, :]
+    places = owners(lax.axis_index("dp"))
+    rows = total.shape[0] // len(places)
+    for at, place in enumerate(places):
+        ordered[pl.ds(pl.multiple_of(place * rows, rows), rows), :] = total[at * rows : (at + 1) * rows, :]
     scores[...] = ordered[...].T
 
 
-def score(size, moved, queries):
+def score(owners, moved, own, other):
     tok_rows = moved.shape[1]
-    n_queries = sum(piece.shape[0] for piece in queries)
-    n_pieces = len(queries)
+    n_queries = own.shape[0]
     return pl.pallas_call(
-        functools.partial(score_kernel, size, n_pieces),
+        functools.partial(score_kernel, owners),
         out_shape=jax.ShapeDtypeStruct((tok_rows, n_queries), jnp.float32),
-        in_specs=[pl.BlockSpec(memory_space=pltpu.VMEM)] * (1 + n_pieces),
+        in_specs=[pl.BlockSpec(memory_space=pltpu.VMEM)] * 3,
         out_specs=pl.BlockSpec(memory_space=pltpu.VMEM),
         scratch_shapes=[
             pltpu.VMEM((n_queries, tok_rows), jnp.float32),
             pltpu.VMEM((n_queries, tok_rows), jnp.float32),
         ],
-        compiler_params=pltpu.CompilerParams(vmem_limit_bytes=32 * 2**20),
+        compiler_params=pltpu.CompilerParams(vmem_limit_bytes=48 * 2**20),
         name="score",
-    )(moved, *queries)
-
-
-def gather_stages(size):
-    if size & (size - 1):
-        return [(1, size)]
-    return [(size >> level, 2) for level in range(1, size.bit_length())]
-
-
-def sum_rounds(size):
-    core = 2 if size % 2 == 0 else 1
-    rest = size // core
-    near = max(d for d in range(1, rest + 1) if rest % d == 0 and d * d <= rest)
-    return [(1, core * near), (core * near, rest // near)]
-
-
-def after(value, other):
-    return lax.optimization_barrier((value, other))[0]
-
-
-def partner(digit, radix, shift):
-    return digit ^ shift if radix & (radix - 1) == 0 else (digit + shift) % radix
-
-
-def swapped(value, size, stride, radix, shift):
-    perm = []
-    for at in range(size):
-        digit = at // stride % radix
-        perm.append((at, at + (partner(digit, radix, shift) - digit) * stride))
-    return lax.ppermute(value, "dp", perm)
-
-
-def owners_of(me, size):
-    owners = [me]
-    for stride, radix in gather_stages(size):
-        digit = lax.rem(lax.div(me, stride), radix)
-        back = [shift if radix & (radix - 1) == 0 else radix - shift for shift in range(radix)]
-        steps = [(partner(digit, radix, shift) - digit) * stride for shift in back]
-        owners = [owner + step for step in steps for owner in owners]
+    )(moved, own, other)
+
+
+def within(chips, core, flip):
+    return [(2 * chip + core, 2 * (chip ^ flip) + core) for chip in range(chips)]
+
+
+def across(chips, core):
+    return [(2 * chip + core, 2 * chip + 1 - core) for chip in range(chips)]
+
+
+def moved_by(pairs, value):
+    return lax.ppermute(value, "dp", pairs)
+
+
+def owners_among(chips, me):
+    chip = lax.div(me, 2)
+    top, under = chips // 2, chips // 4
+    owners = [(chip ^ flip) * 2 + core for core in range(2) for flip in (0, top, under)]
+    owners += [(chip ^ top ^ under) * 2 + core for core in range(2)]
+    flip = under // 2
+    while flip:
+        owners += [owner ^ (2 * flip) for owner in owners]
+        flip //= 2
     return owners
 
 
-def exchanged(held, size, stride, radix):
-    mine = held[0] if len(held) == 1 else jnp.concatenate(held, axis=0)
-    return [mine] + [swapped(mine, size, stride, radix, shift) for shift in range(1, radix)]
+def on_chips(chips, tok_total, acts, grads, proj_act, proj_grad, queries):
+    rows = queries.shape[0]
+    top, under = chips // 2, chips // 4
+    both_cores = [within(chips, 0, flip) + within(chips, 1, flip) for flip in (top, under)]
+    pieces = [queries] + [moved_by(pairs, queries) for pairs in both_cores]
+    act_t, grad_t, own = project(acts, grads, proj_act, proj_grad)
+    *pieces, own = lax.optimization_barrier((*pieces, own))
+
+    mine = jnp.concatenate(pieces, axis=0)
+    held = [mine, moved_by(across(chips, 1), mine)]
+    own = own + moved_by(across(chips, 0), own)
+    *held, own = lax.optimization_barrier((*held, own))
+    far = jnp.concatenate([part[rows : 2 * rows] for part in held], axis=0)
+    held.append(moved_by(within(chips, 0, under), far))
+    held = jnp.concatenate(held, axis=0)
+    come = [held]
+    flip = under // 2
+    while flip:
+        held = come[0] if len(come) == 1 else jnp.concatenate(come, axis=0)
+        come = [held, moved_by(within(chips, 0, flip), held)]
+        own = own + moved_by(within(chips, 1, flip), own)
+        flip //= 2
+    own = own + sum(moved_by(within(chips, 1, flip), own) for flip in (under, top, top | under))
+    other_own = moved_by(across(chips, 1), own)
+    *come, own, other_own = lax.optimization_barrier((*come, own, other_own))
+    held = jnp.concatenate(come, axis=0)
+    other_held = moved_by(across(chips, 0), held)
+    moved = precondition(tok_total, own, other_own, act_t, grad_t)
+    return score(functools.partial(owners_among, chips), moved, held, other_held)
 
 
 def on_device(acts, grads, proj_act, proj_grad, queries):
     size = lax.axis_size("dp")
     tok_total = acts.shape[0] * size
-    stages = gather_stages(size)
-    first, second = sum_rounds(size)
-
-    def gathered(pieces, some):
-        for stage in some:
-            pieces = exchanged(pieces, size, *stage)
-        return pieces
-
-    pieces = gathered([queries], stages[:1])
+    chips = size // 2
+    if size % 2 == 0 and chips >= 4 and chips & (chips - 1) == 0:
+        return on_chips(chips, tok_total, acts, grads, proj_act, proj_grad, queries)
+    held = lax.all_gather(queries, "dp", axis=0, tiled=True)
     act_t, grad_t, own = project(acts, grads, proj_act, proj_grad)
-    *pieces, own = lax.optimization_barrier((*pieces, own))
-    pieces = gathered(pieces, stages[1:2])
-    own = functools.reduce(jnp.add, exchanged([own], size, *first))
-    *pieces, own = lax.optimization_barrier((*pieces, own))
-    pieces = gathered(pieces, stages[2:-1])
-    terms = exchanged([own], size, *second)
-    *both, = lax.optimization_barrier((*pieces, *terms))
-    pieces, terms = both[: len(pieces)], both[len(pieces) :]
-    pieces = gathered(pieces, stages[max(2, len(stages) - 1) :])
-    moved = precondition(tok_total, terms, act_t, grad_t)
-    return score(size, moved, pieces)
+    own = lax.psum(own, "dp")
+    moved = precondition(tok_total, own, own, act_t, grad_t)
+    return score(lambda me: list(range(size)), moved, held, held)
 
 
 def solution(mesh):

time: 32 us -> 44.8 us (1.40)
  starting transfers between devices: 13.4 us -> 21.8 us
  waiting for transfers between devices: 6.63 us -> 10.6 us
    ppermute x10 -> x12, starting transfers between devices: 13.4 us -> 21.8 us  [moved_by(): return lax.ppermute(value, 'dp', pairs)]
    ppermute x10 -> x12, waiting for transfers between devices: 6.63 us -> 10.6 us  [moved_by(): return lax.ppermute(value, 'dp', pairs)]
  transfers between devices with their start and end apart: 10 -> 12, of which waited for: 6 -> 3; matrix products, arithmetic and copies ran while one was open for 0% -> 0% of each run, Pallas kernels for 29% -> 21%
where the time goes in v8:
time: 44.8 us; the launch traced here: 44.5 us
  starting transfers between devices  21.8 us (49%)
  Pallas kernels  11.7 us (26%)
  waiting for transfers between devices  10.6 us (24%)
    ppermute x12, starting transfers between devices, moved_by(): return lax.ppermute(value, 'dp', pairs)  21.8 us
    ppermute x12, waiting for transfers between devices, moved_by(): return lax.ppermute(value, 'dp', pairs)  10.6 us
    pallas_call x1, Pallas kernels, project(): pl.pallas_call(project_kernel, out_shape=(jax.ShapeDtypeStruct((factor, t...  6.06 us
    pallas_call x1, Pallas kernels, precondition(): pl.pallas_call(functools.partial(precondition_kernel, tok_total), out_sha...  3.11 us
    pallas_call x1, Pallas kernels, score(): pl.pallas_call(functools.partial(score_kernel, owners), out_shape=jax.Sha...  2.56 us
  transfers between devices with their start and end apart: 12, of which 3 were waited for; matrix products, arithmetic and copies ran while one was open for 0% of the time, Pallas kernels for 21%

profile of v8, /device:TPU:0, one launch (start us, length us, event | category | flops | bytes accessed | tf_op | source)
XLA Modules:
  0.0 44.5 jit_solution(17754806284618568446)
XLA Ops:
  0.0 4.0 %collective-permute-start = (bf16[8,4096]{1,0:T(8,128)(2,1)}, bf16[8,4096]{1,0:T(8,128)(2,1)S(1)}, u32[]{:S(2)}, u32[]{:S(2)}) collective-permute-start(bf16[8,4096]{1,0:T(8,128)(2,1)} %param.9), channel_id=1, source_target_pairs={{0,8},{2,10},{4,12},{6,14},{8,0},{10,2},{12,4},{14,6},{1,9},{3,11}... | collective-permute-start | bytes 196616 | tf_op jit(solution)/shard_map/ppermute | solution.py:260
  4.0 1.6 %collective-permute-start.1 = (bf16[8,4096]{1,0:T(8,128)(2,1)}, bf16[8,4096]{1,0:T(8,128)(2,1)S(1)}, u32[]{:S(2)}, u32[]{:S(2)}) collective-permute-start(bf16[8,4096]{1,0:T(8,128)(2,1)} %param.9), channel_id=1, source_target_pairs={{0,4},{2,6},{4,0},{6,2},{8,12},{10,14},{12,8},{14,10},{1,5},{3,7},... | collective-permute-start | bytes 196616 | tf_op jit(solution)/shard_map/ppermute | solution.py:260
  5.6 6.1 %project.1 = (f32[64,512]{1,0:T(8,128)S(1)}, f32[64,512]{1,0:T(8,128)S(1)}, f32[64,128]{1,0:T(8,128)S(1)}) custom-call(bf16[512,4096]{1,0:T(8,128)(2,1)} %acts.1, bf16[512,4096]{1,0:T(8,128)(2,1)} %grads.1, bf16[64,4096]{1,0:T(8,128)(2,1)} %bitcast.2, bf16[64,4096]{1,0:T(8,128)(2,1)} %bitcast.3), custom_call_target="tpu_custom_call" | custom-call | flops 536870912 | bytes 8388608 | tf_op jit(solution)/shard_map/project/pallas_call | solution.py:89
  11.7 0.0 collective-permute-done
  11.7 0.0 collective-permute-done.1
  11.8 1.3 %collective-permute-start.2 = (bf16[24,4096]{1,0:T(8,128)(2,1)S(1)}, bf16[24,4096]{1,0:T(8,128)(2,1)S(1)}, u32[]{:S(2)}, u32[]{:S(2)}) collective-permute-start(bf16[24,4096]{1,0:T(8,128)(2,1)S(1)} %constant_dynamic-update-slice_fusion), channel_id=1, source_target_pairs={{1,0},{3,2},{5,4},{7,6},{9,8},{11,10},{13,12},{15,14},{17,16},{19,... | collective-permute-start | bytes 589832 | tf_op jit(solution)/shard_map/ppermute | solution.py:260
  13.1 3.0 %collective-permute-start.3 = (f32[64,128]{1,0:T(8,128)S(1)}, f32[64,128]{1,0:T(8,128)S(1)}, u32[]{:S(2)}, u32[]{:S(2)}) collective-permute-start(f32[64,128]{1,0:T(8,128)S(1)} %get-tuple-element.23), channel_id=1, source_target_pairs={{0,1},{2,3},{4,5},{6,7},{8,9},{10,11},{12,13},{14,15},{16,17},{18,... | collective-permute-start | bytes 98312 | tf_op jit(solution)/shard_map/ppermute | solution.py:260
  16.1 0.8 %collective-permute-done.3 = f32[64,128]{1,0:T(8,128)S(1)} collective-permute-done((f32[64,128]{1,0:T(8,128)S(1)}, f32[64,128]{1,0:T(8,128)S(1)}, u32[]{:S(2)}, u32[]{:S(2)}) %collective-permute-start.3) | collective-permute-done | bytes 32800 | tf_op jit(solution)/shard_map/ppermute | solution.py:260
  16.9 0.0 collective-permute-done.2
  17.0 2.4 %collective-permute-start.4 = (bf16[16,4096]{1,0:T(8,128)(2,1)S(1)}, bf16[16,4096]{1,0:T(8,128)(2,1)S(1)}, u32[]{:S(2)}, u32[]{:S(2)}) collective-permute-start(bf16[16,4096]{1,0:T(8,128)(2,1)S(1)} %pad_maximum_fusion), channel_id=1, source_target_pairs={{0,4},{2,6},{4,0},{6,2},{8,12},{10,14},{12,8},{14,10},{16,20},{18,... | collective-permute-start | bytes 393224 | tf_op jit(solution)/shard_map/ppermute | solution.py:260
  19.4 4.5 %collective-permute-done.4 = bf16[16,4096]{1,0:T(8,128)(2,1)S(1)} collective-permute-done((bf16[16,4096]{1,0:T(8,128)(2,1)S(1)}, bf16[16,4096]{1,0:T(8,128)(2,1)S(1)}, u32[]{:S(2)}, u32[]{:S(2)}) %collective-permute-start.4) | collective-permute-done | bytes 131104 | tf_op jit(solution)/shard_map/ppermute | solution.py:260
  23.9 3.4 %collective-permute-start.5 = (bf16[64,4096]{1,0:T(8,128)(2,1)S(1)}, bf16[64,4096]{1,0:T(8,128)(2,1)S(1)}, u32[]{:S(2)}, u32[]{:S(2)}) collective-permute-start(bf16[64,4096]{1,0:T(8,128)(2,1)S(1)} %constant_dynamic-update-slice_fusion.3), channel_id=1, source_target_pairs={{0,2},{2,0},{4,6},{6,4},{8,10},{10,8},{12,14},{14,12},{16,18},{18,... | collective-permute-start | bytes 1572872 | tf_op jit(solution)/shard_map/ppermute | solution.py:260
  27.3 0.7 %collective-permute-start.6 = (f32[64,128]{1,0:T(8,128)S(1)}, f32[64,128]{1,0:T(8,128)S(1)}, u32[]{:S(2)}, u32[]{:S(2)}) collective-permute-start(f32[64,128]{1,0:T(8,128)S(1)} %add.15), channel_id=1, source_target_pairs={{1,3},{3,1},{5,7},{7,5},{9,11},{11,9},{13,15},{15,13},{17,19},{19,... | collective-permute-start | bytes 98312 | tf_op jit(solution)/shard_map/ppermute | solution.py:260
  28.0 0.7 %collective-permute-start.9 = (f32[64,128]{1,0:T(8,128)S(1)}, f32[64,128]{1,0:T(8,128)S(1)}, u32[]{:S(2)}, u32[]{:S(2)}) collective-permute-start(f32[64,128]{1,0:T(8,128)S(1)} %add.16), channel_id=1, source_target_pairs={{1,13},{3,15},{5,9},{7,11},{9,5},{11,7},{13,1},{15,3},{17,29},{19,... | collective-permute-start | bytes 98312 | tf_op jit(solution)/shard_map/ppermute | solution.py:260
  28.7 0.7 %collective-permute-start.8 = (f32[64,128]{1,0:T(8,128)S(1)}, f32[64,128]{1,0:T(8,128)S(1)}, u32[]{:S(2)}, u32[]{:S(2)}) collective-permute-start(f32[64,128]{1,0:T(8,128)S(1)} %add.16), channel_id=1, source_target_pairs={{1,9},{3,11},{5,13},{7,15},{9,1},{11,3},{13,5},{15,7},{17,25},{19,... | collective-permute-start | bytes 98312 | tf_op jit(solution)/shard_map/ppermute | solution.py:260
  29.4 0.7 %collective-permute-start.7 = (f32[64,128]{1,0:T(8,128)S(1)}, f32[64,128]{1,0:T(8,128)S(1)}, u32[]{:S(2)}, u32[]{:S(2)}) collective-permute-start(f32[64,128]{1,0:T(8,128)S(1)} %add.16), channel_id=1, source_target_pairs={{1,5},{3,7},{5,1},{7,3},{9,13},{11,15},{13,9},{15,11},{17,21},{19,... | collective-permute-start | bytes 98312 | tf_op jit(solution)/shard_map/ppermute | solution.py:260
  30.1 0.0 collective-permute-done.8
  30.1 0.0 collective-permute-done.7
  30.1 1.3 %collective-permute-start.10 = (f32[64,128]{1,0:T(8,128)S(1)}, f32[64,128]{1,0:T(8,128)S(1)}, u32[]{:S(2)}, u32[]{:S(2)}) collective-permute-start(f32[64,128]{1,0:T(8,128)S(1)} %add_add_fusion.own), channel_id=1, source_target_pairs={{1,0},{3,2},{5,4},{7,6},{9,8},{11,10},{13,12},{15,14},{17,16},{19,... | collective-permute-start | bytes 98312 | tf_op jit(solution)/shard_map/ppermute | solution.py:260
  31.4 5.2 %collective-permute-done.10.other = f32[64,128]{1,0:T(8,128)S(1)} collective-permute-done((f32[64,128]{1,0:T(8,128)S(1)}, f32[64,128]{1,0:T(8,128)S(1)}, u32[]{:S(2)}, u32[]{:S(2)}) %collective-permute-start.10) | collective-permute-done | bytes 32800 | tf_op jit(solution)/shard_map/ppermute | solution.py:260
  36.7 2.1 %collective-permute-start.11 = (bf16[128,4096]{1,0:T(8,128)(2,1)S(1)}, bf16[128,4096]{1,0:T(8,128)(2,1)S(1)}, u32[]{:S(2)}, u32[]{:S(2)}) collective-permute-start(bf16[128,4096]{1,0:T(8,128)(2,1)S(1)} %constant_dynamic-update-slice_fusion.6.own), channel_id=1, source_target_pairs={{0,1},{2,3},{4,5},{6,7},{8,9},{10,11},{12,13},{14,15},{16,17},{18,... | collective-permute-start | bytes 3145736 | tf_op jit(solution)/shard_map/ppermute | solution.py:260
  38.9 3.1 %precondition.1.moved = f32[128,512]{1,0:T(8,128)S(1)} custom-call(f32[64,128]{1,0:T(8,128)S(1)} %add_add_fusion.own, f32[64,128]{1,0:T(8,128)S(1)} %collective-permute-done.10.other, f32[64,512]{1,0:T(8,128)S(1)} %get-tuple-element.29.act_t, f32[64,512]{1,0:T(8,128)S(1)} %get-tuple-element.30.grad_t), custom_call_target="tpu_custom_call" | custom-call | flops 3355443200 | bytes 524288 | tf_op jit(solution)/shard_map/precondition/pallas_call | solution.py:192
  42.0 0.0 collective-permute-done.11.other
  42.0 2.6 %score.1 = f32[512,128]{1,0:T(8,128)} custom-call(f32[128,512]{1,0:T(8,128)S(1)} %precondition.1.moved, bf16[128,4096]{1,0:T(8,128)(2,1)S(1)} %constant_dynamic-update-slice_fusion.6.own, bf16[128,4096]{1,0:T(8,128)(2,1)S(1)} %collective-permute-done.11.other), custom_call_target="tpu_custom_call" | custom-call | tf_op jit(solution)/shard_map/score/pallas_call | solution.py:237
  (19 shorter events, 0.2 us)
Async XLA Ops:
  0.0 11.7 %collective-permute-start = (bf16[8,4096]{1,0:T(8,128)(2,1)}, bf16[8,4096]{1,0:T(8,128)(2,1)S(1)}, u32[]{:S(2)}, u32[]{:S(2)}) collective-permute-start(bf16[8,4096]{1,0:T(8,128)(2,1)} %param.9), channel_id=1, source_target_pairs={{0,8},{2,10},{4,12},{6,14},{8,0},{10,2},{12,4},{14,6},{1,9},{3,11}... | collective-permute-start | bytes 196616 | tf_op jit(solution)/shard_map/ppermute | solution.py:260
  4.0 7.7 %collective-permute-start.1 = (bf16[8,4096]{1,0:T(8,128)(2,1)}, bf16[8,4096]{1,0:T(8,128)(2,1)S(1)}, u32[]{:S(2)}, u32[]{:S(2)}) collective-permute-start(bf16[8,4096]{1,0:T(8,128)(2,1)} %param.9), channel_id=1, source_target_pairs={{0,4},{2,6},{4,0},{6,2},{8,12},{10,14},{12,8},{14,10},{1,5},{3,7},... | collective-permute-start | bytes 196616 | tf_op jit(solution)/shard_map/ppermute | solution.py:260
  5.6 6.1 %copy-start = (bf16[8,4096]{1,0:T(8,128)(2,1)S(1)}, bf16[8,4096]{1,0:T(8,128)(2,1)}, u32[]{:S(2)}) copy-start(bf16[8,4096]{1,0:T(8,128)(2,1)} %param.9) | copy-start | bytes 196612
  11.8 5.2 %collective-permute-start.2 = (bf16[24,4096]{1,0:T(8,128)(2,1)S(1)}, bf16[24,4096]{1,0:T(8,128)(2,1)S(1)}, u32[]{:S(2)}, u32[]{:S(2)}) collective-permute-start(bf16[24,4096]{1,0:T(8,128)(2,1)S(1)} %constant_dynamic-update-slice_fusion), channel_id=1, source_target_pairs={{1,0},{3,2},{5,4},{7,6},{9,8},{11,10},{13,12},{15,14},{17,16},{19,... | collective-permute-start | bytes 589832 | tf_op jit(solution)/shard_map/ppermute | solution.py:260
  13.1 3.9 %collective-permute-start.3 = (f32[64,128]{1,0:T(8,128)S(1)}, f32[64,128]{1,0:T(8,128)S(1)}, u32[]{:S(2)}, u32[]{:S(2)}) collective-permute-start(f32[64,128]{1,0:T(8,128)S(1)} %get-tuple-element.23), channel_id=1, source_target_pairs={{0,1},{2,3},{4,5},{6,7},{8,9},{10,11},{12,13},{14,15},{16,17},{18,... | collective-permute-start | bytes 98312 | tf_op jit(solution)/shard_map/ppermute | solution.py:260
  17.0 6.9 %collective-permute-start.4 = (bf16[16,4096]{1,0:T(8,128)(2,1)S(1)}, bf16[16,4096]{1,0:T(8,128)(2,1)S(1)}, u32[]{:S(2)}, u32[]{:S(2)}) collective-permute-start(bf16[16,4096]{1,0:T(8,128)(2,1)S(1)} %pad_maximum_fusion), channel_id=1, source_target_pairs={{0,4},{2,6},{4,0},{6,2},{8,12},{10,14},{12,8},{14,10},{16,20},{18,... | collective-permute-start | bytes 393224 | tf_op jit(solution)/shard_map/ppermute | solution.py:260
  23.9 12.7 %collective-permute-start.5 = (bf16[64,4096]{1,0:T(8,128)(2,1)S(1)}, bf16[64,4096]{1,0:T(8,128)(2,1)S(1)}, u32[]{:S(2)}, u32[]{:S(2)}) collective-permute-start(bf16[64,4096]{1,0:T(8,128)(2,1)S(1)} %constant_dynamic-update-slice_fusion.3), channel_id=1, source_target_pairs={{0,2},{2,0},{4,6},{6,4},{8,10},{10,8},{12,14},{14,12},{16,18},{18,... | collective-permute-start | bytes 1572872 | tf_op jit(solution)/shard_map/ppermute | solution.py:260
  27.3 0.7 %collective-permute-start.6 = (f32[64,128]{1,0:T(8,128)S(1)}, f32[64,128]{1,0:T(8,128)S(1)}, u32[]{:S(2)}, u32[]{:S(2)}) collective-permute-start(f32[64,128]{1,0:T(8,128)S(1)} %add.15), channel_id=1, source_target_pairs={{1,3},{3,1},{5,7},{7,5},{9,11},{11,9},{13,15},{15,13},{17,19},{19,... | collective-permute-start | bytes 98312 | tf_op jit(solution)/shard_map/ppermute | solution.py:260
  28.0 2.0 %collective-permute-start.9 = (f32[64,128]{1,0:T(8,128)S(1)}, f32[64,128]{1,0:T(8,128)S(1)}, u32[]{:S(2)}, u32[]{:S(2)}) collective-permute-start(f32[64,128]{1,0:T(8,128)S(1)} %add.16), channel_id=1, source_target_pairs={{1,13},{3,15},{5,9},{7,11},{9,5},{11,7},{13,1},{15,3},{17,29},{19,... | collective-permute-start | bytes 98312 | tf_op jit(solution)/shard_map/ppermute | solution.py:260
  28.7 1.4 %collective-permute-start.8 = (f32[64,128]{1,0:T(8,128)S(1)}, f32[64,128]{1,0:T(8,128)S(1)}, u32[]{:S(2)}, u32[]{:S(2)}) collective-permute-start(f32[64,128]{1,0:T(8,128)S(1)} %add.16), channel_id=1, source_target_pairs={{1,9},{3,11},{5,13},{7,15},{9,1},{11,3},{13,5},{15,7},{17,25},{19,... | collective-permute-start | bytes 98312 | tf_op jit(solution)/shard_map/ppermute | solution.py:260
  29.4 0.7 %collective-permute-start.7 = (f32[64,128]{1,0:T(8,128)S(1)}, f32[64,128]{1,0:T(8,128)S(1)}, u32[]{:S(2)}, u32[]{:S(2)}) collective-permute-start(f32[64,128]{1,0:T(8,128)S(1)} %add.16), channel_id=1, source_target_pairs={{1,5},{3,7},{5,1},{7,3},{9,13},{11,15},{13,9},{15,11},{17,21},{19,... | collective-permute-start | bytes 98312 | tf_op jit(solution)/shard_map/ppermute | solution.py:260
  30.1 6.5 %collective-permute-start.10 = (f32[64,128]{1,0:T(8,128)S(1)}, f32[64,128]{1,0:T(8,128)S(1)}, u32[]{:S(2)}, u32[]{:S(2)}) collective-permute-start(f32[64,128]{1,0:T(8,128)S(1)} %add_add_fusion.own), channel_id=1, source_target_pairs={{1,0},{3,2},{5,4},{7,6},{9,8},{11,10},{13,12},{15,14},{17,16},{19,... | collective-permute-start | bytes 98312 | tf_op jit(solution)/shard_map/ppermute | solution.py:260
  36.7 5.3 %collective-permute-start.11 = (bf16[128,4096]{1,0:T(8,128)(2,1)S(1)}, bf16[128,4096]{1,0:T(8,128)(2,1)S(1)}, u32[]{:S(2)}, u32[]{:S(2)}) collective-permute-start(bf16[128,4096]{1,0:T(8,128)(2,1)S(1)} %constant_dynamic-update-slice_fusion.6.own), channel_id=1, source_target_pairs={{0,1},{2,3},{4,5},{6,7},{8,9},{10,11},{12,13},{14,15},{16,17},{18,... | collective-permute-start | bytes 3145736 | tf_op jit(solution)/shard_map/ppermute | solution.py:260

commit v9 on v6

--- a/solution.py
+++ b/solution.py
@@ -10,7 +10,8 @@
 DAMP = 0.1
 HIGHEST = lax.Precision.HIGHEST
 COPY_ROWS = 128
-IN_FLIGHT = 4
+IN_FLIGHT = 8
+TOKENS_AT_ONCE = 256
 
 
 def project_kernel(
@@ -47,6 +48,7 @@
             weight_t[at, first : first + 512, :] = block.T.astype(weight_t.dtype)
 
     steps = [(at, part, min(2, n_parts - part)) for at in range(2) for part in range(0, n_parts, 2)]
+    last_act = len(steps) // 2 - 1
     at, part, many = steps.pop()
     steps += [(at, part + one, 1) for one in range(many)]
     grams = [None, None]
@@ -63,12 +65,12 @@
         for copy in tok_copies[at][part : part + many]:
             copy.wait()
             start_next(1)
-        if step == 1:
+        if step == last_act:
             weight_copies[1].wait()
             start_next(1)
         rows = slice(part * COPY_ROWS, (part + many) * COPY_ROWS)
         block = jnp.dot(tok_buf[at, rows, :], weight_t[at], preferred_element_type=jnp.float32)
-        if step == 1:
+        if step == last_act:
             turned(1)
         if before is not None:
             add_gram(*before)
@@ -202,45 +204,58 @@
 
 
 def score_kernel(size, n_pieces, moved, *refs):
-    queries, (scores, total, ordered) = refs[:n_pieces], refs[n_pieces:]
+    queries, (scores, ordered, result, sems) = refs[:n_pieces], refs[n_pieces:]
     factor = moved.shape[0] // 2
+    owners = owners_of(lax.axis_index("dp"), size)
     group = 4
-    act_side = moved[:factor, :]
-    for first in range(0, factor, group):
-        outer = jnp.concatenate(
-            [act_side * moved[factor + i : factor + i + 1, :] for i in range(first, first + group)], axis=0
+    copies = []
+    for part, begin in enumerate(range(0, moved.shape[1], TOKENS_AT_ONCE)):
+        tokens = slice(begin, begin + TOKENS_AT_ONCE)
+        act_side = moved[:factor, tokens]
+        total = None
+        for first in range(0, factor, group):
+            outer = jnp.concatenate(
+                [act_side * moved[factor + i : factor + i + 1, tokens] for i in range(first, first + group)], axis=0
+            )
+            high = outer.astype(jnp.bfloat16)
+            low = (outer - high.astype(jnp.float32)).astype(jnp.bfloat16)
+            columns = slice(first * factor, (first + group) * factor)
+            values = jnp.concatenate([piece[:, columns] for piece in queries], axis=0)
+            term = jnp.dot(
+                jnp.concatenate([values, values], axis=1),
+                jnp.concatenate([high, low], axis=0),
+                preferred_element_type=jnp.float32,
+            )
+            total = term if total is None else total + term
+        rows = total.shape[0] // size
+        for at, owner in enumerate(owners):
+            place = pl.ds(pl.multiple_of(owner * rows, rows), rows)
+            ordered[part, place, :] = total[at * rows : (at + 1) * rows, :]
+        result[tokens, :] = ordered[part].T
+        copies.append(
+            pltpu.make_async_copy(
+                result.at[pl.ds(begin, TOKENS_AT_ONCE), :], scores.at[pl.ds(begin, TOKENS_AT_ONCE), :], sems.at[part]
+            )
         )
-        high = outer.astype(jnp.bfloat16)
-        low = (outer - high.astype(jnp.float32)).astype(jnp.bfloat16)
-        columns = slice(first * factor, (first + group) * factor)
-        values = jnp.concatenate([piece[:, columns] for piece in queries], axis=0)
-        term = jnp.dot(
-            jnp.concatenate([values, values], axis=1),
-            jnp.concatenate([high, low], axis=0),
-            preferred_element_type=jnp.float32,
-        )
-        if first == 0:
-            total[...] = term
-        else:
-            total[...] += term
-    rows = total.shape[0] // size
-    for at, owner in enumerate(owners_of(lax.axis_index("dp"), size)):
-        ordered[pl.ds(pl.multiple_of(owner * rows, rows), rows), :] = total[at * rows : (at + 1) * rows, :]
-    scores[...] = ordered[...].T
+        copies[-1].start()
+    for copy in copies:
+        copy.wait()
 
 
 def score(size, moved, queries):
     tok_rows = moved.shape[1]
     n_queries = sum(piece.shape[0] for piece in queries)
     n_pieces = len(queries)
+    n_parts = tok_rows // TOKENS_AT_ONCE
     return pl.pallas_call(
         functools.partial(score_kernel, size, n_pieces),
         out_shape=jax.ShapeDtypeStruct((tok_rows, n_queries), jnp.float32),
         in_specs=[pl.BlockSpec(memory_space=pltpu.VMEM)] * (1 + n_pieces),
-        out_specs=pl.BlockSpec(memory_space=pltpu.VMEM),
+        out_specs=pl.BlockSpec(memory_space=pl.ANY),
         scratch_shapes=[
-            pltpu.VMEM((n_queries, tok_rows), jnp.float32),
-            pltpu.VMEM((n_queries, tok_rows), jnp.float32),
+            pltpu.VMEM((n_parts, n_queries, TOKENS_AT_ONCE), jnp.float32),
+            pltpu.VMEM((tok_rows, n_queries), jnp.float32),
+            pltpu.SemaphoreType.DMA((n_parts,)),
         ],
         compiler_params=pltpu.CompilerParams(vmem_limit_bytes=32 * 2**20),
         name="score",
@@ -302,10 +317,14 @@
             pieces = exchanged(pieces, size, *stage)
         return pieces
 
-    pieces = gathered([queries], stages[:1])
+    if len(stages) > 1:
+        pieces = [queries] + [swapped(queries, size, *stage, 1) for stage in stages[:2]]
+    else:
+        pieces = exchanged([queries], size, *stages[0])
     act_t, grad_t, own = project(acts, grads, proj_act, proj_grad)
     *pieces, own = lax.optimization_barrier((*pieces, own))
-    pieces = gathered(pieces, stages[1:2])
+    if len(stages) > 1:
+        pieces.append(swapped(pieces[1], size, *stages[1], 1))
     own = functools.reduce(jnp.add, exchanged([own], size, *first))
     *pieces, own = lax.optimization_barrier((*pieces, own))
     pieces = gathered(pieces, stages[2:-1])

time: 32 us -> 32.3 us (level)
  waiting for transfers between devices: 6.63 us -> 5.7 us
  Pallas kernels: 11.6 us -> 12.2 us
  starting transfers between devices: 13.4 us -> 14 us
    ppermute x10 -> x11, waiting for transfers between devices: 6.63 us -> 5.7 us  [swapped(): return lax.ppermute(value, 'dp', perm)]
    pallas_call x1, Pallas kernels: 6.06 us -> 6.69 us  [project(): pl.pallas_call(project_kernel, out_shape=(jax.ShapeDtypeStruct((factor, t...]
    ppermute x10 -> x11, starting transfers between devices: 13.4 us -> 14 us  [swapped(): return lax.ppermute(value, 'dp', perm)]
  transfers between devices with their start and end apart: 10 -> 11, of which waited for: 6 -> 5; matrix products, arithmetic and copies ran while one was open for 0% -> 0% of each run, Pallas kernels for 29% -> 30%
where the time goes in v9:
time: 32.3 us; the launch traced here: 32.1 us
  starting transfers between devices  14 us (43%)
  Pallas kernels  12.2 us (38%)
  waiting for transfers between devices  5.7 us (18%)
    ppermute x11, starting transfers between devices, swapped(): return lax.ppermute(value, 'dp', perm)  14 us
    pallas_call x1, Pallas kernels, project(): pl.pallas_call(project_kernel, out_shape=(jax.ShapeDtypeStruct((factor, t...  6.69 us
    ppermute x11, waiting for transfers between devices, swapped(): return lax.ppermute(value, 'dp', perm)  5.7 us
    pallas_call x1, Pallas kernels, precondition(): pl.pallas_call(functools.partial(precondition_kernel, tok_total, n_terms)...  3.09 us
    pallas_call x1, Pallas kernels, score(): pl.pallas_call(functools.partial(score_kernel, size, n_pieces), out_shape...  2.44 us
  transfers between devices with their start and end apart: 11, of which 5 were waited for; matrix products, arithmetic and copies ran while one was open for 0% of the time, Pallas kernels for 30%

profile of v9, /device:TPU:0, one launch (start us, length us, event | category | flops | bytes accessed | tf_op | source)
XLA Modules:
  0.0 32.1 jit_solution(10909383288178832771)
XLA Ops:
  0.0 4.0 %collective-permute-start = (bf16[8,4096]{1,0:T(8,128)(2,1)}, bf16[8,4096]{1,0:T(8,128)(2,1)S(1)}, u32[]{:S(2)}, u32[]{:S(2)}) collective-permute-start(bf16[8,4096]{1,0:T(8,128)(2,1)} %param.9), channel_id=1, source_target_pairs={{0,8},{1,9},{2,10},{3,11},{4,12},{5,13},{6,14},{7,15},{8,0},{9,1},... | collective-permute-start | bytes 196616 | tf_op jit(solution)/shard_map/ppermute | solution.py:291
  4.0 1.6 %collective-permute-start.1 = (bf16[8,4096]{1,0:T(8,128)(2,1)}, bf16[8,4096]{1,0:T(8,128)(2,1)S(1)}, u32[]{:S(2)}, u32[]{:S(2)}) collective-permute-start(bf16[8,4096]{1,0:T(8,128)(2,1)} %param.9), channel_id=1, source_target_pairs={{0,4},{1,5},{2,6},{3,7},{4,0},{5,1},{6,2},{7,3},{8,12},{9,13},{10,... | collective-permute-start | bytes 196616 | tf_op jit(solution)/shard_map/ppermute | solution.py:291
  5.6 6.7 %project.1 = (f32[64,512]{1,0:T(8,128)S(1)}, f32[64,512]{1,0:T(8,128)S(1)}, f32[64,128]{1,0:T(8,128)S(1)}) custom-call(bf16[512,4096]{1,0:T(8,128)(2,1)} %acts.1, bf16[512,4096]{1,0:T(8,128)(2,1)} %grads.1, bf16[64,4096]{1,0:T(8,128)(2,1)} %bitcast.2, bf16[64,4096]{1,0:T(8,128)(2,1)} %bitcast.3), custom_call_target="tpu_custom_call" | custom-call | flops 536870912 | bytes 8388608 | tf_op jit(solution)/shard_map/project/pallas_call | solution.py:90
  12.3 0.0 collective-permute-done
  12.3 0.0 collective-permute-done.1
  12.3 0.5 %collective-permute-start.5 = (f32[64,128]{1,0:T(8,128)S(1)}, f32[64,128]{1,0:T(8,128)S(1)}, u32[]{:S(2)}, u32[]{:S(2)}) collective-permute-start(f32[64,128]{1,0:T(8,128)S(1)} %get-tuple-element.27), channel_id=1, source_target_pairs={{0,3},{1,2},{2,1},{3,0},{4,7},{5,6},{6,5},{7,4},{8,11},{9,10},{10,... | collective-permute-start | bytes 98312 | tf_op jit(solution)/shard_map/ppermute | solution.py:291
  12.8 1.2 %collective-permute-start.4 = (f32[64,128]{1,0:T(8,128)S(1)}, f32[64,128]{1,0:T(8,128)S(1)}, u32[]{:S(2)}, u32[]{:S(2)}) collective-permute-start(f32[64,128]{1,0:T(8,128)S(1)} %get-tuple-element.27), channel_id=1, source_target_pairs={{0,2},{1,3},{2,0},{3,1},{4,6},{5,7},{6,4},{7,5},{8,10},{9,11},{10,... | collective-permute-start | bytes 98312 | tf_op jit(solution)/shard_map/ppermute | solution.py:291
  14.0 0.3 collective-permute-start.3
  14.3 0.4 %collective-permute-start.2 = (bf16[8,4096]{1,0:T(8,128)(2,1)S(1)}, bf16[8,4096]{1,0:T(8,128)(2,1)S(1)}, u32[]{:S(2)}, u32[]{:S(2)}) collective-permute-start(bf16[8,4096]{1,0:T(8,128)(2,1)S(1)} %collective-permute-done), channel_id=1, source_target_pairs={{0,4},{1,5},{2,6},{3,7},{4,0},{5,1},{6,2},{7,3},{8,12},{9,13},{10,... | collective-permute-start | bytes 196616 | tf_op jit(solution)/shard_map/ppermute | solution.py:291
  14.7 1.3 %collective-permute-done.5 = f32[64,128]{1,0:T(8,128)S(1)} collective-permute-done((f32[64,128]{1,0:T(8,128)S(1)}, f32[64,128]{1,0:T(8,128)S(1)}, u32[]{:S(2)}, u32[]{:S(2)}) %collective-permute-start.5) | collective-permute-done | bytes 32800 | tf_op jit(solution)/shard_map/ppermute | solution.py:291
  16.0 0.8 %collective-permute-done.4 = f32[64,128]{1,0:T(8,128)S(1)} collective-permute-done((f32[64,128]{1,0:T(8,128)S(1)}, f32[64,128]{1,0:T(8,128)S(1)}, u32[]{:S(2)}, u32[]{:S(2)}) %collective-permute-start.4) | collective-permute-done | bytes 32800 | tf_op jit(solution)/shard_map/ppermute | solution.py:291
  16.8 0.0 collective-permute-done.3
  16.8 1.7 %collective-permute-done.2 = bf16[8,4096]{1,0:T(8,128)(2,1)S(1)} collective-permute-done((bf16[8,4096]{1,0:T(8,128)(2,1)S(1)}, bf16[8,4096]{1,0:T(8,128)(2,1)S(1)}, u32[]{:S(2)}, u32[]{:S(2)}) %collective-permute-start.2) | collective-permute-done | bytes 65568 | tf_op jit(solution)/shard_map/ppermute | solution.py:291
  18.6 1.6 %collective-permute-start.6 = (bf16[32,4096]{1,0:T(8,128)(2,1)S(1)}, bf16[32,4096]{1,0:T(8,128)(2,1)S(1)}, u32[]{:S(2)}, u32[]{:S(2)}) collective-permute-start(bf16[32,4096]{1,0:T(8,128)(2,1)S(1)} %constant_dynamic-update-slice_fusion), channel_id=1, source_target_pairs={{0,2},{1,3},{2,0},{3,1},{4,6},{5,7},{6,4},{7,5},{8,10},{9,11},{10,... | collective-permute-start | bytes 786440 | tf_op jit(solution)/shard_map/ppermute | solution.py:291
  20.2 0.2 collective-permute-start.9
  20.4 1.7 %collective-permute-start.8 = (f32[64,128]{1,0:T(8,128)S(1)}, f32[64,128]{1,0:T(8,128)S(1)}, u32[]{:S(2)}, u32[]{:S(2)}) collective-permute-start(f32[64,128]{1,0:T(8,128)S(1)} %add_add_fusion.refs_0_), channel_id=1, source_target_pairs={{0,8},{1,9},{2,10},{3,11},{4,12},{5,13},{6,14},{7,15},{8,0},{9,1},... | collective-permute-start | bytes 98312 | tf_op jit(solution)/shard_map/ppermute | solution.py:291
  22.1 2.5 %collective-permute-start.7 = (f32[64,128]{1,0:T(8,128)S(1)}, f32[64,128]{1,0:T(8,128)S(1)}, u32[]{:S(2)}, u32[]{:S(2)}) collective-permute-start(f32[64,128]{1,0:T(8,128)S(1)} %add_add_fusion.refs_0_), channel_id=1, source_target_pairs={{0,4},{1,5},{2,6},{3,7},{4,0},{5,1},{6,2},{7,3},{8,12},{9,13},{10,... | collective-permute-start | bytes 98312 | tf_op jit(solution)/shard_map/ppermute | solution.py:291
  24.6 1.3 %collective-permute-done.9.refs_3_ = f32[64,128]{1,0:T(8,128)S(1)} collective-permute-done((f32[64,128]{1,0:T(8,128)S(1)}, f32[64,128]{1,0:T(8,128)S(1)}, u32[]{:S(2)}, u32[]{:S(2)}) %collective-permute-start.9) | collective-permute-done | bytes 32800 | tf_op jit(solution)/shard_map/ppermute | solution.py:291
  25.9 0.6 %collective-permute-done.7.refs_1_ = f32[64,128]{1,0:T(8,128)S(1)} collective-permute-done((f32[64,128]{1,0:T(8,128)S(1)}, f32[64,128]{1,0:T(8,128)S(1)}, u32[]{:S(2)}, u32[]{:S(2)}) %collective-permute-start.7) | collective-permute-done | bytes 32800 | tf_op jit(solution)/shard_map/ppermute | solution.py:291
  26.4 0.0 collective-permute-done.6
  26.5 0.1 collective-permute-start.10
  26.6 3.1 %precondition.1.moved = f32[128,512]{1,0:T(8,128)S(1)} custom-call(f32[64,128]{1,0:T(8,128)S(1)} %add_add_fusion.refs_0_, f32[64,128]{1,0:T(8,128)S(1)} %collective-permute-done.7.refs_1_, f32[64,128]{1,0:T(8,128)S(1)} %collective-permute-done.8.refs_2_, f32[64,128]{1,0:T(8,128)S(1)} %collective-permute-done.9.refs_3_, ...), custom_call_target="tpu_custom_call" | custom-call | flops 3355443200 | bytes 524288 | tf_op jit(solution)/shard_map/precondition/pallas_call | solution.py:193
  29.7 0.0 collective-permute-done.10.refs_1_
  29.7 2.4 %score.1 = f32[512,128]{1,0:T(8,128)} custom-call(f32[128,512]{1,0:T(8,128)S(1)} %precondition.1.moved, bf16[64,4096]{1,0:T(8,128)(2,1)S(1)} %constant_dynamic-update-slice_fusion.4.refs_0_, bf16[64,4096]{1,0:T(8,128)(2,1)S(1)} %collective-permute-done.10.refs_1_), custom_call_target="tpu_custom_call" | custom-call | tf_op jit(solution)/shard_map/score/pallas_call | solution.py:250
  (10 shorter events, 0.1 us)
Async XLA Ops:
  0.0 12.3 %collective-permute-start = (bf16[8,4096]{1,0:T(8,128)(2,1)}, bf16[8,4096]{1,0:T(8,128)(2,1)S(1)}, u32[]{:S(2)}, u32[]{:S(2)}) collective-permute-start(bf16[8,4096]{1,0:T(8,128)(2,1)} %param.9), channel_id=1, source_target_pairs={{0,8},{1,9},{2,10},{3,11},{4,12},{5,13},{6,14},{7,15},{8,0},{9,1},... | collective-permute-start | bytes 196616 | tf_op jit(solution)/shard_map/ppermute | solution.py:291
  4.0 8.3 %collective-permute-start.1 = (bf16[8,4096]{1,0:T(8,128)(2,1)}, bf16[8,4096]{1,0:T(8,128)(2,1)S(1)}, u32[]{:S(2)}, u32[]{:S(2)}) collective-permute-start(bf16[8,4096]{1,0:T(8,128)(2,1)} %param.9), channel_id=1, source_target_pairs={{0,4},{1,5},{2,6},{3,7},{4,0},{5,1},{6,2},{7,3},{8,12},{9,13},{10,... | collective-permute-start | bytes 196616 | tf_op jit(solution)/shard_map/ppermute | solution.py:291
  5.6 12.9 %copy-start = (bf16[8,4096]{1,0:T(8,128)(2,1)S(1)}, bf16[8,4096]{1,0:T(8,128)(2,1)}, u32[]{:S(2)}) copy-start(bf16[8,4096]{1,0:T(8,128)(2,1)} %param.9) | copy-start | bytes 196612
  12.3 3.7 %collective-permute-start.5 = (f32[64,128]{1,0:T(8,128)S(1)}, f32[64,128]{1,0:T(8,128)S(1)}, u32[]{:S(2)}, u32[]{:S(2)}) collective-permute-start(f32[64,128]{1,0:T(8,128)S(1)} %get-tuple-element.27), channel_id=1, source_target_pairs={{0,3},{1,2},{2,1},{3,0},{4,7},{5,6},{6,5},{7,4},{8,11},{9,10},{10,... | collective-permute-start | bytes 98312 | tf_op jit(solution)/shard_map/ppermute | solution.py:291
  12.8 4.0 %collective-permute-start.4 = (f32[64,128]{1,0:T(8,128)S(1)}, f32[64,128]{1,0:T(8,128)S(1)}, u32[]{:S(2)}, u32[]{:S(2)}) collective-permute-start(f32[64,128]{1,0:T(8,128)S(1)} %get-tuple-element.27), channel_id=1, source_target_pairs={{0,2},{1,3},{2,0},{3,1},{4,6},{5,7},{6,4},{7,5},{8,10},{9,11},{10,... | collective-permute-start | bytes 98312 | tf_op jit(solution)/shard_map/ppermute | solution.py:291
  14.0 2.8 %collective-permute-start.3 = (f32[64,128]{1,0:T(8,128)S(1)}, f32[64,128]{1,0:T(8,128)S(1)}, u32[]{:S(2)}, u32[]{:S(2)}) collective-permute-start(f32[64,128]{1,0:T(8,128)S(1)} %get-tuple-element.27), channel_id=1, source_target_pairs={{0,1},{1,0},{2,3},{3,2},{4,5},{5,4},{6,7},{7,6},{8,9},{9,8},{10,11... | collective-permute-start | bytes 98312 | tf_op jit(solution)/shard_map/ppermute | solution.py:291
  14.3 4.3 %collective-permute-start.2 = (bf16[8,4096]{1,0:T(8,128)(2,1)S(1)}, bf16[8,4096]{1,0:T(8,128)(2,1)S(1)}, u32[]{:S(2)}, u32[]{:S(2)}) collective-permute-start(bf16[8,4096]{1,0:T(8,128)(2,1)S(1)} %collective-permute-done), channel_id=1, source_target_pairs={{0,4},{1,5},{2,6},{3,7},{4,0},{5,1},{6,2},{7,3},{8,12},{9,13},{10,... | collective-permute-start | bytes 196616 | tf_op jit(solution)/shard_map/ppermute | solution.py:291
  18.6 7.9 %collective-permute-start.6 = (bf16[32,4096]{1,0:T(8,128)(2,1)S(1)}, bf16[32,4096]{1,0:T(8,128)(2,1)S(1)}, u32[]{:S(2)}, u32[]{:S(2)}) collective-permute-start(bf16[32,4096]{1,0:T(8,128)(2,1)S(1)} %constant_dynamic-update-slice_fusion), channel_id=1, source_target_pairs={{0,2},{1,3},{2,0},{3,1},{4,6},{5,7},{6,4},{7,5},{8,10},{9,11},{10,... | collective-permute-start | bytes 786440 | tf_op jit(solution)/shard_map/ppermute | solution.py:291
  20.2 5.7 %collective-permute-start.9 = (f32[64,128]{1,0:T(8,128)S(1)}, f32[64,128]{1,0:T(8,128)S(1)}, u32[]{:S(2)}, u32[]{:S(2)}) collective-permute-start(f32[64,128]{1,0:T(8,128)S(1)} %add_add_fusion.refs_0_), channel_id=1, source_target_pairs={{0,12},{1,13},{2,14},{3,15},{4,8},{5,9},{6,10},{7,11},{8,4},{9,5},... | collective-permute-start | bytes 98312 | tf_op jit(solution)/shard_map/ppermute | solution.py:291
  20.4 5.5 %collective-permute-start.8 = (f32[64,128]{1,0:T(8,128)S(1)}, f32[64,128]{1,0:T(8,128)S(1)}, u32[]{:S(2)}, u32[]{:S(2)}) collective-permute-start(f32[64,128]{1,0:T(8,128)S(1)} %add_add_fusion.refs_0_), channel_id=1, source_target_pairs={{0,8},{1,9},{2,10},{3,11},{4,12},{5,13},{6,14},{7,15},{8,0},{9,1},... | collective-permute-start | bytes 98312 | tf_op jit(solution)/shard_map/ppermute | solution.py:291
  22.1 4.4 %collective-permute-start.7 = (f32[64,128]{1,0:T(8,128)S(1)}, f32[64,128]{1,0:T(8,128)S(1)}, u32[]{:S(2)}, u32[]{:S(2)}) collective-permute-start(f32[64,128]{1,0:T(8,128)S(1)} %add_add_fusion.refs_0_), channel_id=1, source_target_pairs={{0,4},{1,5},{2,6},{3,7},{4,0},{5,1},{6,2},{7,3},{8,12},{9,13},{10,... | collective-permute-start | bytes 98312 | tf_op jit(solution)/shard_map/ppermute | solution.py:291
  26.5 3.2 %collective-permute-start.10 = (bf16[64,4096]{1,0:T(8,128)(2,1)S(1)}, bf16[64,4096]{1,0:T(8,128)(2,1)S(1)}, u32[]{:S(2)}, u32[]{:S(2)}) collective-permute-start(bf16[64,4096]{1,0:T(8,128)(2,1)S(1)} %constant_dynamic-update-slice_fusion.4.refs_0_), channel_id=1, source_target_pairs={{0,1},{1,0},{2,3},{3,2},{4,5},{5,4},{6,7},{7,6},{8,9},{9,8},{10,11... | collective-permute-start | bytes 1572872 | tf_op jit(solution)/shard_map/ppermute | solution.py:291

commit v10 on v9

--- a/solution.py
+++ b/solution.py
@@ -10,7 +10,7 @@
 DAMP = 0.1
 HIGHEST = lax.Precision.HIGHEST
 COPY_ROWS = 128
-IN_FLIGHT = 8
+IN_FLIGHT = 4
 TOKENS_AT_ONCE = 256
 
 
@@ -263,16 +263,15 @@
 
 
 def gather_stages(size):
-    if size & (size - 1):
-        return [(1, size)]
-    return [(size >> level, 2) for level in range(1, size.bit_length())]
-
-
-def sum_rounds(size):
     core = 2 if size % 2 == 0 else 1
     rest = size // core
     near = max(d for d in range(1, rest + 1) if rest % d == 0 and d * d <= rest)
-    return [(1, core * near), (core * near, rest // near)]
+    return [(core * near, rest // near), (core, near), (1, core)]
+
+
+def sum_rounds(size):
+    (stride, radix), *_ = gather_stages(size)
+    return [(1, stride), (stride, radix)]
 
 
 def after(value, other):
@@ -309,29 +308,18 @@
 def on_device(acts, grads, proj_act, proj_grad, queries):
     size = lax.axis_size("dp")
     tok_total = acts.shape[0] * size
-    stages = gather_stages(size)
+    far, near, core = gather_stages(size)
     first, second = sum_rounds(size)
 
-    def gathered(pieces, some):
-        for stage in some:
-            pieces = exchanged(pieces, size, *stage)
-        return pieces
-
-    if len(stages) > 1:
-        pieces = [queries] + [swapped(queries, size, *stage, 1) for stage in stages[:2]]
-    else:
-        pieces = exchanged([queries], size, *stages[0])
+    pieces = exchanged([queries], size, *far)
     act_t, grad_t, own = project(acts, grads, proj_act, proj_grad)
     *pieces, own = lax.optimization_barrier((*pieces, own))
-    if len(stages) > 1:
-        pieces.append(swapped(pieces[1], size, *stages[1], 1))
+    pieces = exchanged(pieces, size, *near)
     own = functools.reduce(jnp.add, exchanged([own], size, *first))
-    *pieces, own = lax.optimization_barrier((*pieces, own))
-    pieces = gathered(pieces, stages[2:-1])
     terms = exchanged([own], size, *second)
     *both, = lax.optimization_barrier((*pieces, *terms))
     pieces, terms = both[: len(pieces)], both[len(pieces) :]
-    pieces = gathered(pieces, stages[max(2, len(stages) - 1) :])
+    pieces = exchanged(pieces, size, *core)
     moved = precondition(tok_total, terms, act_t, grad_t)
     return score(size, moved, pieces)
 

time: 32.3 us -> 30.4 us (0.941)
  waiting for transfers between devices: 5.7 us -> 4.78 us
  Pallas kernels: 12.2 us -> 11.6 us
    ppermute x11, waiting for transfers between devices: 5.7 us -> 4.78 us  [swapped(): return lax.ppermute(value, 'dp', perm)]
    pallas_call x1, Pallas kernels: 6.69 us -> 6.05 us  [project(): pl.pallas_call(project_kernel, out_shape=(jax.ShapeDtypeStruct((factor, t...]
    ppermute x11, starting transfers between devices: 14 us -> 13.7 us  [swapped(): return lax.ppermute(value, 'dp', perm)]
  transfers between devices with their start and end apart: 11 -> 11, of which waited for: 5 -> 4; matrix products, arithmetic and copies ran while one was open for 0% -> 0% of each run, Pallas kernels for 30% -> 30%
where the time goes in v10:
time: 30.4 us; the launch traced here: 30.2 us
  starting transfers between devices  13.7 us (45%)
  Pallas kernels  11.6 us (38%)
  waiting for transfers between devices  4.78 us (16%)
    ppermute x11, starting transfers between devices, swapped(): return lax.ppermute(value, 'dp', perm)  13.7 us
    pallas_call x1, Pallas kernels, project(): pl.pallas_call(project_kernel, out_shape=(jax.ShapeDtypeStruct((factor, t...  6.05 us
    ppermute x11, waiting for transfers between devices, swapped(): return lax.ppermute(value, 'dp', perm)  4.78 us
    pallas_call x1, Pallas kernels, precondition(): pl.pallas_call(functools.partial(precondition_kernel, tok_total, n_terms)...  3.09 us
    pallas_call x1, Pallas kernels, score(): pl.pallas_call(functools.partial(score_kernel, size, n_pieces), out_shape...  2.44 us
  transfers between devices with their start and end apart: 11, of which 4 were waited for; matrix products, arithmetic and copies ran while one was open for 0% of the time, Pallas kernels for 30%

profile of v10, /device:TPU:0, one launch (start us, length us, event | category | flops | bytes accessed | tf_op | source)
XLA Modules:
  0.0 30.2 jit_solution(1388758297447885906)
XLA Ops:
  0.0 4.0 %collective-permute-start.1 = (bf16[8,4096]{1,0:T(8,128)(2,1)}, bf16[8,4096]{1,0:T(8,128)(2,1)S(1)}, u32[]{:S(2)}, u32[]{:S(2)}) collective-permute-start(bf16[8,4096]{1,0:T(8,128)(2,1)} %param.9), channel_id=1, source_target_pairs={{0,8},{1,9},{2,10},{3,11},{4,12},{5,13},{6,14},{7,15},{8,0},{9,1},... | collective-permute-start | bytes 196616 | tf_op jit(solution)/shard_map/ppermute | solution.py:290
  4.0 1.6 %collective-permute-start = (bf16[8,4096]{1,0:T(8,128)(2,1)}, bf16[8,4096]{1,0:T(8,128)(2,1)S(1)}, u32[]{:S(2)}, u32[]{:S(2)}) collective-permute-start(bf16[8,4096]{1,0:T(8,128)(2,1)} %param.9), channel_id=1, source_target_pairs={{0,4},{1,5},{2,6},{3,7},{4,0},{5,1},{6,2},{7,3},{8,12},{9,13},{10,... | collective-permute-start | bytes 196616 | tf_op jit(solution)/shard_map/ppermute | solution.py:290
  5.6 0.0 collective-permute-start.2
  5.6 6.1 %project.1 = (f32[64,512]{1,0:T(8,128)S(1)}, f32[64,512]{1,0:T(8,128)S(1)}, f32[64,128]{1,0:T(8,128)S(1)}) custom-call(bf16[512,4096]{1,0:T(8,128)(2,1)} %acts.1, bf16[512,4096]{1,0:T(8,128)(2,1)} %grads.1, bf16[64,4096]{1,0:T(8,128)(2,1)} %bitcast.2, bf16[64,4096]{1,0:T(8,128)(2,1)} %bitcast.3), custom_call_target="tpu_custom_call" | custom-call | flops 536870912 | bytes 8388608 | tf_op jit(solution)/shard_map/project/pallas_call | solution.py:90
  11.7 0.0 collective-permute-done.1
  11.7 0.0 collective-permute-done
  11.7 0.2 collective-permute-done.2
  11.9 0.3 collective-permute-start.6
  12.2 1.4 %collective-permute-start.5 = (f32[64,128]{1,0:T(8,128)S(1)}, f32[64,128]{1,0:T(8,128)S(1)}, u32[]{:S(2)}, u32[]{:S(2)}) collective-permute-start(f32[64,128]{1,0:T(8,128)S(1)} %get-tuple-element.24), channel_id=1, source_target_pairs={{0,2},{1,3},{2,0},{3,1},{4,6},{5,7},{6,4},{7,5},{8,10},{9,11},{10,... | collective-permute-start | bytes 98312 | tf_op jit(solution)/shard_map/ppermute | solution.py:290
  13.6 0.2 collective-permute-start.4
  13.8 1.7 %collective-permute-start.3 = (bf16[32,4096]{1,0:T(8,128)(2,1)S(1)}, bf16[32,4096]{1,0:T(8,128)(2,1)S(1)}, u32[]{:S(2)}, u32[]{:S(2)}) collective-permute-start(bf16[32,4096]{1,0:T(8,128)(2,1)S(1)} %constant_dynamic-update-slice_fusion), channel_id=1, source_target_pairs={{0,2},{1,3},{2,0},{3,1},{4,6},{5,7},{6,4},{7,5},{8,10},{9,11},{10,... | collective-permute-start | bytes 786440 | tf_op jit(solution)/shard_map/ppermute | solution.py:290
  15.5 0.0 collective-permute-done.6
  15.5 0.6 %collective-permute-done.5 = f32[64,128]{1,0:T(8,128)S(1)} collective-permute-done((f32[64,128]{1,0:T(8,128)S(1)}, f32[64,128]{1,0:T(8,128)S(1)}, u32[]{:S(2)}, u32[]{:S(2)}) %collective-permute-start.5) | collective-permute-done | bytes 32800 | tf_op jit(solution)/shard_map/ppermute | solution.py:290
  16.1 0.0 collective-permute-done.4
  16.1 3.6 %collective-permute-start.9 = (f32[64,128]{1,0:T(8,128)S(1)}, f32[64,128]{1,0:T(8,128)S(1)}, u32[]{:S(2)}, u32[]{:S(2)}) collective-permute-start(f32[64,128]{1,0:T(8,128)S(1)} %add_add_fusion.refs_0_), channel_id=1, source_target_pairs={{0,12},{1,13},{2,14},{3,15},{4,8},{5,9},{6,10},{7,11},{8,4},{9,5},... | collective-permute-start | bytes 98312 | tf_op jit(solution)/shard_map/ppermute | solution.py:290
  19.7 0.0 collective-permute-start.8
  19.7 0.8 %collective-permute-start.7 = (f32[64,128]{1,0:T(8,128)S(1)}, f32[64,128]{1,0:T(8,128)S(1)}, u32[]{:S(2)}, u32[]{:S(2)}) collective-permute-start(f32[64,128]{1,0:T(8,128)S(1)} %add_add_fusion.refs_0_), channel_id=1, source_target_pairs={{0,4},{1,5},{2,6},{3,7},{4,0},{5,1},{6,2},{7,3},{8,12},{9,13},{10,... | collective-permute-start | bytes 98312 | tf_op jit(solution)/shard_map/ppermute | solution.py:290
  20.6 1.5 %collective-permute-done.9.refs_3_ = f32[64,128]{1,0:T(8,128)S(1)} collective-permute-done((f32[64,128]{1,0:T(8,128)S(1)}, f32[64,128]{1,0:T(8,128)S(1)}, u32[]{:S(2)}, u32[]{:S(2)}) %collective-permute-start.9) | collective-permute-done | bytes 32800 | tf_op jit(solution)/shard_map/ppermute | solution.py:290
  22.1 2.5 %collective-permute-done.8.refs_2_ = f32[64,128]{1,0:T(8,128)S(1)} collective-permute-done((f32[64,128]{1,0:T(8,128)S(1)}, f32[64,128]{1,0:T(8,128)S(1)}, u32[]{:S(2)}, u32[]{:S(2)}) %collective-permute-start.8) | collective-permute-done | bytes 32800 | tf_op jit(solution)/shard_map/ppermute | solution.py:290
  24.6 0.0 collective-permute-done.7.refs_1_
  24.6 0.0 collective-permute-done.3
  24.6 0.1 collective-permute-start.10
  24.7 3.1 %precondition.1.moved = f32[128,512]{1,0:T(8,128)S(1)} custom-call(f32[64,128]{1,0:T(8,128)S(1)} %add_add_fusion.refs_0_, f32[64,128]{1,0:T(8,128)S(1)} %collective-permute-done.7.refs_1_, f32[64,128]{1,0:T(8,128)S(1)} %collective-permute-done.8.refs_2_, f32[64,128]{1,0:T(8,128)S(1)} %collective-permute-done.9.refs_3_, ...), custom_call_target="tpu_custom_call" | custom-call | flops 3355443200 | bytes 524288 | tf_op jit(solution)/shard_map/precondition/pallas_call | solution.py:193
  27.8 2.4 %score.1 = f32[512,128]{1,0:T(8,128)} custom-call(f32[128,512]{1,0:T(8,128)S(1)} %precondition.1.moved, bf16[64,4096]{1,0:T(8,128)(2,1)S(1)} %constant_dynamic-update-slice_fusion.4.refs_0_, bf16[64,4096]{1,0:T(8,128)(2,1)S(1)} %collective-permute-done.10.refs_1_), custom_call_target="tpu_custom_call" | custom-call | tf_op jit(solution)/shard_map/score/pallas_call | solution.py:250
  (10 shorter events, 0.1 us)
Async XLA Ops:
  0.0 11.7 %collective-permute-start.1 = (bf16[8,4096]{1,0:T(8,128)(2,1)}, bf16[8,4096]{1,0:T(8,128)(2,1)S(1)}, u32[]{:S(2)}, u32[]{:S(2)}) collective-permute-start(bf16[8,4096]{1,0:T(8,128)(2,1)} %param.9), channel_id=1, source_target_pairs={{0,8},{1,9},{2,10},{3,11},{4,12},{5,13},{6,14},{7,15},{8,0},{9,1},... | collective-permute-start | bytes 196616 | tf_op jit(solution)/shard_map/ppermute | solution.py:290
  4.0 7.7 %collective-permute-start = (bf16[8,4096]{1,0:T(8,128)(2,1)}, bf16[8,4096]{1,0:T(8,128)(2,1)S(1)}, u32[]{:S(2)}, u32[]{:S(2)}) collective-permute-start(bf16[8,4096]{1,0:T(8,128)(2,1)} %param.9), channel_id=1, source_target_pairs={{0,4},{1,5},{2,6},{3,7},{4,0},{5,1},{6,2},{7,3},{8,12},{9,13},{10,... | collective-permute-start | bytes 196616 | tf_op jit(solution)/shard_map/ppermute | solution.py:290
  5.6 6.3 %collective-permute-start.2 = (bf16[8,4096]{1,0:T(8,128)(2,1)}, bf16[8,4096]{1,0:T(8,128)(2,1)S(1)}, u32[]{:S(2)}, u32[]{:S(2)}) collective-permute-start(bf16[8,4096]{1,0:T(8,128)(2,1)} %param.9), channel_id=1, source_target_pairs={{0,12},{1,13},{2,14},{3,15},{4,8},{5,9},{6,10},{7,11},{8,4},{9,5},... | collective-permute-start | bytes 196616 | tf_op jit(solution)/shard_map/ppermute | solution.py:290
  5.6 8.2 %copy-start = (bf16[8,4096]{1,0:T(8,128)(2,1)S(1)}, bf16[8,4096]{1,0:T(8,128)(2,1)}, u32[]{:S(2)}) copy-start(bf16[8,4096]{1,0:T(8,128)(2,1)} %param.9) | copy-start | bytes 196612
  11.9 3.6 %collective-permute-start.6 = (f32[64,128]{1,0:T(8,128)S(1)}, f32[64,128]{1,0:T(8,128)S(1)}, u32[]{:S(2)}, u32[]{:S(2)}) collective-permute-start(f32[64,128]{1,0:T(8,128)S(1)} %get-tuple-element.24), channel_id=1, source_target_pairs={{0,3},{1,2},{2,1},{3,0},{4,7},{5,6},{6,5},{7,4},{8,11},{9,10},{10,... | collective-permute-start | bytes 98312 | tf_op jit(solution)/shard_map/ppermute | solution.py:290
  12.2 3.9 %collective-permute-start.5 = (f32[64,128]{1,0:T(8,128)S(1)}, f32[64,128]{1,0:T(8,128)S(1)}, u32[]{:S(2)}, u32[]{:S(2)}) collective-permute-start(f32[64,128]{1,0:T(8,128)S(1)} %get-tuple-element.24), channel_id=1, source_target_pairs={{0,2},{1,3},{2,0},{3,1},{4,6},{5,7},{6,4},{7,5},{8,10},{9,11},{10,... | collective-permute-start | bytes 98312 | tf_op jit(solution)/shard_map/ppermute | solution.py:290
  13.6 2.5 %collective-permute-start.4 = (f32[64,128]{1,0:T(8,128)S(1)}, f32[64,128]{1,0:T(8,128)S(1)}, u32[]{:S(2)}, u32[]{:S(2)}) collective-permute-start(f32[64,128]{1,0:T(8,128)S(1)} %get-tuple-element.24), channel_id=1, source_target_pairs={{0,1},{1,0},{2,3},{3,2},{4,5},{5,4},{6,7},{7,6},{8,9},{9,8},{10,11... | collective-permute-start | bytes 98312 | tf_op jit(solution)/shard_map/ppermute | solution.py:290
  13.8 10.7 %collective-permute-start.3 = (bf16[32,4096]{1,0:T(8,128)(2,1)S(1)}, bf16[32,4096]{1,0:T(8,128)(2,1)S(1)}, u32[]{:S(2)}, u32[]{:S(2)}) collective-permute-start(bf16[32,4096]{1,0:T(8,128)(2,1)S(1)} %constant_dynamic-update-slice_fusion), channel_id=1, source_target_pairs={{0,2},{1,3},{2,0},{3,1},{4,6},{5,7},{6,4},{7,5},{8,10},{9,11},{10,... | collective-permute-start | bytes 786440 | tf_op jit(solution)/shard_map/ppermute | solution.py:290
  16.1 6.0 %collective-permute-start.9 = (f32[64,128]{1,0:T(8,128)S(1)}, f32[64,128]{1,0:T(8,128)S(1)}, u32[]{:S(2)}, u32[]{:S(2)}) collective-permute-start(f32[64,128]{1,0:T(8,128)S(1)} %add_add_fusion.refs_0_), channel_id=1, source_target_pairs={{0,12},{1,13},{2,14},{3,15},{4,8},{5,9},{6,10},{7,11},{8,4},{9,5},... | collective-permute-start | bytes 98312 | tf_op jit(solution)/shard_map/ppermute | solution.py:290
  19.7 4.8 %collective-permute-start.8 = (f32[64,128]{1,0:T(8,128)S(1)}, f32[64,128]{1,0:T(8,128)S(1)}, u32[]{:S(2)}, u32[]{:S(2)}) collective-permute-start(f32[64,128]{1,0:T(8,128)S(1)} %add_add_fusion.refs_0_), channel_id=1, source_target_pairs={{0,8},{1,9},{2,10},{3,11},{4,12},{5,13},{6,14},{7,15},{8,0},{9,1},... | collective-permute-start | bytes 98312 | tf_op jit(solution)/shard_map/ppermute | solution.py:290
  19.7 4.8 %collective-permute-start.7 = (f32[64,128]{1,0:T(8,128)S(1)}, f32[64,128]{1,0:T(8,128)S(1)}, u32[]{:S(2)}, u32[]{:S(2)}) collective-permute-start(f32[64,128]{1,0:T(8,128)S(1)} %add_add_fusion.refs_0_), channel_id=1, source_target_pairs={{0,4},{1,5},{2,6},{3,7},{4,0},{5,1},{6,2},{7,3},{8,12},{9,13},{10,... | collective-permute-start | bytes 98312 | tf_op jit(solution)/shard_map/ppermute | solution.py:290
  24.6 3.2 %collective-permute-start.10 = (bf16[64,4096]{1,0:T(8,128)(2,1)S(1)}, bf16[64,4096]{1,0:T(8,128)(2,1)S(1)}, u32[]{:S(2)}, u32[]{:S(2)}) collective-permute-start(bf16[64,4096]{1,0:T(8,128)(2,1)S(1)} %constant_dynamic-update-slice_fusion.4.refs_0_), channel_id=1, source_target_pairs={{0,1},{1,0},{2,3},{3,2},{4,5},{5,4},{6,7},{7,6},{8,9},{9,8},{10,11... | collective-permute-start | bytes 1572872 | tf_op jit(solution)/shard_map/ppermute | solution.py:290

commit v11 on v10

--- a/solution.py
+++ b/solution.py
@@ -10,8 +10,9 @@
 DAMP = 0.1
 HIGHEST = lax.Precision.HIGHEST
 COPY_ROWS = 128
-IN_FLIGHT = 4
+IN_FLIGHT = 3
 TOKENS_AT_ONCE = 256
+ORDER = (3, 2, 1)
 
 
 def project_kernel(
@@ -35,7 +36,7 @@
         for at, src in enumerate((acts, grads))
     ]
     queue = [weight_copies[0], *tok_copies[0], *tok_copies[1]]
-    queue.insert(3, weight_copies[1])
+    queue.insert(4, weight_copies[1])
 
     def start_next(many):
         for copy in queue[:many]:
@@ -282,6 +283,10 @@
     return digit ^ shift if radix & (radix - 1) == 0 else (digit + shift) % radix
 
 
+def shifts_of(radix):
+    return ORDER if radix == 4 else range(1, radix)
+
+
 def swapped(value, size, stride, radix, shift):
     perm = []
     for at in range(size):
@@ -294,7 +299,7 @@
     owners = [me]
     for stride, radix in gather_stages(size):
         digit = lax.rem(lax.div(me, stride), radix)
-        back = [shift if radix & (radix - 1) == 0 else radix - shift for shift in range(radix)]
+        back = [shift if radix & (radix - 1) == 0 else radix - shift for shift in (0, *shifts_of(radix))]
         steps = [(partner(digit, radix, shift) - digit) * stride for shift in back]
         owners = [owner + step for step in steps for owner in owners]
     return owners
@@ -302,7 +307,7 @@
 
 def exchanged(held, size, stride, radix):
     mine = held[0] if len(held) == 1 else jnp.concatenate(held, axis=0)
-    return [mine] + [swapped(mine, size, stride, radix, shift) for shift in range(1, radix)]
+    return [mine] + [swapped(mine, size, stride, radix, shift) for shift in shifts_of(radix)]
 
 
 def on_device(acts, grads, proj_act, proj_grad, queries):

time: 30.4 us -> 32.7 us (1.076)
  waiting for transfers between devices: 4.78 us -> 6.25 us
  Pallas kernels: 11.6 us -> 12.4 us
    ppermute x11, waiting for transfers between devices: 4.78 us -> 6.25 us  [swapped(): return lax.ppermute(value, 'dp', perm)]
    pallas_call x1, Pallas kernels: 6.05 us -> 6.88 us  [project(): pl.pallas_call(project_kernel, out_shape=(jax.ShapeDtypeStruct((factor, t...]
  transfers between devices with their start and end apart: 11 -> 11, of which waited for: 4 -> 4; matrix products, arithmetic and copies ran while one was open for 0% -> 0% of each run, Pallas kernels for 30% -> 31%
where the time goes in v11:
time: 32.7 us; the launch traced here: 32.5 us
  starting transfers between devices  13.7 us (42%)
  Pallas kernels  12.4 us (38%)
  waiting for transfers between devices  6.25 us (19%)
    ppermute x11, starting transfers between devices, swapped(): return lax.ppermute(value, 'dp', perm)  13.7 us
    pallas_call x1, Pallas kernels, project(): pl.pallas_call(project_kernel, out_shape=(jax.ShapeDtypeStruct((factor, t...  6.88 us
    ppermute x11, waiting for transfers between devices, swapped(): return lax.ppermute(value, 'dp', perm)  6.25 us
    pallas_call x1, Pallas kernels, precondition(): pl.pallas_call(functools.partial(precondition_kernel, tok_total, n_terms)...  3.09 us
    pallas_call x1, Pallas kernels, score(): pl.pallas_call(functools.partial(score_kernel, size, n_pieces), out_shape...  2.44 us
  transfers between devices with their start and end apart: 11, of which 4 were waited for; matrix products, arithmetic and copies ran while one was open for 0% of the time, Pallas kernels for 31%

profile of v11, /device:TPU:0, one launch (start us, length us, event | category | flops | bytes accessed | tf_op | source)
XLA Modules:
  0.0 32.5 jit_solution(11177358573766457364)
XLA Ops:
  0.0 4.0 %collective-permute-start.1 = (bf16[8,4096]{1,0:T(8,128)(2,1)}, bf16[8,4096]{1,0:T(8,128)(2,1)S(1)}, u32[]{:S(2)}, u32[]{:S(2)}) collective-permute-start(bf16[8,4096]{1,0:T(8,128)(2,1)} %param.9), channel_id=1, source_target_pairs={{0,8},{1,9},{2,10},{3,11},{4,12},{5,13},{6,14},{7,15},{8,0},{9,1},... | collective-permute-start | bytes 196616 | tf_op jit(solution)/shard_map/ppermute | solution.py:295
  4.0 1.3 %collective-permute-start = (bf16[8,4096]{1,0:T(8,128)(2,1)}, bf16[8,4096]{1,0:T(8,128)(2,1)S(1)}, u32[]{:S(2)}, u32[]{:S(2)}) collective-permute-start(bf16[8,4096]{1,0:T(8,128)(2,1)} %param.9), channel_id=1, source_target_pairs={{0,12},{1,13},{2,14},{3,15},{4,8},{5,9},{6,10},{7,11},{8,4},{9,5},... | collective-permute-start | bytes 196616 | tf_op jit(solution)/shard_map/ppermute | solution.py:295
  5.4 0.2 collective-permute-start.2
  5.6 6.9 %project.1 = (f32[64,512]{1,0:T(8,128)S(1)}, f32[64,512]{1,0:T(8,128)S(1)}, f32[64,128]{1,0:T(8,128)S(1)}) custom-call(bf16[512,4096]{1,0:T(8,128)(2,1)} %acts.1, bf16[512,4096]{1,0:T(8,128)(2,1)} %grads.1, bf16[64,4096]{1,0:T(8,128)(2,1)} %bitcast.2, bf16[64,4096]{1,0:T(8,128)(2,1)} %bitcast.3), custom_call_target="tpu_custom_call" | custom-call | flops 536870912 | bytes 8388608 | tf_op jit(solution)/shard_map/project/pallas_call | solution.py:91
  12.5 0.0 collective-permute-done.1
  12.5 0.0 collective-permute-done
  12.5 0.0 collective-permute-done.2
  12.5 0.1 collective-permute-start.6
  12.6 1.6 %collective-permute-start.5 = (f32[64,128]{1,0:T(8,128)S(1)}, f32[64,128]{1,0:T(8,128)S(1)}, u32[]{:S(2)}, u32[]{:S(2)}) collective-permute-start(f32[64,128]{1,0:T(8,128)S(1)} %get-tuple-element.24), channel_id=1, source_target_pairs={{0,2},{1,3},{2,0},{3,1},{4,6},{5,7},{6,4},{7,5},{8,10},{9,11},{10,... | collective-permute-start | bytes 98312 | tf_op jit(solution)/shard_map/ppermute | solution.py:295
  14.2 0.3 collective-permute-start.4
  14.5 1.6 %collective-permute-start.3 = (bf16[32,4096]{1,0:T(8,128)(2,1)S(1)}, bf16[32,4096]{1,0:T(8,128)(2,1)S(1)}, u32[]{:S(2)}, u32[]{:S(2)}) collective-permute-start(bf16[32,4096]{1,0:T(8,128)(2,1)S(1)} %constant_dynamic-update-slice_fusion), channel_id=1, source_target_pairs={{0,2},{1,3},{2,0},{3,1},{4,6},{5,7},{6,4},{7,5},{8,10},{9,11},{10,... | collective-permute-start | bytes 786440 | tf_op jit(solution)/shard_map/ppermute | solution.py:295
  16.1 0.0 collective-permute-done.6
  16.1 0.5 %collective-permute-done.5 = f32[64,128]{1,0:T(8,128)S(1)} collective-permute-done((f32[64,128]{1,0:T(8,128)S(1)}, f32[64,128]{1,0:T(8,128)S(1)}, u32[]{:S(2)}, u32[]{:S(2)}) %collective-permute-start.5) | collective-permute-done | bytes 32800 | tf_op jit(solution)/shard_map/ppermute | solution.py:295
  16.6 0.9 %collective-permute-done.4 = f32[64,128]{1,0:T(8,128)S(1)} collective-permute-done((f32[64,128]{1,0:T(8,128)S(1)}, f32[64,128]{1,0:T(8,128)S(1)}, u32[]{:S(2)}, u32[]{:S(2)}) %collective-permute-start.4) | collective-permute-done | bytes 32800 | tf_op jit(solution)/shard_map/ppermute | solution.py:295
  17.6 1.9 %collective-permute-start.9 = (f32[64,128]{1,0:T(8,128)S(1)}, f32[64,128]{1,0:T(8,128)S(1)}, u32[]{:S(2)}, u32[]{:S(2)}) collective-permute-start(f32[64,128]{1,0:T(8,128)S(1)} %add_add_fusion.refs_0_), channel_id=1, source_target_pairs={{0,4},{1,5},{2,6},{3,7},{4,0},{5,1},{6,2},{7,3},{8,12},{9,13},{10,... | collective-permute-start | bytes 98312 | tf_op jit(solution)/shard_map/ppermute | solution.py:295
  19.4 1.7 %collective-permute-start.8 = (f32[64,128]{1,0:T(8,128)S(1)}, f32[64,128]{1,0:T(8,128)S(1)}, u32[]{:S(2)}, u32[]{:S(2)}) collective-permute-start(f32[64,128]{1,0:T(8,128)S(1)} %add_add_fusion.refs_0_), channel_id=1, source_target_pairs={{0,8},{1,9},{2,10},{3,11},{4,12},{5,13},{6,14},{7,15},{8,0},{9,1},... | collective-permute-start | bytes 98312 | tf_op jit(solution)/shard_map/ppermute | solution.py:295
  21.1 0.9 %collective-permute-start.7 = (f32[64,128]{1,0:T(8,128)S(1)}, f32[64,128]{1,0:T(8,128)S(1)}, u32[]{:S(2)}, u32[]{:S(2)}) collective-permute-start(f32[64,128]{1,0:T(8,128)S(1)} %add_add_fusion.refs_0_), channel_id=1, source_target_pairs={{0,12},{1,13},{2,14},{3,15},{4,8},{5,9},{6,10},{7,11},{8,4},{9,5},... | collective-permute-start | bytes 98312 | tf_op jit(solution)/shard_map/ppermute | solution.py:295
  22.0 0.0 collective-permute-done.9.refs_3_
  22.0 2.8 %collective-permute-done.8.refs_2_ = f32[64,128]{1,0:T(8,128)S(1)} collective-permute-done((f32[64,128]{1,0:T(8,128)S(1)}, f32[64,128]{1,0:T(8,128)S(1)}, u32[]{:S(2)}, u32[]{:S(2)}) %collective-permute-start.8) | collective-permute-done | bytes 32800 | tf_op jit(solution)/shard_map/ppermute | solution.py:295
  24.8 2.0 %collective-permute-done.7.refs_1_ = f32[64,128]{1,0:T(8,128)S(1)} collective-permute-done((f32[64,128]{1,0:T(8,128)S(1)}, f32[64,128]{1,0:T(8,128)S(1)}, u32[]{:S(2)}, u32[]{:S(2)}) %collective-permute-start.7) | collective-permute-done | bytes 32800 | tf_op jit(solution)/shard_map/ppermute | solution.py:295
  26.9 0.1 collective-permute-start.10
  27.0 3.1 %precondition.1.moved = f32[128,512]{1,0:T(8,128)S(1)} custom-call(f32[64,128]{1,0:T(8,128)S(1)} %add_add_fusion.refs_0_, f32[64,128]{1,0:T(8,128)S(1)} %collective-permute-done.7.refs_1_, f32[64,128]{1,0:T(8,128)S(1)} %collective-permute-done.8.refs_2_, f32[64,128]{1,0:T(8,128)S(1)} %collective-permute-done.9.refs_3_, ...), custom_call_target="tpu_custom_call" | custom-call | flops 3355443200 | bytes 524288 | tf_op jit(solution)/shard_map/precondition/pallas_call | solution.py:194
  30.1 0.0 collective-permute-done.10.refs_1_
  30.1 2.4 %score.1 = f32[512,128]{1,0:T(8,128)} custom-call(f32[128,512]{1,0:T(8,128)S(1)} %precondition.1.moved, bf16[64,4096]{1,0:T(8,128)(2,1)S(1)} %constant_dynamic-update-slice_fusion.4.refs_0_, bf16[64,4096]{1,0:T(8,128)(2,1)S(1)} %collective-permute-done.10.refs_1_), custom_call_target="tpu_custom_call" | custom-call | tf_op jit(solution)/shard_map/score/pallas_call | solution.py:251
  (10 shorter events, 0.1 us)
Async XLA Ops:
  0.0 12.5 %collective-permute-start.1 = (bf16[8,4096]{1,0:T(8,128)(2,1)}, bf16[8,4096]{1,0:T(8,128)(2,1)S(1)}, u32[]{:S(2)}, u32[]{:S(2)}) collective-permute-start(bf16[8,4096]{1,0:T(8,128)(2,1)} %param.9), channel_id=1, source_target_pairs={{0,8},{1,9},{2,10},{3,11},{4,12},{5,13},{6,14},{7,15},{8,0},{9,1},... | collective-permute-start | bytes 196616 | tf_op jit(solution)/shard_map/ppermute | solution.py:295
  4.0 8.5 %collective-permute-start = (bf16[8,4096]{1,0:T(8,128)(2,1)}, bf16[8,4096]{1,0:T(8,128)(2,1)S(1)}, u32[]{:S(2)}, u32[]{:S(2)}) collective-permute-start(bf16[8,4096]{1,0:T(8,128)(2,1)} %param.9), channel_id=1, source_target_pairs={{0,12},{1,13},{2,14},{3,15},{4,8},{5,9},{6,10},{7,11},{8,4},{9,5},... | collective-permute-start | bytes 196616 | tf_op jit(solution)/shard_map/ppermute | solution.py:295
  5.4 7.1 %collective-permute-start.2 = (bf16[8,4096]{1,0:T(8,128)(2,1)}, bf16[8,4096]{1,0:T(8,128)(2,1)S(1)}, u32[]{:S(2)}, u32[]{:S(2)}) collective-permute-start(bf16[8,4096]{1,0:T(8,128)(2,1)} %param.9), channel_id=1, source_target_pairs={{0,4},{1,5},{2,6},{3,7},{4,0},{5,1},{6,2},{7,3},{8,12},{9,13},{10,... | collective-permute-start | bytes 196616 | tf_op jit(solution)/shard_map/ppermute | solution.py:295
  5.6 8.9 %copy-start = (bf16[8,4096]{1,0:T(8,128)(2,1)S(1)}, bf16[8,4096]{1,0:T(8,128)(2,1)}, u32[]{:S(2)}) copy-start(bf16[8,4096]{1,0:T(8,128)(2,1)} %param.9) | copy-start | bytes 196612
  12.5 3.6 %collective-permute-start.6 = (f32[64,128]{1,0:T(8,128)S(1)}, f32[64,128]{1,0:T(8,128)S(1)}, u32[]{:S(2)}, u32[]{:S(2)}) collective-permute-start(f32[64,128]{1,0:T(8,128)S(1)} %get-tuple-element.24), channel_id=1, source_target_pairs={{0,1},{1,0},{2,3},{3,2},{4,5},{5,4},{6,7},{7,6},{8,9},{9,8},{10,11... | collective-permute-start | bytes 98312 | tf_op jit(solution)/shard_map/ppermute | solution.py:295
  12.6 4.0 %collective-permute-start.5 = (f32[64,128]{1,0:T(8,128)S(1)}, f32[64,128]{1,0:T(8,128)S(1)}, u32[]{:S(2)}, u32[]{:S(2)}) collective-permute-start(f32[64,128]{1,0:T(8,128)S(1)} %get-tuple-element.24), channel_id=1, source_target_pairs={{0,2},{1,3},{2,0},{3,1},{4,6},{5,7},{6,4},{7,5},{8,10},{9,11},{10,... | collective-permute-start | bytes 98312 | tf_op jit(solution)/shard_map/ppermute | solution.py:295
  14.2 3.3 %collective-permute-start.4 = (f32[64,128]{1,0:T(8,128)S(1)}, f32[64,128]{1,0:T(8,128)S(1)}, u32[]{:S(2)}, u32[]{:S(2)}) collective-permute-start(f32[64,128]{1,0:T(8,128)S(1)} %get-tuple-element.24), channel_id=1, source_target_pairs={{0,3},{1,2},{2,1},{3,0},{4,7},{5,6},{6,5},{7,4},{8,11},{9,10},{10,... | collective-permute-start | bytes 98312 | tf_op jit(solution)/shard_map/ppermute | solution.py:295
  14.5 12.3 %collective-permute-start.3 = (bf16[32,4096]{1,0:T(8,128)(2,1)S(1)}, bf16[32,4096]{1,0:T(8,128)(2,1)S(1)}, u32[]{:S(2)}, u32[]{:S(2)}) collective-permute-start(bf16[32,4096]{1,0:T(8,128)(2,1)S(1)} %constant_dynamic-update-slice_fusion), channel_id=1, source_target_pairs={{0,2},{1,3},{2,0},{3,1},{4,6},{5,7},{6,4},{7,5},{8,10},{9,11},{10,... | collective-permute-start | bytes 786440 | tf_op jit(solution)/shard_map/ppermute | solution.py:295
  17.6 4.5 %collective-permute-start.9 = (f32[64,128]{1,0:T(8,128)S(1)}, f32[64,128]{1,0:T(8,128)S(1)}, u32[]{:S(2)}, u32[]{:S(2)}) collective-permute-start(f32[64,128]{1,0:T(8,128)S(1)} %add_add_fusion.refs_0_), channel_id=1, source_target_pairs={{0,4},{1,5},{2,6},{3,7},{4,0},{5,1},{6,2},{7,3},{8,12},{9,13},{10,... | collective-permute-start | bytes 98312 | tf_op jit(solution)/shard_map/ppermute | solution.py:295
  19.4 5.4 %collective-permute-start.8 = (f32[64,128]{1,0:T(8,128)S(1)}, f32[64,128]{1,0:T(8,128)S(1)}, u32[]{:S(2)}, u32[]{:S(2)}) collective-permute-start(f32[64,128]{1,0:T(8,128)S(1)} %add_add_fusion.refs_0_), channel_id=1, source_target_pairs={{0,8},{1,9},{2,10},{3,11},{4,12},{5,13},{6,14},{7,15},{8,0},{9,1},... | collective-permute-start | bytes 98312 | tf_op jit(solution)/shard_map/ppermute | solution.py:295
  21.1 5.7 %collective-permute-start.7 = (f32[64,128]{1,0:T(8,128)S(1)}, f32[64,128]{1,0:T(8,128)S(1)}, u32[]{:S(2)}, u32[]{:S(2)}) collective-permute-start(f32[64,128]{1,0:T(8,128)S(1)} %add_add_fusion.refs_0_), channel_id=1, source_target_pairs={{0,12},{1,13},{2,14},{3,15},{4,8},{5,9},{6,10},{7,11},{8,4},{9,5},... | collective-permute-start | bytes 98312 | tf_op jit(solution)/shard_map/ppermute | solution.py:295
  26.9 3.2 %collective-permute-start.10 = (bf16[64,4096]{1,0:T(8,128)(2,1)S(1)}, bf16[64,4096]{1,0:T(8,128)(2,1)S(1)}, u32[]{:S(2)}, u32[]{:S(2)}) collective-permute-start(bf16[64,4096]{1,0:T(8,128)(2,1)S(1)} %constant_dynamic-update-slice_fusion.4.refs_0_), channel_id=1, source_target_pairs={{0,1},{1,0},{2,3},{3,2},{4,5},{5,4},{6,7},{7,6},{8,9},{9,8},{10,11... | collective-permute-start | bytes 1572872 | tf_op jit(solution)/shard_map/ppermute | solution.py:295

commit v12 on v10

--- a/solution.py
+++ b/solution.py
@@ -51,16 +51,17 @@
     last_act = len(steps) // 2 - 1
     at, part, many = steps.pop()
     steps += [(at, part + one, 1) for one in range(many)]
-    grams = [None, None]
-
-    def add_gram(at, flipped, block):
-        term = jnp.dot(flipped, block, precision=HIGHEST, preferred_element_type=jnp.float32)
-        grams[at] = term if grams[at] is None else grams[at] + term
+    blocks = [[], []]
+    grams = [[], []]
+
+    def add_gram(at):
+        flipped, plain = [jnp.concatenate(parts, axis=axis) for parts, axis in zip(zip(*blocks[at]), (1, 0))]
+        grams[at].append(jnp.dot(flipped, plain, precision=HIGHEST, preferred_element_type=jnp.float32))
+        blocks[at].clear()
 
     start_next(1 + IN_FLIGHT)
     weight_copies[0].wait()
     turned(0)
-    before = None
     for step, (at, part, many) in enumerate(steps):
         for copy in tok_copies[at][part : part + many]:
             copy.wait()
@@ -72,13 +73,15 @@
         block = jnp.dot(tok_buf[at, rows, :], weight_t[at], preferred_element_type=jnp.float32)
         if step == last_act:
             turned(1)
-        if before is not None:
-            add_gram(*before)
+        if step == last_act + 1:
+            add_gram(0)
+        if step == len(steps) - 1:
+            add_gram(1)
         flipped = block.T
         (act_t, grad_t)[at][:, rows] = flipped
-        before = (at, flipped, block)
-    add_gram(*before)
-    cov[...] = jnp.concatenate(grams, axis=1)
+        blocks[at].append((flipped, block))
+    add_gram(1)
+    cov[...] = jnp.concatenate([functools.reduce(jnp.add, terms) for terms in grams], axis=1)
 
 
 def project(acts, grads, proj_act, proj_grad):
@@ -292,17 +295,19 @@
 
 def owners_of(me, size):
     owners = [me]
-    for stride, radix in gather_stages(size):
+    for at, (stride, radix) in enumerate(gather_stages(size)):
         digit = lax.rem(lax.div(me, stride), radix)
-        back = [shift if radix & (radix - 1) == 0 else radix - shift for shift in range(radix)]
+        shifts = [0, *(range(radix - 1, 0, -1) if at == 0 else range(1, radix))]
+        back = [shift if radix & (radix - 1) == 0 else (radix - shift) % radix for shift in shifts]
         steps = [(partner(digit, radix, shift) - digit) * stride for shift in back]
         owners = [owner + step for step in steps for owner in owners]
     return owners
 
 
-def exchanged(held, size, stride, radix):
+def exchanged(held, size, stride, radix, backwards=False):
     mine = held[0] if len(held) == 1 else jnp.concatenate(held, axis=0)
-    return [mine] + [swapped(mine, size, stride, radix, shift) for shift in range(1, radix)]
+    shifts = range(radix - 1, 0, -1) if backwards else range(1, radix)
+    return [mine] + [swapped(mine, size, stride, radix, shift) for shift in shifts]
 
 
 def on_device(acts, grads, proj_act, proj_grad, queries):
@@ -311,7 +316,7 @@
     far, near, core = gather_stages(size)
     first, second = sum_rounds(size)
 
-    pieces = exchanged([queries], size, *far)
+    pieces = exchanged([queries], size, *far, backwards=True)
     act_t, grad_t, own = project(acts, grads, proj_act, proj_grad)
     *pieces, own = lax.optimization_barrier((*pieces, own))
     pieces = exchanged(pieces, size, *near)

time: 30.4 us -> 29.9 us (0.984)
  waiting for transfers between devices: 4.78 us -> 4.15 us
    ppermute x11, waiting for transfers between devices: 4.78 us -> 4.15 us  [swapped(): return lax.ppermute(value, 'dp', perm)]
  transfers between devices with their start and end apart: 11 -> 11, of which waited for: 4 -> 4; matrix products, arithmetic and copies ran while one was open for 0% -> 0% of each run, Pallas kernels for 30% -> 31%
where the time goes in v12:
time: 29.9 us; the launch traced here: 29.7 us
  starting transfers between devices  13.7 us (46%)
  Pallas kernels  11.7 us (39%)
  waiting for transfers between devices  4.15 us (14%)
    ppermute x11, starting transfers between devices, swapped(): return lax.ppermute(value, 'dp', perm)  13.7 us
    pallas_call x1, Pallas kernels, project(): pl.pallas_call(project_kernel, out_shape=(jax.ShapeDtypeStruct((factor, t...  6.15 us
    ppermute x11, waiting for transfers between devices, swapped(): return lax.ppermute(value, 'dp', perm)  4.15 us
    pallas_call x1, Pallas kernels, precondition(): pl.pallas_call(functools.partial(precondition_kernel, tok_total, n_terms)...  3.09 us
    pallas_call x1, Pallas kernels, score(): pl.pallas_call(functools.partial(score_kernel, size, n_pieces), out_shape...  2.44 us
  transfers between devices with their start and end apart: 11, of which 4 were waited for; matrix products, arithmetic and copies ran while one was open for 0% of the time, Pallas kernels for 31%

profile of v12, /device:TPU:0, one launch (start us, length us, event | category | flops | bytes accessed | tf_op | source)
XLA Modules:
  0.0 29.7 jit_solution(17173548506495876574)
XLA Ops:
  0.0 4.0 %collective-permute-start.1 = (bf16[8,4096]{1,0:T(8,128)(2,1)}, bf16[8,4096]{1,0:T(8,128)(2,1)S(1)}, u32[]{:S(2)}, u32[]{:S(2)}) collective-permute-start(bf16[8,4096]{1,0:T(8,128)(2,1)} %param.9), channel_id=1, source_target_pairs={{0,8},{1,9},{2,10},{3,11},{4,12},{5,13},{6,14},{7,15},{8,0},{9,1},... | collective-permute-start | bytes 196616 | tf_op jit(solution)/shard_map/ppermute | solution.py:293
  4.0 1.3 %collective-permute-start = (bf16[8,4096]{1,0:T(8,128)(2,1)}, bf16[8,4096]{1,0:T(8,128)(2,1)S(1)}, u32[]{:S(2)}, u32[]{:S(2)}) collective-permute-start(bf16[8,4096]{1,0:T(8,128)(2,1)} %param.9), channel_id=1, source_target_pairs={{0,12},{1,13},{2,14},{3,15},{4,8},{5,9},{6,10},{7,11},{8,4},{9,5},... | collective-permute-start | bytes 196616 | tf_op jit(solution)/shard_map/ppermute | solution.py:293
  5.4 0.2 collective-permute-start.2
  5.6 6.1 %project.1 = (f32[64,512]{1,0:T(8,128)S(1)}, f32[64,512]{1,0:T(8,128)S(1)}, f32[64,128]{1,0:T(8,128)S(1)}) custom-call(bf16[512,4096]{1,0:T(8,128)(2,1)} %acts.1, bf16[512,4096]{1,0:T(8,128)(2,1)} %grads.1, bf16[64,4096]{1,0:T(8,128)(2,1)} %bitcast.2, bf16[64,4096]{1,0:T(8,128)(2,1)} %bitcast.3), custom_call_target="tpu_custom_call" | custom-call | flops 536870912 | bytes 8388608 | tf_op jit(solution)/shard_map/project/pallas_call | solution.py:93
  11.8 0.0 collective-permute-done.1
  11.8 0.0 collective-permute-done
  11.8 0.0 collective-permute-done.2
  11.8 0.5 %collective-permute-start.6 = (f32[64,128]{1,0:T(8,128)S(1)}, f32[64,128]{1,0:T(8,128)S(1)}, u32[]{:S(2)}, u32[]{:S(2)}) collective-permute-start(f32[64,128]{1,0:T(8,128)S(1)} %get-tuple-element.24), channel_id=1, source_target_pairs={{0,3},{1,2},{2,1},{3,0},{4,7},{5,6},{6,5},{7,4},{8,11},{9,10},{10,... | collective-permute-start | bytes 98312 | tf_op jit(solution)/shard_map/ppermute | solution.py:293
  12.3 1.2 %collective-permute-start.5 = (f32[64,128]{1,0:T(8,128)S(1)}, f32[64,128]{1,0:T(8,128)S(1)}, u32[]{:S(2)}, u32[]{:S(2)}) collective-permute-start(f32[64,128]{1,0:T(8,128)S(1)} %get-tuple-element.24), channel_id=1, source_target_pairs={{0,2},{1,3},{2,0},{3,1},{4,6},{5,7},{6,4},{7,5},{8,10},{9,11},{10,... | collective-permute-start | bytes 98312 | tf_op jit(solution)/shard_map/ppermute | solution.py:293
  13.5 0.3 collective-permute-start.4
  13.8 1.6 %collective-permute-start.3 = (bf16[32,4096]{1,0:T(8,128)(2,1)S(1)}, bf16[32,4096]{1,0:T(8,128)(2,1)S(1)}, u32[]{:S(2)}, u32[]{:S(2)}) collective-permute-start(bf16[32,4096]{1,0:T(8,128)(2,1)S(1)} %constant_dynamic-update-slice_fusion), channel_id=1, source_target_pairs={{0,2},{1,3},{2,0},{3,1},{4,6},{5,7},{6,4},{7,5},{8,10},{9,11},{10,... | collective-permute-start | bytes 786440 | tf_op jit(solution)/shard_map/ppermute | solution.py:293
  15.4 0.1 collective-permute-done.6
  15.5 0.8 %collective-permute-done.5 = f32[64,128]{1,0:T(8,128)S(1)} collective-permute-done((f32[64,128]{1,0:T(8,128)S(1)}, f32[64,128]{1,0:T(8,128)S(1)}, u32[]{:S(2)}, u32[]{:S(2)}) %collective-permute-start.5) | collective-permute-done | bytes 32800 | tf_op jit(solution)/shard_map/ppermute | solution.py:293
  16.3 0.0 collective-permute-done.4
  16.3 2.6 %collective-permute-start.9 = (f32[64,128]{1,0:T(8,128)S(1)}, f32[64,128]{1,0:T(8,128)S(1)}, u32[]{:S(2)}, u32[]{:S(2)}) collective-permute-start(f32[64,128]{1,0:T(8,128)S(1)} %add_add_fusion.refs_0_), channel_id=1, source_target_pairs={{0,12},{1,13},{2,14},{3,15},{4,8},{5,9},{6,10},{7,11},{8,4},{9,5},... | collective-permute-start | bytes 98312 | tf_op jit(solution)/shard_map/ppermute | solution.py:293
  18.9 0.3 %collective-permute-start.8 = (f32[64,128]{1,0:T(8,128)S(1)}, f32[64,128]{1,0:T(8,128)S(1)}, u32[]{:S(2)}, u32[]{:S(2)}) collective-permute-start(f32[64,128]{1,0:T(8,128)S(1)} %add_add_fusion.refs_0_), channel_id=1, source_target_pairs={{0,8},{1,9},{2,10},{3,11},{4,12},{5,13},{6,14},{7,15},{8,0},{9,1},... | collective-permute-start | bytes 98312 | tf_op jit(solution)/shard_map/ppermute | solution.py:293
  19.3 1.5 %collective-permute-start.7 = (f32[64,128]{1,0:T(8,128)S(1)}, f32[64,128]{1,0:T(8,128)S(1)}, u32[]{:S(2)}, u32[]{:S(2)}) collective-permute-start(f32[64,128]{1,0:T(8,128)S(1)} %add_add_fusion.refs_0_), channel_id=1, source_target_pairs={{0,4},{1,5},{2,6},{3,7},{4,0},{5,1},{6,2},{7,3},{8,12},{9,13},{10,... | collective-permute-start | bytes 98312 | tf_op jit(solution)/shard_map/ppermute | solution.py:293
  20.7 1.4 %collective-permute-done.9.refs_3_ = f32[64,128]{1,0:T(8,128)S(1)} collective-permute-done((f32[64,128]{1,0:T(8,128)S(1)}, f32[64,128]{1,0:T(8,128)S(1)}, u32[]{:S(2)}, u32[]{:S(2)}) %collective-permute-start.9) | collective-permute-done | bytes 32800 | tf_op jit(solution)/shard_map/ppermute | solution.py:293
  22.2 1.8 %collective-permute-done.8.refs_2_ = f32[64,128]{1,0:T(8,128)S(1)} collective-permute-done((f32[64,128]{1,0:T(8,128)S(1)}, f32[64,128]{1,0:T(8,128)S(1)}, u32[]{:S(2)}, u32[]{:S(2)}) %collective-permute-start.8) | collective-permute-done | bytes 32800 | tf_op jit(solution)/shard_map/ppermute | solution.py:293
  24.0 0.0 collective-permute-done.3
  24.0 0.1 collective-permute-start.10
  24.1 3.1 %precondition.1.moved = f32[128,512]{1,0:T(8,128)S(1)} custom-call(f32[64,128]{1,0:T(8,128)S(1)} %add_add_fusion.refs_0_, f32[64,128]{1,0:T(8,128)S(1)} %collective-permute-done.7.refs_1_, f32[64,128]{1,0:T(8,128)S(1)} %collective-permute-done.8.refs_2_, f32[64,128]{1,0:T(8,128)S(1)} %collective-permute-done.9.refs_3_, ...), custom_call_target="tpu_custom_call" | custom-call | flops 3355443200 | bytes 524288 | tf_op jit(solution)/shard_map/precondition/pallas_call | solution.py:196
  27.2 0.0 collective-permute-done.10.refs_1_
  27.2 2.4 %score.1 = f32[512,128]{1,0:T(8,128)} custom-call(f32[128,512]{1,0:T(8,128)S(1)} %precondition.1.moved, bf16[64,4096]{1,0:T(8,128)(2,1)S(1)} %constant_dynamic-update-slice_fusion.4.refs_0_, bf16[64,4096]{1,0:T(8,128)(2,1)S(1)} %collective-permute-done.10.refs_1_), custom_call_target="tpu_custom_call" | custom-call | tf_op jit(solution)/shard_map/score/pallas_call | solution.py:253
  (10 shorter events, 0.1 us)
Async XLA Ops:
  0.0 11.8 %collective-permute-start.1 = (bf16[8,4096]{1,0:T(8,128)(2,1)}, bf16[8,4096]{1,0:T(8,128)(2,1)S(1)}, u32[]{:S(2)}, u32[]{:S(2)}) collective-permute-start(bf16[8,4096]{1,0:T(8,128)(2,1)} %param.9), channel_id=1, source_target_pairs={{0,8},{1,9},{2,10},{3,11},{4,12},{5,13},{6,14},{7,15},{8,0},{9,1},... | collective-permute-start | bytes 196616 | tf_op jit(solution)/shard_map/ppermute | solution.py:293
  4.0 7.8 %collective-permute-start = (bf16[8,4096]{1,0:T(8,128)(2,1)}, bf16[8,4096]{1,0:T(8,128)(2,1)S(1)}, u32[]{:S(2)}, u32[]{:S(2)}) collective-permute-start(bf16[8,4096]{1,0:T(8,128)(2,1)} %param.9), channel_id=1, source_target_pairs={{0,12},{1,13},{2,14},{3,15},{4,8},{5,9},{6,10},{7,11},{8,4},{9,5},... | collective-permute-start | bytes 196616 | tf_op jit(solution)/shard_map/ppermute | solution.py:293
  5.4 6.4 %collective-permute-start.2 = (bf16[8,4096]{1,0:T(8,128)(2,1)}, bf16[8,4096]{1,0:T(8,128)(2,1)S(1)}, u32[]{:S(2)}, u32[]{:S(2)}) collective-permute-start(bf16[8,4096]{1,0:T(8,128)(2,1)} %param.9), channel_id=1, source_target_pairs={{0,4},{1,5},{2,6},{3,7},{4,0},{5,1},{6,2},{7,3},{8,12},{9,13},{10,... | collective-permute-start | bytes 196616 | tf_op jit(solution)/shard_map/ppermute | solution.py:293
  5.6 8.1 %copy-start = (bf16[8,4096]{1,0:T(8,128)(2,1)S(1)}, bf16[8,4096]{1,0:T(8,128)(2,1)}, u32[]{:S(2)}) copy-start(bf16[8,4096]{1,0:T(8,128)(2,1)} %param.9) | copy-start | bytes 196612
  11.8 3.7 %collective-permute-start.6 = (f32[64,128]{1,0:T(8,128)S(1)}, f32[64,128]{1,0:T(8,128)S(1)}, u32[]{:S(2)}, u32[]{:S(2)}) collective-permute-start(f32[64,128]{1,0:T(8,128)S(1)} %get-tuple-element.24), channel_id=1, source_target_pairs={{0,3},{1,2},{2,1},{3,0},{4,7},{5,6},{6,5},{7,4},{8,11},{9,10},{10,... | collective-permute-start | bytes 98312 | tf_op jit(solution)/shard_map/ppermute | solution.py:293
  12.3 4.0 %collective-permute-start.5 = (f32[64,128]{1,0:T(8,128)S(1)}, f32[64,128]{1,0:T(8,128)S(1)}, u32[]{:S(2)}, u32[]{:S(2)}) collective-permute-start(f32[64,128]{1,0:T(8,128)S(1)} %get-tuple-element.24), channel_id=1, source_target_pairs={{0,2},{1,3},{2,0},{3,1},{4,6},{5,7},{6,4},{7,5},{8,10},{9,11},{10,... | collective-permute-start | bytes 98312 | tf_op jit(solution)/shard_map/ppermute | solution.py:293
  13.5 2.8 %collective-permute-start.4 = (f32[64,128]{1,0:T(8,128)S(1)}, f32[64,128]{1,0:T(8,128)S(1)}, u32[]{:S(2)}, u32[]{:S(2)}) collective-permute-start(f32[64,128]{1,0:T(8,128)S(1)} %get-tuple-element.24), channel_id=1, source_target_pairs={{0,1},{1,0},{2,3},{3,2},{4,5},{5,4},{6,7},{7,6},{8,9},{9,8},{10,11... | collective-permute-start | bytes 98312 | tf_op jit(solution)/shard_map/ppermute | solution.py:293
  13.8 10.2 %collective-permute-start.3 = (bf16[32,4096]{1,0:T(8,128)(2,1)S(1)}, bf16[32,4096]{1,0:T(8,128)(2,1)S(1)}, u32[]{:S(2)}, u32[]{:S(2)}) collective-permute-start(bf16[32,4096]{1,0:T(8,128)(2,1)S(1)} %constant_dynamic-update-slice_fusion), channel_id=1, source_target_pairs={{0,2},{1,3},{2,0},{3,1},{4,6},{5,7},{6,4},{7,5},{8,10},{9,11},{10,... | collective-permute-start | bytes 786440 | tf_op jit(solution)/shard_map/ppermute | solution.py:293
  16.3 5.9 %collective-permute-start.9 = (f32[64,128]{1,0:T(8,128)S(1)}, f32[64,128]{1,0:T(8,128)S(1)}, u32[]{:S(2)}, u32[]{:S(2)}) collective-permute-start(f32[64,128]{1,0:T(8,128)S(1)} %add_add_fusion.refs_0_), channel_id=1, source_target_pairs={{0,12},{1,13},{2,14},{3,15},{4,8},{5,9},{6,10},{7,11},{8,4},{9,5},... | collective-permute-start | bytes 98312 | tf_op jit(solution)/shard_map/ppermute | solution.py:293
  18.9 5.1 %collective-permute-start.8 = (f32[64,128]{1,0:T(8,128)S(1)}, f32[64,128]{1,0:T(8,128)S(1)}, u32[]{:S(2)}, u32[]{:S(2)}) collective-permute-start(f32[64,128]{1,0:T(8,128)S(1)} %add_add_fusion.refs_0_), channel_id=1, source_target_pairs={{0,8},{1,9},{2,10},{3,11},{4,12},{5,13},{6,14},{7,15},{8,0},{9,1},... | collective-permute-start | bytes 98312 | tf_op jit(solution)/shard_map/ppermute | solution.py:293
  19.3 4.7 %collective-permute-start.7 = (f32[64,128]{1,0:T(8,128)S(1)}, f32[64,128]{1,0:T(8,128)S(1)}, u32[]{:S(2)}, u32[]{:S(2)}) collective-permute-start(f32[64,128]{1,0:T(8,128)S(1)} %add_add_fusion.refs_0_), channel_id=1, source_target_pairs={{0,4},{1,5},{2,6},{3,7},{4,0},{5,1},{6,2},{7,3},{8,12},{9,13},{10,... | collective-permute-start | bytes 98312 | tf_op jit(solution)/shard_map/ppermute | solution.py:293
  24.0 3.2 %collective-permute-start.10 = (bf16[64,4096]{1,0:T(8,128)(2,1)S(1)}, bf16[64,4096]{1,0:T(8,128)(2,1)S(1)}, u32[]{:S(2)}, u32[]{:S(2)}) collective-permute-start(bf16[64,4096]{1,0:T(8,128)(2,1)S(1)} %constant_dynamic-update-slice_fusion.4.refs_0_), channel_id=1, source_target_pairs={{0,1},{1,0},{2,3},{3,2},{4,5},{5,4},{6,7},{7,6},{8,9},{9,8},{10,11... | collective-permute-start | bytes 1572872 | tf_op jit(solution)/shard_map/ppermute | solution.py:293

commit v13 on v12

--- a/solution.py
+++ b/solution.py
@@ -70,7 +70,12 @@
             weight_copies[1].wait()
             start_next(1)
         rows = slice(part * COPY_ROWS, (part + many) * COPY_ROWS)
-        block = jnp.dot(tok_buf[at, rows, :], weight_t[at], preferred_element_type=jnp.float32)
+        quarters = [slice(begin, begin + width // 4) for begin in range(0, width, width // 4)]
+        terms = [
+            jnp.dot(tok_buf[at, rows, some], weight_t[at, some, :], preferred_element_type=jnp.float32)
+            for some in quarters
+        ]
+        block = (terms[0] + terms[1]) + (terms[2] + terms[3])
         if step == last_act:
             turned(1)
         if step == last_act + 1:
@@ -114,6 +119,12 @@
     )(*operands)
 
 
+def inverse_of(value):
+    guess = pl.reciprocal(value, approx=True)
+    guess = guess * (2.0 - value * guess)
+    return guess * (2.0 - value * guess)
+
+
 def inverse_pair(both):
     factor = both.shape[0]
     tile = (8, both.shape[1])
@@ -143,23 +154,25 @@
         r0, r1, r2, r3 = [
             jnp.where(on_block, jnp.where(inner == k + a, 1.0, 0.0), row(parts[home], off + a)) for a in range(4)
         ]
-        scale = 1.0 / (p00 * p11 - p01 * p01)
-        e02 = scale * (p11 * p02 - p01 * p12)
-        e03 = scale * (p11 * p03 - p01 * p13)
-        e12 = scale * (p00 * p12 - p01 * p02)
-        e13 = scale * (p00 * p13 - p01 * p03)
-        s22 = p22 - (p02 * e02 + p12 * e12)
-        s23 = p23 - (p02 * e03 + p12 * e13)
-        s33 = p33 - (p03 * e03 + p13 * e13)
-        scale_s = 1.0 / (s22 * s33 - s23 * s23)
-        y0 = scale * (p11 * r0 - p01 * r1)
-        y1 = scale * (p00 * r1 - p01 * r0)
-        t2 = r2 - (p02 * y0 + p12 * y1)
-        t3 = r3 - (p03 * y0 + p13 * y1)
-        w2 = scale_s * (s33 * t2 - s23 * t3)
-        w3 = scale_s * (s22 * t3 - s23 * t2)
-        w0 = y0 - (e02 * w2 + e03 * w3)
-        w1 = y1 - (e12 * w2 + e13 * w3)
+        scale = inverse_of(p00 * p11 - p01 * p01)
+        m02 = p11 * p02 - p01 * p12
+        m03 = p11 * p03 - p01 * p13
+        m12 = p00 * p12 - p01 * p02
+        m13 = p00 * p13 - p01 * p03
+        z0 = p11 * r0 - p01 * r1
+        z1 = p00 * r1 - p01 * r0
+        s22 = p22 - scale * (p02 * m02 + p12 * m12)
+        s23 = p23 - scale * (p02 * m03 + p12 * m13)
+        s33 = p33 - scale * (p03 * m03 + p13 * m13)
+        t2 = r2 - scale * (p02 * z0 + p12 * z1)
+        t3 = r3 - scale * (p03 * z0 + p13 * z1)
+        scale_s = inverse_of(s22 * s33 - s23 * s23)
+        u2 = s33 * t2 - s23 * t3
+        u3 = s22 * t3 - s23 * t2
+        w2 = scale_s * u2
+        w3 = scale_s * u3
+        w0 = scale * z0 - scale_s * (scale * m02 * u2 + scale * m03 * u3)
+        w1 = scale * z1 - scale_s * (scale * m12 * u2 + scale * m13 * u3)
         solved = (w0, w1, w2, w3)
         for m, part in enumerate(parts):
             change = (columns[0][m] * w0 + columns[1][m] * w1) + (columns[2][m] * w2 + columns[3][m] * w3)

time: 29.9 us -> 29.9 us (level)
  no operation moved by 1% of the time
where the time goes in v13:
time: 29.9 us; the launch traced here: 29.7 us
  starting transfers between devices  13.6 us (45%)
  Pallas kernels  11.7 us (39%)
  waiting for transfers between devices  4.16 us (14%)
    ppermute x11, starting transfers between devices, swapped(): return lax.ppermute(value, 'dp', perm)  13.6 us
    pallas_call x1, Pallas kernels, project(): pl.pallas_call(project_kernel, out_shape=(jax.ShapeDtypeStruct((factor, t...  6.16 us
    ppermute x11, waiting for transfers between devices, swapped(): return lax.ppermute(value, 'dp', perm)  4.16 us
    pallas_call x1, Pallas kernels, precondition(): pl.pallas_call(functools.partial(precondition_kernel, tok_total, n_terms)...  3.12 us
    pallas_call x1, Pallas kernels, score(): pl.pallas_call(functools.partial(score_kernel, size, n_pieces), out_shape...  2.44 us
  transfers between devices with their start and end apart: 11, of which 4 were waited for; matrix products, arithmetic and copies ran while one was open for 0% of the time, Pallas kernels for 31%

profile of v13, /device:TPU:0, one launch (start us, length us, event | category | flops | bytes accessed | tf_op | source)
XLA Modules:
  0.0 29.7 jit_solution(16084520336500508223)
XLA Ops:
  0.0 4.0 %collective-permute-start.1 = (bf16[8,4096]{1,0:T(8,128)(2,1)}, bf16[8,4096]{1,0:T(8,128)(2,1)S(1)}, u32[]{:S(2)}, u32[]{:S(2)}) collective-permute-start(bf16[8,4096]{1,0:T(8,128)(2,1)} %param.9), channel_id=1, source_target_pairs={{0,8},{1,9},{2,10},{3,11},{4,12},{5,13},{6,14},{7,15},{8,0},{9,1},... | collective-permute-start | bytes 196616 | tf_op jit(solution)/shard_map/ppermute | solution.py:306
  4.0 1.3 %collective-permute-start = (bf16[8,4096]{1,0:T(8,128)(2,1)}, bf16[8,4096]{1,0:T(8,128)(2,1)S(1)}, u32[]{:S(2)}, u32[]{:S(2)}) collective-permute-start(bf16[8,4096]{1,0:T(8,128)(2,1)} %param.9), channel_id=1, source_target_pairs={{0,12},{1,13},{2,14},{3,15},{4,8},{5,9},{6,10},{7,11},{8,4},{9,5},... | collective-permute-start | bytes 196616 | tf_op jit(solution)/shard_map/ppermute | solution.py:306
  5.4 0.2 collective-permute-start.2
  5.6 6.2 %project.1 = (f32[64,512]{1,0:T(8,128)S(1)}, f32[64,512]{1,0:T(8,128)S(1)}, f32[64,128]{1,0:T(8,128)S(1)}) custom-call(bf16[512,4096]{1,0:T(8,128)(2,1)} %acts.1, bf16[512,4096]{1,0:T(8,128)(2,1)} %grads.1, bf16[64,4096]{1,0:T(8,128)(2,1)} %bitcast.2, bf16[64,4096]{1,0:T(8,128)(2,1)} %bitcast.3), custom_call_target="tpu_custom_call" | custom-call | flops 536870912 | bytes 8388608 | tf_op jit(solution)/shard_map/project/pallas_call | solution.py:98
  11.8 0.0 collective-permute-done.1
  11.8 0.0 collective-permute-done
  11.8 0.0 collective-permute-done.2
  11.8 0.5 %collective-permute-start.6 = (f32[64,128]{1,0:T(8,128)S(1)}, f32[64,128]{1,0:T(8,128)S(1)}, u32[]{:S(2)}, u32[]{:S(2)}) collective-permute-start(f32[64,128]{1,0:T(8,128)S(1)} %get-tuple-element.24), channel_id=1, source_target_pairs={{0,3},{1,2},{2,1},{3,0},{4,7},{5,6},{6,5},{7,4},{8,11},{9,10},{10,... | collective-permute-start | bytes 98312 | tf_op jit(solution)/shard_map/ppermute | solution.py:306
  12.3 1.2 %collective-permute-start.5 = (f32[64,128]{1,0:T(8,128)S(1)}, f32[64,128]{1,0:T(8,128)S(1)}, u32[]{:S(2)}, u32[]{:S(2)}) collective-permute-start(f32[64,128]{1,0:T(8,128)S(1)} %get-tuple-element.24), channel_id=1, source_target_pairs={{0,2},{1,3},{2,0},{3,1},{4,6},{5,7},{6,4},{7,5},{8,10},{9,11},{10,... | collective-permute-start | bytes 98312 | tf_op jit(solution)/shard_map/ppermute | solution.py:306
  13.5 0.3 collective-permute-start.4
  13.8 1.6 %collective-permute-start.3 = (bf16[32,4096]{1,0:T(8,128)(2,1)S(1)}, bf16[32,4096]{1,0:T(8,128)(2,1)S(1)}, u32[]{:S(2)}, u32[]{:S(2)}) collective-permute-start(bf16[32,4096]{1,0:T(8,128)(2,1)S(1)} %constant_dynamic-update-slice_fusion), channel_id=1, source_target_pairs={{0,2},{1,3},{2,0},{3,1},{4,6},{5,7},{6,4},{7,5},{8,10},{9,11},{10,... | collective-permute-start | bytes 786440 | tf_op jit(solution)/shard_map/ppermute | solution.py:306
  15.4 0.1 collective-permute-done.6
  15.5 0.8 %collective-permute-done.5 = f32[64,128]{1,0:T(8,128)S(1)} collective-permute-done((f32[64,128]{1,0:T(8,128)S(1)}, f32[64,128]{1,0:T(8,128)S(1)}, u32[]{:S(2)}, u32[]{:S(2)}) %collective-permute-start.5) | collective-permute-done | bytes 32800 | tf_op jit(solution)/shard_map/ppermute | solution.py:306
  16.3 2.6 %collective-permute-start.9 = (f32[64,128]{1,0:T(8,128)S(1)}, f32[64,128]{1,0:T(8,128)S(1)}, u32[]{:S(2)}, u32[]{:S(2)}) collective-permute-start(f32[64,128]{1,0:T(8,128)S(1)} %add_add_fusion.refs_0_), channel_id=1, source_target_pairs={{0,12},{1,13},{2,14},{3,15},{4,8},{5,9},{6,10},{7,11},{8,4},{9,5},... | collective-permute-start | bytes 98312 | tf_op jit(solution)/shard_map/ppermute | solution.py:306
  18.9 0.3 %collective-permute-start.8 = (f32[64,128]{1,0:T(8,128)S(1)}, f32[64,128]{1,0:T(8,128)S(1)}, u32[]{:S(2)}, u32[]{:S(2)}) collective-permute-start(f32[64,128]{1,0:T(8,128)S(1)} %add_add_fusion.refs_0_), channel_id=1, source_target_pairs={{0,8},{1,9},{2,10},{3,11},{4,12},{5,13},{6,14},{7,15},{8,0},{9,1},... | collective-permute-start | bytes 98312 | tf_op jit(solution)/shard_map/ppermute | solution.py:306
  19.3 1.5 %collective-permute-start.7 = (f32[64,128]{1,0:T(8,128)S(1)}, f32[64,128]{1,0:T(8,128)S(1)}, u32[]{:S(2)}, u32[]{:S(2)}) collective-permute-start(f32[64,128]{1,0:T(8,128)S(1)} %add_add_fusion.refs_0_), channel_id=1, source_target_pairs={{0,4},{1,5},{2,6},{3,7},{4,0},{5,1},{6,2},{7,3},{8,12},{9,13},{10,... | collective-permute-start | bytes 98312 | tf_op jit(solution)/shard_map/ppermute | solution.py:306
  20.7 1.4 %collective-permute-done.9.refs_3_ = f32[64,128]{1,0:T(8,128)S(1)} collective-permute-done((f32[64,128]{1,0:T(8,128)S(1)}, f32[64,128]{1,0:T(8,128)S(1)}, u32[]{:S(2)}, u32[]{:S(2)}) %collective-permute-start.9) | collective-permute-done | bytes 32800 | tf_op jit(solution)/shard_map/ppermute | solution.py:306
  22.2 1.8 %collective-permute-done.8.refs_2_ = f32[64,128]{1,0:T(8,128)S(1)} collective-permute-done((f32[64,128]{1,0:T(8,128)S(1)}, f32[64,128]{1,0:T(8,128)S(1)}, u32[]{:S(2)}, u32[]{:S(2)}) %collective-permute-start.8) | collective-permute-done | bytes 32800 | tf_op jit(solution)/shard_map/ppermute | solution.py:306
  24.0 0.0 collective-permute-done.7.refs_1_
  24.0 0.0 collective-permute-done.3
  24.1 0.1 collective-permute-start.10
  24.1 3.1 %precondition.1.moved = f32[128,512]{1,0:T(8,128)S(1)} custom-call(f32[64,128]{1,0:T(8,128)S(1)} %add_add_fusion.refs_0_, f32[64,128]{1,0:T(8,128)S(1)} %collective-permute-done.7.refs_1_, f32[64,128]{1,0:T(8,128)S(1)} %collective-permute-done.8.refs_2_, f32[64,128]{1,0:T(8,128)S(1)} %collective-permute-done.9.refs_3_, ...), custom_call_target="tpu_custom_call" | custom-call | flops 3355443200 | bytes 524288 | tf_op jit(solution)/shard_map/precondition/pallas_call | solution.py:209
  27.3 0.0 collective-permute-done.10.refs_1_
  27.3 2.4 %score.1 = f32[512,128]{1,0:T(8,128)} custom-call(f32[128,512]{1,0:T(8,128)S(1)} %precondition.1.moved, bf16[64,4096]{1,0:T(8,128)(2,1)S(1)} %constant_dynamic-update-slice_fusion.4.refs_0_, bf16[64,4096]{1,0:T(8,128)(2,1)S(1)} %collective-permute-done.10.refs_1_), custom_call_target="tpu_custom_call" | custom-call | tf_op jit(solution)/shard_map/score/pallas_call | solution.py:266
  (10 shorter events, 0.1 us)
Async XLA Ops:
  0.0 11.8 %collective-permute-start.1 = (bf16[8,4096]{1,0:T(8,128)(2,1)}, bf16[8,4096]{1,0:T(8,128)(2,1)S(1)}, u32[]{:S(2)}, u32[]{:S(2)}) collective-permute-start(bf16[8,4096]{1,0:T(8,128)(2,1)} %param.9), channel_id=1, source_target_pairs={{0,8},{1,9},{2,10},{3,11},{4,12},{5,13},{6,14},{7,15},{8,0},{9,1},... | collective-permute-start | bytes 196616 | tf_op jit(solution)/shard_map/ppermute | solution.py:306
  4.0 7.8 %collective-permute-start = (bf16[8,4096]{1,0:T(8,128)(2,1)}, bf16[8,4096]{1,0:T(8,128)(2,1)S(1)}, u32[]{:S(2)}, u32[]{:S(2)}) collective-permute-start(bf16[8,4096]{1,0:T(8,128)(2,1)} %param.9), channel_id=1, source_target_pairs={{0,12},{1,13},{2,14},{3,15},{4,8},{5,9},{6,10},{7,11},{8,4},{9,5},... | collective-permute-start | bytes 196616 | tf_op jit(solution)/shard_map/ppermute | solution.py:306
  5.4 6.4 %collective-permute-start.2 = (bf16[8,4096]{1,0:T(8,128)(2,1)}, bf16[8,4096]{1,0:T(8,128)(2,1)S(1)}, u32[]{:S(2)}, u32[]{:S(2)}) collective-permute-start(bf16[8,4096]{1,0:T(8,128)(2,1)} %param.9), channel_id=1, source_target_pairs={{0,4},{1,5},{2,6},{3,7},{4,0},{5,1},{6,2},{7,3},{8,12},{9,13},{10,... | collective-permute-start | bytes 196616 | tf_op jit(solution)/shard_map/ppermute | solution.py:306
  5.6 8.1 %copy-start = (bf16[8,4096]{1,0:T(8,128)(2,1)S(1)}, bf16[8,4096]{1,0:T(8,128)(2,1)}, u32[]{:S(2)}) copy-start(bf16[8,4096]{1,0:T(8,128)(2,1)} %param.9) | copy-start | bytes 196612
  11.8 3.7 %collective-permute-start.6 = (f32[64,128]{1,0:T(8,128)S(1)}, f32[64,128]{1,0:T(8,128)S(1)}, u32[]{:S(2)}, u32[]{:S(2)}) collective-permute-start(f32[64,128]{1,0:T(8,128)S(1)} %get-tuple-element.24), channel_id=1, source_target_pairs={{0,3},{1,2},{2,1},{3,0},{4,7},{5,6},{6,5},{7,4},{8,11},{9,10},{10,... | collective-permute-start | bytes 98312 | tf_op jit(solution)/shard_map/ppermute | solution.py:306
  12.3 4.0 %collective-permute-start.5 = (f32[64,128]{1,0:T(8,128)S(1)}, f32[64,128]{1,0:T(8,128)S(1)}, u32[]{:S(2)}, u32[]{:S(2)}) collective-permute-start(f32[64,128]{1,0:T(8,128)S(1)} %get-tuple-element.24), channel_id=1, source_target_pairs={{0,2},{1,3},{2,0},{3,1},{4,6},{5,7},{6,4},{7,5},{8,10},{9,11},{10,... | collective-permute-start | bytes 98312 | tf_op jit(solution)/shard_map/ppermute | solution.py:306
  13.5 2.8 %collective-permute-start.4 = (f32[64,128]{1,0:T(8,128)S(1)}, f32[64,128]{1,0:T(8,128)S(1)}, u32[]{:S(2)}, u32[]{:S(2)}) collective-permute-start(f32[64,128]{1,0:T(8,128)S(1)} %get-tuple-element.24), channel_id=1, source_target_pairs={{0,1},{1,0},{2,3},{3,2},{4,5},{5,4},{6,7},{7,6},{8,9},{9,8},{10,11... | collective-permute-start | bytes 98312 | tf_op jit(solution)/shard_map/ppermute | solution.py:306
  13.8 10.2 %collective-permute-start.3 = (bf16[32,4096]{1,0:T(8,128)(2,1)S(1)}, bf16[32,4096]{1,0:T(8,128)(2,1)S(1)}, u32[]{:S(2)}, u32[]{:S(2)}) collective-permute-start(bf16[32,4096]{1,0:T(8,128)(2,1)S(1)} %constant_dynamic-update-slice_fusion), channel_id=1, source_target_pairs={{0,2},{1,3},{2,0},{3,1},{4,6},{5,7},{6,4},{7,5},{8,10},{9,11},{10,... | collective-permute-start | bytes 786440 | tf_op jit(solution)/shard_map/ppermute | solution.py:306
  16.3 5.9 %collective-permute-start.9 = (f32[64,128]{1,0:T(8,128)S(1)}, f32[64,128]{1,0:T(8,128)S(1)}, u32[]{:S(2)}, u32[]{:S(2)}) collective-permute-start(f32[64,128]{1,0:T(8,128)S(1)} %add_add_fusion.refs_0_), channel_id=1, source_target_pairs={{0,12},{1,13},{2,14},{3,15},{4,8},{5,9},{6,10},{7,11},{8,4},{9,5},... | collective-permute-start | bytes 98312 | tf_op jit(solution)/shard_map/ppermute | solution.py:306
  18.9 5.1 %collective-permute-start.8 = (f32[64,128]{1,0:T(8,128)S(1)}, f32[64,128]{1,0:T(8,128)S(1)}, u32[]{:S(2)}, u32[]{:S(2)}) collective-permute-start(f32[64,128]{1,0:T(8,128)S(1)} %add_add_fusion.refs_0_), channel_id=1, source_target_pairs={{0,8},{1,9},{2,10},{3,11},{4,12},{5,13},{6,14},{7,15},{8,0},{9,1},... | collective-permute-start | bytes 98312 | tf_op jit(solution)/shard_map/ppermute | solution.py:306
  19.3 4.7 %collective-permute-start.7 = (f32[64,128]{1,0:T(8,128)S(1)}, f32[64,128]{1,0:T(8,128)S(1)}, u32[]{:S(2)}, u32[]{:S(2)}) collective-permute-start(f32[64,128]{1,0:T(8,128)S(1)} %add_add_fusion.refs_0_), channel_id=1, source_target_pairs={{0,4},{1,5},{2,6},{3,7},{4,0},{5,1},{6,2},{7,3},{8,12},{9,13},{10,... | collective-permute-start | bytes 98312 | tf_op jit(solution)/shard_map/ppermute | solution.py:306
  24.1 3.2 %collective-permute-start.10 = (bf16[64,4096]{1,0:T(8,128)(2,1)S(1)}, bf16[64,4096]{1,0:T(8,128)(2,1)S(1)}, u32[]{:S(2)}, u32[]{:S(2)}) collective-permute-start(bf16[64,4096]{1,0:T(8,128)(2,1)S(1)} %constant_dynamic-update-slice_fusion.4.refs_0_), channel_id=1, source_target_pairs={{0,1},{1,0},{2,3},{3,2},{4,5},{5,4},{6,7},{7,6},{8,9},{9,8},{10,11... | collective-permute-start | bytes 1572872 | tf_op jit(solution)/shard_map/ppermute | solution.py:306

commit v14 on v12

--- a/solution.py
+++ b/solution.py
@@ -10,7 +10,7 @@
 DAMP = 0.1
 HIGHEST = lax.Precision.HIGHEST
 COPY_ROWS = 128
-IN_FLIGHT = 4
+IN_FLIGHT = 5
 TOKENS_AT_ONCE = 256
 
 
@@ -124,9 +124,8 @@
     parts = [both[at : at + 8, :] for at in range(0, factor, 8)]
 
     def column(part, at):
-        left = jnp.broadcast_to(part[:, at : at + 1], tile)
-        right = jnp.broadcast_to(part[:, factor + at : factor + at + 1], tile)
-        return jnp.where(left_half, left, right)
+        index = jnp.where(left_half, at, factor + at)
+        return jnp.take_along_axis(part, index, axis=1, mode="promise_in_bounds")
 
     def row(part, at):
         return jnp.broadcast_to(part[at : at + 1, :], tile)

time: 29.9 us -> 29.1 us (0.973)
  Pallas kernels: 11.7 us -> 11 us
    pallas_call x1, Pallas kernels: 3.09 us -> 2.59 us  [precondition(): pl.pallas_call(functools.partial(precondition_kernel, tok_total, n_terms)...]
  transfers between devices with their start and end apart: 11 -> 11, of which waited for: 4 -> 4; matrix products, arithmetic and copies ran while one was open for 0% -> 0% of each run, Pallas kernels for 31% -> 29%
where the time goes in v14:
time: 29.1 us; the launch traced here: 29 us
  starting transfers between devices  13.6 us (47%)
  Pallas kernels  11 us (38%)
  waiting for transfers between devices  4.16 us (14%)
    ppermute x11, starting transfers between devices, swapped(): return lax.ppermute(value, 'dp', perm)  13.6 us
    pallas_call x1, Pallas kernels, project(): pl.pallas_call(project_kernel, out_shape=(jax.ShapeDtypeStruct((factor, t...  5.93 us
    ppermute x11, waiting for transfers between devices, swapped(): return lax.ppermute(value, 'dp', perm)  4.16 us
    pallas_call x1, Pallas kernels, precondition(): pl.pallas_call(functools.partial(precondition_kernel, tok_total, n_terms)...  2.59 us
    pallas_call x1, Pallas kernels, score(): pl.pallas_call(functools.partial(score_kernel, size, n_pieces), out_shape...  2.44 us
  transfers between devices with their start and end apart: 11, of which 4 were waited for; matrix products, arithmetic and copies ran while one was open for 0% of the time, Pallas kernels for 29%

profile of v14, /device:TPU:0, one launch (start us, length us, event | category | flops | bytes accessed | tf_op | source)
XLA Modules:
  0.0 29.0 jit_solution(13797220030758477848)
XLA Ops:
  0.0 4.0 %collective-permute-start.1 = (bf16[8,4096]{1,0:T(8,128)(2,1)}, bf16[8,4096]{1,0:T(8,128)(2,1)S(1)}, u32[]{:S(2)}, u32[]{:S(2)}) collective-permute-start(bf16[8,4096]{1,0:T(8,128)(2,1)} %param.9), channel_id=1, source_target_pairs={{0,8},{1,9},{2,10},{3,11},{4,12},{5,13},{6,14},{7,15},{8,0},{9,1},... | collective-permute-start | bytes 196616 | tf_op jit(solution)/shard_map/ppermute | solution.py:292
  4.0 1.3 %collective-permute-start = (bf16[8,4096]{1,0:T(8,128)(2,1)}, bf16[8,4096]{1,0:T(8,128)(2,1)S(1)}, u32[]{:S(2)}, u32[]{:S(2)}) collective-permute-start(bf16[8,4096]{1,0:T(8,128)(2,1)} %param.9), channel_id=1, source_target_pairs={{0,12},{1,13},{2,14},{3,15},{4,8},{5,9},{6,10},{7,11},{8,4},{9,5},... | collective-permute-start | bytes 196616 | tf_op jit(solution)/shard_map/ppermute | solution.py:292
  5.4 0.2 collective-permute-start.2
  5.6 5.9 %project.1 = (f32[64,512]{1,0:T(8,128)S(1)}, f32[64,512]{1,0:T(8,128)S(1)}, f32[64,128]{1,0:T(8,128)S(1)}) custom-call(bf16[512,4096]{1,0:T(8,128)(2,1)} %acts.1, bf16[512,4096]{1,0:T(8,128)(2,1)} %grads.1, bf16[64,4096]{1,0:T(8,128)(2,1)} %bitcast.2, bf16[64,4096]{1,0:T(8,128)(2,1)} %bitcast.3), custom_call_target="tpu_custom_call" | custom-call | flops 536870912 | bytes 8388608 | tf_op jit(solution)/shard_map/project/pallas_call | solution.py:93
  11.6 0.0 collective-permute-done.1
  11.6 0.0 collective-permute-done
  11.6 0.0 collective-permute-done.2
  11.6 0.5 %collective-permute-start.6 = (f32[64,128]{1,0:T(8,128)S(1)}, f32[64,128]{1,0:T(8,128)S(1)}, u32[]{:S(2)}, u32[]{:S(2)}) collective-permute-start(f32[64,128]{1,0:T(8,128)S(1)} %get-tuple-element.24), channel_id=1, source_target_pairs={{0,3},{1,2},{2,1},{3,0},{4,7},{5,6},{6,5},{7,4},{8,11},{9,10},{10,... | collective-permute-start | bytes 98312 | tf_op jit(solution)/shard_map/ppermute | solution.py:292
  12.1 1.2 %collective-permute-start.5 = (f32[64,128]{1,0:T(8,128)S(1)}, f32[64,128]{1,0:T(8,128)S(1)}, u32[]{:S(2)}, u32[]{:S(2)}) collective-permute-start(f32[64,128]{1,0:T(8,128)S(1)} %get-tuple-element.24), channel_id=1, source_target_pairs={{0,2},{1,3},{2,0},{3,1},{4,6},{5,7},{6,4},{7,5},{8,10},{9,11},{10,... | collective-permute-start | bytes 98312 | tf_op jit(solution)/shard_map/ppermute | solution.py:292
  13.3 0.3 collective-permute-start.4
  13.6 1.6 %collective-permute-start.3 = (bf16[32,4096]{1,0:T(8,128)(2,1)S(1)}, bf16[32,4096]{1,0:T(8,128)(2,1)S(1)}, u32[]{:S(2)}, u32[]{:S(2)}) collective-permute-start(bf16[32,4096]{1,0:T(8,128)(2,1)S(1)} %constant_dynamic-update-slice_fusion), channel_id=1, source_target_pairs={{0,2},{1,3},{2,0},{3,1},{4,6},{5,7},{6,4},{7,5},{8,10},{9,11},{10,... | collective-permute-start | bytes 786440 | tf_op jit(solution)/shard_map/ppermute | solution.py:292
  15.2 0.1 collective-permute-done.6
  15.3 0.8 %collective-permute-done.5 = f32[64,128]{1,0:T(8,128)S(1)} collective-permute-done((f32[64,128]{1,0:T(8,128)S(1)}, f32[64,128]{1,0:T(8,128)S(1)}, u32[]{:S(2)}, u32[]{:S(2)}) %collective-permute-start.5) | collective-permute-done | bytes 32800 | tf_op jit(solution)/shard_map/ppermute | solution.py:292
  16.1 0.0 collective-permute-done.4
  16.1 2.6 %collective-permute-start.9 = (f32[64,128]{1,0:T(8,128)S(1)}, f32[64,128]{1,0:T(8,128)S(1)}, u32[]{:S(2)}, u32[]{:S(2)}) collective-permute-start(f32[64,128]{1,0:T(8,128)S(1)} %add_add_fusion.refs_0_), channel_id=1, source_target_pairs={{0,12},{1,13},{2,14},{3,15},{4,8},{5,9},{6,10},{7,11},{8,4},{9,5},... | collective-permute-start | bytes 98312 | tf_op jit(solution)/shard_map/ppermute | solution.py:292
  18.7 0.3 %collective-permute-start.8 = (f32[64,128]{1,0:T(8,128)S(1)}, f32[64,128]{1,0:T(8,128)S(1)}, u32[]{:S(2)}, u32[]{:S(2)}) collective-permute-start(f32[64,128]{1,0:T(8,128)S(1)} %add_add_fusion.refs_0_), channel_id=1, source_target_pairs={{0,8},{1,9},{2,10},{3,11},{4,12},{5,13},{6,14},{7,15},{8,0},{9,1},... | collective-permute-start | bytes 98312 | tf_op jit(solution)/shard_map/ppermute | solution.py:292
  19.1 1.5 %collective-permute-start.7 = (f32[64,128]{1,0:T(8,128)S(1)}, f32[64,128]{1,0:T(8,128)S(1)}, u32[]{:S(2)}, u32[]{:S(2)}) collective-permute-start(f32[64,128]{1,0:T(8,128)S(1)} %add_add_fusion.refs_0_), channel_id=1, source_target_pairs={{0,4},{1,5},{2,6},{3,7},{4,0},{5,1},{6,2},{7,3},{8,12},{9,13},{10,... | collective-permute-start | bytes 98312 | tf_op jit(solution)/shard_map/ppermute | solution.py:292
  20.5 1.4 %collective-permute-done.9.refs_3_ = f32[64,128]{1,0:T(8,128)S(1)} collective-permute-done((f32[64,128]{1,0:T(8,128)S(1)}, f32[64,128]{1,0:T(8,128)S(1)}, u32[]{:S(2)}, u32[]{:S(2)}) %collective-permute-start.9) | collective-permute-done | bytes 32800 | tf_op jit(solution)/shard_map/ppermute | solution.py:292
  22.0 1.8 %collective-permute-done.8.refs_2_ = f32[64,128]{1,0:T(8,128)S(1)} collective-permute-done((f32[64,128]{1,0:T(8,128)S(1)}, f32[64,128]{1,0:T(8,128)S(1)}, u32[]{:S(2)}, u32[]{:S(2)}) %collective-permute-start.8) | collective-permute-done | bytes 32800 | tf_op jit(solution)/shard_map/ppermute | solution.py:292
  23.8 0.0 collective-permute-done.7.refs_1_
  23.8 0.0 collective-permute-done.3
  23.8 0.1 collective-permute-start.10
  23.9 2.6 %precondition.1.moved = f32[128,512]{1,0:T(8,128)S(1)} custom-call(f32[64,128]{1,0:T(8,128)S(1)} %add_add_fusion.refs_0_, f32[64,128]{1,0:T(8,128)S(1)} %collective-permute-done.7.refs_1_, f32[64,128]{1,0:T(8,128)S(1)} %collective-permute-done.8.refs_2_, f32[64,128]{1,0:T(8,128)S(1)} %collective-permute-done.9.refs_3_, ...), custom_call_target="tpu_custom_call" | custom-call | flops 3355443200 | bytes 524288 | tf_op jit(solution)/shard_map/precondition/pallas_call | solution.py:195
  26.5 2.4 %score.1 = f32[512,128]{1,0:T(8,128)} custom-call(f32[128,512]{1,0:T(8,128)S(1)} %precondition.1.moved, bf16[64,4096]{1,0:T(8,128)(2,1)S(1)} %constant_dynamic-update-slice_fusion.4.refs_0_, bf16[64,4096]{1,0:T(8,128)(2,1)S(1)} %collective-permute-done.10.refs_1_), custom_call_target="tpu_custom_call" | custom-call | tf_op jit(solution)/shard_map/score/pallas_call | solution.py:252
  (10 shorter events, 0.1 us)
Async XLA Ops:
  0.0 11.6 %collective-permute-start.1 = (bf16[8,4096]{1,0:T(8,128)(2,1)}, bf16[8,4096]{1,0:T(8,128)(2,1)S(1)}, u32[]{:S(2)}, u32[]{:S(2)}) collective-permute-start(bf16[8,4096]{1,0:T(8,128)(2,1)} %param.9), channel_id=1, source_target_pairs={{0,8},{1,9},{2,10},{3,11},{4,12},{5,13},{6,14},{7,15},{8,0},{9,1},... | collective-permute-start | bytes 196616 | tf_op jit(solution)/shard_map/ppermute | solution.py:292
  4.0 7.5 %collective-permute-start = (bf16[8,4096]{1,0:T(8,128)(2,1)}, bf16[8,4096]{1,0:T(8,128)(2,1)S(1)}, u32[]{:S(2)}, u32[]{:S(2)}) collective-permute-start(bf16[8,4096]{1,0:T(8,128)(2,1)} %param.9), channel_id=1, source_target_pairs={{0,12},{1,13},{2,14},{3,15},{4,8},{5,9},{6,10},{7,11},{8,4},{9,5},... | collective-permute-start | bytes 196616 | tf_op jit(solution)/shard_map/ppermute | solution.py:292
  5.4 6.2 %collective-permute-start.2 = (bf16[8,4096]{1,0:T(8,128)(2,1)}, bf16[8,4096]{1,0:T(8,128)(2,1)S(1)}, u32[]{:S(2)}, u32[]{:S(2)}) collective-permute-start(bf16[8,4096]{1,0:T(8,128)(2,1)} %param.9), channel_id=1, source_target_pairs={{0,4},{1,5},{2,6},{3,7},{4,0},{5,1},{6,2},{7,3},{8,12},{9,13},{10,... | collective-permute-start | bytes 196616 | tf_op jit(solution)/shard_map/ppermute | solution.py:292
  5.6 7.9 %copy-start = (bf16[8,4096]{1,0:T(8,128)(2,1)S(1)}, bf16[8,4096]{1,0:T(8,128)(2,1)}, u32[]{:S(2)}) copy-start(bf16[8,4096]{1,0:T(8,128)(2,1)} %param.9) | copy-start | bytes 196612
  11.6 3.7 %collective-permute-start.6 = (f32[64,128]{1,0:T(8,128)S(1)}, f32[64,128]{1,0:T(8,128)S(1)}, u32[]{:S(2)}, u32[]{:S(2)}) collective-permute-start(f32[64,128]{1,0:T(8,128)S(1)} %get-tuple-element.24), channel_id=1, source_target_pairs={{0,3},{1,2},{2,1},{3,0},{4,7},{5,6},{6,5},{7,4},{8,11},{9,10},{10,... | collective-permute-start | bytes 98312 | tf_op jit(solution)/shard_map/ppermute | solution.py:292
  12.1 4.0 %collective-permute-start.5 = (f32[64,128]{1,0:T(8,128)S(1)}, f32[64,128]{1,0:T(8,128)S(1)}, u32[]{:S(2)}, u32[]{:S(2)}) collective-permute-start(f32[64,128]{1,0:T(8,128)S(1)} %get-tuple-element.24), channel_id=1, source_target_pairs={{0,2},{1,3},{2,0},{3,1},{4,6},{5,7},{6,4},{7,5},{8,10},{9,11},{10,... | collective-permute-start | bytes 98312 | tf_op jit(solution)/shard_map/ppermute | solution.py:292
  13.3 2.8 %collective-permute-start.4 = (f32[64,128]{1,0:T(8,128)S(1)}, f32[64,128]{1,0:T(8,128)S(1)}, u32[]{:S(2)}, u32[]{:S(2)}) collective-permute-start(f32[64,128]{1,0:T(8,128)S(1)} %get-tuple-element.24), channel_id=1, source_target_pairs={{0,1},{1,0},{2,3},{3,2},{4,5},{5,4},{6,7},{7,6},{8,9},{9,8},{10,11... | collective-permute-start | bytes 98312 | tf_op jit(solution)/shard_map/ppermute | solution.py:292
  13.6 10.2 %collective-permute-start.3 = (bf16[32,4096]{1,0:T(8,128)(2,1)S(1)}, bf16[32,4096]{1,0:T(8,128)(2,1)S(1)}, u32[]{:S(2)}, u32[]{:S(2)}) collective-permute-start(bf16[32,4096]{1,0:T(8,128)(2,1)S(1)} %constant_dynamic-update-slice_fusion), channel_id=1, source_target_pairs={{0,2},{1,3},{2,0},{3,1},{4,6},{5,7},{6,4},{7,5},{8,10},{9,11},{10,... | collective-permute-start | bytes 786440 | tf_op jit(solution)/shard_map/ppermute | solution.py:292
  16.1 5.9 %collective-permute-start.9 = (f32[64,128]{1,0:T(8,128)S(1)}, f32[64,128]{1,0:T(8,128)S(1)}, u32[]{:S(2)}, u32[]{:S(2)}) collective-permute-start(f32[64,128]{1,0:T(8,128)S(1)} %add_add_fusion.refs_0_), channel_id=1, source_target_pairs={{0,12},{1,13},{2,14},{3,15},{4,8},{5,9},{6,10},{7,11},{8,4},{9,5},... | collective-permute-start | bytes 98312 | tf_op jit(solution)/shard_map/ppermute | solution.py:292
  18.7 5.1 %collective-permute-start.8 = (f32[64,128]{1,0:T(8,128)S(1)}, f32[64,128]{1,0:T(8,128)S(1)}, u32[]{:S(2)}, u32[]{:S(2)}) collective-permute-start(f32[64,128]{1,0:T(8,128)S(1)} %add_add_fusion.refs_0_), channel_id=1, source_target_pairs={{0,8},{1,9},{2,10},{3,11},{4,12},{5,13},{6,14},{7,15},{8,0},{9,1},... | collective-permute-start | bytes 98312 | tf_op jit(solution)/shard_map/ppermute | solution.py:292
  19.1 4.7 %collective-permute-start.7 = (f32[64,128]{1,0:T(8,128)S(1)}, f32[64,128]{1,0:T(8,128)S(1)}, u32[]{:S(2)}, u32[]{:S(2)}) collective-permute-start(f32[64,128]{1,0:T(8,128)S(1)} %add_add_fusion.refs_0_), channel_id=1, source_target_pairs={{0,4},{1,5},{2,6},{3,7},{4,0},{5,1},{6,2},{7,3},{8,12},{9,13},{10,... | collective-permute-start | bytes 98312 | tf_op jit(solution)/shard_map/ppermute | solution.py:292
  23.8 2.7 %collective-permute-start.10 = (bf16[64,4096]{1,0:T(8,128)(2,1)S(1)}, bf16[64,4096]{1,0:T(8,128)(2,1)S(1)}, u32[]{:S(2)}, u32[]{:S(2)}) collective-permute-start(bf16[64,4096]{1,0:T(8,128)(2,1)S(1)} %constant_dynamic-update-slice_fusion.4.refs_0_), channel_id=1, source_target_pairs={{0,1},{1,0},{2,3},{3,2},{4,5},{5,4},{6,7},{7,6},{8,9},{9,8},{10,11... | collective-permute-start | bytes 1572872 | tf_op jit(solution)/shard_map/ppermute | solution.py:292

commit v15 on v14

--- a/solution.py
+++ b/solution.py
@@ -12,6 +12,32 @@
 COPY_ROWS = 128
 IN_FLIGHT = 5
 TOKENS_AT_ONCE = 256
+
+
+def places(factor):
+    return [lax.broadcasted_iota(jnp.int32, (factor, factor), axis) for axis in (0, 1)]
+
+
+def packed(act, grad):
+    factor = act.shape[0]
+    row_at, lane = places(factor)
+    mixed = jnp.where(row_at <= lane, act, grad)
+    diagonal = jnp.sum(jnp.where(row_at == lane, grad, 0.0), axis=0, keepdims=True)
+    last = jnp.broadcast_to(jnp.concatenate([diagonal, diagonal], axis=1), (8, 2 * factor))
+    half = factor // 2
+    return jnp.concatenate([jnp.concatenate([mixed[:half], mixed[half:]], axis=1), last], axis=0)
+
+
+def unpacked(value):
+    factor = value.shape[1] // 2
+    half = factor // 2
+    row_at, lane = places(factor)
+    mixed = jnp.concatenate([value[:half, :factor], value[:half, factor:]], axis=0)
+    flipped = mixed.T
+    diagonal = jnp.broadcast_to(value[half : half + 1, :factor], (factor, factor))
+    act = jnp.where(row_at <= lane, mixed, flipped)
+    grad = jnp.where(row_at > lane, mixed, jnp.where(row_at < lane, flipped, diagonal))
+    return jnp.concatenate([act, grad], axis=1)
 
 
 def project_kernel(
@@ -81,7 +107,7 @@
         (act_t, grad_t)[at][:, rows] = flipped
         blocks[at].append((flipped, block))
     add_gram(1)
-    cov[...] = jnp.concatenate([functools.reduce(jnp.add, terms) for terms in grams], axis=1)
+    cov[...] = packed(*[functools.reduce(jnp.add, terms) for terms in grams])
 
 
 def project(acts, grads, proj_act, proj_grad):
@@ -95,7 +121,7 @@
         out_shape=(
             jax.ShapeDtypeStruct((factor, tok_rows), jnp.float32),
             jax.ShapeDtypeStruct((factor, tok_rows), jnp.float32),
-            jax.ShapeDtypeStruct((factor, 2 * factor), jnp.float32),
+            jax.ShapeDtypeStruct((factor // 2 + 8, 2 * factor), jnp.float32),
         ),
         in_specs=[pl.BlockSpec(memory_space=pltpu.HBM)] * 4,
         out_specs=[pl.BlockSpec(memory_space=pltpu.VMEM)] * 3,
@@ -175,6 +201,7 @@
     both = terms[0][...]
     for term in terms[1:]:
         both = both + term[...]
+    both = unpacked(both)
     factor = both.shape[0]
     lane = lax.broadcasted_iota(jnp.int32, both.shape, 1)
     row_at = lax.broadcasted_iota(jnp.int32, both.shape, 0)

time: 29.1 us -> 29 us (level)
  waiting for transfers between devices: 4.16 us -> 3.75 us
    ppermute x11, waiting for transfers between devices: 4.16 us -> 3.75 us  [swapped(): return lax.ppermute(value, 'dp', perm)]
  transfers between devices with their start and end apart: 11 -> 11, of which waited for: 4 -> 3; matrix products, arithmetic and copies ran while one was open for 0% -> 0% of each run, Pallas kernels for 29% -> 31%
where the time goes in v15:
time: 29 us; the launch traced here: 28.8 us
  starting transfers between devices  13.6 us (47%)
  Pallas kernels  11.2 us (39%)
  waiting for transfers between devices  3.75 us (13%)
    ppermute x11, starting transfers between devices, swapped(): return lax.ppermute(value, 'dp', perm)  13.6 us
    pallas_call x1, Pallas kernels, project(): pl.pallas_call(project_kernel, out_shape=(jax.ShapeDtypeStruct((factor, t...  5.93 us
    ppermute x11, waiting for transfers between devices, swapped(): return lax.ppermute(value, 'dp', perm)  3.75 us
    pallas_call x1, Pallas kernels, precondition(): pl.pallas_call(functools.partial(precondition_kernel, tok_total, n_terms)...  2.86 us
    pallas_call x1, Pallas kernels, score(): pl.pallas_call(functools.partial(score_kernel, size, n_pieces), out_shape...  2.44 us
  transfers between devices with their start and end apart: 11, of which 3 were waited for; matrix products, arithmetic and copies ran while one was open for 0% of the time, Pallas kernels for 31%

profile of v15, /device:TPU:0, one launch (start us, length us, event | category | flops | bytes accessed | tf_op | source)
XLA Modules:
  0.0 28.8 jit_solution(12083089863657375780)
XLA Ops:
  0.0 4.0 %collective-permute-start.1 = (bf16[8,4096]{1,0:T(8,128)(2,1)}, bf16[8,4096]{1,0:T(8,128)(2,1)S(1)}, u32[]{:S(2)}, u32[]{:S(2)}) collective-permute-start(bf16[8,4096]{1,0:T(8,128)(2,1)} %param.9), channel_id=1, source_target_pairs={{0,8},{1,9},{2,10},{3,11},{4,12},{5,13},{6,14},{7,15},{8,0},{9,1},... | collective-permute-start | bytes 196616 | tf_op jit(solution)/shard_map/ppermute | solution.py:319
  4.0 1.3 %collective-permute-start = (bf16[8,4096]{1,0:T(8,128)(2,1)}, bf16[8,4096]{1,0:T(8,128)(2,1)S(1)}, u32[]{:S(2)}, u32[]{:S(2)}) collective-permute-start(bf16[8,4096]{1,0:T(8,128)(2,1)} %param.9), channel_id=1, source_target_pairs={{0,12},{1,13},{2,14},{3,15},{4,8},{5,9},{6,10},{7,11},{8,4},{9,5},... | collective-permute-start | bytes 196616 | tf_op jit(solution)/shard_map/ppermute | solution.py:319
  5.4 0.2 collective-permute-start.2
  5.6 5.9 %project.1 = (f32[64,512]{1,0:T(8,128)S(1)}, f32[64,512]{1,0:T(8,128)S(1)}, f32[40,128]{1,0:T(8,128)S(1)}) custom-call(bf16[512,4096]{1,0:T(8,128)(2,1)} %acts.1, bf16[512,4096]{1,0:T(8,128)(2,1)} %grads.1, bf16[64,4096]{1,0:T(8,128)(2,1)} %bitcast.2, bf16[64,4096]{1,0:T(8,128)(2,1)} %bitcast.3), custom_call_target="tpu_custom_call" | custom-call | flops 536870912 | bytes 8388608 | tf_op jit(solution)/shard_map/project/pallas_call | solution.py:119
  11.6 0.0 collective-permute-done.1
  11.6 0.0 collective-permute-done
  11.6 0.0 collective-permute-done.2
  11.6 0.5 %collective-permute-start.6 = (f32[40,128]{1,0:T(8,128)S(1)}, f32[40,128]{1,0:T(8,128)S(1)}, u32[]{:S(2)}, u32[]{:S(2)}) collective-permute-start(f32[40,128]{1,0:T(8,128)S(1)} %get-tuple-element.24), channel_id=1, source_target_pairs={{0,3},{1,2},{2,1},{3,0},{4,7},{5,6},{6,5},{7,4},{8,11},{9,10},{10,... | collective-permute-start | bytes 61448 | tf_op jit(solution)/shard_map/ppermute | solution.py:319
  12.1 1.2 %collective-permute-start.5 = (f32[40,128]{1,0:T(8,128)S(1)}, f32[40,128]{1,0:T(8,128)S(1)}, u32[]{:S(2)}, u32[]{:S(2)}) collective-permute-start(f32[40,128]{1,0:T(8,128)S(1)} %get-tuple-element.24), channel_id=1, source_target_pairs={{0,2},{1,3},{2,0},{3,1},{4,6},{5,7},{6,4},{7,5},{8,10},{9,11},{10,... | collective-permute-start | bytes 61448 | tf_op jit(solution)/shard_map/ppermute | solution.py:319
  13.3 0.3 collective-permute-start.4
  13.6 1.6 %collective-permute-start.3 = (bf16[32,4096]{1,0:T(8,128)(2,1)S(1)}, bf16[32,4096]{1,0:T(8,128)(2,1)S(1)}, u32[]{:S(2)}, u32[]{:S(2)}) collective-permute-start(bf16[32,4096]{1,0:T(8,128)(2,1)S(1)} %constant_dynamic-update-slice_fusion), channel_id=1, source_target_pairs={{0,2},{1,3},{2,0},{3,1},{4,6},{5,7},{6,4},{7,5},{8,10},{9,11},{10,... | collective-permute-start | bytes 786440 | tf_op jit(solution)/shard_map/ppermute | solution.py:319
  15.2 0.0 collective-permute-done.6
  15.2 0.7 %collective-permute-done.5 = f32[40,128]{1,0:T(8,128)S(1)} collective-permute-done((f32[40,128]{1,0:T(8,128)S(1)}, f32[40,128]{1,0:T(8,128)S(1)}, u32[]{:S(2)}, u32[]{:S(2)}) %collective-permute-start.5) | collective-permute-done | bytes 20512 | tf_op jit(solution)/shard_map/ppermute | solution.py:319
  15.8 0.0 collective-permute-done.4
  15.9 2.7 %collective-permute-start.9 = (f32[40,128]{1,0:T(8,128)S(1)}, f32[40,128]{1,0:T(8,128)S(1)}, u32[]{:S(2)}, u32[]{:S(2)}) collective-permute-start(f32[40,128]{1,0:T(8,128)S(1)} %add_add_fusion.refs_0_), channel_id=1, source_target_pairs={{0,12},{1,13},{2,14},{3,15},{4,8},{5,9},{6,10},{7,11},{8,4},{9,5},... | collective-permute-start | bytes 61448 | tf_op jit(solution)/shard_map/ppermute | solution.py:319
  18.6 0.3 %collective-permute-start.8 = (f32[40,128]{1,0:T(8,128)S(1)}, f32[40,128]{1,0:T(8,128)S(1)}, u32[]{:S(2)}, u32[]{:S(2)}) collective-permute-start(f32[40,128]{1,0:T(8,128)S(1)} %add_add_fusion.refs_0_), channel_id=1, source_target_pairs={{0,8},{1,9},{2,10},{3,11},{4,12},{5,13},{6,14},{7,15},{8,0},{9,1},... | collective-permute-start | bytes 61448 | tf_op jit(solution)/shard_map/ppermute | solution.py:319
  18.9 1.4 %collective-permute-start.7 = (f32[40,128]{1,0:T(8,128)S(1)}, f32[40,128]{1,0:T(8,128)S(1)}, u32[]{:S(2)}, u32[]{:S(2)}) collective-permute-start(f32[40,128]{1,0:T(8,128)S(1)} %add_add_fusion.refs_0_), channel_id=1, source_target_pairs={{0,4},{1,5},{2,6},{3,7},{4,0},{5,1},{6,2},{7,3},{8,12},{9,13},{10,... | collective-permute-start | bytes 61448 | tf_op jit(solution)/shard_map/ppermute | solution.py:319
  20.3 1.2 %collective-permute-done.9.refs_3_ = f32[40,128]{1,0:T(8,128)S(1)} collective-permute-done((f32[40,128]{1,0:T(8,128)S(1)}, f32[40,128]{1,0:T(8,128)S(1)}, u32[]{:S(2)}, u32[]{:S(2)}) %collective-permute-start.9) | collective-permute-done | bytes 20512 | tf_op jit(solution)/shard_map/ppermute | solution.py:319
  21.5 1.8 %collective-permute-done.8.refs_2_ = f32[40,128]{1,0:T(8,128)S(1)} collective-permute-done((f32[40,128]{1,0:T(8,128)S(1)}, f32[40,128]{1,0:T(8,128)S(1)}, u32[]{:S(2)}, u32[]{:S(2)}) %collective-permute-start.8) | collective-permute-done | bytes 20512 | tf_op jit(solution)/shard_map/ppermute | solution.py:319
  23.4 0.0 collective-permute-done.7.refs_1_
  23.4 0.0 collective-permute-done.3
  23.4 0.1 collective-permute-start.10
  23.5 2.9 %precondition.1.moved = f32[128,512]{1,0:T(8,128)S(1)} custom-call(f32[40,128]{1,0:T(8,128)S(1)} %add_add_fusion.refs_0_, f32[40,128]{1,0:T(8,128)S(1)} %collective-permute-done.7.refs_1_, f32[40,128]{1,0:T(8,128)S(1)} %collective-permute-done.8.refs_2_, f32[40,128]{1,0:T(8,128)S(1)} %collective-permute-done.9.refs_3_, ...), custom_call_target="tpu_custom_call" | custom-call | flops 3355443200 | bytes 524288 | tf_op jit(solution)/shard_map/precondition/pallas_call | solution.py:222
  26.4 2.4 %score.1 = f32[512,128]{1,0:T(8,128)} custom-call(f32[128,512]{1,0:T(8,128)S(1)} %precondition.1.moved, bf16[64,4096]{1,0:T(8,128)(2,1)S(1)} %constant_dynamic-update-slice_fusion.4.refs_0_, bf16[64,4096]{1,0:T(8,128)(2,1)S(1)} %collective-permute-done.10.refs_1_), custom_call_target="tpu_custom_call" | custom-call | tf_op jit(solution)/shard_map/score/pallas_call | solution.py:279
  (10 shorter events, 0.1 us)
Async XLA Ops:
  0.0 11.6 %collective-permute-start.1 = (bf16[8,4096]{1,0:T(8,128)(2,1)}, bf16[8,4096]{1,0:T(8,128)(2,1)S(1)}, u32[]{:S(2)}, u32[]{:S(2)}) collective-permute-start(bf16[8,4096]{1,0:T(8,128)(2,1)} %param.9), channel_id=1, source_target_pairs={{0,8},{1,9},{2,10},{3,11},{4,12},{5,13},{6,14},{7,15},{8,0},{9,1},... | collective-permute-start | bytes 196616 | tf_op jit(solution)/shard_map/ppermute | solution.py:319
  4.0 7.5 %collective-permute-start = (bf16[8,4096]{1,0:T(8,128)(2,1)}, bf16[8,4096]{1,0:T(8,128)(2,1)S(1)}, u32[]{:S(2)}, u32[]{:S(2)}) collective-permute-start(bf16[8,4096]{1,0:T(8,128)(2,1)} %param.9), channel_id=1, source_target_pairs={{0,12},{1,13},{2,14},{3,15},{4,8},{5,9},{6,10},{7,11},{8,4},{9,5},... | collective-permute-start | bytes 196616 | tf_op jit(solution)/shard_map/ppermute | solution.py:319
  5.4 6.2 %collective-permute-start.2 = (bf16[8,4096]{1,0:T(8,128)(2,1)}, bf16[8,4096]{1,0:T(8,128)(2,1)S(1)}, u32[]{:S(2)}, u32[]{:S(2)}) collective-permute-start(bf16[8,4096]{1,0:T(8,128)(2,1)} %param.9), channel_id=1, source_target_pairs={{0,4},{1,5},{2,6},{3,7},{4,0},{5,1},{6,2},{7,3},{8,12},{9,13},{10,... | collective-permute-start | bytes 196616 | tf_op jit(solution)/shard_map/ppermute | solution.py:319
  5.6 7.9 %copy-start = (bf16[8,4096]{1,0:T(8,128)(2,1)S(1)}, bf16[8,4096]{1,0:T(8,128)(2,1)}, u32[]{:S(2)}) copy-start(bf16[8,4096]{1,0:T(8,128)(2,1)} %param.9) | copy-start | bytes 196612
  11.6 3.6 %collective-permute-start.6 = (f32[40,128]{1,0:T(8,128)S(1)}, f32[40,128]{1,0:T(8,128)S(1)}, u32[]{:S(2)}, u32[]{:S(2)}) collective-permute-start(f32[40,128]{1,0:T(8,128)S(1)} %get-tuple-element.24), channel_id=1, source_target_pairs={{0,3},{1,2},{2,1},{3,0},{4,7},{5,6},{6,5},{7,4},{8,11},{9,10},{10,... | collective-permute-start | bytes 61448 | tf_op jit(solution)/shard_map/ppermute | solution.py:319
  12.1 3.8 %collective-permute-start.5 = (f32[40,128]{1,0:T(8,128)S(1)}, f32[40,128]{1,0:T(8,128)S(1)}, u32[]{:S(2)}, u32[]{:S(2)}) collective-permute-start(f32[40,128]{1,0:T(8,128)S(1)} %get-tuple-element.24), channel_id=1, source_target_pairs={{0,2},{1,3},{2,0},{3,1},{4,6},{5,7},{6,4},{7,5},{8,10},{9,11},{10,... | collective-permute-start | bytes 61448 | tf_op jit(solution)/shard_map/ppermute | solution.py:319
  13.3 2.6 %collective-permute-start.4 = (f32[40,128]{1,0:T(8,128)S(1)}, f32[40,128]{1,0:T(8,128)S(1)}, u32[]{:S(2)}, u32[]{:S(2)}) collective-permute-start(f32[40,128]{1,0:T(8,128)S(1)} %get-tuple-element.24), channel_id=1, source_target_pairs={{0,1},{1,0},{2,3},{3,2},{4,5},{5,4},{6,7},{7,6},{8,9},{9,8},{10,11... | collective-permute-start | bytes 61448 | tf_op jit(solution)/shard_map/ppermute | solution.py:319
  13.6 9.8 %collective-permute-start.3 = (bf16[32,4096]{1,0:T(8,128)(2,1)S(1)}, bf16[32,4096]{1,0:T(8,128)(2,1)S(1)}, u32[]{:S(2)}, u32[]{:S(2)}) collective-permute-start(bf16[32,4096]{1,0:T(8,128)(2,1)S(1)} %constant_dynamic-update-slice_fusion), channel_id=1, source_target_pairs={{0,2},{1,3},{2,0},{3,1},{4,6},{5,7},{6,4},{7,5},{8,10},{9,11},{10,... | collective-permute-start | bytes 786440 | tf_op jit(solution)/shard_map/ppermute | solution.py:319
  15.9 5.7 %collective-permute-start.9 = (f32[40,128]{1,0:T(8,128)S(1)}, f32[40,128]{1,0:T(8,128)S(1)}, u32[]{:S(2)}, u32[]{:S(2)}) collective-permute-start(f32[40,128]{1,0:T(8,128)S(1)} %add_add_fusion.refs_0_), channel_id=1, source_target_pairs={{0,12},{1,13},{2,14},{3,15},{4,8},{5,9},{6,10},{7,11},{8,4},{9,5},... | collective-permute-start | bytes 61448 | tf_op jit(solution)/shard_map/ppermute | solution.py:319
  18.6 4.8 %collective-permute-start.8 = (f32[40,128]{1,0:T(8,128)S(1)}, f32[40,128]{1,0:T(8,128)S(1)}, u32[]{:S(2)}, u32[]{:S(2)}) collective-permute-start(f32[40,128]{1,0:T(8,128)S(1)} %add_add_fusion.refs_0_), channel_id=1, source_target_pairs={{0,8},{1,9},{2,10},{3,11},{4,12},{5,13},{6,14},{7,15},{8,0},{9,1},... | collective-permute-start | bytes 61448 | tf_op jit(solution)/shard_map/ppermute | solution.py:319
  18.9 4.5 %collective-permute-start.7 = (f32[40,128]{1,0:T(8,128)S(1)}, f32[40,128]{1,0:T(8,128)S(1)}, u32[]{:S(2)}, u32[]{:S(2)}) collective-permute-start(f32[40,128]{1,0:T(8,128)S(1)} %add_add_fusion.refs_0_), channel_id=1, source_target_pairs={{0,4},{1,5},{2,6},{3,7},{4,0},{5,1},{6,2},{7,3},{8,12},{9,13},{10,... | collective-permute-start | bytes 61448 | tf_op jit(solution)/shard_map/ppermute | solution.py:319
  23.4 2.9 %collective-permute-start.10 = (bf16[64,4096]{1,0:T(8,128)(2,1)S(1)}, bf16[64,4096]{1,0:T(8,128)(2,1)S(1)}, u32[]{:S(2)}, u32[]{:S(2)}) collective-permute-start(bf16[64,4096]{1,0:T(8,128)(2,1)S(1)} %constant_dynamic-update-slice_fusion.4.refs_0_), channel_id=1, source_target_pairs={{0,1},{1,0},{2,3},{3,2},{4,5},{5,4},{6,7},{7,6},{8,9},{9,8},{10,11... | collective-permute-start | bytes 1572872 | tf_op jit(solution)/shard_map/ppermute | solution.py:319

commit v16 on v15

--- a/solution.py
+++ b/solution.py
@@ -10,7 +10,7 @@
 DAMP = 0.1
 HIGHEST = lax.Precision.HIGHEST
 COPY_ROWS = 128
-IN_FLIGHT = 5
+IN_FLIGHT = 6
 TOKENS_AT_ONCE = 256
 
 
@@ -236,25 +236,29 @@
     queries, (scores, ordered, result, sems) = refs[:n_pieces], refs[n_pieces:]
     factor = moved.shape[0] // 2
     owners = owners_of(lax.axis_index("dp"), size)
-    group = 4
+    group = 2
     copies = []
     for part, begin in enumerate(range(0, moved.shape[1], TOKENS_AT_ONCE)):
         tokens = slice(begin, begin + TOKENS_AT_ONCE)
         act_side = moved[:factor, tokens]
-        total = None
-        for first in range(0, factor, group):
+
+        def split(first):
             outer = jnp.concatenate(
                 [act_side * moved[factor + i : factor + i + 1, tokens] for i in range(first, first + group)], axis=0
             )
             high = outer.astype(jnp.bfloat16)
             low = (outer - high.astype(jnp.float32)).astype(jnp.bfloat16)
+            return jnp.concatenate([high, low], axis=0)
+
+        total = None
+        later = split(0)
+        for first in range(0, factor, group):
+            both = later
+            if first + group < factor:
+                later = split(first + group)
             columns = slice(first * factor, (first + group) * factor)
             values = jnp.concatenate([piece[:, columns] for piece in queries], axis=0)
-            term = jnp.dot(
-                jnp.concatenate([values, values], axis=1),
-                jnp.concatenate([high, low], axis=0),
-                preferred_element_type=jnp.float32,
-            )
+            term = jnp.dot(jnp.concatenate([values, values], axis=1), both, preferred_element_type=jnp.float32)
             total = term if total is None else total + term
         rows = total.shape[0] // size
         for at, owner in enumerate(owners):

time: 29 us -> 29.2 us (level)
  no operation moved by 1% of the time
where the time goes in v16:
time: 29.2 us; the launch traced here: 29 us
  starting transfers between devices  13.6 us (47%)
  Pallas kernels  11.4 us (39%)
  waiting for transfers between devices  3.75 us (13%)
    ppermute x11, starting transfers between devices, swapped(): return lax.ppermute(value, 'dp', perm)  13.6 us
    pallas_call x1, Pallas kernels, project(): pl.pallas_call(project_kernel, out_shape=(jax.ShapeDtypeStruct((factor, t...  6.16 us
    ppermute x11, waiting for transfers between devices, swapped(): return lax.ppermute(value, 'dp', perm)  3.75 us
    pallas_call x1, Pallas kernels, precondition(): pl.pallas_call(functools.partial(precondition_kernel, tok_total, n_terms)...  2.86 us
    pallas_call x1, Pallas kernels, score(): pl.pallas_call(functools.partial(score_kernel, size, n_pieces), out_shape...  2.39 us
  transfers between devices with their start and end apart: 11, of which 3 were waited for; matrix products, arithmetic and copies ran while one was open for 0% of the time, Pallas kernels for 31%

profile of v16, /device:TPU:0, one launch (start us, length us, event | category | flops | bytes accessed | tf_op | source)
XLA Modules:
  0.0 29.0 jit_solution(12956577536675647745)
XLA Ops:
  0.0 4.0 %collective-permute-start.1 = (bf16[8,4096]{1,0:T(8,128)(2,1)}, bf16[8,4096]{1,0:T(8,128)(2,1)S(1)}, u32[]{:S(2)}, u32[]{:S(2)}) collective-permute-start(bf16[8,4096]{1,0:T(8,128)(2,1)} %param.9), channel_id=1, source_target_pairs={{0,8},{1,9},{2,10},{3,11},{4,12},{5,13},{6,14},{7,15},{8,0},{9,1},... | collective-permute-start | bytes 196616 | tf_op jit(solution)/shard_map/ppermute | solution.py:323
  4.0 1.3 %collective-permute-start = (bf16[8,4096]{1,0:T(8,128)(2,1)}, bf16[8,4096]{1,0:T(8,128)(2,1)S(1)}, u32[]{:S(2)}, u32[]{:S(2)}) collective-permute-start(bf16[8,4096]{1,0:T(8,128)(2,1)} %param.9), channel_id=1, source_target_pairs={{0,12},{1,13},{2,14},{3,15},{4,8},{5,9},{6,10},{7,11},{8,4},{9,5},... | collective-permute-start | bytes 196616 | tf_op jit(solution)/shard_map/ppermute | solution.py:323
  5.4 0.2 collective-permute-start.2
  5.6 6.2 %project.1 = (f32[64,512]{1,0:T(8,128)S(1)}, f32[64,512]{1,0:T(8,128)S(1)}, f32[40,128]{1,0:T(8,128)S(1)}) custom-call(bf16[512,4096]{1,0:T(8,128)(2,1)} %acts.1, bf16[512,4096]{1,0:T(8,128)(2,1)} %grads.1, bf16[64,4096]{1,0:T(8,128)(2,1)} %bitcast.2, bf16[64,4096]{1,0:T(8,128)(2,1)} %bitcast.3), custom_call_target="tpu_custom_call" | custom-call | flops 536870912 | bytes 8388608 | tf_op jit(solution)/shard_map/project/pallas_call | solution.py:119
  11.8 0.0 collective-permute-done.1
  11.8 0.0 collective-permute-done
  11.8 0.0 collective-permute-done.2
  11.8 0.5 %collective-permute-start.6 = (f32[40,128]{1,0:T(8,128)S(1)}, f32[40,128]{1,0:T(8,128)S(1)}, u32[]{:S(2)}, u32[]{:S(2)}) collective-permute-start(f32[40,128]{1,0:T(8,128)S(1)} %get-tuple-element.24), channel_id=1, source_target_pairs={{0,3},{1,2},{2,1},{3,0},{4,7},{5,6},{6,5},{7,4},{8,11},{9,10},{10,... | collective-permute-start | bytes 61448 | tf_op jit(solution)/shard_map/ppermute | solution.py:323
  12.3 1.2 %collective-permute-start.5 = (f32[40,128]{1,0:T(8,128)S(1)}, f32[40,128]{1,0:T(8,128)S(1)}, u32[]{:S(2)}, u32[]{:S(2)}) collective-permute-start(f32[40,128]{1,0:T(8,128)S(1)} %get-tuple-element.24), channel_id=1, source_target_pairs={{0,2},{1,3},{2,0},{3,1},{4,6},{5,7},{6,4},{7,5},{8,10},{9,11},{10,... | collective-permute-start | bytes 61448 | tf_op jit(solution)/shard_map/ppermute | solution.py:323
  13.5 0.3 collective-permute-start.4
  13.8 1.6 %collective-permute-start.3 = (bf16[32,4096]{1,0:T(8,128)(2,1)S(1)}, bf16[32,4096]{1,0:T(8,128)(2,1)S(1)}, u32[]{:S(2)}, u32[]{:S(2)}) collective-permute-start(bf16[32,4096]{1,0:T(8,128)(2,1)S(1)} %constant_dynamic-update-slice_fusion), channel_id=1, source_target_pairs={{0,2},{1,3},{2,0},{3,1},{4,6},{5,7},{6,4},{7,5},{8,10},{9,11},{10,... | collective-permute-start | bytes 786440 | tf_op jit(solution)/shard_map/ppermute | solution.py:323
  15.4 0.0 collective-permute-done.6
  15.4 0.7 %collective-permute-done.5 = f32[40,128]{1,0:T(8,128)S(1)} collective-permute-done((f32[40,128]{1,0:T(8,128)S(1)}, f32[40,128]{1,0:T(8,128)S(1)}, u32[]{:S(2)}, u32[]{:S(2)}) %collective-permute-start.5) | collective-permute-done | bytes 20512 | tf_op jit(solution)/shard_map/ppermute | solution.py:323
  16.1 0.0 collective-permute-done.4
  16.1 2.7 %collective-permute-start.9 = (f32[40,128]{1,0:T(8,128)S(1)}, f32[40,128]{1,0:T(8,128)S(1)}, u32[]{:S(2)}, u32[]{:S(2)}) collective-permute-start(f32[40,128]{1,0:T(8,128)S(1)} %add_add_fusion.refs_0_), channel_id=1, source_target_pairs={{0,12},{1,13},{2,14},{3,15},{4,8},{5,9},{6,10},{7,11},{8,4},{9,5},... | collective-permute-start | bytes 61448 | tf_op jit(solution)/shard_map/ppermute | solution.py:323
  18.8 0.3 %collective-permute-start.8 = (f32[40,128]{1,0:T(8,128)S(1)}, f32[40,128]{1,0:T(8,128)S(1)}, u32[]{:S(2)}, u32[]{:S(2)}) collective-permute-start(f32[40,128]{1,0:T(8,128)S(1)} %add_add_fusion.refs_0_), channel_id=1, source_target_pairs={{0,8},{1,9},{2,10},{3,11},{4,12},{5,13},{6,14},{7,15},{8,0},{9,1},... | collective-permute-start | bytes 61448 | tf_op jit(solution)/shard_map/ppermute | solution.py:323
  19.1 1.4 %collective-permute-start.7 = (f32[40,128]{1,0:T(8,128)S(1)}, f32[40,128]{1,0:T(8,128)S(1)}, u32[]{:S(2)}, u32[]{:S(2)}) collective-permute-start(f32[40,128]{1,0:T(8,128)S(1)} %add_add_fusion.refs_0_), channel_id=1, source_target_pairs={{0,4},{1,5},{2,6},{3,7},{4,0},{5,1},{6,2},{7,3},{8,12},{9,13},{10,... | collective-permute-start | bytes 61448 | tf_op jit(solution)/shard_map/ppermute | solution.py:323
  20.5 1.2 %collective-permute-done.9.refs_3_ = f32[40,128]{1,0:T(8,128)S(1)} collective-permute-done((f32[40,128]{1,0:T(8,128)S(1)}, f32[40,128]{1,0:T(8,128)S(1)}, u32[]{:S(2)}, u32[]{:S(2)}) %collective-permute-start.9) | collective-permute-done | bytes 20512 | tf_op jit(solution)/shard_map/ppermute | solution.py:323
  21.7 1.9 %collective-permute-done.8.refs_2_ = f32[40,128]{1,0:T(8,128)S(1)} collective-permute-done((f32[40,128]{1,0:T(8,128)S(1)}, f32[40,128]{1,0:T(8,128)S(1)}, u32[]{:S(2)}, u32[]{:S(2)}) %collective-permute-start.8) | collective-permute-done | bytes 20512 | tf_op jit(solution)/shard_map/ppermute | solution.py:323
  23.6 0.0 collective-permute-done.7.refs_1_
  23.7 0.1 collective-permute-start.10
  23.7 2.9 %precondition.1.moved = f32[128,512]{1,0:T(8,128)S(1)} custom-call(f32[40,128]{1,0:T(8,128)S(1)} %add_add_fusion.refs_0_, f32[40,128]{1,0:T(8,128)S(1)} %collective-permute-done.7.refs_1_, f32[40,128]{1,0:T(8,128)S(1)} %collective-permute-done.8.refs_2_, f32[40,128]{1,0:T(8,128)S(1)} %collective-permute-done.9.refs_3_, ...), custom_call_target="tpu_custom_call" | custom-call | flops 3355443200 | bytes 524288 | tf_op jit(solution)/shard_map/precondition/pallas_call | solution.py:222
  26.6 0.0 collective-permute-done.10.refs_1_
  26.6 2.4 %score.1 = f32[512,128]{1,0:T(8,128)} custom-call(f32[128,512]{1,0:T(8,128)S(1)} %precondition.1.moved, bf16[64,4096]{1,0:T(8,128)(2,1)S(1)} %constant_dynamic-update-slice_fusion.4.refs_0_, bf16[64,4096]{1,0:T(8,128)(2,1)S(1)} %collective-permute-done.10.refs_1_), custom_call_target="tpu_custom_call" | custom-call | tf_op jit(solution)/shard_map/score/pallas_call | solution.py:283
  (10 shorter events, 0.1 us)
Async XLA Ops:
  0.0 11.8 %collective-permute-start.1 = (bf16[8,4096]{1,0:T(8,128)(2,1)}, bf16[8,4096]{1,0:T(8,128)(2,1)S(1)}, u32[]{:S(2)}, u32[]{:S(2)}) collective-permute-start(bf16[8,4096]{1,0:T(8,128)(2,1)} %param.9), channel_id=1, source_target_pairs={{0,8},{1,9},{2,10},{3,11},{4,12},{5,13},{6,14},{7,15},{8,0},{9,1},... | collective-permute-start | bytes 196616 | tf_op jit(solution)/shard_map/ppermute | solution.py:323
  4.0 7.8 %collective-permute-start = (bf16[8,4096]{1,0:T(8,128)(2,1)}, bf16[8,4096]{1,0:T(8,128)(2,1)S(1)}, u32[]{:S(2)}, u32[]{:S(2)}) collective-permute-start(bf16[8,4096]{1,0:T(8,128)(2,1)} %param.9), channel_id=1, source_target_pairs={{0,12},{1,13},{2,14},{3,15},{4,8},{5,9},{6,10},{7,11},{8,4},{9,5},... | collective-permute-start | bytes 196616 | tf_op jit(solution)/shard_map/ppermute | solution.py:323
  5.4 6.4 %collective-permute-start.2 = (bf16[8,4096]{1,0:T(8,128)(2,1)}, bf16[8,4096]{1,0:T(8,128)(2,1)S(1)}, u32[]{:S(2)}, u32[]{:S(2)}) collective-permute-start(bf16[8,4096]{1,0:T(8,128)(2,1)} %param.9), channel_id=1, source_target_pairs={{0,4},{1,5},{2,6},{3,7},{4,0},{5,1},{6,2},{7,3},{8,12},{9,13},{10,... | collective-permute-start | bytes 196616 | tf_op jit(solution)/shard_map/ppermute | solution.py:323
  5.6 8.1 %copy-start = (bf16[8,4096]{1,0:T(8,128)(2,1)S(1)}, bf16[8,4096]{1,0:T(8,128)(2,1)}, u32[]{:S(2)}) copy-start(bf16[8,4096]{1,0:T(8,128)(2,1)} %param.9) | copy-start | bytes 196612
  11.8 3.6 %collective-permute-start.6 = (f32[40,128]{1,0:T(8,128)S(1)}, f32[40,128]{1,0:T(8,128)S(1)}, u32[]{:S(2)}, u32[]{:S(2)}) collective-permute-start(f32[40,128]{1,0:T(8,128)S(1)} %get-tuple-element.24), channel_id=1, source_target_pairs={{0,3},{1,2},{2,1},{3,0},{4,7},{5,6},{6,5},{7,4},{8,11},{9,10},{10,... | collective-permute-start | bytes 61448 | tf_op jit(solution)/shard_map/ppermute | solution.py:323
  12.3 3.8 %collective-permute-start.5 = (f32[40,128]{1,0:T(8,128)S(1)}, f32[40,128]{1,0:T(8,128)S(1)}, u32[]{:S(2)}, u32[]{:S(2)}) collective-permute-start(f32[40,128]{1,0:T(8,128)S(1)} %get-tuple-element.24), channel_id=1, source_target_pairs={{0,2},{1,3},{2,0},{3,1},{4,6},{5,7},{6,4},{7,5},{8,10},{9,11},{10,... | collective-permute-start | bytes 61448 | tf_op jit(solution)/shard_map/ppermute | solution.py:323
  13.5 2.6 %collective-permute-start.4 = (f32[40,128]{1,0:T(8,128)S(1)}, f32[40,128]{1,0:T(8,128)S(1)}, u32[]{:S(2)}, u32[]{:S(2)}) collective-permute-start(f32[40,128]{1,0:T(8,128)S(1)} %get-tuple-element.24), channel_id=1, source_target_pairs={{0,1},{1,0},{2,3},{3,2},{4,5},{5,4},{6,7},{7,6},{8,9},{9,8},{10,11... | collective-permute-start | bytes 61448 | tf_op jit(solution)/shard_map/ppermute | solution.py:323
  13.8 9.8 %collective-permute-start.3 = (bf16[32,4096]{1,0:T(8,128)(2,1)S(1)}, bf16[32,4096]{1,0:T(8,128)(2,1)S(1)}, u32[]{:S(2)}, u32[]{:S(2)}) collective-permute-start(bf16[32,4096]{1,0:T(8,128)(2,1)S(1)} %constant_dynamic-update-slice_fusion), channel_id=1, source_target_pairs={{0,2},{1,3},{2,0},{3,1},{4,6},{5,7},{6,4},{7,5},{8,10},{9,11},{10,... | collective-permute-start | bytes 786440 | tf_op jit(solution)/shard_map/ppermute | solution.py:323
  16.1 5.7 %collective-permute-start.9 = (f32[40,128]{1,0:T(8,128)S(1)}, f32[40,128]{1,0:T(8,128)S(1)}, u32[]{:S(2)}, u32[]{:S(2)}) collective-permute-start(f32[40,128]{1,0:T(8,128)S(1)} %add_add_fusion.refs_0_), channel_id=1, source_target_pairs={{0,12},{1,13},{2,14},{3,15},{4,8},{5,9},{6,10},{7,11},{8,4},{9,5},... | collective-permute-start | bytes 61448 | tf_op jit(solution)/shard_map/ppermute | solution.py:323
  18.8 4.8 %collective-permute-start.8 = (f32[40,128]{1,0:T(8,128)S(1)}, f32[40,128]{1,0:T(8,128)S(1)}, u32[]{:S(2)}, u32[]{:S(2)}) collective-permute-start(f32[40,128]{1,0:T(8,128)S(1)} %add_add_fusion.refs_0_), channel_id=1, source_target_pairs={{0,8},{1,9},{2,10},{3,11},{4,12},{5,13},{6,14},{7,15},{8,0},{9,1},... | collective-permute-start | bytes 61448 | tf_op jit(solution)/shard_map/ppermute | solution.py:323
  19.1 4.5 %collective-permute-start.7 = (f32[40,128]{1,0:T(8,128)S(1)}, f32[40,128]{1,0:T(8,128)S(1)}, u32[]{:S(2)}, u32[]{:S(2)}) collective-permute-start(f32[40,128]{1,0:T(8,128)S(1)} %add_add_fusion.refs_0_), channel_id=1, source_target_pairs={{0,4},{1,5},{2,6},{3,7},{4,0},{5,1},{6,2},{7,3},{8,12},{9,13},{10,... | collective-permute-start | bytes 61448 | tf_op jit(solution)/shard_map/ppermute | solution.py:323
  23.7 2.9 %collective-permute-start.10 = (bf16[64,4096]{1,0:T(8,128)(2,1)S(1)}, bf16[64,4096]{1,0:T(8,128)(2,1)S(1)}, u32[]{:S(2)}, u32[]{:S(2)}) collective-permute-start(bf16[64,4096]{1,0:T(8,128)(2,1)S(1)} %constant_dynamic-update-slice_fusion.4.refs_0_), channel_id=1, source_target_pairs={{0,1},{1,0},{2,3},{3,2},{4,5},{5,4},{6,7},{7,6},{8,9},{9,8},{10,11... | collective-permute-start | bytes 1572872 | tf_op jit(solution)/shard_map/ppermute | solution.py:323

commit v17 on v16

--- a/solution.py
+++ b/solution.py
@@ -10,7 +10,7 @@
 DAMP = 0.1
 HIGHEST = lax.Precision.HIGHEST
 COPY_ROWS = 128
-IN_FLIGHT = 6
+IN_FLIGHT = 5
 TOKENS_AT_ONCE = 256
 
 
@@ -75,8 +75,6 @@
 
     steps = [(at, part, min(2, n_parts - part)) for at in range(2) for part in range(0, n_parts, 2)]
     last_act = len(steps) // 2 - 1
-    at, part, many = steps.pop()
-    steps += [(at, part + one, 1) for one in range(many)]
     blocks = [[], []]
     grams = [[], []]
 
@@ -169,22 +167,22 @@
             jnp.where(on_block, jnp.where(inner == k + a, 1.0, 0.0), row(parts[home], off + a)) for a in range(4)
         ]
         scale = 1.0 / (p00 * p11 - p01 * p01)
-        e02 = scale * (p11 * p02 - p01 * p12)
-        e03 = scale * (p11 * p03 - p01 * p13)
-        e12 = scale * (p00 * p12 - p01 * p02)
-        e13 = scale * (p00 * p13 - p01 * p03)
-        s22 = p22 - (p02 * e02 + p12 * e12)
-        s23 = p23 - (p02 * e03 + p12 * e13)
-        s33 = p33 - (p03 * e03 + p13 * e13)
+        m02 = p11 * p02 - p01 * p12
+        m03 = p11 * p03 - p01 * p13
+        m12 = p00 * p12 - p01 * p02
+        m13 = p00 * p13 - p01 * p03
+        z0 = p11 * r0 - p01 * r1
+        z1 = p00 * r1 - p01 * r0
+        s22 = p22 - scale * (p02 * m02 + p12 * m12)
+        s23 = p23 - scale * (p02 * m03 + p12 * m13)
+        s33 = p33 - scale * (p03 * m03 + p13 * m13)
+        t2 = r2 - scale * (p02 * z0 + p12 * z1)
+        t3 = r3 - scale * (p03 * z0 + p13 * z1)
         scale_s = 1.0 / (s22 * s33 - s23 * s23)
-        y0 = scale * (p11 * r0 - p01 * r1)
-        y1 = scale * (p00 * r1 - p01 * r0)
-        t2 = r2 - (p02 * y0 + p12 * y1)
-        t3 = r3 - (p03 * y0 + p13 * y1)
         w2 = scale_s * (s33 * t2 - s23 * t3)
         w3 = scale_s * (s22 * t3 - s23 * t2)
-        w0 = y0 - (e02 * w2 + e03 * w3)
-        w1 = y1 - (e12 * w2 + e13 * w3)
+        w0 = scale * (z0 - (m02 * w2 + m03 * w3))
+        w1 = scale * (z1 - (m12 * w2 + m13 * w3))
         solved = (w0, w1, w2, w3)
         for m, part in enumerate(parts):
             change = (columns[0][m] * w0 + columns[1][m] * w1) + (columns[2][m] * w2 + columns[3][m] * w3)

time: 29.2 us -> 28.6 us (0.979)
  Pallas kernels: 11.4 us -> 10.8 us
    pallas_call x1, Pallas kernels: 6.16 us -> 5.66 us  [project(): pl.pallas_call(project_kernel, out_shape=(jax.ShapeDtypeStruct((factor, t...]
  transfers between devices with their start and end apart: 11 -> 11, of which waited for: 3 -> 3; matrix products, arithmetic and copies ran while one was open for 0% -> 0% of each run, Pallas kernels for 31% -> 30%
where the time goes in v17:
time: 28.6 us; the launch traced here: 28.4 us
  starting transfers between devices  13.6 us (48%)
  Pallas kernels  10.8 us (38%)
  waiting for transfers between devices  3.75 us (13%)
    ppermute x11, starting transfers between devices, swapped(): return lax.ppermute(value, 'dp', perm)  13.6 us
    pallas_call x1, Pallas kernels, project(): pl.pallas_call(project_kernel, out_shape=(jax.ShapeDtypeStruct((factor, t...  5.66 us
    ppermute x11, waiting for transfers between devices, swapped(): return lax.ppermute(value, 'dp', perm)  3.75 us
    pallas_call x1, Pallas kernels, precondition(): pl.pallas_call(functools.partial(precondition_kernel, tok_total, n_terms)...  2.77 us
    pallas_call x1, Pallas kernels, score(): pl.pallas_call(functools.partial(score_kernel, size, n_pieces), out_shape...  2.39 us
  transfers between devices with their start and end apart: 11, of which 3 were waited for; matrix products, arithmetic and copies ran while one was open for 0% of the time, Pallas kernels for 30%

profile of v17, /device:TPU:0, one launch (start us, length us, event | category | flops | bytes accessed | tf_op | source)
XLA Modules:
  0.0 28.4 jit_solution(14962051752733802267)
XLA Ops:
  0.0 4.0 %collective-permute-start.1 = (bf16[8,4096]{1,0:T(8,128)(2,1)}, bf16[8,4096]{1,0:T(8,128)(2,1)S(1)}, u32[]{:S(2)}, u32[]{:S(2)}) collective-permute-start(bf16[8,4096]{1,0:T(8,128)(2,1)} %param.9), channel_id=1, source_target_pairs={{0,8},{1,9},{2,10},{3,11},{4,12},{5,13},{6,14},{7,15},{8,0},{9,1},... | collective-permute-start | bytes 196616 | tf_op jit(solution)/shard_map/ppermute | solution.py:321
  4.0 1.3 %collective-permute-start = (bf16[8,4096]{1,0:T(8,128)(2,1)}, bf16[8,4096]{1,0:T(8,128)(2,1)S(1)}, u32[]{:S(2)}, u32[]{:S(2)}) collective-permute-start(bf16[8,4096]{1,0:T(8,128)(2,1)} %param.9), channel_id=1, source_target_pairs={{0,12},{1,13},{2,14},{3,15},{4,8},{5,9},{6,10},{7,11},{8,4},{9,5},... | collective-permute-start | bytes 196616 | tf_op jit(solution)/shard_map/ppermute | solution.py:321
  5.4 0.2 collective-permute-start.2
  5.6 5.7 %project.1 = (f32[64,512]{1,0:T(8,128)S(1)}, f32[64,512]{1,0:T(8,128)S(1)}, f32[40,128]{1,0:T(8,128)S(1)}) custom-call(bf16[512,4096]{1,0:T(8,128)(2,1)} %acts.1, bf16[512,4096]{1,0:T(8,128)(2,1)} %grads.1, bf16[64,4096]{1,0:T(8,128)(2,1)} %bitcast.2, bf16[64,4096]{1,0:T(8,128)(2,1)} %bitcast.3), custom_call_target="tpu_custom_call" | custom-call | flops 536870912 | bytes 8388608 | tf_op jit(solution)/shard_map/project/pallas_call | solution.py:117
  11.3 0.0 collective-permute-done.1
  11.3 0.0 collective-permute-done
  11.3 0.0 collective-permute-done.2
  11.3 0.5 %collective-permute-start.6 = (f32[40,128]{1,0:T(8,128)S(1)}, f32[40,128]{1,0:T(8,128)S(1)}, u32[]{:S(2)}, u32[]{:S(2)}) collective-permute-start(f32[40,128]{1,0:T(8,128)S(1)} %get-tuple-element.24), channel_id=1, source_target_pairs={{0,3},{1,2},{2,1},{3,0},{4,7},{5,6},{6,5},{7,4},{8,11},{9,10},{10,... | collective-permute-start | bytes 61448 | tf_op jit(solution)/shard_map/ppermute | solution.py:321
  11.8 1.2 %collective-permute-start.5 = (f32[40,128]{1,0:T(8,128)S(1)}, f32[40,128]{1,0:T(8,128)S(1)}, u32[]{:S(2)}, u32[]{:S(2)}) collective-permute-start(f32[40,128]{1,0:T(8,128)S(1)} %get-tuple-element.24), channel_id=1, source_target_pairs={{0,2},{1,3},{2,0},{3,1},{4,6},{5,7},{6,4},{7,5},{8,10},{9,11},{10,... | collective-permute-start | bytes 61448 | tf_op jit(solution)/shard_map/ppermute | solution.py:321
  13.0 0.3 collective-permute-start.4
  13.3 1.6 %collective-permute-start.3 = (bf16[32,4096]{1,0:T(8,128)(2,1)S(1)}, bf16[32,4096]{1,0:T(8,128)(2,1)S(1)}, u32[]{:S(2)}, u32[]{:S(2)}) collective-permute-start(bf16[32,4096]{1,0:T(8,128)(2,1)S(1)} %constant_dynamic-update-slice_fusion), channel_id=1, source_target_pairs={{0,2},{1,3},{2,0},{3,1},{4,6},{5,7},{6,4},{7,5},{8,10},{9,11},{10,... | collective-permute-start | bytes 786440 | tf_op jit(solution)/shard_map/ppermute | solution.py:321
  14.9 0.0 collective-permute-done.6
  14.9 0.7 %collective-permute-done.5 = f32[40,128]{1,0:T(8,128)S(1)} collective-permute-done((f32[40,128]{1,0:T(8,128)S(1)}, f32[40,128]{1,0:T(8,128)S(1)}, u32[]{:S(2)}, u32[]{:S(2)}) %collective-permute-start.5) | collective-permute-done | bytes 20512 | tf_op jit(solution)/shard_map/ppermute | solution.py:321
  15.6 0.0 collective-permute-done.4
  15.6 2.7 %collective-permute-start.9 = (f32[40,128]{1,0:T(8,128)S(1)}, f32[40,128]{1,0:T(8,128)S(1)}, u32[]{:S(2)}, u32[]{:S(2)}) collective-permute-start(f32[40,128]{1,0:T(8,128)S(1)} %add_add_fusion.refs_0_), channel_id=1, source_target_pairs={{0,12},{1,13},{2,14},{3,15},{4,8},{5,9},{6,10},{7,11},{8,4},{9,5},... | collective-permute-start | bytes 61448 | tf_op jit(solution)/shard_map/ppermute | solution.py:321
  18.3 0.3 %collective-permute-start.8 = (f32[40,128]{1,0:T(8,128)S(1)}, f32[40,128]{1,0:T(8,128)S(1)}, u32[]{:S(2)}, u32[]{:S(2)}) collective-permute-start(f32[40,128]{1,0:T(8,128)S(1)} %add_add_fusion.refs_0_), channel_id=1, source_target_pairs={{0,8},{1,9},{2,10},{3,11},{4,12},{5,13},{6,14},{7,15},{8,0},{9,1},... | collective-permute-start | bytes 61448 | tf_op jit(solution)/shard_map/ppermute | solution.py:321
  18.6 1.4 %collective-permute-start.7 = (f32[40,128]{1,0:T(8,128)S(1)}, f32[40,128]{1,0:T(8,128)S(1)}, u32[]{:S(2)}, u32[]{:S(2)}) collective-permute-start(f32[40,128]{1,0:T(8,128)S(1)} %add_add_fusion.refs_0_), channel_id=1, source_target_pairs={{0,4},{1,5},{2,6},{3,7},{4,0},{5,1},{6,2},{7,3},{8,12},{9,13},{10,... | collective-permute-start | bytes 61448 | tf_op jit(solution)/shard_map/ppermute | solution.py:321
  20.0 1.2 %collective-permute-done.9.refs_3_ = f32[40,128]{1,0:T(8,128)S(1)} collective-permute-done((f32[40,128]{1,0:T(8,128)S(1)}, f32[40,128]{1,0:T(8,128)S(1)}, u32[]{:S(2)}, u32[]{:S(2)}) %collective-permute-start.9) | collective-permute-done | bytes 20512 | tf_op jit(solution)/shard_map/ppermute | solution.py:321
  21.3 1.8 %collective-permute-done.8.refs_2_ = f32[40,128]{1,0:T(8,128)S(1)} collective-permute-done((f32[40,128]{1,0:T(8,128)S(1)}, f32[40,128]{1,0:T(8,128)S(1)}, u32[]{:S(2)}, u32[]{:S(2)}) %collective-permute-start.8) | collective-permute-done | bytes 20512 | tf_op jit(solution)/shard_map/ppermute | solution.py:321
  23.1 0.0 collective-permute-done.7.refs_1_
  23.1 0.0 collective-permute-done.3
  23.1 0.1 collective-permute-start.10
  23.2 2.8 %precondition.1.moved = f32[128,512]{1,0:T(8,128)S(1)} custom-call(f32[40,128]{1,0:T(8,128)S(1)} %add_add_fusion.refs_0_, f32[40,128]{1,0:T(8,128)S(1)} %collective-permute-done.7.refs_1_, f32[40,128]{1,0:T(8,128)S(1)} %collective-permute-done.8.refs_2_, f32[40,128]{1,0:T(8,128)S(1)} %collective-permute-done.9.refs_3_, ...), custom_call_target="tpu_custom_call" | custom-call | flops 3355443200 | bytes 524288 | tf_op jit(solution)/shard_map/precondition/pallas_call | solution.py:220
  26.0 2.4 %score.1 = f32[512,128]{1,0:T(8,128)} custom-call(f32[128,512]{1,0:T(8,128)S(1)} %precondition.1.moved, bf16[64,4096]{1,0:T(8,128)(2,1)S(1)} %constant_dynamic-update-slice_fusion.4.refs_0_, bf16[64,4096]{1,0:T(8,128)(2,1)S(1)} %collective-permute-done.10.refs_1_), custom_call_target="tpu_custom_call" | custom-call | tf_op jit(solution)/shard_map/score/pallas_call | solution.py:281
  (10 shorter events, 0.1 us)
Async XLA Ops:
  0.0 11.3 %collective-permute-start.1 = (bf16[8,4096]{1,0:T(8,128)(2,1)}, bf16[8,4096]{1,0:T(8,128)(2,1)S(1)}, u32[]{:S(2)}, u32[]{:S(2)}) collective-permute-start(bf16[8,4096]{1,0:T(8,128)(2,1)} %param.9), channel_id=1, source_target_pairs={{0,8},{1,9},{2,10},{3,11},{4,12},{5,13},{6,14},{7,15},{8,0},{9,1},... | collective-permute-start | bytes 196616 | tf_op jit(solution)/shard_map/ppermute | solution.py:321
  4.0 7.3 %collective-permute-start = (bf16[8,4096]{1,0:T(8,128)(2,1)}, bf16[8,4096]{1,0:T(8,128)(2,1)S(1)}, u32[]{:S(2)}, u32[]{:S(2)}) collective-permute-start(bf16[8,4096]{1,0:T(8,128)(2,1)} %param.9), channel_id=1, source_target_pairs={{0,12},{1,13},{2,14},{3,15},{4,8},{5,9},{6,10},{7,11},{8,4},{9,5},... | collective-permute-start | bytes 196616 | tf_op jit(solution)/shard_map/ppermute | solution.py:321
  5.4 5.9 %collective-permute-start.2 = (bf16[8,4096]{1,0:T(8,128)(2,1)}, bf16[8,4096]{1,0:T(8,128)(2,1)S(1)}, u32[]{:S(2)}, u32[]{:S(2)}) collective-permute-start(bf16[8,4096]{1,0:T(8,128)(2,1)} %param.9), channel_id=1, source_target_pairs={{0,4},{1,5},{2,6},{3,7},{4,0},{5,1},{6,2},{7,3},{8,12},{9,13},{10,... | collective-permute-start | bytes 196616 | tf_op jit(solution)/shard_map/ppermute | solution.py:321
  5.6 7.6 %copy-start = (bf16[8,4096]{1,0:T(8,128)(2,1)S(1)}, bf16[8,4096]{1,0:T(8,128)(2,1)}, u32[]{:S(2)}) copy-start(bf16[8,4096]{1,0:T(8,128)(2,1)} %param.9) | copy-start | bytes 196612
  11.3 3.6 %collective-permute-start.6 = (f32[40,128]{1,0:T(8,128)S(1)}, f32[40,128]{1,0:T(8,128)S(1)}, u32[]{:S(2)}, u32[]{:S(2)}) collective-permute-start(f32[40,128]{1,0:T(8,128)S(1)} %get-tuple-element.24), channel_id=1, source_target_pairs={{0,3},{1,2},{2,1},{3,0},{4,7},{5,6},{6,5},{7,4},{8,11},{9,10},{10,... | collective-permute-start | bytes 61448 | tf_op jit(solution)/shard_map/ppermute | solution.py:321
  11.8 3.8 %collective-permute-start.5 = (f32[40,128]{1,0:T(8,128)S(1)}, f32[40,128]{1,0:T(8,128)S(1)}, u32[]{:S(2)}, u32[]{:S(2)}) collective-permute-start(f32[40,128]{1,0:T(8,128)S(1)} %get-tuple-element.24), channel_id=1, source_target_pairs={{0,2},{1,3},{2,0},{3,1},{4,6},{5,7},{6,4},{7,5},{8,10},{9,11},{10,... | collective-permute-start | bytes 61448 | tf_op jit(solution)/shard_map/ppermute | solution.py:321
  13.0 2.6 %collective-permute-start.4 = (f32[40,128]{1,0:T(8,128)S(1)}, f32[40,128]{1,0:T(8,128)S(1)}, u32[]{:S(2)}, u32[]{:S(2)}) collective-permute-start(f32[40,128]{1,0:T(8,128)S(1)} %get-tuple-element.24), channel_id=1, source_target_pairs={{0,1},{1,0},{2,3},{3,2},{4,5},{5,4},{6,7},{7,6},{8,9},{9,8},{10,11... | collective-permute-start | bytes 61448 | tf_op jit(solution)/shard_map/ppermute | solution.py:321
  13.3 9.8 %collective-permute-start.3 = (bf16[32,4096]{1,0:T(8,128)(2,1)S(1)}, bf16[32,4096]{1,0:T(8,128)(2,1)S(1)}, u32[]{:S(2)}, u32[]{:S(2)}) collective-permute-start(bf16[32,4096]{1,0:T(8,128)(2,1)S(1)} %constant_dynamic-update-slice_fusion), channel_id=1, source_target_pairs={{0,2},{1,3},{2,0},{3,1},{4,6},{5,7},{6,4},{7,5},{8,10},{9,11},{10,... | collective-permute-start | bytes 786440 | tf_op jit(solution)/shard_map/ppermute | solution.py:321
  15.6 5.7 %collective-permute-start.9 = (f32[40,128]{1,0:T(8,128)S(1)}, f32[40,128]{1,0:T(8,128)S(1)}, u32[]{:S(2)}, u32[]{:S(2)}) collective-permute-start(f32[40,128]{1,0:T(8,128)S(1)} %add_add_fusion.refs_0_), channel_id=1, source_target_pairs={{0,12},{1,13},{2,14},{3,15},{4,8},{5,9},{6,10},{7,11},{8,4},{9,5},... | collective-permute-start | bytes 61448 | tf_op jit(solution)/shard_map/ppermute | solution.py:321
  18.3 4.8 %collective-permute-start.8 = (f32[40,128]{1,0:T(8,128)S(1)}, f32[40,128]{1,0:T(8,128)S(1)}, u32[]{:S(2)}, u32[]{:S(2)}) collective-permute-start(f32[40,128]{1,0:T(8,128)S(1)} %add_add_fusion.refs_0_), channel_id=1, source_target_pairs={{0,8},{1,9},{2,10},{3,11},{4,12},{5,13},{6,14},{7,15},{8,0},{9,1},... | collective-permute-start | bytes 61448 | tf_op jit(solution)/shard_map/ppermute | solution.py:321
  18.6 4.5 %collective-permute-start.7 = (f32[40,128]{1,0:T(8,128)S(1)}, f32[40,128]{1,0:T(8,128)S(1)}, u32[]{:S(2)}, u32[]{:S(2)}) collective-permute-start(f32[40,128]{1,0:T(8,128)S(1)} %add_add_fusion.refs_0_), channel_id=1, source_target_pairs={{0,4},{1,5},{2,6},{3,7},{4,0},{5,1},{6,2},{7,3},{8,12},{9,13},{10,... | collective-permute-start | bytes 61448 | tf_op jit(solution)/shard_map/ppermute | solution.py:321
  23.1 2.9 %collective-permute-start.10 = (bf16[64,4096]{1,0:T(8,128)(2,1)S(1)}, bf16[64,4096]{1,0:T(8,128)(2,1)S(1)}, u32[]{:S(2)}, u32[]{:S(2)}) collective-permute-start(bf16[64,4096]{1,0:T(8,128)(2,1)S(1)} %constant_dynamic-update-slice_fusion.4.refs_0_), channel_id=1, source_target_pairs={{0,1},{1,0},{2,3},{3,2},{4,5},{5,4},{6,7},{7,6},{8,9},{9,8},{10,11... | collective-permute-start | bytes 1572872 | tf_op jit(solution)/shard_map/ppermute | solution.py:321

commit v18 on v17

--- a/solution.py
+++ b/solution.py
@@ -70,8 +70,7 @@
 
     def turned(at):
         for first in range(0, width, 512):
-            block = weight_buf[at, :, first : first + 512].astype(jnp.float32)
-            weight_t[at, first : first + 512, :] = block.T.astype(weight_t.dtype)
+            weight_t[at, first : first + 512, :] = weight_buf[at, :, first : first + 512].T
 
     steps = [(at, part, min(2, n_parts - part)) for at in range(2) for part in range(0, n_parts, 2)]
     last_act = len(steps) // 2 - 1

time: 28.6 us -> 28.6 us (level)
  no operation moved by 1% of the time
where the time goes in v18:
time: 28.6 us; the launch traced here: 28.4 us
  starting transfers between devices  13.6 us (48%)
  Pallas kernels  10.8 us (38%)
  waiting for transfers between devices  3.76 us (13%)
    ppermute x11, starting transfers between devices, swapped(): return lax.ppermute(value, 'dp', perm)  13.6 us
    pallas_call x1, Pallas kernels, project(): pl.pallas_call(project_kernel, out_shape=(jax.ShapeDtypeStruct((factor, t...  5.67 us
    ppermute x11, waiting for transfers between devices, swapped(): return lax.ppermute(value, 'dp', perm)  3.76 us
    pallas_call x1, Pallas kernels, precondition(): pl.pallas_call(functools.partial(precondition_kernel, tok_total, n_terms)...  2.78 us
    pallas_call x1, Pallas kernels, score(): pl.pallas_call(functools.partial(score_kernel, size, n_pieces), out_shape...  2.4 us
  transfers between devices with their start and end apart: 11, of which 3 were waited for; matrix products, arithmetic and copies ran while one was open for 0% of the time, Pallas kernels for 30%

profile of v18, /device:TPU:0, one launch (start us, length us, event | category | flops | bytes accessed | tf_op | source)
XLA Modules:
  0.0 28.4 jit_solution(13638394721945259988)
XLA Ops:
  0.0 4.0 %collective-permute-start.1 = (bf16[8,4096]{1,0:T(8,128)(2,1)}, bf16[8,4096]{1,0:T(8,128)(2,1)S(1)}, u32[]{:S(2)}, u32[]{:S(2)}) collective-permute-start(bf16[8,4096]{1,0:T(8,128)(2,1)} %param.9), channel_id=1, source_target_pairs={{0,8},{1,9},{2,10},{3,11},{4,12},{5,13},{6,14},{7,15},{8,0},{9,1},... | collective-permute-start | bytes 196616 | tf_op jit(solution)/shard_map/ppermute | solution.py:320
  4.0 1.3 %collective-permute-start = (bf16[8,4096]{1,0:T(8,128)(2,1)}, bf16[8,4096]{1,0:T(8,128)(2,1)S(1)}, u32[]{:S(2)}, u32[]{:S(2)}) collective-permute-start(bf16[8,4096]{1,0:T(8,128)(2,1)} %param.9), channel_id=1, source_target_pairs={{0,12},{1,13},{2,14},{3,15},{4,8},{5,9},{6,10},{7,11},{8,4},{9,5},... | collective-permute-start | bytes 196616 | tf_op jit(solution)/shard_map/ppermute | solution.py:320
  5.4 0.2 collective-permute-start.2
  5.6 5.7 %project.1 = (f32[64,512]{1,0:T(8,128)S(1)}, f32[64,512]{1,0:T(8,128)S(1)}, f32[40,128]{1,0:T(8,128)S(1)}) custom-call(bf16[512,4096]{1,0:T(8,128)(2,1)} %acts.1, bf16[512,4096]{1,0:T(8,128)(2,1)} %grads.1, bf16[64,4096]{1,0:T(8,128)(2,1)} %bitcast.2, bf16[64,4096]{1,0:T(8,128)(2,1)} %bitcast.3), custom_call_target="tpu_custom_call" | custom-call | flops 536870912 | bytes 8388608 | tf_op jit(solution)/shard_map/project/pallas_call | solution.py:116
  11.3 0.0 collective-permute-done.1
  11.3 0.0 collective-permute-done
  11.3 0.0 collective-permute-done.2
  11.3 0.5 %collective-permute-start.6 = (f32[40,128]{1,0:T(8,128)S(1)}, f32[40,128]{1,0:T(8,128)S(1)}, u32[]{:S(2)}, u32[]{:S(2)}) collective-permute-start(f32[40,128]{1,0:T(8,128)S(1)} %get-tuple-element.24), channel_id=1, source_target_pairs={{0,3},{1,2},{2,1},{3,0},{4,7},{5,6},{6,5},{7,4},{8,11},{9,10},{10,... | collective-permute-start | bytes 61448 | tf_op jit(solution)/shard_map/ppermute | solution.py:320
  11.8 1.2 %collective-permute-start.5 = (f32[40,128]{1,0:T(8,128)S(1)}, f32[40,128]{1,0:T(8,128)S(1)}, u32[]{:S(2)}, u32[]{:S(2)}) collective-permute-start(f32[40,128]{1,0:T(8,128)S(1)} %get-tuple-element.24), channel_id=1, source_target_pairs={{0,2},{1,3},{2,0},{3,1},{4,6},{5,7},{6,4},{7,5},{8,10},{9,11},{10,... | collective-permute-start | bytes 61448 | tf_op jit(solution)/shard_map/ppermute | solution.py:320
  13.0 0.3 collective-permute-start.4
  13.3 1.6 %collective-permute-start.3 = (bf16[32,4096]{1,0:T(8,128)(2,1)S(1)}, bf16[32,4096]{1,0:T(8,128)(2,1)S(1)}, u32[]{:S(2)}, u32[]{:S(2)}) collective-permute-start(bf16[32,4096]{1,0:T(8,128)(2,1)S(1)} %constant_dynamic-update-slice_fusion), channel_id=1, source_target_pairs={{0,2},{1,3},{2,0},{3,1},{4,6},{5,7},{6,4},{7,5},{8,10},{9,11},{10,... | collective-permute-start | bytes 786440 | tf_op jit(solution)/shard_map/ppermute | solution.py:320
  14.9 0.0 collective-permute-done.6
  14.9 0.7 %collective-permute-done.5 = f32[40,128]{1,0:T(8,128)S(1)} collective-permute-done((f32[40,128]{1,0:T(8,128)S(1)}, f32[40,128]{1,0:T(8,128)S(1)}, u32[]{:S(2)}, u32[]{:S(2)}) %collective-permute-start.5) | collective-permute-done | bytes 20512 | tf_op jit(solution)/shard_map/ppermute | solution.py:320
  15.6 0.0 collective-permute-done.4
  15.6 2.7 %collective-permute-start.9 = (f32[40,128]{1,0:T(8,128)S(1)}, f32[40,128]{1,0:T(8,128)S(1)}, u32[]{:S(2)}, u32[]{:S(2)}) collective-permute-start(f32[40,128]{1,0:T(8,128)S(1)} %add_add_fusion.refs_0_), channel_id=1, source_target_pairs={{0,12},{1,13},{2,14},{3,15},{4,8},{5,9},{6,10},{7,11},{8,4},{9,5},... | collective-permute-start | bytes 61448 | tf_op jit(solution)/shard_map/ppermute | solution.py:320
  18.3 0.3 %collective-permute-start.8 = (f32[40,128]{1,0:T(8,128)S(1)}, f32[40,128]{1,0:T(8,128)S(1)}, u32[]{:S(2)}, u32[]{:S(2)}) collective-permute-start(f32[40,128]{1,0:T(8,128)S(1)} %add_add_fusion.refs_0_), channel_id=1, source_target_pairs={{0,8},{1,9},{2,10},{3,11},{4,12},{5,13},{6,14},{7,15},{8,0},{9,1},... | collective-permute-start | bytes 61448 | tf_op jit(solution)/shard_map/ppermute | solution.py:320
  18.7 1.4 %collective-permute-start.7 = (f32[40,128]{1,0:T(8,128)S(1)}, f32[40,128]{1,0:T(8,128)S(1)}, u32[]{:S(2)}, u32[]{:S(2)}) collective-permute-start(f32[40,128]{1,0:T(8,128)S(1)} %add_add_fusion.refs_0_), channel_id=1, source_target_pairs={{0,4},{1,5},{2,6},{3,7},{4,0},{5,1},{6,2},{7,3},{8,12},{9,13},{10,... | collective-permute-start | bytes 61448 | tf_op jit(solution)/shard_map/ppermute | solution.py:320
  20.0 1.2 %collective-permute-done.9.refs_3_ = f32[40,128]{1,0:T(8,128)S(1)} collective-permute-done((f32[40,128]{1,0:T(8,128)S(1)}, f32[40,128]{1,0:T(8,128)S(1)}, u32[]{:S(2)}, u32[]{:S(2)}) %collective-permute-start.9) | collective-permute-done | bytes 20512 | tf_op jit(solution)/shard_map/ppermute | solution.py:320
  21.2 1.9 %collective-permute-done.8.refs_2_ = f32[40,128]{1,0:T(8,128)S(1)} collective-permute-done((f32[40,128]{1,0:T(8,128)S(1)}, f32[40,128]{1,0:T(8,128)S(1)}, u32[]{:S(2)}, u32[]{:S(2)}) %collective-permute-start.8) | collective-permute-done | bytes 20512 | tf_op jit(solution)/shard_map/ppermute | solution.py:320
  23.1 0.0 collective-permute-done.7.refs_1_
  23.2 0.1 collective-permute-start.10
  23.2 2.8 %precondition.1.moved = f32[128,512]{1,0:T(8,128)S(1)} custom-call(f32[40,128]{1,0:T(8,128)S(1)} %add_add_fusion.refs_0_, f32[40,128]{1,0:T(8,128)S(1)} %collective-permute-done.7.refs_1_, f32[40,128]{1,0:T(8,128)S(1)} %collective-permute-done.8.refs_2_, f32[40,128]{1,0:T(8,128)S(1)} %collective-permute-done.9.refs_3_, ...), custom_call_target="tpu_custom_call" | custom-call | flops 3355443200 | bytes 524288 | tf_op jit(solution)/shard_map/precondition/pallas_call | solution.py:219
  26.0 0.0 collective-permute-done.10.refs_1_
  26.0 2.4 %score.1 = f32[512,128]{1,0:T(8,128)} custom-call(f32[128,512]{1,0:T(8,128)S(1)} %precondition.1.moved, bf16[64,4096]{1,0:T(8,128)(2,1)S(1)} %constant_dynamic-update-slice_fusion.4.refs_0_, bf16[64,4096]{1,0:T(8,128)(2,1)S(1)} %collective-permute-done.10.refs_1_), custom_call_target="tpu_custom_call" | custom-call | tf_op jit(solution)/shard_map/score/pallas_call | solution.py:280
  (10 shorter events, 0.1 us)
Async XLA Ops:
  0.0 11.3 %collective-permute-start.1 = (bf16[8,4096]{1,0:T(8,128)(2,1)}, bf16[8,4096]{1,0:T(8,128)(2,1)S(1)}, u32[]{:S(2)}, u32[]{:S(2)}) collective-permute-start(bf16[8,4096]{1,0:T(8,128)(2,1)} %param.9), channel_id=1, source_target_pairs={{0,8},{1,9},{2,10},{3,11},{4,12},{5,13},{6,14},{7,15},{8,0},{9,1},... | collective-permute-start | bytes 196616 | tf_op jit(solution)/shard_map/ppermute | solution.py:320
  4.0 7.3 %collective-permute-start = (bf16[8,4096]{1,0:T(8,128)(2,1)}, bf16[8,4096]{1,0:T(8,128)(2,1)S(1)}, u32[]{:S(2)}, u32[]{:S(2)}) collective-permute-start(bf16[8,4096]{1,0:T(8,128)(2,1)} %param.9), channel_id=1, source_target_pairs={{0,12},{1,13},{2,14},{3,15},{4,8},{5,9},{6,10},{7,11},{8,4},{9,5},... | collective-permute-start | bytes 196616 | tf_op jit(solution)/shard_map/ppermute | solution.py:320
  5.4 5.9 %collective-permute-start.2 = (bf16[8,4096]{1,0:T(8,128)(2,1)}, bf16[8,4096]{1,0:T(8,128)(2,1)S(1)}, u32[]{:S(2)}, u32[]{:S(2)}) collective-permute-start(bf16[8,4096]{1,0:T(8,128)(2,1)} %param.9), channel_id=1, source_target_pairs={{0,4},{1,5},{2,6},{3,7},{4,0},{5,1},{6,2},{7,3},{8,12},{9,13},{10,... | collective-permute-start | bytes 196616 | tf_op jit(solution)/shard_map/ppermute | solution.py:320
  5.6 7.6 %copy-start = (bf16[8,4096]{1,0:T(8,128)(2,1)S(1)}, bf16[8,4096]{1,0:T(8,128)(2,1)}, u32[]{:S(2)}) copy-start(bf16[8,4096]{1,0:T(8,128)(2,1)} %param.9) | copy-start | bytes 196612
  11.3 3.6 %collective-permute-start.6 = (f32[40,128]{1,0:T(8,128)S(1)}, f32[40,128]{1,0:T(8,128)S(1)}, u32[]{:S(2)}, u32[]{:S(2)}) collective-permute-start(f32[40,128]{1,0:T(8,128)S(1)} %get-tuple-element.24), channel_id=1, source_target_pairs={{0,3},{1,2},{2,1},{3,0},{4,7},{5,6},{6,5},{7,4},{8,11},{9,10},{10,... | collective-permute-start | bytes 61448 | tf_op jit(solution)/shard_map/ppermute | solution.py:320
  11.8 3.8 %collective-permute-start.5 = (f32[40,128]{1,0:T(8,128)S(1)}, f32[40,128]{1,0:T(8,128)S(1)}, u32[]{:S(2)}, u32[]{:S(2)}) collective-permute-start(f32[40,128]{1,0:T(8,128)S(1)} %get-tuple-element.24), channel_id=1, source_target_pairs={{0,2},{1,3},{2,0},{3,1},{4,6},{5,7},{6,4},{7,5},{8,10},{9,11},{10,... | collective-permute-start | bytes 61448 | tf_op jit(solution)/shard_map/ppermute | solution.py:320
  13.0 2.6 %collective-permute-start.4 = (f32[40,128]{1,0:T(8,128)S(1)}, f32[40,128]{1,0:T(8,128)S(1)}, u32[]{:S(2)}, u32[]{:S(2)}) collective-permute-start(f32[40,128]{1,0:T(8,128)S(1)} %get-tuple-element.24), channel_id=1, source_target_pairs={{0,1},{1,0},{2,3},{3,2},{4,5},{5,4},{6,7},{7,6},{8,9},{9,8},{10,11... | collective-permute-start | bytes 61448 | tf_op jit(solution)/shard_map/ppermute | solution.py:320
  13.3 9.8 %collective-permute-start.3 = (bf16[32,4096]{1,0:T(8,128)(2,1)S(1)}, bf16[32,4096]{1,0:T(8,128)(2,1)S(1)}, u32[]{:S(2)}, u32[]{:S(2)}) collective-permute-start(bf16[32,4096]{1,0:T(8,128)(2,1)S(1)} %constant_dynamic-update-slice_fusion), channel_id=1, source_target_pairs={{0,2},{1,3},{2,0},{3,1},{4,6},{5,7},{6,4},{7,5},{8,10},{9,11},{10,... | collective-permute-start | bytes 786440 | tf_op jit(solution)/shard_map/ppermute | solution.py:320
  15.6 5.7 %collective-permute-start.9 = (f32[40,128]{1,0:T(8,128)S(1)}, f32[40,128]{1,0:T(8,128)S(1)}, u32[]{:S(2)}, u32[]{:S(2)}) collective-permute-start(f32[40,128]{1,0:T(8,128)S(1)} %add_add_fusion.refs_0_), channel_id=1, source_target_pairs={{0,12},{1,13},{2,14},{3,15},{4,8},{5,9},{6,10},{7,11},{8,4},{9,5},... | collective-permute-start | bytes 61448 | tf_op jit(solution)/shard_map/ppermute | solution.py:320
  18.3 4.8 %collective-permute-start.8 = (f32[40,128]{1,0:T(8,128)S(1)}, f32[40,128]{1,0:T(8,128)S(1)}, u32[]{:S(2)}, u32[]{:S(2)}) collective-permute-start(f32[40,128]{1,0:T(8,128)S(1)} %add_add_fusion.refs_0_), channel_id=1, source_target_pairs={{0,8},{1,9},{2,10},{3,11},{4,12},{5,13},{6,14},{7,15},{8,0},{9,1},... | collective-permute-start | bytes 61448 | tf_op jit(solution)/shard_map/ppermute | solution.py:320
  18.7 4.5 %collective-permute-start.7 = (f32[40,128]{1,0:T(8,128)S(1)}, f32[40,128]{1,0:T(8,128)S(1)}, u32[]{:S(2)}, u32[]{:S(2)}) collective-permute-start(f32[40,128]{1,0:T(8,128)S(1)} %add_add_fusion.refs_0_), channel_id=1, source_target_pairs={{0,4},{1,5},{2,6},{3,7},{4,0},{5,1},{6,2},{7,3},{8,12},{9,13},{10,... | collective-permute-start | bytes 61448 | tf_op jit(solution)/shard_map/ppermute | solution.py:320
  23.2 2.9 %collective-permute-start.10 = (bf16[64,4096]{1,0:T(8,128)(2,1)S(1)}, bf16[64,4096]{1,0:T(8,128)(2,1)S(1)}, u32[]{:S(2)}, u32[]{:S(2)}) collective-permute-start(bf16[64,4096]{1,0:T(8,128)(2,1)S(1)} %constant_dynamic-update-slice_fusion.4.refs_0_), channel_id=1, source_target_pairs={{0,1},{1,0},{2,3},{3,2},{4,5},{5,4},{6,7},{7,6},{8,9},{9,8},{10,11... | collective-permute-start | bytes 1572872 | tf_op jit(solution)/shard_map/ppermute | solution.py:320

commit v19 on v18

--- a/solution.py
+++ b/solution.py
@@ -10,7 +10,6 @@
 DAMP = 0.1
 HIGHEST = lax.Precision.HIGHEST
 COPY_ROWS = 128
-IN_FLIGHT = 5
 TOKENS_AT_ONCE = 256
 
 
@@ -61,7 +60,7 @@
         for at, src in enumerate((acts, grads))
     ]
     queue = [weight_copies[0], *tok_copies[0], *tok_copies[1]]
-    queue.insert(3, weight_copies[1])
+    queue.insert(5, weight_copies[1])
 
     def start_next(many):
         for copy in queue[:many]:
@@ -82,8 +81,9 @@
         grams[at].append(jnp.dot(flipped, plain, precision=HIGHEST, preferred_element_type=jnp.float32))
         blocks[at].clear()
 
-    start_next(1 + IN_FLIGHT)
+    start_next(3)
     weight_copies[0].wait()
+    start_next(3)
     turned(0)
     for step, (at, part, many) in enumerate(steps):
         for copy in tok_copies[at][part : part + many]:
@@ -91,7 +91,6 @@
             start_next(1)
         if step == last_act:
             weight_copies[1].wait()
-            start_next(1)
         rows = slice(part * COPY_ROWS, (part + many) * COPY_ROWS)
         block = jnp.dot(tok_buf[at, rows, :], weight_t[at], preferred_element_type=jnp.float32)
         if step == last_act:

time: 28.6 us -> 28.8 us (level)
  Pallas kernels: 10.8 us -> 11.1 us
where the time goes in v19:
time: 28.8 us; the launch traced here: 28.6 us
  starting transfers between devices  13.6 us (47%)
  Pallas kernels  11.1 us (39%)
  waiting for transfers between devices  3.75 us (13%)
    ppermute x11, starting transfers between devices, swapped(): return lax.ppermute(value, 'dp', perm)  13.6 us
    pallas_call x1, Pallas kernels, project(): pl.pallas_call(project_kernel, out_shape=(jax.ShapeDtypeStruct((factor, t...  5.9 us
    ppermute x11, waiting for transfers between devices, swapped(): return lax.ppermute(value, 'dp', perm)  3.75 us
    pallas_call x1, Pallas kernels, precondition(): pl.pallas_call(functools.partial(precondition_kernel, tok_total, n_terms)...  2.78 us
    pallas_call x1, Pallas kernels, score(): pl.pallas_call(functools.partial(score_kernel, size, n_pieces), out_shape...  2.38 us
  transfers between devices with their start and end apart: 11, of which 3 were waited for; matrix products, arithmetic and copies ran while one was open for 0% of the time, Pallas kernels for 30%

profile of v19, /device:TPU:0, one launch (start us, length us, event | category | flops | bytes accessed | tf_op | source)
XLA Modules:
  0.0 28.6 jit_solution(6489811679087671157)
XLA Ops:
  0.0 4.0 %collective-permute-start.1 = (bf16[8,4096]{1,0:T(8,128)(2,1)}, bf16[8,4096]{1,0:T(8,128)(2,1)S(1)}, u32[]{:S(2)}, u32[]{:S(2)}) collective-permute-start(bf16[8,4096]{1,0:T(8,128)(2,1)} %param.9), channel_id=1, source_target_pairs={{0,8},{1,9},{2,10},{3,11},{4,12},{5,13},{6,14},{7,15},{8,0},{9,1},... | collective-permute-start | bytes 196616 | tf_op jit(solution)/shard_map/ppermute | solution.py:319
  4.0 1.3 %collective-permute-start = (bf16[8,4096]{1,0:T(8,128)(2,1)}, bf16[8,4096]{1,0:T(8,128)(2,1)S(1)}, u32[]{:S(2)}, u32[]{:S(2)}) collective-permute-start(bf16[8,4096]{1,0:T(8,128)(2,1)} %param.9), channel_id=1, source_target_pairs={{0,12},{1,13},{2,14},{3,15},{4,8},{5,9},{6,10},{7,11},{8,4},{9,5},... | collective-permute-start | bytes 196616 | tf_op jit(solution)/shard_map/ppermute | solution.py:319
  5.4 0.2 collective-permute-start.2
  5.6 5.9 %project.1 = (f32[64,512]{1,0:T(8,128)S(1)}, f32[64,512]{1,0:T(8,128)S(1)}, f32[40,128]{1,0:T(8,128)S(1)}) custom-call(bf16[512,4096]{1,0:T(8,128)(2,1)} %acts.1, bf16[512,4096]{1,0:T(8,128)(2,1)} %grads.1, bf16[64,4096]{1,0:T(8,128)(2,1)} %bitcast.2, bf16[64,4096]{1,0:T(8,128)(2,1)} %bitcast.3), custom_call_target="tpu_custom_call" | custom-call | flops 536870912 | bytes 8388608 | tf_op jit(solution)/shard_map/project/pallas_call | solution.py:115
  11.5 0.0 collective-permute-done.1
  11.5 0.0 collective-permute-done
  11.5 0.0 collective-permute-done.2
  11.6 0.5 %collective-permute-start.6 = (f32[40,128]{1,0:T(8,128)S(1)}, f32[40,128]{1,0:T(8,128)S(1)}, u32[]{:S(2)}, u32[]{:S(2)}) collective-permute-start(f32[40,128]{1,0:T(8,128)S(1)} %get-tuple-element.24), channel_id=1, source_target_pairs={{0,3},{1,2},{2,1},{3,0},{4,7},{5,6},{6,5},{7,4},{8,11},{9,10},{10,... | collective-permute-start | bytes 61448 | tf_op jit(solution)/shard_map/ppermute | solution.py:319
  12.0 1.2 %collective-permute-start.5 = (f32[40,128]{1,0:T(8,128)S(1)}, f32[40,128]{1,0:T(8,128)S(1)}, u32[]{:S(2)}, u32[]{:S(2)}) collective-permute-start(f32[40,128]{1,0:T(8,128)S(1)} %get-tuple-element.24), channel_id=1, source_target_pairs={{0,2},{1,3},{2,0},{3,1},{4,6},{5,7},{6,4},{7,5},{8,10},{9,11},{10,... | collective-permute-start | bytes 61448 | tf_op jit(solution)/shard_map/ppermute | solution.py:319
  13.2 0.3 collective-permute-start.4
  13.5 1.6 %collective-permute-start.3 = (bf16[32,4096]{1,0:T(8,128)(2,1)S(1)}, bf16[32,4096]{1,0:T(8,128)(2,1)S(1)}, u32[]{:S(2)}, u32[]{:S(2)}) collective-permute-start(bf16[32,4096]{1,0:T(8,128)(2,1)S(1)} %constant_dynamic-update-slice_fusion), channel_id=1, source_target_pairs={{0,2},{1,3},{2,0},{3,1},{4,6},{5,7},{6,4},{7,5},{8,10},{9,11},{10,... | collective-permute-start | bytes 786440 | tf_op jit(solution)/shard_map/ppermute | solution.py:319
  15.1 0.0 collective-permute-done.6
  15.1 0.7 %collective-permute-done.5 = f32[40,128]{1,0:T(8,128)S(1)} collective-permute-done((f32[40,128]{1,0:T(8,128)S(1)}, f32[40,128]{1,0:T(8,128)S(1)}, u32[]{:S(2)}, u32[]{:S(2)}) %collective-permute-start.5) | collective-permute-done | bytes 20512 | tf_op jit(solution)/shard_map/ppermute | solution.py:319
  15.8 0.0 collective-permute-done.4
  15.8 2.7 %collective-permute-start.9 = (f32[40,128]{1,0:T(8,128)S(1)}, f32[40,128]{1,0:T(8,128)S(1)}, u32[]{:S(2)}, u32[]{:S(2)}) collective-permute-start(f32[40,128]{1,0:T(8,128)S(1)} %add_add_fusion.refs_0_), channel_id=1, source_target_pairs={{0,12},{1,13},{2,14},{3,15},{4,8},{5,9},{6,10},{7,11},{8,4},{9,5},... | collective-permute-start | bytes 61448 | tf_op jit(solution)/shard_map/ppermute | solution.py:319
  18.5 0.3 %collective-permute-start.8 = (f32[40,128]{1,0:T(8,128)S(1)}, f32[40,128]{1,0:T(8,128)S(1)}, u32[]{:S(2)}, u32[]{:S(2)}) collective-permute-start(f32[40,128]{1,0:T(8,128)S(1)} %add_add_fusion.refs_0_), channel_id=1, source_target_pairs={{0,8},{1,9},{2,10},{3,11},{4,12},{5,13},{6,14},{7,15},{8,0},{9,1},... | collective-permute-start | bytes 61448 | tf_op jit(solution)/shard_map/ppermute | solution.py:319
  18.9 1.4 %collective-permute-start.7 = (f32[40,128]{1,0:T(8,128)S(1)}, f32[40,128]{1,0:T(8,128)S(1)}, u32[]{:S(2)}, u32[]{:S(2)}) collective-permute-start(f32[40,128]{1,0:T(8,128)S(1)} %add_add_fusion.refs_0_), channel_id=1, source_target_pairs={{0,4},{1,5},{2,6},{3,7},{4,0},{5,1},{6,2},{7,3},{8,12},{9,13},{10,... | collective-permute-start | bytes 61448 | tf_op jit(solution)/shard_map/ppermute | solution.py:319
  20.3 1.2 %collective-permute-done.9.refs_3_ = f32[40,128]{1,0:T(8,128)S(1)} collective-permute-done((f32[40,128]{1,0:T(8,128)S(1)}, f32[40,128]{1,0:T(8,128)S(1)}, u32[]{:S(2)}, u32[]{:S(2)}) %collective-permute-start.9) | collective-permute-done | bytes 20512 | tf_op jit(solution)/shard_map/ppermute | solution.py:319
  21.5 1.9 %collective-permute-done.8.refs_2_ = f32[40,128]{1,0:T(8,128)S(1)} collective-permute-done((f32[40,128]{1,0:T(8,128)S(1)}, f32[40,128]{1,0:T(8,128)S(1)}, u32[]{:S(2)}, u32[]{:S(2)}) %collective-permute-start.8) | collective-permute-done | bytes 20512 | tf_op jit(solution)/shard_map/ppermute | solution.py:319
  23.3 0.0 collective-permute-done.7.refs_1_
  23.3 0.0 collective-permute-done.3
  23.4 0.1 collective-permute-start.10
  23.5 2.8 %precondition.1.moved = f32[128,512]{1,0:T(8,128)S(1)} custom-call(f32[40,128]{1,0:T(8,128)S(1)} %add_add_fusion.refs_0_, f32[40,128]{1,0:T(8,128)S(1)} %collective-permute-done.7.refs_1_, f32[40,128]{1,0:T(8,128)S(1)} %collective-permute-done.8.refs_2_, f32[40,128]{1,0:T(8,128)S(1)} %collective-permute-done.9.refs_3_, ...), custom_call_target="tpu_custom_call" | custom-call | flops 3355443200 | bytes 524288 | tf_op jit(solution)/shard_map/precondition/pallas_call | solution.py:218
  26.3 2.4 %score.1 = f32[512,128]{1,0:T(8,128)} custom-call(f32[128,512]{1,0:T(8,128)S(1)} %precondition.1.moved, bf16[64,4096]{1,0:T(8,128)(2,1)S(1)} %constant_dynamic-update-slice_fusion.4.refs_0_, bf16[64,4096]{1,0:T(8,128)(2,1)S(1)} %collective-permute-done.10.refs_1_), custom_call_target="tpu_custom_call" | custom-call | tf_op jit(solution)/shard_map/score/pallas_call | solution.py:279
  (10 shorter events, 0.1 us)
Async XLA Ops:
  0.0 11.5 %collective-permute-start.1 = (bf16[8,4096]{1,0:T(8,128)(2,1)}, bf16[8,4096]{1,0:T(8,128)(2,1)S(1)}, u32[]{:S(2)}, u32[]{:S(2)}) collective-permute-start(bf16[8,4096]{1,0:T(8,128)(2,1)} %param.9), channel_id=1, source_target_pairs={{0,8},{1,9},{2,10},{3,11},{4,12},{5,13},{6,14},{7,15},{8,0},{9,1},... | collective-permute-start | bytes 196616 | tf_op jit(solution)/shard_map/ppermute | solution.py:319
  4.0 7.5 %collective-permute-start = (bf16[8,4096]{1,0:T(8,128)(2,1)}, bf16[8,4096]{1,0:T(8,128)(2,1)S(1)}, u32[]{:S(2)}, u32[]{:S(2)}) collective-permute-start(bf16[8,4096]{1,0:T(8,128)(2,1)} %param.9), channel_id=1, source_target_pairs={{0,12},{1,13},{2,14},{3,15},{4,8},{5,9},{6,10},{7,11},{8,4},{9,5},... | collective-permute-start | bytes 196616 | tf_op jit(solution)/shard_map/ppermute | solution.py:319
  5.4 6.2 %collective-permute-start.2 = (bf16[8,4096]{1,0:T(8,128)(2,1)}, bf16[8,4096]{1,0:T(8,128)(2,1)S(1)}, u32[]{:S(2)}, u32[]{:S(2)}) collective-permute-start(bf16[8,4096]{1,0:T(8,128)(2,1)} %param.9), channel_id=1, source_target_pairs={{0,4},{1,5},{2,6},{3,7},{4,0},{5,1},{6,2},{7,3},{8,12},{9,13},{10,... | collective-permute-start | bytes 196616 | tf_op jit(solution)/shard_map/ppermute | solution.py:319
  5.6 7.9 %copy-start = (bf16[8,4096]{1,0:T(8,128)(2,1)S(1)}, bf16[8,4096]{1,0:T(8,128)(2,1)}, u32[]{:S(2)}) copy-start(bf16[8,4096]{1,0:T(8,128)(2,1)} %param.9) | copy-start | bytes 196612
  11.6 3.6 %collective-permute-start.6 = (f32[40,128]{1,0:T(8,128)S(1)}, f32[40,128]{1,0:T(8,128)S(1)}, u32[]{:S(2)}, u32[]{:S(2)}) collective-permute-start(f32[40,128]{1,0:T(8,128)S(1)} %get-tuple-element.24), channel_id=1, source_target_pairs={{0,3},{1,2},{2,1},{3,0},{4,7},{5,6},{6,5},{7,4},{8,11},{9,10},{10,... | collective-permute-start | bytes 61448 | tf_op jit(solution)/shard_map/ppermute | solution.py:319
  12.0 3.8 %collective-permute-start.5 = (f32[40,128]{1,0:T(8,128)S(1)}, f32[40,128]{1,0:T(8,128)S(1)}, u32[]{:S(2)}, u32[]{:S(2)}) collective-permute-start(f32[40,128]{1,0:T(8,128)S(1)} %get-tuple-element.24), channel_id=1, source_target_pairs={{0,2},{1,3},{2,0},{3,1},{4,6},{5,7},{6,4},{7,5},{8,10},{9,11},{10,... | collective-permute-start | bytes 61448 | tf_op jit(solution)/shard_map/ppermute | solution.py:319
  13.2 2.6 %collective-permute-start.4 = (f32[40,128]{1,0:T(8,128)S(1)}, f32[40,128]{1,0:T(8,128)S(1)}, u32[]{:S(2)}, u32[]{:S(2)}) collective-permute-start(f32[40,128]{1,0:T(8,128)S(1)} %get-tuple-element.24), channel_id=1, source_target_pairs={{0,1},{1,0},{2,3},{3,2},{4,5},{5,4},{6,7},{7,6},{8,9},{9,8},{10,11... | collective-permute-start | bytes 61448 | tf_op jit(solution)/shard_map/ppermute | solution.py:319
  13.5 9.8 %collective-permute-start.3 = (bf16[32,4096]{1,0:T(8,128)(2,1)S(1)}, bf16[32,4096]{1,0:T(8,128)(2,1)S(1)}, u32[]{:S(2)}, u32[]{:S(2)}) collective-permute-start(bf16[32,4096]{1,0:T(8,128)(2,1)S(1)} %constant_dynamic-update-slice_fusion), channel_id=1, source_target_pairs={{0,2},{1,3},{2,0},{3,1},{4,6},{5,7},{6,4},{7,5},{8,10},{9,11},{10,... | collective-permute-start | bytes 786440 | tf_op jit(solution)/shard_map/ppermute | solution.py:319
  15.8 5.7 %collective-permute-start.9 = (f32[40,128]{1,0:T(8,128)S(1)}, f32[40,128]{1,0:T(8,128)S(1)}, u32[]{:S(2)}, u32[]{:S(2)}) collective-permute-start(f32[40,128]{1,0:T(8,128)S(1)} %add_add_fusion.refs_0_), channel_id=1, source_target_pairs={{0,12},{1,13},{2,14},{3,15},{4,8},{5,9},{6,10},{7,11},{8,4},{9,5},... | collective-permute-start | bytes 61448 | tf_op jit(solution)/shard_map/ppermute | solution.py:319
  18.5 4.8 %collective-permute-start.8 = (f32[40,128]{1,0:T(8,128)S(1)}, f32[40,128]{1,0:T(8,128)S(1)}, u32[]{:S(2)}, u32[]{:S(2)}) collective-permute-start(f32[40,128]{1,0:T(8,128)S(1)} %add_add_fusion.refs_0_), channel_id=1, source_target_pairs={{0,8},{1,9},{2,10},{3,11},{4,12},{5,13},{6,14},{7,15},{8,0},{9,1},... | collective-permute-start | bytes 61448 | tf_op jit(solution)/shard_map/ppermute | solution.py:319
  18.9 4.5 %collective-permute-start.7 = (f32[40,128]{1,0:T(8,128)S(1)}, f32[40,128]{1,0:T(8,128)S(1)}, u32[]{:S(2)}, u32[]{:S(2)}) collective-permute-start(f32[40,128]{1,0:T(8,128)S(1)} %add_add_fusion.refs_0_), channel_id=1, source_target_pairs={{0,4},{1,5},{2,6},{3,7},{4,0},{5,1},{6,2},{7,3},{8,12},{9,13},{10,... | collective-permute-start | bytes 61448 | tf_op jit(solution)/shard_map/ppermute | solution.py:319
  23.4 2.9 %collective-permute-start.10 = (bf16[64,4096]{1,0:T(8,128)(2,1)S(1)}, bf16[64,4096]{1,0:T(8,128)(2,1)S(1)}, u32[]{:S(2)}, u32[]{:S(2)}) collective-permute-start(bf16[64,4096]{1,0:T(8,128)(2,1)S(1)} %constant_dynamic-update-slice_fusion.4.refs_0_), channel_id=1, source_target_pairs={{0,1},{1,0},{2,3},{3,2},{4,5},{5,4},{6,7},{7,6},{8,9},{9,8},{10,11... | collective-permute-start | bytes 1572872 | tf_op jit(solution)/shard_map/ppermute | solution.py:319

commit v20 on v18

--- a/solution.py
+++ b/solution.py
@@ -31,13 +31,22 @@
 def unpacked(value):
     factor = value.shape[1] // 2
     half = factor // 2
-    row_at, lane = places(factor)
-    mixed = jnp.concatenate([value[:half, :factor], value[:half, factor:]], axis=0)
-    flipped = mixed.T
-    diagonal = jnp.broadcast_to(value[half : half + 1, :factor], (factor, factor))
-    act = jnp.where(row_at <= lane, mixed, flipped)
-    grad = jnp.where(row_at > lane, mixed, jnp.where(row_at < lane, flipped, diagonal))
-    return jnp.concatenate([act, grad], axis=1)
+    row_at = lax.broadcasted_iota(jnp.int32, (factor, 2 * factor), 0)
+    lane = lax.broadcasted_iota(jnp.int32, (factor, 2 * factor), 1)
+    left_half = lane < factor
+    inner = jnp.where(left_half, lane, lane - factor)
+    rolled = pltpu.roll(value[:half], factor, axis=1)
+    mixed = jnp.concatenate(
+        [
+            jnp.where(left_half[:half], value[:half], rolled),
+            jnp.where(left_half[:half], rolled, value[:half]),
+        ],
+        axis=0,
+    )
+    flipped = jnp.concatenate([mixed, mixed], axis=0).T[:factor]
+    diagonal = jnp.broadcast_to(value[half : half + 1], mixed.shape)
+    below = jnp.where(row_at > inner, mixed, jnp.where(row_at < inner, flipped, diagonal))
+    return jnp.where(left_half, jnp.where(row_at <= inner, mixed, flipped), below)
 
 
 def project_kernel(
@@ -62,10 +71,11 @@
     ]
     queue = [weight_copies[0], *tok_copies[0], *tok_copies[1]]
     queue.insert(3, weight_copies[1])
+    queue = [(copy, at % 2) for at, copy in enumerate(queue)]
 
     def start_next(many):
-        for copy in queue[:many]:
-            copy.start()
+        for copy, lane in queue[:many]:
+            copy.start(priority=lane)
         del queue[:many]
 
     def turned(at):
@@ -204,7 +214,7 @@
     row_at = lax.broadcasted_iota(jnp.int32, both.shape, 0)
     left_half = lane < factor
     inner = jnp.where(left_half, lane, lane - factor)
-    both = both / tok_total + jnp.where(inner == row_at, DAMP, 0.0)
+    both = both * (1.0 / tok_total) + jnp.where(inner == row_at, DAMP, 0.0)
     both = inverse_pair(both)
     blocks = jnp.concatenate(
         [jnp.where(left_half, both, 0.0), jnp.where(left_half, 0.0, both)], axis=0

time: 28.6 us -> 28.5 us (level)
  transfers between devices with their start and end apart: 11 -> 11, of which waited for: 3 -> 3; matrix products, arithmetic and copies ran while one was open for 0% -> 0% of each run, Pallas kernels for 30% -> 29%
where the time goes in v20:
time: 28.5 us; the launch traced here: 28.3 us
  starting transfers between devices  13.6 us (48%)
  Pallas kernels  10.7 us (38%)
  waiting for transfers between devices  3.76 us (13%)
    ppermute x11, starting transfers between devices, swapped(): return lax.ppermute(value, 'dp', perm)  13.6 us
    pallas_call x1, Pallas kernels, project(): pl.pallas_call(project_kernel, out_shape=(jax.ShapeDtypeStruct((factor, t...  5.66 us
    ppermute x11, waiting for transfers between devices, swapped(): return lax.ppermute(value, 'dp', perm)  3.76 us
    pallas_call x1, Pallas kernels, precondition(): pl.pallas_call(functools.partial(precondition_kernel, tok_total, n_terms)...  2.68 us
    pallas_call x1, Pallas kernels, score(): pl.pallas_call(functools.partial(score_kernel, size, n_pieces), out_shape...  2.4 us
  transfers between devices with their start and end apart: 11, of which 3 were waited for; matrix products, arithmetic and copies ran while one was open for 0% of the time, Pallas kernels for 29%

profile of v20, /device:TPU:0, one launch (start us, length us, event | category | flops | bytes accessed | tf_op | source)
XLA Modules:
  0.0 28.3 jit_solution(12471696178742988153)
XLA Ops:
  0.0 4.0 %collective-permute-start.1 = (bf16[8,4096]{1,0:T(8,128)(2,1)}, bf16[8,4096]{1,0:T(8,128)(2,1)S(1)}, u32[]{:S(2)}, u32[]{:S(2)}) collective-permute-start(bf16[8,4096]{1,0:T(8,128)(2,1)} %param.9), channel_id=1, source_target_pairs={{0,8},{1,9},{2,10},{3,11},{4,12},{5,13},{6,14},{7,15},{8,0},{9,1},... | collective-permute-start | bytes 196616 | tf_op jit(solution)/shard_map/ppermute | solution.py:330
  4.0 1.3 %collective-permute-start = (bf16[8,4096]{1,0:T(8,128)(2,1)}, bf16[8,4096]{1,0:T(8,128)(2,1)S(1)}, u32[]{:S(2)}, u32[]{:S(2)}) collective-permute-start(bf16[8,4096]{1,0:T(8,128)(2,1)} %param.9), channel_id=1, source_target_pairs={{0,12},{1,13},{2,14},{3,15},{4,8},{5,9},{6,10},{7,11},{8,4},{9,5},... | collective-permute-start | bytes 196616 | tf_op jit(solution)/shard_map/ppermute | solution.py:330
  5.4 0.2 collective-permute-start.2
  5.6 5.7 %project.1 = (f32[64,512]{1,0:T(8,128)S(1)}, f32[64,512]{1,0:T(8,128)S(1)}, f32[40,128]{1,0:T(8,128)S(1)}) custom-call(bf16[512,4096]{1,0:T(8,128)(2,1)} %acts.1, bf16[512,4096]{1,0:T(8,128)(2,1)} %grads.1, bf16[64,4096]{1,0:T(8,128)(2,1)} %bitcast.2, bf16[64,4096]{1,0:T(8,128)(2,1)} %bitcast.3), custom_call_target="tpu_custom_call" | custom-call | flops 536870912 | bytes 8388608 | tf_op jit(solution)/shard_map/project/pallas_call | solution.py:126
  11.3 0.0 collective-permute-done.1
  11.3 0.0 collective-permute-done
  11.3 0.0 collective-permute-done.2
  11.3 0.5 %collective-permute-start.6 = (f32[40,128]{1,0:T(8,128)S(1)}, f32[40,128]{1,0:T(8,128)S(1)}, u32[]{:S(2)}, u32[]{:S(2)}) collective-permute-start(f32[40,128]{1,0:T(8,128)S(1)} %get-tuple-element.24), channel_id=1, source_target_pairs={{0,3},{1,2},{2,1},{3,0},{4,7},{5,6},{6,5},{7,4},{8,11},{9,10},{10,... | collective-permute-start | bytes 61448 | tf_op jit(solution)/shard_map/ppermute | solution.py:330
  11.8 1.2 %collective-permute-start.5 = (f32[40,128]{1,0:T(8,128)S(1)}, f32[40,128]{1,0:T(8,128)S(1)}, u32[]{:S(2)}, u32[]{:S(2)}) collective-permute-start(f32[40,128]{1,0:T(8,128)S(1)} %get-tuple-element.24), channel_id=1, source_target_pairs={{0,2},{1,3},{2,0},{3,1},{4,6},{5,7},{6,4},{7,5},{8,10},{9,11},{10,... | collective-permute-start | bytes 61448 | tf_op jit(solution)/shard_map/ppermute | solution.py:330
  13.0 0.3 collective-permute-start.4
  13.3 1.6 %collective-permute-start.3 = (bf16[32,4096]{1,0:T(8,128)(2,1)S(1)}, bf16[32,4096]{1,0:T(8,128)(2,1)S(1)}, u32[]{:S(2)}, u32[]{:S(2)}) collective-permute-start(bf16[32,4096]{1,0:T(8,128)(2,1)S(1)} %constant_dynamic-update-slice_fusion), channel_id=1, source_target_pairs={{0,2},{1,3},{2,0},{3,1},{4,6},{5,7},{6,4},{7,5},{8,10},{9,11},{10,... | collective-permute-start | bytes 786440 | tf_op jit(solution)/shard_map/ppermute | solution.py:330
  14.9 0.0 collective-permute-done.6
  14.9 0.7 %collective-permute-done.5 = f32[40,128]{1,0:T(8,128)S(1)} collective-permute-done((f32[40,128]{1,0:T(8,128)S(1)}, f32[40,128]{1,0:T(8,128)S(1)}, u32[]{:S(2)}, u32[]{:S(2)}) %collective-permute-start.5) | collective-permute-done | bytes 20512 | tf_op jit(solution)/shard_map/ppermute | solution.py:330
  15.6 0.0 collective-permute-done.4
  15.6 2.7 %collective-permute-start.9 = (f32[40,128]{1,0:T(8,128)S(1)}, f32[40,128]{1,0:T(8,128)S(1)}, u32[]{:S(2)}, u32[]{:S(2)}) collective-permute-start(f32[40,128]{1,0:T(8,128)S(1)} %add_add_fusion.refs_0_), channel_id=1, source_target_pairs={{0,12},{1,13},{2,14},{3,15},{4,8},{5,9},{6,10},{7,11},{8,4},{9,5},... | collective-permute-start | bytes 61448 | tf_op jit(solution)/shard_map/ppermute | solution.py:330
  18.3 0.3 %collective-permute-start.8 = (f32[40,128]{1,0:T(8,128)S(1)}, f32[40,128]{1,0:T(8,128)S(1)}, u32[]{:S(2)}, u32[]{:S(2)}) collective-permute-start(f32[40,128]{1,0:T(8,128)S(1)} %add_add_fusion.refs_0_), channel_id=1, source_target_pairs={{0,8},{1,9},{2,10},{3,11},{4,12},{5,13},{6,14},{7,15},{8,0},{9,1},... | collective-permute-start | bytes 61448 | tf_op jit(solution)/shard_map/ppermute | solution.py:330
  18.6 1.4 %collective-permute-start.7 = (f32[40,128]{1,0:T(8,128)S(1)}, f32[40,128]{1,0:T(8,128)S(1)}, u32[]{:S(2)}, u32[]{:S(2)}) collective-permute-start(f32[40,128]{1,0:T(8,128)S(1)} %add_add_fusion.refs_0_), channel_id=1, source_target_pairs={{0,4},{1,5},{2,6},{3,7},{4,0},{5,1},{6,2},{7,3},{8,12},{9,13},{10,... | collective-permute-start | bytes 61448 | tf_op jit(solution)/shard_map/ppermute | solution.py:330
  20.0 1.2 %collective-permute-done.9.refs_3_ = f32[40,128]{1,0:T(8,128)S(1)} collective-permute-done((f32[40,128]{1,0:T(8,128)S(1)}, f32[40,128]{1,0:T(8,128)S(1)}, u32[]{:S(2)}, u32[]{:S(2)}) %collective-permute-start.9) | collective-permute-done | bytes 20512 | tf_op jit(solution)/shard_map/ppermute | solution.py:330
  21.2 1.9 %collective-permute-done.8.refs_2_ = f32[40,128]{1,0:T(8,128)S(1)} collective-permute-done((f32[40,128]{1,0:T(8,128)S(1)}, f32[40,128]{1,0:T(8,128)S(1)}, u32[]{:S(2)}, u32[]{:S(2)}) %collective-permute-start.8) | collective-permute-done | bytes 20512 | tf_op jit(solution)/shard_map/ppermute | solution.py:330
  23.1 0.0 collective-permute-done.7.refs_1_
  23.1 0.0 collective-permute-done.3
  23.2 0.1 collective-permute-start.10
  23.2 2.7 %precondition.1.moved = f32[128,512]{1,0:T(8,128)S(1)} custom-call(f32[40,128]{1,0:T(8,128)S(1)} %add_add_fusion.refs_0_, f32[40,128]{1,0:T(8,128)S(1)} %collective-permute-done.7.refs_1_, f32[40,128]{1,0:T(8,128)S(1)} %collective-permute-done.8.refs_2_, f32[40,128]{1,0:T(8,128)S(1)} %collective-permute-done.9.refs_3_, ...), custom_call_target="tpu_custom_call" | custom-call | flops 3355443200 | bytes 524288 | tf_op jit(solution)/shard_map/precondition/pallas_call | solution.py:229
  25.9 2.4 %score.1 = f32[512,128]{1,0:T(8,128)} custom-call(f32[128,512]{1,0:T(8,128)S(1)} %precondition.1.moved, bf16[64,4096]{1,0:T(8,128)(2,1)S(1)} %constant_dynamic-update-slice_fusion.4.refs_0_, bf16[64,4096]{1,0:T(8,128)(2,1)S(1)} %collective-permute-done.10.refs_1_), custom_call_target="tpu_custom_call" | custom-call | tf_op jit(solution)/shard_map/score/pallas_call | solution.py:290
  (10 shorter events, 0.1 us)
Async XLA Ops:
  0.0 11.3 %collective-permute-start.1 = (bf16[8,4096]{1,0:T(8,128)(2,1)}, bf16[8,4096]{1,0:T(8,128)(2,1)S(1)}, u32[]{:S(2)}, u32[]{:S(2)}) collective-permute-start(bf16[8,4096]{1,0:T(8,128)(2,1)} %param.9), channel_id=1, source_target_pairs={{0,8},{1,9},{2,10},{3,11},{4,12},{5,13},{6,14},{7,15},{8,0},{9,1},... | collective-permute-start | bytes 196616 | tf_op jit(solution)/shard_map/ppermute | solution.py:330
  4.0 7.3 %collective-permute-start = (bf16[8,4096]{1,0:T(8,128)(2,1)}, bf16[8,4096]{1,0:T(8,128)(2,1)S(1)}, u32[]{:S(2)}, u32[]{:S(2)}) collective-permute-start(bf16[8,4096]{1,0:T(8,128)(2,1)} %param.9), channel_id=1, source_target_pairs={{0,12},{1,13},{2,14},{3,15},{4,8},{5,9},{6,10},{7,11},{8,4},{9,5},... | collective-permute-start | bytes 196616 | tf_op jit(solution)/shard_map/ppermute | solution.py:330
  5.4 5.9 %collective-permute-start.2 = (bf16[8,4096]{1,0:T(8,128)(2,1)}, bf16[8,4096]{1,0:T(8,128)(2,1)S(1)}, u32[]{:S(2)}, u32[]{:S(2)}) collective-permute-start(bf16[8,4096]{1,0:T(8,128)(2,1)} %param.9), channel_id=1, source_target_pairs={{0,4},{1,5},{2,6},{3,7},{4,0},{5,1},{6,2},{7,3},{8,12},{9,13},{10,... | collective-permute-start | bytes 196616 | tf_op jit(solution)/shard_map/ppermute | solution.py:330
  5.6 7.6 %copy-start = (bf16[8,4096]{1,0:T(8,128)(2,1)S(1)}, bf16[8,4096]{1,0:T(8,128)(2,1)}, u32[]{:S(2)}) copy-start(bf16[8,4096]{1,0:T(8,128)(2,1)} %param.9) | copy-start | bytes 196612
  11.3 3.6 %collective-permute-start.6 = (f32[40,128]{1,0:T(8,128)S(1)}, f32[40,128]{1,0:T(8,128)S(1)}, u32[]{:S(2)}, u32[]{:S(2)}) collective-permute-start(f32[40,128]{1,0:T(8,128)S(1)} %get-tuple-element.24), channel_id=1, source_target_pairs={{0,3},{1,2},{2,1},{3,0},{4,7},{5,6},{6,5},{7,4},{8,11},{9,10},{10,... | collective-permute-start | bytes 61448 | tf_op jit(solution)/shard_map/ppermute | solution.py:330
  11.8 3.8 %collective-permute-start.5 = (f32[40,128]{1,0:T(8,128)S(1)}, f32[40,128]{1,0:T(8,128)S(1)}, u32[]{:S(2)}, u32[]{:S(2)}) collective-permute-start(f32[40,128]{1,0:T(8,128)S(1)} %get-tuple-element.24), channel_id=1, source_target_pairs={{0,2},{1,3},{2,0},{3,1},{4,6},{5,7},{6,4},{7,5},{8,10},{9,11},{10,... | collective-permute-start | bytes 61448 | tf_op jit(solution)/shard_map/ppermute | solution.py:330
  13.0 2.6 %collective-permute-start.4 = (f32[40,128]{1,0:T(8,128)S(1)}, f32[40,128]{1,0:T(8,128)S(1)}, u32[]{:S(2)}, u32[]{:S(2)}) collective-permute-start(f32[40,128]{1,0:T(8,128)S(1)} %get-tuple-element.24), channel_id=1, source_target_pairs={{0,1},{1,0},{2,3},{3,2},{4,5},{5,4},{6,7},{7,6},{8,9},{9,8},{10,11... | collective-permute-start | bytes 61448 | tf_op jit(solution)/shard_map/ppermute | solution.py:330
  13.3 9.8 %collective-permute-start.3 = (bf16[32,4096]{1,0:T(8,128)(2,1)S(1)}, bf16[32,4096]{1,0:T(8,128)(2,1)S(1)}, u32[]{:S(2)}, u32[]{:S(2)}) collective-permute-start(bf16[32,4096]{1,0:T(8,128)(2,1)S(1)} %constant_dynamic-update-slice_fusion), channel_id=1, source_target_pairs={{0,2},{1,3},{2,0},{3,1},{4,6},{5,7},{6,4},{7,5},{8,10},{9,11},{10,... | collective-permute-start | bytes 786440 | tf_op jit(solution)/shard_map/ppermute | solution.py:330
  15.6 5.7 %collective-permute-start.9 = (f32[40,128]{1,0:T(8,128)S(1)}, f32[40,128]{1,0:T(8,128)S(1)}, u32[]{:S(2)}, u32[]{:S(2)}) collective-permute-start(f32[40,128]{1,0:T(8,128)S(1)} %add_add_fusion.refs_0_), channel_id=1, source_target_pairs={{0,12},{1,13},{2,14},{3,15},{4,8},{5,9},{6,10},{7,11},{8,4},{9,5},... | collective-permute-start | bytes 61448 | tf_op jit(solution)/shard_map/ppermute | solution.py:330
  18.3 4.8 %collective-permute-start.8 = (f32[40,128]{1,0:T(8,128)S(1)}, f32[40,128]{1,0:T(8,128)S(1)}, u32[]{:S(2)}, u32[]{:S(2)}) collective-permute-start(f32[40,128]{1,0:T(8,128)S(1)} %add_add_fusion.refs_0_), channel_id=1, source_target_pairs={{0,8},{1,9},{2,10},{3,11},{4,12},{5,13},{6,14},{7,15},{8,0},{9,1},... | collective-permute-start | bytes 61448 | tf_op jit(solution)/shard_map/ppermute | solution.py:330
  18.6 4.5 %collective-permute-start.7 = (f32[40,128]{1,0:T(8,128)S(1)}, f32[40,128]{1,0:T(8,128)S(1)}, u32[]{:S(2)}, u32[]{:S(2)}) collective-permute-start(f32[40,128]{1,0:T(8,128)S(1)} %add_add_fusion.refs_0_), channel_id=1, source_target_pairs={{0,4},{1,5},{2,6},{3,7},{4,0},{5,1},{6,2},{7,3},{8,12},{9,13},{10,... | collective-permute-start | bytes 61448 | tf_op jit(solution)/shard_map/ppermute | solution.py:330
  23.2 2.8 %collective-permute-start.10 = (bf16[64,4096]{1,0:T(8,128)(2,1)S(1)}, bf16[64,4096]{1,0:T(8,128)(2,1)S(1)}, u32[]{:S(2)}, u32[]{:S(2)}) collective-permute-start(bf16[64,4096]{1,0:T(8,128)(2,1)S(1)} %constant_dynamic-update-slice_fusion.4.refs_0_), channel_id=1, source_target_pairs={{0,1},{1,0},{2,3},{3,2},{4,5},{5,4},{6,7},{7,6},{8,9},{9,8},{10,11... | collective-permute-start | bytes 1572872 | tf_op jit(solution)/shard_map/ppermute | solution.py:330

commit v21 on v20

--- a/solution.py
+++ b/solution.py
@@ -71,11 +71,10 @@
     ]
     queue = [weight_copies[0], *tok_copies[0], *tok_copies[1]]
     queue.insert(3, weight_copies[1])
-    queue = [(copy, at % 2) for at, copy in enumerate(queue)]
 
     def start_next(many):
-        for copy, lane in queue[:many]:
-            copy.start(priority=lane)
+        for copy in queue[:many]:
+            copy.start()
         del queue[:many]
 
     def turned(at):
@@ -96,20 +95,19 @@
     weight_copies[0].wait()
     turned(0)
     for step, (at, part, many) in enumerate(steps):
-        for copy in tok_copies[at][part : part + many]:
-            copy.wait()
-            start_next(1)
         if step == last_act:
             weight_copies[1].wait()
             start_next(1)
-        rows = slice(part * COPY_ROWS, (part + many) * COPY_ROWS)
-        block = jnp.dot(tok_buf[at, rows, :], weight_t[at], preferred_element_type=jnp.float32)
-        if step == last_act:
             turned(1)
         if step == last_act + 1:
             add_gram(0)
         if step == len(steps) - 1:
             add_gram(1)
+        for copy in tok_copies[at][part : part + many]:
+            copy.wait()
+            start_next(1)
+        rows = slice(part * COPY_ROWS, (part + many) * COPY_ROWS)
+        block = jnp.dot(tok_buf[at, rows, :], weight_t[at], preferred_element_type=jnp.float32)
         flipped = block.T
         (act_t, grad_t)[at][:, rows] = flipped
         blocks[at].append((flipped, block))

time: 28.5 us -> 28.8 us (1.011)
  Pallas kernels: 10.7 us -> 11 us
    pallas_call x1, Pallas kernels: 5.66 us -> 5.98 us  [project(): pl.pallas_call(project_kernel, out_shape=(jax.ShapeDtypeStruct((factor, t...]
  transfers between devices with their start and end apart: 11 -> 11, of which waited for: 3 -> 3; matrix products, arithmetic and copies ran while one was open for 0% -> 0% of each run, Pallas kernels for 29% -> 30%
where the time goes in v21:
time: 28.8 us; the launch traced here: 28.6 us
  starting transfers between devices  13.6 us (47%)
  Pallas kernels  11 us (38%)
  waiting for transfers between devices  3.75 us (13%)
    ppermute x11, starting transfers between devices, swapped(): return lax.ppermute(value, 'dp', perm)  13.6 us
    pallas_call x1, Pallas kernels, project(): pl.pallas_call(project_kernel, out_shape=(jax.ShapeDtypeStruct((factor, t...  5.98 us
    ppermute x11, waiting for transfers between devices, swapped(): return lax.ppermute(value, 'dp', perm)  3.75 us
    pallas_call x1, Pallas kernels, precondition(): pl.pallas_call(functools.partial(precondition_kernel, tok_total, n_terms)...  2.68 us
    pallas_call x1, Pallas kernels, score(): pl.pallas_call(functools.partial(score_kernel, size, n_pieces), out_shape...  2.39 us
  transfers between devices with their start and end apart: 11, of which 3 were waited for; matrix products, arithmetic and copies ran while one was open for 0% of the time, Pallas kernels for 30%

profile of v21, /device:TPU:0, one launch (start us, length us, event | category | flops | bytes accessed | tf_op | source)
XLA Modules:
  0.0 28.6 jit_solution(16145499385012422270)
XLA Ops:
  0.0 4.0 %collective-permute-start.1 = (bf16[8,4096]{1,0:T(8,128)(2,1)}, bf16[8,4096]{1,0:T(8,128)(2,1)S(1)}, u32[]{:S(2)}, u32[]{:S(2)}) collective-permute-start(bf16[8,4096]{1,0:T(8,128)(2,1)} %param.9), channel_id=1, source_target_pairs={{0,8},{1,9},{2,10},{3,11},{4,12},{5,13},{6,14},{7,15},{8,0},{9,1},... | collective-permute-start | bytes 196616 | tf_op jit(solution)/shard_map/ppermute | solution.py:328
  4.0 1.3 %collective-permute-start = (bf16[8,4096]{1,0:T(8,128)(2,1)}, bf16[8,4096]{1,0:T(8,128)(2,1)S(1)}, u32[]{:S(2)}, u32[]{:S(2)}) collective-permute-start(bf16[8,4096]{1,0:T(8,128)(2,1)} %param.9), channel_id=1, source_target_pairs={{0,12},{1,13},{2,14},{3,15},{4,8},{5,9},{6,10},{7,11},{8,4},{9,5},... | collective-permute-start | bytes 196616 | tf_op jit(solution)/shard_map/ppermute | solution.py:328
  5.4 0.2 collective-permute-start.2
  5.6 6.0 %project.1 = (f32[64,512]{1,0:T(8,128)S(1)}, f32[64,512]{1,0:T(8,128)S(1)}, f32[40,128]{1,0:T(8,128)S(1)}) custom-call(bf16[512,4096]{1,0:T(8,128)(2,1)} %acts.1, bf16[512,4096]{1,0:T(8,128)(2,1)} %grads.1, bf16[64,4096]{1,0:T(8,128)(2,1)} %bitcast.2, bf16[64,4096]{1,0:T(8,128)(2,1)} %bitcast.3), custom_call_target="tpu_custom_call" | custom-call | flops 536870912 | bytes 8388608 | tf_op jit(solution)/shard_map/project/pallas_call | solution.py:124
  11.6 0.0 collective-permute-done.1
  11.6 0.0 collective-permute-done
  11.6 0.0 collective-permute-done.2
  11.6 0.5 %collective-permute-start.6 = (f32[40,128]{1,0:T(8,128)S(1)}, f32[40,128]{1,0:T(8,128)S(1)}, u32[]{:S(2)}, u32[]{:S(2)}) collective-permute-start(f32[40,128]{1,0:T(8,128)S(1)} %get-tuple-element.24), channel_id=1, source_target_pairs={{0,3},{1,2},{2,1},{3,0},{4,7},{5,6},{6,5},{7,4},{8,11},{9,10},{10,... | collective-permute-start | bytes 61448 | tf_op jit(solution)/shard_map/ppermute | solution.py:328
  12.1 1.2 %collective-permute-start.5 = (f32[40,128]{1,0:T(8,128)S(1)}, f32[40,128]{1,0:T(8,128)S(1)}, u32[]{:S(2)}, u32[]{:S(2)}) collective-permute-start(f32[40,128]{1,0:T(8,128)S(1)} %get-tuple-element.24), channel_id=1, source_target_pairs={{0,2},{1,3},{2,0},{3,1},{4,6},{5,7},{6,4},{7,5},{8,10},{9,11},{10,... | collective-permute-start | bytes 61448 | tf_op jit(solution)/shard_map/ppermute | solution.py:328
  13.3 0.3 collective-permute-start.4
  13.6 1.6 %collective-permute-start.3 = (bf16[32,4096]{1,0:T(8,128)(2,1)S(1)}, bf16[32,4096]{1,0:T(8,128)(2,1)S(1)}, u32[]{:S(2)}, u32[]{:S(2)}) collective-permute-start(bf16[32,4096]{1,0:T(8,128)(2,1)S(1)} %constant_dynamic-update-slice_fusion), channel_id=1, source_target_pairs={{0,2},{1,3},{2,0},{3,1},{4,6},{5,7},{6,4},{7,5},{8,10},{9,11},{10,... | collective-permute-start | bytes 786440 | tf_op jit(solution)/shard_map/ppermute | solution.py:328
  15.2 0.0 collective-permute-done.6
  15.2 0.7 %collective-permute-done.5 = f32[40,128]{1,0:T(8,128)S(1)} collective-permute-done((f32[40,128]{1,0:T(8,128)S(1)}, f32[40,128]{1,0:T(8,128)S(1)}, u32[]{:S(2)}, u32[]{:S(2)}) %collective-permute-start.5) | collective-permute-done | bytes 20512 | tf_op jit(solution)/shard_map/ppermute | solution.py:328
  15.9 0.0 collective-permute-done.4
  15.9 2.7 %collective-permute-start.9 = (f32[40,128]{1,0:T(8,128)S(1)}, f32[40,128]{1,0:T(8,128)S(1)}, u32[]{:S(2)}, u32[]{:S(2)}) collective-permute-start(f32[40,128]{1,0:T(8,128)S(1)} %add_add_fusion.refs_0_), channel_id=1, source_target_pairs={{0,12},{1,13},{2,14},{3,15},{4,8},{5,9},{6,10},{7,11},{8,4},{9,5},... | collective-permute-start | bytes 61448 | tf_op jit(solution)/shard_map/ppermute | solution.py:328
  18.6 0.3 %collective-permute-start.8 = (f32[40,128]{1,0:T(8,128)S(1)}, f32[40,128]{1,0:T(8,128)S(1)}, u32[]{:S(2)}, u32[]{:S(2)}) collective-permute-start(f32[40,128]{1,0:T(8,128)S(1)} %add_add_fusion.refs_0_), channel_id=1, source_target_pairs={{0,8},{1,9},{2,10},{3,11},{4,12},{5,13},{6,14},{7,15},{8,0},{9,1},... | collective-permute-start | bytes 61448 | tf_op jit(solution)/shard_map/ppermute | solution.py:328
  19.0 1.4 %collective-permute-start.7 = (f32[40,128]{1,0:T(8,128)S(1)}, f32[40,128]{1,0:T(8,128)S(1)}, u32[]{:S(2)}, u32[]{:S(2)}) collective-permute-start(f32[40,128]{1,0:T(8,128)S(1)} %add_add_fusion.refs_0_), channel_id=1, source_target_pairs={{0,4},{1,5},{2,6},{3,7},{4,0},{5,1},{6,2},{7,3},{8,12},{9,13},{10,... | collective-permute-start | bytes 61448 | tf_op jit(solution)/shard_map/ppermute | solution.py:328
  20.4 1.2 %collective-permute-done.9.refs_3_ = f32[40,128]{1,0:T(8,128)S(1)} collective-permute-done((f32[40,128]{1,0:T(8,128)S(1)}, f32[40,128]{1,0:T(8,128)S(1)}, u32[]{:S(2)}, u32[]{:S(2)}) %collective-permute-start.9) | collective-permute-done | bytes 20512 | tf_op jit(solution)/shard_map/ppermute | solution.py:328
  21.6 1.8 %collective-permute-done.8.refs_2_ = f32[40,128]{1,0:T(8,128)S(1)} collective-permute-done((f32[40,128]{1,0:T(8,128)S(1)}, f32[40,128]{1,0:T(8,128)S(1)}, u32[]{:S(2)}, u32[]{:S(2)}) %collective-permute-start.8) | collective-permute-done | bytes 20512 | tf_op jit(solution)/shard_map/ppermute | solution.py:328
  23.4 0.0 collective-permute-done.7.refs_1_
  23.4 0.0 collective-permute-done.3
  23.5 0.1 collective-permute-start.10
  23.5 2.7 %precondition.1.moved = f32[128,512]{1,0:T(8,128)S(1)} custom-call(f32[40,128]{1,0:T(8,128)S(1)} %add_add_fusion.refs_0_, f32[40,128]{1,0:T(8,128)S(1)} %collective-permute-done.7.refs_1_, f32[40,128]{1,0:T(8,128)S(1)} %collective-permute-done.8.refs_2_, f32[40,128]{1,0:T(8,128)S(1)} %collective-permute-done.9.refs_3_, ...), custom_call_target="tpu_custom_call" | custom-call | flops 3355443200 | bytes 524288 | tf_op jit(solution)/shard_map/precondition/pallas_call | solution.py:227
  26.2 2.4 %score.1 = f32[512,128]{1,0:T(8,128)} custom-call(f32[128,512]{1,0:T(8,128)S(1)} %precondition.1.moved, bf16[64,4096]{1,0:T(8,128)(2,1)S(1)} %constant_dynamic-update-slice_fusion.4.refs_0_, bf16[64,4096]{1,0:T(8,128)(2,1)S(1)} %collective-permute-done.10.refs_1_), custom_call_target="tpu_custom_call" | custom-call | tf_op jit(solution)/shard_map/score/pallas_call | solution.py:288
  (10 shorter events, 0.1 us)
Async XLA Ops:
  0.0 11.6 %collective-permute-start.1 = (bf16[8,4096]{1,0:T(8,128)(2,1)}, bf16[8,4096]{1,0:T(8,128)(2,1)S(1)}, u32[]{:S(2)}, u32[]{:S(2)}) collective-permute-start(bf16[8,4096]{1,0:T(8,128)(2,1)} %param.9), channel_id=1, source_target_pairs={{0,8},{1,9},{2,10},{3,11},{4,12},{5,13},{6,14},{7,15},{8,0},{9,1},... | collective-permute-start | bytes 196616 | tf_op jit(solution)/shard_map/ppermute | solution.py:328
  4.0 7.6 %collective-permute-start = (bf16[8,4096]{1,0:T(8,128)(2,1)}, bf16[8,4096]{1,0:T(8,128)(2,1)S(1)}, u32[]{:S(2)}, u32[]{:S(2)}) collective-permute-start(bf16[8,4096]{1,0:T(8,128)(2,1)} %param.9), channel_id=1, source_target_pairs={{0,12},{1,13},{2,14},{3,15},{4,8},{5,9},{6,10},{7,11},{8,4},{9,5},... | collective-permute-start | bytes 196616 | tf_op jit(solution)/shard_map/ppermute | solution.py:328
  5.4 6.2 %collective-permute-start.2 = (bf16[8,4096]{1,0:T(8,128)(2,1)}, bf16[8,4096]{1,0:T(8,128)(2,1)S(1)}, u32[]{:S(2)}, u32[]{:S(2)}) collective-permute-start(bf16[8,4096]{1,0:T(8,128)(2,1)} %param.9), channel_id=1, source_target_pairs={{0,4},{1,5},{2,6},{3,7},{4,0},{5,1},{6,2},{7,3},{8,12},{9,13},{10,... | collective-permute-start | bytes 196616 | tf_op jit(solution)/shard_map/ppermute | solution.py:328
  5.6 7.9 %copy-start = (bf16[8,4096]{1,0:T(8,128)(2,1)S(1)}, bf16[8,4096]{1,0:T(8,128)(2,1)}, u32[]{:S(2)}) copy-start(bf16[8,4096]{1,0:T(8,128)(2,1)} %param.9) | copy-start | bytes 196612
  11.6 3.6 %collective-permute-start.6 = (f32[40,128]{1,0:T(8,128)S(1)}, f32[40,128]{1,0:T(8,128)S(1)}, u32[]{:S(2)}, u32[]{:S(2)}) collective-permute-start(f32[40,128]{1,0:T(8,128)S(1)} %get-tuple-element.24), channel_id=1, source_target_pairs={{0,3},{1,2},{2,1},{3,0},{4,7},{5,6},{6,5},{7,4},{8,11},{9,10},{10,... | collective-permute-start | bytes 61448 | tf_op jit(solution)/shard_map/ppermute | solution.py:328
  12.1 3.8 %collective-permute-start.5 = (f32[40,128]{1,0:T(8,128)S(1)}, f32[40,128]{1,0:T(8,128)S(1)}, u32[]{:S(2)}, u32[]{:S(2)}) collective-permute-start(f32[40,128]{1,0:T(8,128)S(1)} %get-tuple-element.24), channel_id=1, source_target_pairs={{0,2},{1,3},{2,0},{3,1},{4,6},{5,7},{6,4},{7,5},{8,10},{9,11},{10,... | collective-permute-start | bytes 61448 | tf_op jit(solution)/shard_map/ppermute | solution.py:328
  13.3 2.6 %collective-permute-start.4 = (f32[40,128]{1,0:T(8,128)S(1)}, f32[40,128]{1,0:T(8,128)S(1)}, u32[]{:S(2)}, u32[]{:S(2)}) collective-permute-start(f32[40,128]{1,0:T(8,128)S(1)} %get-tuple-element.24), channel_id=1, source_target_pairs={{0,1},{1,0},{2,3},{3,2},{4,5},{5,4},{6,7},{7,6},{8,9},{9,8},{10,11... | collective-permute-start | bytes 61448 | tf_op jit(solution)/shard_map/ppermute | solution.py:328
  13.6 9.8 %collective-permute-start.3 = (bf16[32,4096]{1,0:T(8,128)(2,1)S(1)}, bf16[32,4096]{1,0:T(8,128)(2,1)S(1)}, u32[]{:S(2)}, u32[]{:S(2)}) collective-permute-start(bf16[32,4096]{1,0:T(8,128)(2,1)S(1)} %constant_dynamic-update-slice_fusion), channel_id=1, source_target_pairs={{0,2},{1,3},{2,0},{3,1},{4,6},{5,7},{6,4},{7,5},{8,10},{9,11},{10,... | collective-permute-start | bytes 786440 | tf_op jit(solution)/shard_map/ppermute | solution.py:328
  15.9 5.7 %collective-permute-start.9 = (f32[40,128]{1,0:T(8,128)S(1)}, f32[40,128]{1,0:T(8,128)S(1)}, u32[]{:S(2)}, u32[]{:S(2)}) collective-permute-start(f32[40,128]{1,0:T(8,128)S(1)} %add_add_fusion.refs_0_), channel_id=1, source_target_pairs={{0,12},{1,13},{2,14},{3,15},{4,8},{5,9},{6,10},{7,11},{8,4},{9,5},... | collective-permute-start | bytes 61448 | tf_op jit(solution)/shard_map/ppermute | solution.py:328
  18.6 4.8 %collective-permute-start.8 = (f32[40,128]{1,0:T(8,128)S(1)}, f32[40,128]{1,0:T(8,128)S(1)}, u32[]{:S(2)}, u32[]{:S(2)}) collective-permute-start(f32[40,128]{1,0:T(8,128)S(1)} %add_add_fusion.refs_0_), channel_id=1, source_target_pairs={{0,8},{1,9},{2,10},{3,11},{4,12},{5,13},{6,14},{7,15},{8,0},{9,1},... | collective-permute-start | bytes 61448 | tf_op jit(solution)/shard_map/ppermute | solution.py:328
  19.0 4.5 %collective-permute-start.7 = (f32[40,128]{1,0:T(8,128)S(1)}, f32[40,128]{1,0:T(8,128)S(1)}, u32[]{:S(2)}, u32[]{:S(2)}) collective-permute-start(f32[40,128]{1,0:T(8,128)S(1)} %add_add_fusion.refs_0_), channel_id=1, source_target_pairs={{0,4},{1,5},{2,6},{3,7},{4,0},{5,1},{6,2},{7,3},{8,12},{9,13},{10,... | collective-permute-start | bytes 61448 | tf_op jit(solution)/shard_map/ppermute | solution.py:328
  23.5 2.8 %collective-permute-start.10 = (bf16[64,4096]{1,0:T(8,128)(2,1)S(1)}, bf16[64,4096]{1,0:T(8,128)(2,1)S(1)}, u32[]{:S(2)}, u32[]{:S(2)}) collective-permute-start(bf16[64,4096]{1,0:T(8,128)(2,1)S(1)} %constant_dynamic-update-slice_fusion.4.refs_0_), channel_id=1, source_target_pairs={{0,1},{1,0},{2,3},{3,2},{4,5},{5,4},{6,7},{7,6},{8,9},{9,8},{10,11... | collective-permute-start | bytes 1572872 | tf_op jit(solution)/shard_map/ppermute | solution.py:328

commit v22 on v20

--- a/solution.py
+++ b/solution.py
@@ -71,11 +71,10 @@
     ]
     queue = [weight_copies[0], *tok_copies[0], *tok_copies[1]]
     queue.insert(3, weight_copies[1])
-    queue = [(copy, at % 2) for at, copy in enumerate(queue)]
 
     def start_next(many):
-        for copy, lane in queue[:many]:
-            copy.start(priority=lane)
+        for copy in queue[:many]:
+            copy.start()
         del queue[:many]
 
     def turned(at):
@@ -334,16 +333,16 @@
     owners = [me]
     for at, (stride, radix) in enumerate(gather_stages(size)):
         digit = lax.rem(lax.div(me, stride), radix)
-        shifts = [0, *(range(radix - 1, 0, -1) if at == 0 else range(1, radix))]
+        shifts = [0, *range(2, radix), 1] if at == 0 else range(radix)
         back = [shift if radix & (radix - 1) == 0 else (radix - shift) % radix for shift in shifts]
         steps = [(partner(digit, radix, shift) - digit) * stride for shift in back]
         owners = [owner + step for step in steps for owner in owners]
     return owners
 
 
-def exchanged(held, size, stride, radix, backwards=False):
+def exchanged(held, size, stride, radix, near_last=False):
     mine = held[0] if len(held) == 1 else jnp.concatenate(held, axis=0)
-    shifts = range(radix - 1, 0, -1) if backwards else range(1, radix)
+    shifts = [*range(2, radix), 1] if near_last else range(1, radix)
     return [mine] + [swapped(mine, size, stride, radix, shift) for shift in shifts]
 
 
@@ -353,7 +352,7 @@
     far, near, core = gather_stages(size)
     first, second = sum_rounds(size)
 
-    pieces = exchanged([queries], size, *far, backwards=True)
+    pieces = exchanged([queries], size, *far, near_last=True)
     act_t, grad_t, own = project(acts, grads, proj_act, proj_grad)
     *pieces, own = lax.optimization_barrier((*pieces, own))
     pieces = exchanged(pieces, size, *near)

time: 28.5 us -> 29.3 us (1.028)
  waiting for transfers between devices: 3.76 us -> 4.31 us
  starting transfers between devices: 13.6 us -> 13.9 us
    ppermute x11, waiting for transfers between devices: 3.76 us -> 4.31 us  [swapped(): return lax.ppermute(value, 'dp', perm)]
where the time goes in v22:
time: 29.3 us; the launch traced here: 29.1 us
  starting transfers between devices  13.9 us (47%)
  Pallas kernels  10.7 us (37%)
  waiting for transfers between devices  4.31 us (15%)
    ppermute x11, starting transfers between devices, swapped(): return lax.ppermute(value, 'dp', perm)  13.9 us
    pallas_call x1, Pallas kernels, project(): pl.pallas_call(project_kernel, out_shape=(jax.ShapeDtypeStruct((factor, t...  5.67 us
    ppermute x11, waiting for transfers between devices, swapped(): return lax.ppermute(value, 'dp', perm)  4.31 us
    pallas_call x1, Pallas kernels, precondition(): pl.pallas_call(functools.partial(precondition_kernel, tok_total, n_terms)...  2.67 us
    pallas_call x1, Pallas kernels, score(): pl.pallas_call(functools.partial(score_kernel, size, n_pieces), out_shape...  2.39 us
  transfers between devices with their start and end apart: 11, of which 3 were waited for; matrix products, arithmetic and copies ran while one was open for 0% of the time, Pallas kernels for 29%

profile of v22, /device:TPU:0, one launch (start us, length us, event | category | flops | bytes accessed | tf_op | source)
XLA Modules:
  0.0 29.1 jit_solution(7117638148053531590)
XLA Ops:
  0.0 5.0 %collective-permute-start.1 = (bf16[8,4096]{1,0:T(8,128)(2,1)}, bf16[8,4096]{1,0:T(8,128)(2,1)S(1)}, u32[]{:S(2)}, u32[]{:S(2)}) collective-permute-start(bf16[8,4096]{1,0:T(8,128)(2,1)} %param.9), channel_id=1, source_target_pairs={{0,12},{1,13},{2,14},{3,15},{4,8},{5,9},{6,10},{7,11},{8,4},{9,5},... | collective-permute-start | bytes 196616 | tf_op jit(solution)/shard_map/ppermute | solution.py:329
  5.0 0.0 collective-permute-start
  5.1 0.6 %collective-permute-start.2 = (bf16[8,4096]{1,0:T(8,128)(2,1)}, bf16[8,4096]{1,0:T(8,128)(2,1)S(1)}, u32[]{:S(2)}, u32[]{:S(2)}) collective-permute-start(bf16[8,4096]{1,0:T(8,128)(2,1)} %param.9), channel_id=1, source_target_pairs={{0,4},{1,5},{2,6},{3,7},{4,0},{5,1},{6,2},{7,3},{8,12},{9,13},{10,... | collective-permute-start | bytes 196616 | tf_op jit(solution)/shard_map/ppermute | solution.py:329
  5.6 5.7 %project.1 = (f32[64,512]{1,0:T(8,128)S(1)}, f32[64,512]{1,0:T(8,128)S(1)}, f32[40,128]{1,0:T(8,128)S(1)}) custom-call(bf16[512,4096]{1,0:T(8,128)(2,1)} %acts.1, bf16[512,4096]{1,0:T(8,128)(2,1)} %grads.1, bf16[64,4096]{1,0:T(8,128)(2,1)} %bitcast.2, bf16[64,4096]{1,0:T(8,128)(2,1)} %bitcast.3), custom_call_target="tpu_custom_call" | custom-call | flops 536870912 | bytes 8388608 | tf_op jit(solution)/shard_map/project/pallas_call | solution.py:125
  11.3 0.0 collective-permute-done.1
  11.3 0.0 collective-permute-done
  11.3 0.0 collective-permute-done.2
  11.3 0.5 %collective-permute-start.6 = (f32[40,128]{1,0:T(8,128)S(1)}, f32[40,128]{1,0:T(8,128)S(1)}, u32[]{:S(2)}, u32[]{:S(2)}) collective-permute-start(f32[40,128]{1,0:T(8,128)S(1)} %get-tuple-element.24), channel_id=1, source_target_pairs={{0,3},{1,2},{2,1},{3,0},{4,7},{5,6},{6,5},{7,4},{8,11},{9,10},{10,... | collective-permute-start | bytes 61448 | tf_op jit(solution)/shard_map/ppermute | solution.py:329
  11.8 1.4 %collective-permute-start.5 = (f32[40,128]{1,0:T(8,128)S(1)}, f32[40,128]{1,0:T(8,128)S(1)}, u32[]{:S(2)}, u32[]{:S(2)}) collective-permute-start(f32[40,128]{1,0:T(8,128)S(1)} %get-tuple-element.24), channel_id=1, source_target_pairs={{0,2},{1,3},{2,0},{3,1},{4,6},{5,7},{6,4},{7,5},{8,10},{9,11},{10,... | collective-permute-start | bytes 61448 | tf_op jit(solution)/shard_map/ppermute | solution.py:329
  13.2 0.1 collective-permute-start.4
  13.3 1.8 %collective-permute-start.3 = (bf16[32,4096]{1,0:T(8,128)(2,1)S(1)}, bf16[32,4096]{1,0:T(8,128)(2,1)S(1)}, u32[]{:S(2)}, u32[]{:S(2)}) collective-permute-start(bf16[32,4096]{1,0:T(8,128)(2,1)S(1)} %constant_dynamic-update-slice_fusion), channel_id=1, source_target_pairs={{0,2},{1,3},{2,0},{3,1},{4,6},{5,7},{6,4},{7,5},{8,10},{9,11},{10,... | collective-permute-start | bytes 786440 | tf_op jit(solution)/shard_map/ppermute | solution.py:329
  15.1 0.0 collective-permute-done.6
  15.1 0.5 %collective-permute-done.5 = f32[40,128]{1,0:T(8,128)S(1)} collective-permute-done((f32[40,128]{1,0:T(8,128)S(1)}, f32[40,128]{1,0:T(8,128)S(1)}, u32[]{:S(2)}, u32[]{:S(2)}) %collective-permute-start.5) | collective-permute-done | bytes 20512 | tf_op jit(solution)/shard_map/ppermute | solution.py:329
  15.6 0.0 collective-permute-done.4
  15.6 3.6 %collective-permute-start.9 = (f32[40,128]{1,0:T(8,128)S(1)}, f32[40,128]{1,0:T(8,128)S(1)}, u32[]{:S(2)}, u32[]{:S(2)}) collective-permute-start(f32[40,128]{1,0:T(8,128)S(1)} %add_add_fusion.refs_0_), channel_id=1, source_target_pairs={{0,12},{1,13},{2,14},{3,15},{4,8},{5,9},{6,10},{7,11},{8,4},{9,5},... | collective-permute-start | bytes 61448 | tf_op jit(solution)/shard_map/ppermute | solution.py:329
  19.2 0.0 collective-permute-start.8
  19.2 0.9 %collective-permute-start.7 = (f32[40,128]{1,0:T(8,128)S(1)}, f32[40,128]{1,0:T(8,128)S(1)}, u32[]{:S(2)}, u32[]{:S(2)}) collective-permute-start(f32[40,128]{1,0:T(8,128)S(1)} %add_add_fusion.refs_0_), channel_id=1, source_target_pairs={{0,4},{1,5},{2,6},{3,7},{4,0},{5,1},{6,2},{7,3},{8,12},{9,13},{10,... | collective-permute-start | bytes 61448 | tf_op jit(solution)/shard_map/ppermute | solution.py:329
  20.1 1.2 %collective-permute-done.9.refs_3_ = f32[40,128]{1,0:T(8,128)S(1)} collective-permute-done((f32[40,128]{1,0:T(8,128)S(1)}, f32[40,128]{1,0:T(8,128)S(1)}, u32[]{:S(2)}, u32[]{:S(2)}) %collective-permute-start.9) | collective-permute-done | bytes 20512 | tf_op jit(solution)/shard_map/ppermute | solution.py:329
  21.3 2.6 %collective-permute-done.8.refs_2_ = f32[40,128]{1,0:T(8,128)S(1)} collective-permute-done((f32[40,128]{1,0:T(8,128)S(1)}, f32[40,128]{1,0:T(8,128)S(1)}, u32[]{:S(2)}, u32[]{:S(2)}) %collective-permute-start.8) | collective-permute-done | bytes 20512 | tf_op jit(solution)/shard_map/ppermute | solution.py:329
  23.9 0.0 collective-permute-done.7.refs_1_
  23.9 0.0 collective-permute-done.3
  23.9 0.1 collective-permute-start.10
  24.0 2.7 %precondition.1.moved = f32[128,512]{1,0:T(8,128)S(1)} custom-call(f32[40,128]{1,0:T(8,128)S(1)} %add_add_fusion.refs_0_, f32[40,128]{1,0:T(8,128)S(1)} %collective-permute-done.7.refs_1_, f32[40,128]{1,0:T(8,128)S(1)} %collective-permute-done.8.refs_2_, f32[40,128]{1,0:T(8,128)S(1)} %collective-permute-done.9.refs_3_, ...), custom_call_target="tpu_custom_call" | custom-call | flops 3355443200 | bytes 524288 | tf_op jit(solution)/shard_map/precondition/pallas_call | solution.py:228
  26.7 2.4 %score.1 = f32[512,128]{1,0:T(8,128)} custom-call(f32[128,512]{1,0:T(8,128)S(1)} %precondition.1.moved, bf16[64,4096]{1,0:T(8,128)(2,1)S(1)} %constant_dynamic-update-slice_fusion.4.refs_0_, bf16[64,4096]{1,0:T(8,128)(2,1)S(1)} %collective-permute-done.10.refs_1_), custom_call_target="tpu_custom_call" | custom-call | tf_op jit(solution)/shard_map/score/pallas_call | solution.py:289
  (10 shorter events, 0.1 us)
Async XLA Ops:
  0.0 11.3 %collective-permute-start.1 = (bf16[8,4096]{1,0:T(8,128)(2,1)}, bf16[8,4096]{1,0:T(8,128)(2,1)S(1)}, u32[]{:S(2)}, u32[]{:S(2)}) collective-permute-start(bf16[8,4096]{1,0:T(8,128)(2,1)} %param.9), channel_id=1, source_target_pairs={{0,12},{1,13},{2,14},{3,15},{4,8},{5,9},{6,10},{7,11},{8,4},{9,5},... | collective-permute-start | bytes 196616 | tf_op jit(solution)/shard_map/ppermute | solution.py:329
  5.0 6.3 %collective-permute-start = (bf16[8,4096]{1,0:T(8,128)(2,1)}, bf16[8,4096]{1,0:T(8,128)(2,1)S(1)}, u32[]{:S(2)}, u32[]{:S(2)}) collective-permute-start(bf16[8,4096]{1,0:T(8,128)(2,1)} %param.9), channel_id=1, source_target_pairs={{0,8},{1,9},{2,10},{3,11},{4,12},{5,13},{6,14},{7,15},{8,0},{9,1},... | collective-permute-start | bytes 196616 | tf_op jit(solution)/shard_map/ppermute | solution.py:329
  5.1 6.3 %collective-permute-start.2 = (bf16[8,4096]{1,0:T(8,128)(2,1)}, bf16[8,4096]{1,0:T(8,128)(2,1)S(1)}, u32[]{:S(2)}, u32[]{:S(2)}) collective-permute-start(bf16[8,4096]{1,0:T(8,128)(2,1)} %param.9), channel_id=1, source_target_pairs={{0,4},{1,5},{2,6},{3,7},{4,0},{5,1},{6,2},{7,3},{8,12},{9,13},{10,... | collective-permute-start | bytes 196616 | tf_op jit(solution)/shard_map/ppermute | solution.py:329
  5.6 7.7 %copy-start = (bf16[8,4096]{1,0:T(8,128)(2,1)S(1)}, bf16[8,4096]{1,0:T(8,128)(2,1)}, u32[]{:S(2)}) copy-start(bf16[8,4096]{1,0:T(8,128)(2,1)} %param.9) | copy-start | bytes 196612
  11.3 3.8 %collective-permute-start.6 = (f32[40,128]{1,0:T(8,128)S(1)}, f32[40,128]{1,0:T(8,128)S(1)}, u32[]{:S(2)}, u32[]{:S(2)}) collective-permute-start(f32[40,128]{1,0:T(8,128)S(1)} %get-tuple-element.24), channel_id=1, source_target_pairs={{0,3},{1,2},{2,1},{3,0},{4,7},{5,6},{6,5},{7,4},{8,11},{9,10},{10,... | collective-permute-start | bytes 61448 | tf_op jit(solution)/shard_map/ppermute | solution.py:329
  11.8 3.8 %collective-permute-start.5 = (f32[40,128]{1,0:T(8,128)S(1)}, f32[40,128]{1,0:T(8,128)S(1)}, u32[]{:S(2)}, u32[]{:S(2)}) collective-permute-start(f32[40,128]{1,0:T(8,128)S(1)} %get-tuple-element.24), channel_id=1, source_target_pairs={{0,2},{1,3},{2,0},{3,1},{4,6},{5,7},{6,4},{7,5},{8,10},{9,11},{10,... | collective-permute-start | bytes 61448 | tf_op jit(solution)/shard_map/ppermute | solution.py:329
  13.2 2.4 %collective-permute-start.4 = (f32[40,128]{1,0:T(8,128)S(1)}, f32[40,128]{1,0:T(8,128)S(1)}, u32[]{:S(2)}, u32[]{:S(2)}) collective-permute-start(f32[40,128]{1,0:T(8,128)S(1)} %get-tuple-element.24), channel_id=1, source_target_pairs={{0,1},{1,0},{2,3},{3,2},{4,5},{5,4},{6,7},{7,6},{8,9},{9,8},{10,11... | collective-permute-start | bytes 61448 | tf_op jit(solution)/shard_map/ppermute | solution.py:329
  13.3 10.6 %collective-permute-start.3 = (bf16[32,4096]{1,0:T(8,128)(2,1)S(1)}, bf16[32,4096]{1,0:T(8,128)(2,1)S(1)}, u32[]{:S(2)}, u32[]{:S(2)}) collective-permute-start(bf16[32,4096]{1,0:T(8,128)(2,1)S(1)} %constant_dynamic-update-slice_fusion), channel_id=1, source_target_pairs={{0,2},{1,3},{2,0},{3,1},{4,6},{5,7},{6,4},{7,5},{8,10},{9,11},{10,... | collective-permute-start | bytes 786440 | tf_op jit(solution)/shard_map/ppermute | solution.py:329
  15.6 5.6 %collective-permute-start.9 = (f32[40,128]{1,0:T(8,128)S(1)}, f32[40,128]{1,0:T(8,128)S(1)}, u32[]{:S(2)}, u32[]{:S(2)}) collective-permute-start(f32[40,128]{1,0:T(8,128)S(1)} %add_add_fusion.refs_0_), channel_id=1, source_target_pairs={{0,12},{1,13},{2,14},{3,15},{4,8},{5,9},{6,10},{7,11},{8,4},{9,5},... | collective-permute-start | bytes 61448 | tf_op jit(solution)/shard_map/ppermute | solution.py:329
  19.2 4.7 %collective-permute-start.8 = (f32[40,128]{1,0:T(8,128)S(1)}, f32[40,128]{1,0:T(8,128)S(1)}, u32[]{:S(2)}, u32[]{:S(2)}) collective-permute-start(f32[40,128]{1,0:T(8,128)S(1)} %add_add_fusion.refs_0_), channel_id=1, source_target_pairs={{0,8},{1,9},{2,10},{3,11},{4,12},{5,13},{6,14},{7,15},{8,0},{9,1},... | collective-permute-start | bytes 61448 | tf_op jit(solution)/shard_map/ppermute | solution.py:329
  19.2 4.7 %collective-permute-start.7 = (f32[40,128]{1,0:T(8,128)S(1)}, f32[40,128]{1,0:T(8,128)S(1)}, u32[]{:S(2)}, u32[]{:S(2)}) collective-permute-start(f32[40,128]{1,0:T(8,128)S(1)} %add_add_fusion.refs_0_), channel_id=1, source_target_pairs={{0,4},{1,5},{2,6},{3,7},{4,0},{5,1},{6,2},{7,3},{8,12},{9,13},{10,... | collective-permute-start | bytes 61448 | tf_op jit(solution)/shard_map/ppermute | solution.py:329
  23.9 2.8 %collective-permute-start.10 = (bf16[64,4096]{1,0:T(8,128)(2,1)S(1)}, bf16[64,4096]{1,0:T(8,128)(2,1)S(1)}, u32[]{:S(2)}, u32[]{:S(2)}) collective-permute-start(bf16[64,4096]{1,0:T(8,128)(2,1)S(1)} %constant_dynamic-update-slice_fusion.4.refs_0_), channel_id=1, source_target_pairs={{0,1},{1,0},{2,3},{3,2},{4,5},{5,4},{6,7},{7,6},{8,9},{9,8},{10,11... | collective-permute-start | bytes 1572872 | tf_op jit(solution)/shard_map/ppermute | solution.py:329

commit v23 on v22

--- a/solution.py
+++ b/solution.py
@@ -333,17 +333,16 @@
     owners = [me]
     for at, (stride, radix) in enumerate(gather_stages(size)):
         digit = lax.rem(lax.div(me, stride), radix)
-        shifts = [0, *range(2, radix), 1] if at == 0 else range(radix)
+        shifts = [0, *(range(radix - 1, 0, -1) if at == 0 else range(1, radix))]
         back = [shift if radix & (radix - 1) == 0 else (radix - shift) % radix for shift in shifts]
         steps = [(partner(digit, radix, shift) - digit) * stride for shift in back]
         owners = [owner + step for step in steps for owner in owners]
     return owners
 
 
-def exchanged(held, size, stride, radix, near_last=False):
+def exchanged(held, size, stride, radix, order=None):
     mine = held[0] if len(held) == 1 else jnp.concatenate(held, axis=0)
-    shifts = [*range(2, radix), 1] if near_last else range(1, radix)
-    return [mine] + [swapped(mine, size, stride, radix, shift) for shift in shifts]
+    return [mine] + [swapped(mine, size, stride, radix, shift) for shift in order or range(1, radix)]
 
 
 def on_device(acts, grads, proj_act, proj_grad, queries):
@@ -352,12 +351,12 @@
     far, near, core = gather_stages(size)
     first, second = sum_rounds(size)
 
-    pieces = exchanged([queries], size, *far, near_last=True)
+    pieces = exchanged([queries], size, *far, order=range(far[1] - 1, 0, -1))
     act_t, grad_t, own = project(acts, grads, proj_act, proj_grad)
     *pieces, own = lax.optimization_barrier((*pieces, own))
     pieces = exchanged(pieces, size, *near)
     own = functools.reduce(jnp.add, exchanged([own], size, *first))
-    terms = exchanged([own], size, *second)
+    terms = exchanged([own], size, *second, order=[*range(1, min(2, second[1])), *range(second[1] - 1, 1, -1)])
     *both, = lax.optimization_barrier((*pieces, *terms))
     pieces, terms = both[: len(pieces)], both[len(pieces) :]
     pieces = exchanged(pieces, size, *core)

time: 29.3 us -> 29.2 us (level)
  starting transfers between devices: 13.9 us -> 13.2 us
  waiting for transfers between devices: 4.31 us -> 4.92 us
    ppermute x11, starting transfers between devices: 13.9 us -> 13.2 us  [swapped(): return lax.ppermute(value, 'dp', perm)]
    ppermute x11, waiting for transfers between devices: 4.31 us -> 4.92 us  [swapped(): return lax.ppermute(value, 'dp', perm)]
where the time goes in v23:
time: 29.2 us; the launch traced here: 29 us
  starting transfers between devices  13.2 us (45%)
  Pallas kernels  10.7 us (37%)
  waiting for transfers between devices  4.92 us (17%)
    ppermute x11, starting transfers between devices, swapped(): return lax.ppermute(value, 'dp', perm)  13.2 us
    pallas_call x1, Pallas kernels, project(): pl.pallas_call(project_kernel, out_shape=(jax.ShapeDtypeStruct((factor, t...  5.67 us
    ppermute x11, waiting for transfers between devices, swapped(): return lax.ppermute(value, 'dp', perm)  4.92 us
    pallas_call x1, Pallas kernels, precondition(): pl.pallas_call(functools.partial(precondition_kernel, tok_total, n_terms)...  2.67 us
    pallas_call x1, Pallas kernels, score(): pl.pallas_call(functools.partial(score_kernel, size, n_pieces), out_shape...  2.39 us
  transfers between devices with their start and end apart: 11, of which 3 were waited for; matrix products, arithmetic and copies ran while one was open for 0% of the time, Pallas kernels for 29%

profile of v23, /device:TPU:0, one launch (start us, length us, event | category | flops | bytes accessed | tf_op | source)
XLA Modules:
  0.0 29.0 jit_solution(13800858224524339188)
XLA Ops:
  0.0 4.0 %collective-permute-start.1 = (bf16[8,4096]{1,0:T(8,128)(2,1)}, bf16[8,4096]{1,0:T(8,128)(2,1)S(1)}, u32[]{:S(2)}, u32[]{:S(2)}) collective-permute-start(bf16[8,4096]{1,0:T(8,128)(2,1)} %param.9), channel_id=1, source_target_pairs={{0,8},{1,9},{2,10},{3,11},{4,12},{5,13},{6,14},{7,15},{8,0},{9,1},... | collective-permute-start | bytes 196616 | tf_op jit(solution)/shard_map/ppermute | solution.py:329
  4.0 1.3 %collective-permute-start = (bf16[8,4096]{1,0:T(8,128)(2,1)}, bf16[8,4096]{1,0:T(8,128)(2,1)S(1)}, u32[]{:S(2)}, u32[]{:S(2)}) collective-permute-start(bf16[8,4096]{1,0:T(8,128)(2,1)} %param.9), channel_id=1, source_target_pairs={{0,12},{1,13},{2,14},{3,15},{4,8},{5,9},{6,10},{7,11},{8,4},{9,5},... | collective-permute-start | bytes 196616 | tf_op jit(solution)/shard_map/ppermute | solution.py:329
  5.4 0.2 collective-permute-start.2
  5.6 5.7 %project.1 = (f32[64,512]{1,0:T(8,128)S(1)}, f32[64,512]{1,0:T(8,128)S(1)}, f32[40,128]{1,0:T(8,128)S(1)}) custom-call(bf16[512,4096]{1,0:T(8,128)(2,1)} %acts.1, bf16[512,4096]{1,0:T(8,128)(2,1)} %grads.1, bf16[64,4096]{1,0:T(8,128)(2,1)} %bitcast.2, bf16[64,4096]{1,0:T(8,128)(2,1)} %bitcast.3), custom_call_target="tpu_custom_call" | custom-call | flops 536870912 | bytes 8388608 | tf_op jit(solution)/shard_map/project/pallas_call | solution.py:125
  11.3 0.0 collective-permute-done.1
  11.3 0.0 collective-permute-done
  11.3 0.0 collective-permute-done.2
  11.3 0.5 %collective-permute-start.6 = (f32[40,128]{1,0:T(8,128)S(1)}, f32[40,128]{1,0:T(8,128)S(1)}, u32[]{:S(2)}, u32[]{:S(2)}) collective-permute-start(f32[40,128]{1,0:T(8,128)S(1)} %get-tuple-element.24), channel_id=1, source_target_pairs={{0,3},{1,2},{2,1},{3,0},{4,7},{5,6},{6,5},{7,4},{8,11},{9,10},{10,... | collective-permute-start | bytes 61448 | tf_op jit(solution)/shard_map/ppermute | solution.py:329
  11.8 1.2 %collective-permute-start.5 = (f32[40,128]{1,0:T(8,128)S(1)}, f32[40,128]{1,0:T(8,128)S(1)}, u32[]{:S(2)}, u32[]{:S(2)}) collective-permute-start(f32[40,128]{1,0:T(8,128)S(1)} %get-tuple-element.24), channel_id=1, source_target_pairs={{0,2},{1,3},{2,0},{3,1},{4,6},{5,7},{6,4},{7,5},{8,10},{9,11},{10,... | collective-permute-start | bytes 61448 | tf_op jit(solution)/shard_map/ppermute | solution.py:329
  13.0 0.3 collective-permute-start.4
  13.3 1.6 %collective-permute-start.3 = (bf16[32,4096]{1,0:T(8,128)(2,1)S(1)}, bf16[32,4096]{1,0:T(8,128)(2,1)S(1)}, u32[]{:S(2)}, u32[]{:S(2)}) collective-permute-start(bf16[32,4096]{1,0:T(8,128)(2,1)S(1)} %constant_dynamic-update-slice_fusion), channel_id=1, source_target_pairs={{0,2},{1,3},{2,0},{3,1},{4,6},{5,7},{6,4},{7,5},{8,10},{9,11},{10,... | collective-permute-start | bytes 786440 | tf_op jit(solution)/shard_map/ppermute | solution.py:329
  14.9 0.0 collective-permute-done.6
  14.9 0.7 %collective-permute-done.5 = f32[40,128]{1,0:T(8,128)S(1)} collective-permute-done((f32[40,128]{1,0:T(8,128)S(1)}, f32[40,128]{1,0:T(8,128)S(1)}, u32[]{:S(2)}, u32[]{:S(2)}) %collective-permute-start.5) | collective-permute-done | bytes 20512 | tf_op jit(solution)/shard_map/ppermute | solution.py:329
  15.6 0.0 collective-permute-done.4
  15.6 2.6 %collective-permute-start.9 = (f32[40,128]{1,0:T(8,128)S(1)}, f32[40,128]{1,0:T(8,128)S(1)}, u32[]{:S(2)}, u32[]{:S(2)}) collective-permute-start(f32[40,128]{1,0:T(8,128)S(1)} %add_add_fusion.refs_0_), channel_id=1, source_target_pairs={{0,8},{1,9},{2,10},{3,11},{4,12},{5,13},{6,14},{7,15},{8,0},{9,1},... | collective-permute-start | bytes 61448 | tf_op jit(solution)/shard_map/ppermute | solution.py:329
  18.2 1.3 %collective-permute-start.8 = (f32[40,128]{1,0:T(8,128)S(1)}, f32[40,128]{1,0:T(8,128)S(1)}, u32[]{:S(2)}, u32[]{:S(2)}) collective-permute-start(f32[40,128]{1,0:T(8,128)S(1)} %add_add_fusion.refs_0_), channel_id=1, source_target_pairs={{0,12},{1,13},{2,14},{3,15},{4,8},{5,9},{6,10},{7,11},{8,4},{9,5},... | collective-permute-start | bytes 61448 | tf_op jit(solution)/shard_map/ppermute | solution.py:329
  19.6 0.0 collective-permute-start.7
  19.6 0.8 %collective-permute-done.9.refs_3_ = f32[40,128]{1,0:T(8,128)S(1)} collective-permute-done((f32[40,128]{1,0:T(8,128)S(1)}, f32[40,128]{1,0:T(8,128)S(1)}, u32[]{:S(2)}, u32[]{:S(2)}) %collective-permute-start.9) | collective-permute-done | bytes 20512 | tf_op jit(solution)/shard_map/ppermute | solution.py:329
  20.3 3.5 %collective-permute-done.8.refs_2_ = f32[40,128]{1,0:T(8,128)S(1)} collective-permute-done((f32[40,128]{1,0:T(8,128)S(1)}, f32[40,128]{1,0:T(8,128)S(1)}, u32[]{:S(2)}, u32[]{:S(2)}) %collective-permute-start.8) | collective-permute-done | bytes 20512 | tf_op jit(solution)/shard_map/ppermute | solution.py:329
  23.8 0.0 collective-permute-done.7.refs_1_
  23.8 0.1 collective-permute-start.10
  23.9 2.7 %precondition.1.moved = f32[128,512]{1,0:T(8,128)S(1)} custom-call(f32[40,128]{1,0:T(8,128)S(1)} %add_add_fusion.refs_0_, f32[40,128]{1,0:T(8,128)S(1)} %collective-permute-done.7.refs_1_, f32[40,128]{1,0:T(8,128)S(1)} %collective-permute-done.8.refs_2_, f32[40,128]{1,0:T(8,128)S(1)} %collective-permute-done.9.refs_3_, ...), custom_call_target="tpu_custom_call" | custom-call | flops 3355443200 | bytes 524288 | tf_op jit(solution)/shard_map/precondition/pallas_call | solution.py:228
  26.6 0.0 collective-permute-done.10.refs_1_
  26.6 2.4 %score.1 = f32[512,128]{1,0:T(8,128)} custom-call(f32[128,512]{1,0:T(8,128)S(1)} %precondition.1.moved, bf16[64,4096]{1,0:T(8,128)(2,1)S(1)} %constant_dynamic-update-slice_fusion.4.refs_0_, bf16[64,4096]{1,0:T(8,128)(2,1)S(1)} %collective-permute-done.10.refs_1_), custom_call_target="tpu_custom_call" | custom-call | tf_op jit(solution)/shard_map/score/pallas_call | solution.py:289
  (10 shorter events, 0.1 us)
Async XLA Ops:
  0.0 11.3 %collective-permute-start.1 = (bf16[8,4096]{1,0:T(8,128)(2,1)}, bf16[8,4096]{1,0:T(8,128)(2,1)S(1)}, u32[]{:S(2)}, u32[]{:S(2)}) collective-permute-start(bf16[8,4096]{1,0:T(8,128)(2,1)} %param.9), channel_id=1, source_target_pairs={{0,8},{1,9},{2,10},{3,11},{4,12},{5,13},{6,14},{7,15},{8,0},{9,1},... | collective-permute-start | bytes 196616 | tf_op jit(solution)/shard_map/ppermute | solution.py:329
  4.0 7.3 %collective-permute-start = (bf16[8,4096]{1,0:T(8,128)(2,1)}, bf16[8,4096]{1,0:T(8,128)(2,1)S(1)}, u32[]{:S(2)}, u32[]{:S(2)}) collective-permute-start(bf16[8,4096]{1,0:T(8,128)(2,1)} %param.9), channel_id=1, source_target_pairs={{0,12},{1,13},{2,14},{3,15},{4,8},{5,9},{6,10},{7,11},{8,4},{9,5},... | collective-permute-start | bytes 196616 | tf_op jit(solution)/shard_map/ppermute | solution.py:329
  5.4 5.9 %collective-permute-start.2 = (bf16[8,4096]{1,0:T(8,128)(2,1)}, bf16[8,4096]{1,0:T(8,128)(2,1)S(1)}, u32[]{:S(2)}, u32[]{:S(2)}) collective-permute-start(bf16[8,4096]{1,0:T(8,128)(2,1)} %param.9), channel_id=1, source_target_pairs={{0,4},{1,5},{2,6},{3,7},{4,0},{5,1},{6,2},{7,3},{8,12},{9,13},{10,... | collective-permute-start | bytes 196616 | tf_op jit(solution)/shard_map/ppermute | solution.py:329
  5.6 7.6 %copy-start = (bf16[8,4096]{1,0:T(8,128)(2,1)S(1)}, bf16[8,4096]{1,0:T(8,128)(2,1)}, u32[]{:S(2)}) copy-start(bf16[8,4096]{1,0:T(8,128)(2,1)} %param.9) | copy-start | bytes 196612
  11.3 3.6 %collective-permute-start.6 = (f32[40,128]{1,0:T(8,128)S(1)}, f32[40,128]{1,0:T(8,128)S(1)}, u32[]{:S(2)}, u32[]{:S(2)}) collective-permute-start(f32[40,128]{1,0:T(8,128)S(1)} %get-tuple-element.24), channel_id=1, source_target_pairs={{0,3},{1,2},{2,1},{3,0},{4,7},{5,6},{6,5},{7,4},{8,11},{9,10},{10,... | collective-permute-start | bytes 61448 | tf_op jit(solution)/shard_map/ppermute | solution.py:329
  11.8 3.8 %collective-permute-start.5 = (f32[40,128]{1,0:T(8,128)S(1)}, f32[40,128]{1,0:T(8,128)S(1)}, u32[]{:S(2)}, u32[]{:S(2)}) collective-permute-start(f32[40,128]{1,0:T(8,128)S(1)} %get-tuple-element.24), channel_id=1, source_target_pairs={{0,2},{1,3},{2,0},{3,1},{4,6},{5,7},{6,4},{7,5},{8,10},{9,11},{10,... | collective-permute-start | bytes 61448 | tf_op jit(solution)/shard_map/ppermute | solution.py:329
  13.0 2.6 %collective-permute-start.4 = (f32[40,128]{1,0:T(8,128)S(1)}, f32[40,128]{1,0:T(8,128)S(1)}, u32[]{:S(2)}, u32[]{:S(2)}) collective-permute-start(f32[40,128]{1,0:T(8,128)S(1)} %get-tuple-element.24), channel_id=1, source_target_pairs={{0,1},{1,0},{2,3},{3,2},{4,5},{5,4},{6,7},{7,6},{8,9},{9,8},{10,11... | collective-permute-start | bytes 61448 | tf_op jit(solution)/shard_map/ppermute | solution.py:329
  13.3 10.5 %collective-permute-start.3 = (bf16[32,4096]{1,0:T(8,128)(2,1)S(1)}, bf16[32,4096]{1,0:T(8,128)(2,1)S(1)}, u32[]{:S(2)}, u32[]{:S(2)}) collective-permute-start(bf16[32,4096]{1,0:T(8,128)(2,1)S(1)} %constant_dynamic-update-slice_fusion), channel_id=1, source_target_pairs={{0,2},{1,3},{2,0},{3,1},{4,6},{5,7},{6,4},{7,5},{8,10},{9,11},{10,... | collective-permute-start | bytes 786440 | tf_op jit(solution)/shard_map/ppermute | solution.py:329
  15.6 4.7 %collective-permute-start.9 = (f32[40,128]{1,0:T(8,128)S(1)}, f32[40,128]{1,0:T(8,128)S(1)}, u32[]{:S(2)}, u32[]{:S(2)}) collective-permute-start(f32[40,128]{1,0:T(8,128)S(1)} %add_add_fusion.refs_0_), channel_id=1, source_target_pairs={{0,8},{1,9},{2,10},{3,11},{4,12},{5,13},{6,14},{7,15},{8,0},{9,1},... | collective-permute-start | bytes 61448 | tf_op jit(solution)/shard_map/ppermute | solution.py:329
  18.2 5.6 %collective-permute-start.8 = (f32[40,128]{1,0:T(8,128)S(1)}, f32[40,128]{1,0:T(8,128)S(1)}, u32[]{:S(2)}, u32[]{:S(2)}) collective-permute-start(f32[40,128]{1,0:T(8,128)S(1)} %add_add_fusion.refs_0_), channel_id=1, source_target_pairs={{0,12},{1,13},{2,14},{3,15},{4,8},{5,9},{6,10},{7,11},{8,4},{9,5},... | collective-permute-start | bytes 61448 | tf_op jit(solution)/shard_map/ppermute | solution.py:329
  19.6 4.2 %collective-permute-start.7 = (f32[40,128]{1,0:T(8,128)S(1)}, f32[40,128]{1,0:T(8,128)S(1)}, u32[]{:S(2)}, u32[]{:S(2)}) collective-permute-start(f32[40,128]{1,0:T(8,128)S(1)} %add_add_fusion.refs_0_), channel_id=1, source_target_pairs={{0,4},{1,5},{2,6},{3,7},{4,0},{5,1},{6,2},{7,3},{8,12},{9,13},{10,... | collective-permute-start | bytes 61448 | tf_op jit(solution)/shard_map/ppermute | solution.py:329
  23.8 2.8 %collective-permute-start.10 = (bf16[64,4096]{1,0:T(8,128)(2,1)S(1)}, bf16[64,4096]{1,0:T(8,128)(2,1)S(1)}, u32[]{:S(2)}, u32[]{:S(2)}) collective-permute-start(bf16[64,4096]{1,0:T(8,128)(2,1)S(1)} %constant_dynamic-update-slice_fusion.4.refs_0_), channel_id=1, source_target_pairs={{0,1},{1,0},{2,3},{3,2},{4,5},{5,4},{6,7},{7,6},{8,9},{9,8},{10,11... | collective-permute-start | bytes 1572872 | tf_op jit(solution)/shard_map/ppermute | solution.py:329

commit v24 on v23

--- a/solution.py
+++ b/solution.py
@@ -356,7 +356,7 @@
     *pieces, own = lax.optimization_barrier((*pieces, own))
     pieces = exchanged(pieces, size, *near)
     own = functools.reduce(jnp.add, exchanged([own], size, *first))
-    terms = exchanged([own], size, *second, order=[*range(1, min(2, second[1])), *range(second[1] - 1, 1, -1)])
+    terms = exchanged([own], size, *second)
     *both, = lax.optimization_barrier((*pieces, *terms))
     pieces, terms = both[: len(pieces)], both[len(pieces) :]
     pieces = exchanged(pieces, size, *core)

time: 29.2 us -> 28.5 us (0.976)
  waiting for transfers between devices: 4.92 us -> 3.76 us
  starting transfers between devices: 13.2 us -> 13.6 us
    ppermute x11, waiting for transfers between devices: 4.92 us -> 3.76 us  [swapped(): return lax.ppermute(value, 'dp', perm)]
    ppermute x11, starting transfers between devices: 13.2 us -> 13.6 us  [swapped(): return lax.ppermute(value, 'dp', perm)]
  transfers between devices with their start and end apart: 11 -> 11, of which waited for: 3 -> 3; matrix products, arithmetic and copies ran while one was open for 0% -> 0% of each run, Pallas kernels for 29% -> 30%
where the time goes in v24:
time: 28.5 us; the launch traced here: 28.3 us
  starting transfers between devices  13.6 us (48%)
  Pallas kernels  10.8 us (38%)
  waiting for transfers between devices  3.76 us (13%)
    ppermute x11, starting transfers between devices, swapped(): return lax.ppermute(value, 'dp', perm)  13.6 us
    pallas_call x1, Pallas kernels, project(): pl.pallas_call(project_kernel, out_shape=(jax.ShapeDtypeStruct((factor, t...  5.67 us
    ppermute x11, waiting for transfers between devices, swapped(): return lax.ppermute(value, 'dp', perm)  3.76 us
    pallas_call x1, Pallas kernels, precondition(): pl.pallas_call(functools.partial(precondition_kernel, tok_total, n_terms)...  2.68 us
    pallas_call x1, Pallas kernels, score(): pl.pallas_call(functools.partial(score_kernel, size, n_pieces), out_shape...  2.4 us
  transfers between devices with their start and end apart: 11, of which 3 were waited for; matrix products, arithmetic and copies ran while one was open for 0% of the time, Pallas kernels for 30%

profile of v24, /device:TPU:0, one launch (start us, length us, event | category | flops | bytes accessed | tf_op | source)
XLA Modules:
  0.0 28.3 jit_solution(13687227909253852612)
XLA Ops:
  0.0 4.0 %collective-permute-start.1 = (bf16[8,4096]{1,0:T(8,128)(2,1)}, bf16[8,4096]{1,0:T(8,128)(2,1)S(1)}, u32[]{:S(2)}, u32[]{:S(2)}) collective-permute-start(bf16[8,4096]{1,0:T(8,128)(2,1)} %param.9), channel_id=1, source_target_pairs={{0,8},{1,9},{2,10},{3,11},{4,12},{5,13},{6,14},{7,15},{8,0},{9,1},... | collective-permute-start | bytes 196616 | tf_op jit(solution)/shard_map/ppermute | solution.py:329
  4.0 1.3 %collective-permute-start = (bf16[8,4096]{1,0:T(8,128)(2,1)}, bf16[8,4096]{1,0:T(8,128)(2,1)S(1)}, u32[]{:S(2)}, u32[]{:S(2)}) collective-permute-start(bf16[8,4096]{1,0:T(8,128)(2,1)} %param.9), channel_id=1, source_target_pairs={{0,12},{1,13},{2,14},{3,15},{4,8},{5,9},{6,10},{7,11},{8,4},{9,5},... | collective-permute-start | bytes 196616 | tf_op jit(solution)/shard_map/ppermute | solution.py:329
  5.4 0.2 collective-permute-start.2
  5.6 5.7 %project.1 = (f32[64,512]{1,0:T(8,128)S(1)}, f32[64,512]{1,0:T(8,128)S(1)}, f32[40,128]{1,0:T(8,128)S(1)}) custom-call(bf16[512,4096]{1,0:T(8,128)(2,1)} %acts.1, bf16[512,4096]{1,0:T(8,128)(2,1)} %grads.1, bf16[64,4096]{1,0:T(8,128)(2,1)} %bitcast.2, bf16[64,4096]{1,0:T(8,128)(2,1)} %bitcast.3), custom_call_target="tpu_custom_call" | custom-call | flops 536870912 | bytes 8388608 | tf_op jit(solution)/shard_map/project/pallas_call | solution.py:125
  11.3 0.0 collective-permute-done.1
  11.3 0.0 collective-permute-done
  11.3 0.0 collective-permute-done.2
  11.3 0.5 %collective-permute-start.6 = (f32[40,128]{1,0:T(8,128)S(1)}, f32[40,128]{1,0:T(8,128)S(1)}, u32[]{:S(2)}, u32[]{:S(2)}) collective-permute-start(f32[40,128]{1,0:T(8,128)S(1)} %get-tuple-element.24), channel_id=1, source_target_pairs={{0,3},{1,2},{2,1},{3,0},{4,7},{5,6},{6,5},{7,4},{8,11},{9,10},{10,... | collective-permute-start | bytes 61448 | tf_op jit(solution)/shard_map/ppermute | solution.py:329
  11.8 1.2 %collective-permute-start.5 = (f32[40,128]{1,0:T(8,128)S(1)}, f32[40,128]{1,0:T(8,128)S(1)}, u32[]{:S(2)}, u32[]{:S(2)}) collective-permute-start(f32[40,128]{1,0:T(8,128)S(1)} %get-tuple-element.24), channel_id=1, source_target_pairs={{0,2},{1,3},{2,0},{3,1},{4,6},{5,7},{6,4},{7,5},{8,10},{9,11},{10,... | collective-permute-start | bytes 61448 | tf_op jit(solution)/shard_map/ppermute | solution.py:329
  13.0 0.3 collective-permute-start.4
  13.3 1.6 %collective-permute-start.3 = (bf16[32,4096]{1,0:T(8,128)(2,1)S(1)}, bf16[32,4096]{1,0:T(8,128)(2,1)S(1)}, u32[]{:S(2)}, u32[]{:S(2)}) collective-permute-start(bf16[32,4096]{1,0:T(8,128)(2,1)S(1)} %constant_dynamic-update-slice_fusion), channel_id=1, source_target_pairs={{0,2},{1,3},{2,0},{3,1},{4,6},{5,7},{6,4},{7,5},{8,10},{9,11},{10,... | collective-permute-start | bytes 786440 | tf_op jit(solution)/shard_map/ppermute | solution.py:329
  14.9 0.0 collective-permute-done.6
  14.9 0.7 %collective-permute-done.5 = f32[40,128]{1,0:T(8,128)S(1)} collective-permute-done((f32[40,128]{1,0:T(8,128)S(1)}, f32[40,128]{1,0:T(8,128)S(1)}, u32[]{:S(2)}, u32[]{:S(2)}) %collective-permute-start.5) | collective-permute-done | bytes 20512 | tf_op jit(solution)/shard_map/ppermute | solution.py:329
  15.6 0.0 collective-permute-done.4
  15.6 2.7 %collective-permute-start.9 = (f32[40,128]{1,0:T(8,128)S(1)}, f32[40,128]{1,0:T(8,128)S(1)}, u32[]{:S(2)}, u32[]{:S(2)}) collective-permute-start(f32[40,128]{1,0:T(8,128)S(1)} %add_add_fusion.refs_0_), channel_id=1, source_target_pairs={{0,12},{1,13},{2,14},{3,15},{4,8},{5,9},{6,10},{7,11},{8,4},{9,5},... | collective-permute-start | bytes 61448 | tf_op jit(solution)/shard_map/ppermute | solution.py:329
  18.3 0.3 %collective-permute-start.8 = (f32[40,128]{1,0:T(8,128)S(1)}, f32[40,128]{1,0:T(8,128)S(1)}, u32[]{:S(2)}, u32[]{:S(2)}) collective-permute-start(f32[40,128]{1,0:T(8,128)S(1)} %add_add_fusion.refs_0_), channel_id=1, source_target_pairs={{0,8},{1,9},{2,10},{3,11},{4,12},{5,13},{6,14},{7,15},{8,0},{9,1},... | collective-permute-start | bytes 61448 | tf_op jit(solution)/shard_map/ppermute | solution.py:329
  18.7 1.4 %collective-permute-start.7 = (f32[40,128]{1,0:T(8,128)S(1)}, f32[40,128]{1,0:T(8,128)S(1)}, u32[]{:S(2)}, u32[]{:S(2)}) collective-permute-start(f32[40,128]{1,0:T(8,128)S(1)} %add_add_fusion.refs_0_), channel_id=1, source_target_pairs={{0,4},{1,5},{2,6},{3,7},{4,0},{5,1},{6,2},{7,3},{8,12},{9,13},{10,... | collective-permute-start | bytes 61448 | tf_op jit(solution)/shard_map/ppermute | solution.py:329
  20.0 1.2 %collective-permute-done.9.refs_3_ = f32[40,128]{1,0:T(8,128)S(1)} collective-permute-done((f32[40,128]{1,0:T(8,128)S(1)}, f32[40,128]{1,0:T(8,128)S(1)}, u32[]{:S(2)}, u32[]{:S(2)}) %collective-permute-start.9) | collective-permute-done | bytes 20512 | tf_op jit(solution)/shard_map/ppermute | solution.py:329
  21.2 1.9 %collective-permute-done.8.refs_2_ = f32[40,128]{1,0:T(8,128)S(1)} collective-permute-done((f32[40,128]{1,0:T(8,128)S(1)}, f32[40,128]{1,0:T(8,128)S(1)}, u32[]{:S(2)}, u32[]{:S(2)}) %collective-permute-start.8) | collective-permute-done | bytes 20512 | tf_op jit(solution)/shard_map/ppermute | solution.py:329
  23.1 0.0 collective-permute-done.7.refs_1_
  23.1 0.0 collective-permute-done.3
  23.2 0.1 collective-permute-start.10
  23.2 2.7 %precondition.1.moved = f32[128,512]{1,0:T(8,128)S(1)} custom-call(f32[40,128]{1,0:T(8,128)S(1)} %add_add_fusion.refs_0_, f32[40,128]{1,0:T(8,128)S(1)} %collective-permute-done.7.refs_1_, f32[40,128]{1,0:T(8,128)S(1)} %collective-permute-done.8.refs_2_, f32[40,128]{1,0:T(8,128)S(1)} %collective-permute-done.9.refs_3_, ...), custom_call_target="tpu_custom_call" | custom-call | flops 3355443200 | bytes 524288 | tf_op jit(solution)/shard_map/precondition/pallas_call | solution.py:228
  25.9 2.4 %score.1 = f32[512,128]{1,0:T(8,128)} custom-call(f32[128,512]{1,0:T(8,128)S(1)} %precondition.1.moved, bf16[64,4096]{1,0:T(8,128)(2,1)S(1)} %constant_dynamic-update-slice_fusion.4.refs_0_, bf16[64,4096]{1,0:T(8,128)(2,1)S(1)} %collective-permute-done.10.refs_1_), custom_call_target="tpu_custom_call" | custom-call | tf_op jit(solution)/shard_map/score/pallas_call | solution.py:289
  (10 shorter events, 0.1 us)
Async XLA Ops:
  0.0 11.3 %collective-permute-start.1 = (bf16[8,4096]{1,0:T(8,128)(2,1)}, bf16[8,4096]{1,0:T(8,128)(2,1)S(1)}, u32[]{:S(2)}, u32[]{:S(2)}) collective-permute-start(bf16[8,4096]{1,0:T(8,128)(2,1)} %param.9), channel_id=1, source_target_pairs={{0,8},{1,9},{2,10},{3,11},{4,12},{5,13},{6,14},{7,15},{8,0},{9,1},... | collective-permute-start | bytes 196616 | tf_op jit(solution)/shard_map/ppermute | solution.py:329
  4.0 7.3 %collective-permute-start = (bf16[8,4096]{1,0:T(8,128)(2,1)}, bf16[8,4096]{1,0:T(8,128)(2,1)S(1)}, u32[]{:S(2)}, u32[]{:S(2)}) collective-permute-start(bf16[8,4096]{1,0:T(8,128)(2,1)} %param.9), channel_id=1, source_target_pairs={{0,12},{1,13},{2,14},{3,15},{4,8},{5,9},{6,10},{7,11},{8,4},{9,5},... | collective-permute-start | bytes 196616 | tf_op jit(solution)/shard_map/ppermute | solution.py:329
  5.4 5.9 %collective-permute-start.2 = (bf16[8,4096]{1,0:T(8,128)(2,1)}, bf16[8,4096]{1,0:T(8,128)(2,1)S(1)}, u32[]{:S(2)}, u32[]{:S(2)}) collective-permute-start(bf16[8,4096]{1,0:T(8,128)(2,1)} %param.9), channel_id=1, source_target_pairs={{0,4},{1,5},{2,6},{3,7},{4,0},{5,1},{6,2},{7,3},{8,12},{9,13},{10,... | collective-permute-start | bytes 196616 | tf_op jit(solution)/shard_map/ppermute | solution.py:329
  5.6 7.6 %copy-start = (bf16[8,4096]{1,0:T(8,128)(2,1)S(1)}, bf16[8,4096]{1,0:T(8,128)(2,1)}, u32[]{:S(2)}) copy-start(bf16[8,4096]{1,0:T(8,128)(2,1)} %param.9) | copy-start | bytes 196612
  11.3 3.6 %collective-permute-start.6 = (f32[40,128]{1,0:T(8,128)S(1)}, f32[40,128]{1,0:T(8,128)S(1)}, u32[]{:S(2)}, u32[]{:S(2)}) collective-permute-start(f32[40,128]{1,0:T(8,128)S(1)} %get-tuple-element.24), channel_id=1, source_target_pairs={{0,3},{1,2},{2,1},{3,0},{4,7},{5,6},{6,5},{7,4},{8,11},{9,10},{10,... | collective-permute-start | bytes 61448 | tf_op jit(solution)/shard_map/ppermute | solution.py:329
  11.8 3.8 %collective-permute-start.5 = (f32[40,128]{1,0:T(8,128)S(1)}, f32[40,128]{1,0:T(8,128)S(1)}, u32[]{:S(2)}, u32[]{:S(2)}) collective-permute-start(f32[40,128]{1,0:T(8,128)S(1)} %get-tuple-element.24), channel_id=1, source_target_pairs={{0,2},{1,3},{2,0},{3,1},{4,6},{5,7},{6,4},{7,5},{8,10},{9,11},{10,... | collective-permute-start | bytes 61448 | tf_op jit(solution)/shard_map/ppermute | solution.py:329
  13.0 2.6 %collective-permute-start.4 = (f32[40,128]{1,0:T(8,128)S(1)}, f32[40,128]{1,0:T(8,128)S(1)}, u32[]{:S(2)}, u32[]{:S(2)}) collective-permute-start(f32[40,128]{1,0:T(8,128)S(1)} %get-tuple-element.24), channel_id=1, source_target_pairs={{0,1},{1,0},{2,3},{3,2},{4,5},{5,4},{6,7},{7,6},{8,9},{9,8},{10,11... | collective-permute-start | bytes 61448 | tf_op jit(solution)/shard_map/ppermute | solution.py:329
  13.3 9.8 %collective-permute-start.3 = (bf16[32,4096]{1,0:T(8,128)(2,1)S(1)}, bf16[32,4096]{1,0:T(8,128)(2,1)S(1)}, u32[]{:S(2)}, u32[]{:S(2)}) collective-permute-start(bf16[32,4096]{1,0:T(8,128)(2,1)S(1)} %constant_dynamic-update-slice_fusion), channel_id=1, source_target_pairs={{0,2},{1,3},{2,0},{3,1},{4,6},{5,7},{6,4},{7,5},{8,10},{9,11},{10,... | collective-permute-start | bytes 786440 | tf_op jit(solution)/shard_map/ppermute | solution.py:329
  15.6 5.7 %collective-permute-start.9 = (f32[40,128]{1,0:T(8,128)S(1)}, f32[40,128]{1,0:T(8,128)S(1)}, u32[]{:S(2)}, u32[]{:S(2)}) collective-permute-start(f32[40,128]{1,0:T(8,128)S(1)} %add_add_fusion.refs_0_), channel_id=1, source_target_pairs={{0,12},{1,13},{2,14},{3,15},{4,8},{5,9},{6,10},{7,11},{8,4},{9,5},... | collective-permute-start | bytes 61448 | tf_op jit(solution)/shard_map/ppermute | solution.py:329
  18.3 4.8 %collective-permute-start.8 = (f32[40,128]{1,0:T(8,128)S(1)}, f32[40,128]{1,0:T(8,128)S(1)}, u32[]{:S(2)}, u32[]{:S(2)}) collective-permute-start(f32[40,128]{1,0:T(8,128)S(1)} %add_add_fusion.refs_0_), channel_id=1, source_target_pairs={{0,8},{1,9},{2,10},{3,11},{4,12},{5,13},{6,14},{7,15},{8,0},{9,1},... | collective-permute-start | bytes 61448 | tf_op jit(solution)/shard_map/ppermute | solution.py:329
  18.7 4.5 %collective-permute-start.7 = (f32[40,128]{1,0:T(8,128)S(1)}, f32[40,128]{1,0:T(8,128)S(1)}, u32[]{:S(2)}, u32[]{:S(2)}) collective-permute-start(f32[40,128]{1,0:T(8,128)S(1)} %add_add_fusion.refs_0_), channel_id=1, source_target_pairs={{0,4},{1,5},{2,6},{3,7},{4,0},{5,1},{6,2},{7,3},{8,12},{9,13},{10,... | collective-permute-start | bytes 61448 | tf_op jit(solution)/shard_map/ppermute | solution.py:329
  23.2 2.8 %collective-permute-start.10 = (bf16[64,4096]{1,0:T(8,128)(2,1)S(1)}, bf16[64,4096]{1,0:T(8,128)(2,1)S(1)}, u32[]{:S(2)}, u32[]{:S(2)}) collective-permute-start(bf16[64,4096]{1,0:T(8,128)(2,1)S(1)} %constant_dynamic-update-slice_fusion.4.refs_0_), channel_id=1, source_target_pairs={{0,1},{1,0},{2,3},{3,2},{4,5},{5,4},{6,7},{7,6},{8,9},{9,8},{10,11... | collective-permute-start | bytes 1572872 | tf_op jit(solution)/shard_map/ppermute | solution.py:329

commit v25 on v24

--- a/solution.py
+++ b/solution.py
@@ -242,7 +242,7 @@
     queries, (scores, ordered, result, sems) = refs[:n_pieces], refs[n_pieces:]
     factor = moved.shape[0] // 2
     owners = owners_of(lax.axis_index("dp"), size)
-    group = 2
+    group = 4
     copies = []
     for part, begin in enumerate(range(0, moved.shape[1], TOKENS_AT_ONCE)):
         tokens = slice(begin, begin + TOKENS_AT_ONCE)

time: 28.5 us -> 28.6 us (level)
  transfers between devices with their start and end apart: 11 -> 11, of which waited for: 3 -> 3; matrix products, arithmetic and copies ran while one was open for 0% -> 0% of each run, Pallas kernels for 30% -> 29%
where the time goes in v25:
time: 28.6 us; the launch traced here: 28.4 us
  starting transfers between devices  13.6 us (48%)
  Pallas kernels  10.8 us (38%)
  waiting for transfers between devices  3.76 us (13%)
    ppermute x11, starting transfers between devices, swapped(): return lax.ppermute(value, 'dp', perm)  13.6 us
    pallas_call x1, Pallas kernels, project(): pl.pallas_call(project_kernel, out_shape=(jax.ShapeDtypeStruct((factor, t...  5.67 us
    ppermute x11, waiting for transfers between devices, swapped(): return lax.ppermute(value, 'dp', perm)  3.76 us
    pallas_call x1, Pallas kernels, precondition(): pl.pallas_call(functools.partial(precondition_kernel, tok_total, n_terms)...  2.68 us
    pallas_call x1, Pallas kernels, score(): pl.pallas_call(functools.partial(score_kernel, size, n_pieces), out_shape...  2.44 us
  transfers between devices with their start and end apart: 11, of which 3 were waited for; matrix products, arithmetic and copies ran while one was open for 0% of the time, Pallas kernels for 29%

profile of v25, /device:TPU:0, one launch (start us, length us, event | category | flops | bytes accessed | tf_op | source)
XLA Modules:
  0.0 28.4 jit_solution(7883810265119015640)
XLA Ops:
  0.0 4.0 %collective-permute-start.1 = (bf16[8,4096]{1,0:T(8,128)(2,1)}, bf16[8,4096]{1,0:T(8,128)(2,1)S(1)}, u32[]{:S(2)}, u32[]{:S(2)}) collective-permute-start(bf16[8,4096]{1,0:T(8,128)(2,1)} %param.9), channel_id=1, source_target_pairs={{0,8},{1,9},{2,10},{3,11},{4,12},{5,13},{6,14},{7,15},{8,0},{9,1},... | collective-permute-start | bytes 196616 | tf_op jit(solution)/shard_map/ppermute | solution.py:329
  4.0 1.3 %collective-permute-start = (bf16[8,4096]{1,0:T(8,128)(2,1)}, bf16[8,4096]{1,0:T(8,128)(2,1)S(1)}, u32[]{:S(2)}, u32[]{:S(2)}) collective-permute-start(bf16[8,4096]{1,0:T(8,128)(2,1)} %param.9), channel_id=1, source_target_pairs={{0,12},{1,13},{2,14},{3,15},{4,8},{5,9},{6,10},{7,11},{8,4},{9,5},... | collective-permute-start | bytes 196616 | tf_op jit(solution)/shard_map/ppermute | solution.py:329
  5.4 0.2 collective-permute-start.2
  5.6 5.7 %project.1 = (f32[64,512]{1,0:T(8,128)S(1)}, f32[64,512]{1,0:T(8,128)S(1)}, f32[40,128]{1,0:T(8,128)S(1)}) custom-call(bf16[512,4096]{1,0:T(8,128)(2,1)} %acts.1, bf16[512,4096]{1,0:T(8,128)(2,1)} %grads.1, bf16[64,4096]{1,0:T(8,128)(2,1)} %bitcast.2, bf16[64,4096]{1,0:T(8,128)(2,1)} %bitcast.3), custom_call_target="tpu_custom_call" | custom-call | flops 536870912 | bytes 8388608 | tf_op jit(solution)/shard_map/project/pallas_call | solution.py:125
  11.3 0.0 collective-permute-done.1
  11.3 0.0 collective-permute-done
  11.3 0.0 collective-permute-done.2
  11.3 0.5 %collective-permute-start.6 = (f32[40,128]{1,0:T(8,128)S(1)}, f32[40,128]{1,0:T(8,128)S(1)}, u32[]{:S(2)}, u32[]{:S(2)}) collective-permute-start(f32[40,128]{1,0:T(8,128)S(1)} %get-tuple-element.24), channel_id=1, source_target_pairs={{0,3},{1,2},{2,1},{3,0},{4,7},{5,6},{6,5},{7,4},{8,11},{9,10},{10,... | collective-permute-start | bytes 61448 | tf_op jit(solution)/shard_map/ppermute | solution.py:329
  11.8 1.2 %collective-permute-start.5 = (f32[40,128]{1,0:T(8,128)S(1)}, f32[40,128]{1,0:T(8,128)S(1)}, u32[]{:S(2)}, u32[]{:S(2)}) collective-permute-start(f32[40,128]{1,0:T(8,128)S(1)} %get-tuple-element.24), channel_id=1, source_target_pairs={{0,2},{1,3},{2,0},{3,1},{4,6},{5,7},{6,4},{7,5},{8,10},{9,11},{10,... | collective-permute-start | bytes 61448 | tf_op jit(solution)/shard_map/ppermute | solution.py:329
  13.0 0.3 collective-permute-start.4
  13.3 1.6 %collective-permute-start.3 = (bf16[32,4096]{1,0:T(8,128)(2,1)S(1)}, bf16[32,4096]{1,0:T(8,128)(2,1)S(1)}, u32[]{:S(2)}, u32[]{:S(2)}) collective-permute-start(bf16[32,4096]{1,0:T(8,128)(2,1)S(1)} %constant_dynamic-update-slice_fusion), channel_id=1, source_target_pairs={{0,2},{1,3},{2,0},{3,1},{4,6},{5,7},{6,4},{7,5},{8,10},{9,11},{10,... | collective-permute-start | bytes 786440 | tf_op jit(solution)/shard_map/ppermute | solution.py:329
  14.9 0.0 collective-permute-done.6
  14.9 0.7 %collective-permute-done.5 = f32[40,128]{1,0:T(8,128)S(1)} collective-permute-done((f32[40,128]{1,0:T(8,128)S(1)}, f32[40,128]{1,0:T(8,128)S(1)}, u32[]{:S(2)}, u32[]{:S(2)}) %collective-permute-start.5) | collective-permute-done | bytes 20512 | tf_op jit(solution)/shard_map/ppermute | solution.py:329
  15.6 0.0 collective-permute-done.4
  15.6 2.7 %collective-permute-start.9 = (f32[40,128]{1,0:T(8,128)S(1)}, f32[40,128]{1,0:T(8,128)S(1)}, u32[]{:S(2)}, u32[]{:S(2)}) collective-permute-start(f32[40,128]{1,0:T(8,128)S(1)} %add_add_fusion.refs_0_), channel_id=1, source_target_pairs={{0,12},{1,13},{2,14},{3,15},{4,8},{5,9},{6,10},{7,11},{8,4},{9,5},... | collective-permute-start | bytes 61448 | tf_op jit(solution)/shard_map/ppermute | solution.py:329
  18.3 0.3 %collective-permute-start.8 = (f32[40,128]{1,0:T(8,128)S(1)}, f32[40,128]{1,0:T(8,128)S(1)}, u32[]{:S(2)}, u32[]{:S(2)}) collective-permute-start(f32[40,128]{1,0:T(8,128)S(1)} %add_add_fusion.refs_0_), channel_id=1, source_target_pairs={{0,8},{1,9},{2,10},{3,11},{4,12},{5,13},{6,14},{7,15},{8,0},{9,1},... | collective-permute-start | bytes 61448 | tf_op jit(solution)/shard_map/ppermute | solution.py:329
  18.7 1.4 %collective-permute-start.7 = (f32[40,128]{1,0:T(8,128)S(1)}, f32[40,128]{1,0:T(8,128)S(1)}, u32[]{:S(2)}, u32[]{:S(2)}) collective-permute-start(f32[40,128]{1,0:T(8,128)S(1)} %add_add_fusion.refs_0_), channel_id=1, source_target_pairs={{0,4},{1,5},{2,6},{3,7},{4,0},{5,1},{6,2},{7,3},{8,12},{9,13},{10,... | collective-permute-start | bytes 61448 | tf_op jit(solution)/shard_map/ppermute | solution.py:329
  20.0 1.2 %collective-permute-done.9.refs_3_ = f32[40,128]{1,0:T(8,128)S(1)} collective-permute-done((f32[40,128]{1,0:T(8,128)S(1)}, f32[40,128]{1,0:T(8,128)S(1)}, u32[]{:S(2)}, u32[]{:S(2)}) %collective-permute-start.9) | collective-permute-done | bytes 20512 | tf_op jit(solution)/shard_map/ppermute | solution.py:329
  21.2 1.9 %collective-permute-done.8.refs_2_ = f32[40,128]{1,0:T(8,128)S(1)} collective-permute-done((f32[40,128]{1,0:T(8,128)S(1)}, f32[40,128]{1,0:T(8,128)S(1)}, u32[]{:S(2)}, u32[]{:S(2)}) %collective-permute-start.8) | collective-permute-done | bytes 20512 | tf_op jit(solution)/shard_map/ppermute | solution.py:329
  23.1 0.0 collective-permute-done.7.refs_1_
  23.1 0.0 collective-permute-done.3
  23.2 0.1 collective-permute-start.10
  23.2 2.7 %precondition.1.moved = f32[128,512]{1,0:T(8,128)S(1)} custom-call(f32[40,128]{1,0:T(8,128)S(1)} %add_add_fusion.refs_0_, f32[40,128]{1,0:T(8,128)S(1)} %collective-permute-done.7.refs_1_, f32[40,128]{1,0:T(8,128)S(1)} %collective-permute-done.8.refs_2_, f32[40,128]{1,0:T(8,128)S(1)} %collective-permute-done.9.refs_3_, ...), custom_call_target="tpu_custom_call" | custom-call | flops 3355443200 | bytes 524288 | tf_op jit(solution)/shard_map/precondition/pallas_call | solution.py:228
  25.9 2.4 %score.1 = f32[512,128]{1,0:T(8,128)} custom-call(f32[128,512]{1,0:T(8,128)S(1)} %precondition.1.moved, bf16[64,4096]{1,0:T(8,128)(2,1)S(1)} %constant_dynamic-update-slice_fusion.4.refs_0_, bf16[64,4096]{1,0:T(8,128)(2,1)S(1)} %collective-permute-done.10.refs_1_), custom_call_target="tpu_custom_call" | custom-call | tf_op jit(solution)/shard_map/score/pallas_call | solution.py:289
  (10 shorter events, 0.1 us)
Async XLA Ops:
  0.0 11.3 %collective-permute-start.1 = (bf16[8,4096]{1,0:T(8,128)(2,1)}, bf16[8,4096]{1,0:T(8,128)(2,1)S(1)}, u32[]{:S(2)}, u32[]{:S(2)}) collective-permute-start(bf16[8,4096]{1,0:T(8,128)(2,1)} %param.9), channel_id=1, source_target_pairs={{0,8},{1,9},{2,10},{3,11},{4,12},{5,13},{6,14},{7,15},{8,0},{9,1},... | collective-permute-start | bytes 196616 | tf_op jit(solution)/shard_map/ppermute | solution.py:329
  4.0 7.3 %collective-permute-start = (bf16[8,4096]{1,0:T(8,128)(2,1)}, bf16[8,4096]{1,0:T(8,128)(2,1)S(1)}, u32[]{:S(2)}, u32[]{:S(2)}) collective-permute-start(bf16[8,4096]{1,0:T(8,128)(2,1)} %param.9), channel_id=1, source_target_pairs={{0,12},{1,13},{2,14},{3,15},{4,8},{5,9},{6,10},{7,11},{8,4},{9,5},... | collective-permute-start | bytes 196616 | tf_op jit(solution)/shard_map/ppermute | solution.py:329
  5.4 5.9 %collective-permute-start.2 = (bf16[8,4096]{1,0:T(8,128)(2,1)}, bf16[8,4096]{1,0:T(8,128)(2,1)S(1)}, u32[]{:S(2)}, u32[]{:S(2)}) collective-permute-start(bf16[8,4096]{1,0:T(8,128)(2,1)} %param.9), channel_id=1, source_target_pairs={{0,4},{1,5},{2,6},{3,7},{4,0},{5,1},{6,2},{7,3},{8,12},{9,13},{10,... | collective-permute-start | bytes 196616 | tf_op jit(solution)/shard_map/ppermute | solution.py:329
  5.6 7.6 %copy-start = (bf16[8,4096]{1,0:T(8,128)(2,1)S(1)}, bf16[8,4096]{1,0:T(8,128)(2,1)}, u32[]{:S(2)}) copy-start(bf16[8,4096]{1,0:T(8,128)(2,1)} %param.9) | copy-start | bytes 196612
  11.3 3.6 %collective-permute-start.6 = (f32[40,128]{1,0:T(8,128)S(1)}, f32[40,128]{1,0:T(8,128)S(1)}, u32[]{:S(2)}, u32[]{:S(2)}) collective-permute-start(f32[40,128]{1,0:T(8,128)S(1)} %get-tuple-element.24), channel_id=1, source_target_pairs={{0,3},{1,2},{2,1},{3,0},{4,7},{5,6},{6,5},{7,4},{8,11},{9,10},{10,... | collective-permute-start | bytes 61448 | tf_op jit(solution)/shard_map/ppermute | solution.py:329
  11.8 3.8 %collective-permute-start.5 = (f32[40,128]{1,0:T(8,128)S(1)}, f32[40,128]{1,0:T(8,128)S(1)}, u32[]{:S(2)}, u32[]{:S(2)}) collective-permute-start(f32[40,128]{1,0:T(8,128)S(1)} %get-tuple-element.24), channel_id=1, source_target_pairs={{0,2},{1,3},{2,0},{3,1},{4,6},{5,7},{6,4},{7,5},{8,10},{9,11},{10,... | collective-permute-start | bytes 61448 | tf_op jit(solution)/shard_map/ppermute | solution.py:329
  13.0 2.6 %collective-permute-start.4 = (f32[40,128]{1,0:T(8,128)S(1)}, f32[40,128]{1,0:T(8,128)S(1)}, u32[]{:S(2)}, u32[]{:S(2)}) collective-permute-start(f32[40,128]{1,0:T(8,128)S(1)} %get-tuple-element.24), channel_id=1, source_target_pairs={{0,1},{1,0},{2,3},{3,2},{4,5},{5,4},{6,7},{7,6},{8,9},{9,8},{10,11... | collective-permute-start | bytes 61448 | tf_op jit(solution)/shard_map/ppermute | solution.py:329
  13.3 9.8 %collective-permute-start.3 = (bf16[32,4096]{1,0:T(8,128)(2,1)S(1)}, bf16[32,4096]{1,0:T(8,128)(2,1)S(1)}, u32[]{:S(2)}, u32[]{:S(2)}) collective-permute-start(bf16[32,4096]{1,0:T(8,128)(2,1)S(1)} %constant_dynamic-update-slice_fusion), channel_id=1, source_target_pairs={{0,2},{1,3},{2,0},{3,1},{4,6},{5,7},{6,4},{7,5},{8,10},{9,11},{10,... | collective-permute-start | bytes 786440 | tf_op jit(solution)/shard_map/ppermute | solution.py:329
  15.6 5.7 %collective-permute-start.9 = (f32[40,128]{1,0:T(8,128)S(1)}, f32[40,128]{1,0:T(8,128)S(1)}, u32[]{:S(2)}, u32[]{:S(2)}) collective-permute-start(f32[40,128]{1,0:T(8,128)S(1)} %add_add_fusion.refs_0_), channel_id=1, source_target_pairs={{0,12},{1,13},{2,14},{3,15},{4,8},{5,9},{6,10},{7,11},{8,4},{9,5},... | collective-permute-start | bytes 61448 | tf_op jit(solution)/shard_map/ppermute | solution.py:329
  18.3 4.8 %collective-permute-start.8 = (f32[40,128]{1,0:T(8,128)S(1)}, f32[40,128]{1,0:T(8,128)S(1)}, u32[]{:S(2)}, u32[]{:S(2)}) collective-permute-start(f32[40,128]{1,0:T(8,128)S(1)} %add_add_fusion.refs_0_), channel_id=1, source_target_pairs={{0,8},{1,9},{2,10},{3,11},{4,12},{5,13},{6,14},{7,15},{8,0},{9,1},... | collective-permute-start | bytes 61448 | tf_op jit(solution)/shard_map/ppermute | solution.py:329
  18.7 4.5 %collective-permute-start.7 = (f32[40,128]{1,0:T(8,128)S(1)}, f32[40,128]{1,0:T(8,128)S(1)}, u32[]{:S(2)}, u32[]{:S(2)}) collective-permute-start(f32[40,128]{1,0:T(8,128)S(1)} %add_add_fusion.refs_0_), channel_id=1, source_target_pairs={{0,4},{1,5},{2,6},{3,7},{4,0},{5,1},{6,2},{7,3},{8,12},{9,13},{10,... | collective-permute-start | bytes 61448 | tf_op jit(solution)/shard_map/ppermute | solution.py:329
  23.2 2.8 %collective-permute-start.10 = (bf16[64,4096]{1,0:T(8,128)(2,1)S(1)}, bf16[64,4096]{1,0:T(8,128)(2,1)S(1)}, u32[]{:S(2)}, u32[]{:S(2)}) collective-permute-start(bf16[64,4096]{1,0:T(8,128)(2,1)S(1)} %constant_dynamic-update-slice_fusion.4.refs_0_), channel_id=1, source_target_pairs={{0,1},{1,0},{2,3},{3,2},{4,5},{5,4},{6,7},{7,6},{8,9},{9,8},{10,11... | collective-permute-start | bytes 1572872 | tf_op jit(solution)/shard_map/ppermute | solution.py:329

commit v26 on v24

--- a/solution.py
+++ b/solution.py
@@ -9,8 +9,8 @@
 
 DAMP = 0.1
 HIGHEST = lax.Precision.HIGHEST
-COPY_ROWS = 128
-IN_FLIGHT = 5
+COPY_ROWS = 256
+IN_FLIGHT = 3
 TOKENS_AT_ONCE = 256
 
 
@@ -70,7 +70,7 @@
         for at, src in enumerate((acts, grads))
     ]
     queue = [weight_copies[0], *tok_copies[0], *tok_copies[1]]
-    queue.insert(3, weight_copies[1])
+    queue.insert(2, weight_copies[1])
 
     def start_next(many):
         for copy in queue[:many]:
@@ -81,7 +81,7 @@
         for first in range(0, width, 512):
             weight_t[at, first : first + 512, :] = weight_buf[at, :, first : first + 512].T
 
-    steps = [(at, part, min(2, n_parts - part)) for at in range(2) for part in range(0, n_parts, 2)]
+    steps = [(at, part, 1) for at in range(2) for part in range(n_parts)]
     last_act = len(steps) // 2 - 1
     blocks = [[], []]
     grams = [[], []]

time: 28.5 us -> 28.3 us (level)
  Pallas kernels: 10.8 us -> 10.5 us
  transfers between devices with their start and end apart: 11 -> 11, of which waited for: 3 -> 3; matrix products, arithmetic and copies ran while one was open for 0% -> 0% of each run, Pallas kernels for 30% -> 29%
where the time goes in v26:
time: 28.3 us; the launch traced here: 28.1 us
  starting transfers between devices  13.6 us (48%)
  Pallas kernels  10.5 us (37%)
  waiting for transfers between devices  3.75 us (13%)
    ppermute x11, starting transfers between devices, swapped(): return lax.ppermute(value, 'dp', perm)  13.6 us
    pallas_call x1, Pallas kernels, project(): pl.pallas_call(project_kernel, out_shape=(jax.ShapeDtypeStruct((factor, t...  5.48 us
    ppermute x11, waiting for transfers between devices, swapped(): return lax.ppermute(value, 'dp', perm)  3.75 us
    pallas_call x1, Pallas kernels, precondition(): pl.pallas_call(functools.partial(precondition_kernel, tok_total, n_terms)...  2.68 us
    pallas_call x1, Pallas kernels, score(): pl.pallas_call(functools.partial(score_kernel, size, n_pieces), out_shape...  2.39 us
  transfers between devices with their start and end apart: 11, of which 3 were waited for; matrix products, arithmetic and copies ran while one was open for 0% of the time, Pallas kernels for 29%

profile of v26, /device:TPU:0, one launch (start us, length us, event | category | flops | bytes accessed | tf_op | source)
XLA Modules:
  0.0 28.1 jit_solution(959086981126052849)
XLA Ops:
  0.0 4.0 %collective-permute-start.1 = (bf16[8,4096]{1,0:T(8,128)(2,1)}, bf16[8,4096]{1,0:T(8,128)(2,1)S(1)}, u32[]{:S(2)}, u32[]{:S(2)}) collective-permute-start(bf16[8,4096]{1,0:T(8,128)(2,1)} %param.9), channel_id=1, source_target_pairs={{0,8},{1,9},{2,10},{3,11},{4,12},{5,13},{6,14},{7,15},{8,0},{9,1},... | collective-permute-start | bytes 196616 | tf_op jit(solution)/shard_map/ppermute | solution.py:329
  4.0 1.3 %collective-permute-start = (bf16[8,4096]{1,0:T(8,128)(2,1)}, bf16[8,4096]{1,0:T(8,128)(2,1)S(1)}, u32[]{:S(2)}, u32[]{:S(2)}) collective-permute-start(bf16[8,4096]{1,0:T(8,128)(2,1)} %param.9), channel_id=1, source_target_pairs={{0,12},{1,13},{2,14},{3,15},{4,8},{5,9},{6,10},{7,11},{8,4},{9,5},... | collective-permute-start | bytes 196616 | tf_op jit(solution)/shard_map/ppermute | solution.py:329
  5.4 0.2 collective-permute-start.2
  5.6 5.5 %project.1 = (f32[64,512]{1,0:T(8,128)S(1)}, f32[64,512]{1,0:T(8,128)S(1)}, f32[40,128]{1,0:T(8,128)S(1)}) custom-call(bf16[512,4096]{1,0:T(8,128)(2,1)} %acts.1, bf16[512,4096]{1,0:T(8,128)(2,1)} %grads.1, bf16[64,4096]{1,0:T(8,128)(2,1)} %bitcast.2, bf16[64,4096]{1,0:T(8,128)(2,1)} %bitcast.3), custom_call_target="tpu_custom_call" | custom-call | flops 536870912 | bytes 8388608 | tf_op jit(solution)/shard_map/project/pallas_call | solution.py:125
  11.1 0.0 collective-permute-done.1
  11.1 0.0 collective-permute-done
  11.1 0.0 collective-permute-done.2
  11.1 0.5 %collective-permute-start.6 = (f32[40,128]{1,0:T(8,128)S(1)}, f32[40,128]{1,0:T(8,128)S(1)}, u32[]{:S(2)}, u32[]{:S(2)}) collective-permute-start(f32[40,128]{1,0:T(8,128)S(1)} %get-tuple-element.24), channel_id=1, source_target_pairs={{0,3},{1,2},{2,1},{3,0},{4,7},{5,6},{6,5},{7,4},{8,11},{9,10},{10,... | collective-permute-start | bytes 61448 | tf_op jit(solution)/shard_map/ppermute | solution.py:329
  11.6 1.2 %collective-permute-start.5 = (f32[40,128]{1,0:T(8,128)S(1)}, f32[40,128]{1,0:T(8,128)S(1)}, u32[]{:S(2)}, u32[]{:S(2)}) collective-permute-start(f32[40,128]{1,0:T(8,128)S(1)} %get-tuple-element.24), channel_id=1, source_target_pairs={{0,2},{1,3},{2,0},{3,1},{4,6},{5,7},{6,4},{7,5},{8,10},{9,11},{10,... | collective-permute-start | bytes 61448 | tf_op jit(solution)/shard_map/ppermute | solution.py:329
  12.8 0.3 collective-permute-start.4
  13.1 1.6 %collective-permute-start.3 = (bf16[32,4096]{1,0:T(8,128)(2,1)S(1)}, bf16[32,4096]{1,0:T(8,128)(2,1)S(1)}, u32[]{:S(2)}, u32[]{:S(2)}) collective-permute-start(bf16[32,4096]{1,0:T(8,128)(2,1)S(1)} %constant_dynamic-update-slice_fusion), channel_id=1, source_target_pairs={{0,2},{1,3},{2,0},{3,1},{4,6},{5,7},{6,4},{7,5},{8,10},{9,11},{10,... | collective-permute-start | bytes 786440 | tf_op jit(solution)/shard_map/ppermute | solution.py:329
  14.7 0.0 collective-permute-done.6
  14.7 0.7 %collective-permute-done.5 = f32[40,128]{1,0:T(8,128)S(1)} collective-permute-done((f32[40,128]{1,0:T(8,128)S(1)}, f32[40,128]{1,0:T(8,128)S(1)}, u32[]{:S(2)}, u32[]{:S(2)}) %collective-permute-start.5) | collective-permute-done | bytes 20512 | tf_op jit(solution)/shard_map/ppermute | solution.py:329
  15.4 2.7 %collective-permute-start.9 = (f32[40,128]{1,0:T(8,128)S(1)}, f32[40,128]{1,0:T(8,128)S(1)}, u32[]{:S(2)}, u32[]{:S(2)}) collective-permute-start(f32[40,128]{1,0:T(8,128)S(1)} %add_add_fusion.refs_0_), channel_id=1, source_target_pairs={{0,12},{1,13},{2,14},{3,15},{4,8},{5,9},{6,10},{7,11},{8,4},{9,5},... | collective-permute-start | bytes 61448 | tf_op jit(solution)/shard_map/ppermute | solution.py:329
  18.1 0.3 %collective-permute-start.8 = (f32[40,128]{1,0:T(8,128)S(1)}, f32[40,128]{1,0:T(8,128)S(1)}, u32[]{:S(2)}, u32[]{:S(2)}) collective-permute-start(f32[40,128]{1,0:T(8,128)S(1)} %add_add_fusion.refs_0_), channel_id=1, source_target_pairs={{0,8},{1,9},{2,10},{3,11},{4,12},{5,13},{6,14},{7,15},{8,0},{9,1},... | collective-permute-start | bytes 61448 | tf_op jit(solution)/shard_map/ppermute | solution.py:329
  18.5 1.4 %collective-permute-start.7 = (f32[40,128]{1,0:T(8,128)S(1)}, f32[40,128]{1,0:T(8,128)S(1)}, u32[]{:S(2)}, u32[]{:S(2)}) collective-permute-start(f32[40,128]{1,0:T(8,128)S(1)} %add_add_fusion.refs_0_), channel_id=1, source_target_pairs={{0,4},{1,5},{2,6},{3,7},{4,0},{5,1},{6,2},{7,3},{8,12},{9,13},{10,... | collective-permute-start | bytes 61448 | tf_op jit(solution)/shard_map/ppermute | solution.py:329
  19.9 1.2 %collective-permute-done.9.refs_3_ = f32[40,128]{1,0:T(8,128)S(1)} collective-permute-done((f32[40,128]{1,0:T(8,128)S(1)}, f32[40,128]{1,0:T(8,128)S(1)}, u32[]{:S(2)}, u32[]{:S(2)}) %collective-permute-start.9) | collective-permute-done | bytes 20512 | tf_op jit(solution)/shard_map/ppermute | solution.py:329
  21.1 1.8 %collective-permute-done.8.refs_2_ = f32[40,128]{1,0:T(8,128)S(1)} collective-permute-done((f32[40,128]{1,0:T(8,128)S(1)}, f32[40,128]{1,0:T(8,128)S(1)}, u32[]{:S(2)}, u32[]{:S(2)}) %collective-permute-start.8) | collective-permute-done | bytes 20512 | tf_op jit(solution)/shard_map/ppermute | solution.py:329
  22.9 0.0 collective-permute-done.7.refs_1_
  22.9 0.0 collective-permute-done.3
  23.0 0.1 collective-permute-start.10
  23.0 2.7 %precondition.1.moved = f32[128,512]{1,0:T(8,128)S(1)} custom-call(f32[40,128]{1,0:T(8,128)S(1)} %add_add_fusion.refs_0_, f32[40,128]{1,0:T(8,128)S(1)} %collective-permute-done.7.refs_1_, f32[40,128]{1,0:T(8,128)S(1)} %collective-permute-done.8.refs_2_, f32[40,128]{1,0:T(8,128)S(1)} %collective-permute-done.9.refs_3_, ...), custom_call_target="tpu_custom_call" | custom-call | flops 3355443200 | bytes 524288 | tf_op jit(solution)/shard_map/precondition/pallas_call | solution.py:228
  25.7 0.0 collective-permute-done.10.refs_1_
  25.7 2.4 %score.1 = f32[512,128]{1,0:T(8,128)} custom-call(f32[128,512]{1,0:T(8,128)S(1)} %precondition.1.moved, bf16[64,4096]{1,0:T(8,128)(2,1)S(1)} %constant_dynamic-update-slice_fusion.4.refs_0_, bf16[64,4096]{1,0:T(8,128)(2,1)S(1)} %collective-permute-done.10.refs_1_), custom_call_target="tpu_custom_call" | custom-call | tf_op jit(solution)/shard_map/score/pallas_call | solution.py:289
  (10 shorter events, 0.1 us)
Async XLA Ops:
  0.0 11.1 %collective-permute-start.1 = (bf16[8,4096]{1,0:T(8,128)(2,1)}, bf16[8,4096]{1,0:T(8,128)(2,1)S(1)}, u32[]{:S(2)}, u32[]{:S(2)}) collective-permute-start(bf16[8,4096]{1,0:T(8,128)(2,1)} %param.9), channel_id=1, source_target_pairs={{0,8},{1,9},{2,10},{3,11},{4,12},{5,13},{6,14},{7,15},{8,0},{9,1},... | collective-permute-start | bytes 196616 | tf_op jit(solution)/shard_map/ppermute | solution.py:329
  4.0 7.1 %collective-permute-start = (bf16[8,4096]{1,0:T(8,128)(2,1)}, bf16[8,4096]{1,0:T(8,128)(2,1)S(1)}, u32[]{:S(2)}, u32[]{:S(2)}) collective-permute-start(bf16[8,4096]{1,0:T(8,128)(2,1)} %param.9), channel_id=1, source_target_pairs={{0,12},{1,13},{2,14},{3,15},{4,8},{5,9},{6,10},{7,11},{8,4},{9,5},... | collective-permute-start | bytes 196616 | tf_op jit(solution)/shard_map/ppermute | solution.py:329
  5.4 5.7 %collective-permute-start.2 = (bf16[8,4096]{1,0:T(8,128)(2,1)}, bf16[8,4096]{1,0:T(8,128)(2,1)S(1)}, u32[]{:S(2)}, u32[]{:S(2)}) collective-permute-start(bf16[8,4096]{1,0:T(8,128)(2,1)} %param.9), channel_id=1, source_target_pairs={{0,4},{1,5},{2,6},{3,7},{4,0},{5,1},{6,2},{7,3},{8,12},{9,13},{10,... | collective-permute-start | bytes 196616 | tf_op jit(solution)/shard_map/ppermute | solution.py:329
  5.6 7.5 %copy-start = (bf16[8,4096]{1,0:T(8,128)(2,1)S(1)}, bf16[8,4096]{1,0:T(8,128)(2,1)}, u32[]{:S(2)}) copy-start(bf16[8,4096]{1,0:T(8,128)(2,1)} %param.9) | copy-start | bytes 196612
  11.1 3.6 %collective-permute-start.6 = (f32[40,128]{1,0:T(8,128)S(1)}, f32[40,128]{1,0:T(8,128)S(1)}, u32[]{:S(2)}, u32[]{:S(2)}) collective-permute-start(f32[40,128]{1,0:T(8,128)S(1)} %get-tuple-element.24), channel_id=1, source_target_pairs={{0,3},{1,2},{2,1},{3,0},{4,7},{5,6},{6,5},{7,4},{8,11},{9,10},{10,... | collective-permute-start | bytes 61448 | tf_op jit(solution)/shard_map/ppermute | solution.py:329
  11.6 3.8 %collective-permute-start.5 = (f32[40,128]{1,0:T(8,128)S(1)}, f32[40,128]{1,0:T(8,128)S(1)}, u32[]{:S(2)}, u32[]{:S(2)}) collective-permute-start(f32[40,128]{1,0:T(8,128)S(1)} %get-tuple-element.24), channel_id=1, source_target_pairs={{0,2},{1,3},{2,0},{3,1},{4,6},{5,7},{6,4},{7,5},{8,10},{9,11},{10,... | collective-permute-start | bytes 61448 | tf_op jit(solution)/shard_map/ppermute | solution.py:329
  12.8 2.6 %collective-permute-start.4 = (f32[40,128]{1,0:T(8,128)S(1)}, f32[40,128]{1,0:T(8,128)S(1)}, u32[]{:S(2)}, u32[]{:S(2)}) collective-permute-start(f32[40,128]{1,0:T(8,128)S(1)} %get-tuple-element.24), channel_id=1, source_target_pairs={{0,1},{1,0},{2,3},{3,2},{4,5},{5,4},{6,7},{7,6},{8,9},{9,8},{10,11... | collective-permute-start | bytes 61448 | tf_op jit(solution)/shard_map/ppermute | solution.py:329
  13.1 9.8 %collective-permute-start.3 = (bf16[32,4096]{1,0:T(8,128)(2,1)S(1)}, bf16[32,4096]{1,0:T(8,128)(2,1)S(1)}, u32[]{:S(2)}, u32[]{:S(2)}) collective-permute-start(bf16[32,4096]{1,0:T(8,128)(2,1)S(1)} %constant_dynamic-update-slice_fusion), channel_id=1, source_target_pairs={{0,2},{1,3},{2,0},{3,1},{4,6},{5,7},{6,4},{7,5},{8,10},{9,11},{10,... | collective-permute-start | bytes 786440 | tf_op jit(solution)/shard_map/ppermute | solution.py:329
  15.4 5.7 %collective-permute-start.9 = (f32[40,128]{1,0:T(8,128)S(1)}, f32[40,128]{1,0:T(8,128)S(1)}, u32[]{:S(2)}, u32[]{:S(2)}) collective-permute-start(f32[40,128]{1,0:T(8,128)S(1)} %add_add_fusion.refs_0_), channel_id=1, source_target_pairs={{0,12},{1,13},{2,14},{3,15},{4,8},{5,9},{6,10},{7,11},{8,4},{9,5},... | collective-permute-start | bytes 61448 | tf_op jit(solution)/shard_map/ppermute | solution.py:329
  18.1 4.8 %collective-permute-start.8 = (f32[40,128]{1,0:T(8,128)S(1)}, f32[40,128]{1,0:T(8,128)S(1)}, u32[]{:S(2)}, u32[]{:S(2)}) collective-permute-start(f32[40,128]{1,0:T(8,128)S(1)} %add_add_fusion.refs_0_), channel_id=1, source_target_pairs={{0,8},{1,9},{2,10},{3,11},{4,12},{5,13},{6,14},{7,15},{8,0},{9,1},... | collective-permute-start | bytes 61448 | tf_op jit(solution)/shard_map/ppermute | solution.py:329
  18.5 4.5 %collective-permute-start.7 = (f32[40,128]{1,0:T(8,128)S(1)}, f32[40,128]{1,0:T(8,128)S(1)}, u32[]{:S(2)}, u32[]{:S(2)}) collective-permute-start(f32[40,128]{1,0:T(8,128)S(1)} %add_add_fusion.refs_0_), channel_id=1, source_target_pairs={{0,4},{1,5},{2,6},{3,7},{4,0},{5,1},{6,2},{7,3},{8,12},{9,13},{10,... | collective-permute-start | bytes 61448 | tf_op jit(solution)/shard_map/ppermute | solution.py:329
  23.0 2.8 %collective-permute-start.10 = (bf16[64,4096]{1,0:T(8,128)(2,1)S(1)}, bf16[64,4096]{1,0:T(8,128)(2,1)S(1)}, u32[]{:S(2)}, u32[]{:S(2)}) collective-permute-start(bf16[64,4096]{1,0:T(8,128)(2,1)S(1)} %constant_dynamic-update-slice_fusion.4.refs_0_), channel_id=1, source_target_pairs={{0,1},{1,0},{2,3},{3,2},{4,5},{5,4},{6,7},{7,6},{8,9},{9,8},{10,11... | collective-permute-start | bytes 1572872 | tf_op jit(solution)/shard_map/ppermute | solution.py:329

commit v27 on v26

--- a/solution.py
+++ b/solution.py
@@ -10,7 +10,7 @@
 DAMP = 0.1
 HIGHEST = lax.Precision.HIGHEST
 COPY_ROWS = 256
-IN_FLIGHT = 3
+IN_FLIGHT = 4
 TOKENS_AT_ONCE = 256
 
 

time: 28.3 us -> 28.4 us (level)
  no operation moved by 1% of the time
where the time goes in v27:
time: 28.4 us; the launch traced here: 28.1 us
  starting transfers between devices  13.6 us (48%)
  Pallas kernels  10.6 us (37%)
  waiting for transfers between devices  3.76 us (13%)
    ppermute x11, starting transfers between devices, swapped(): return lax.ppermute(value, 'dp', perm)  13.6 us
    pallas_call x1, Pallas kernels, project(): pl.pallas_call(project_kernel, out_shape=(jax.ShapeDtypeStruct((factor, t...  5.5 us
    ppermute x11, waiting for transfers between devices, swapped(): return lax.ppermute(value, 'dp', perm)  3.76 us
    pallas_call x1, Pallas kernels, precondition(): pl.pallas_call(functools.partial(precondition_kernel, tok_total, n_terms)...  2.67 us
    pallas_call x1, Pallas kernels, score(): pl.pallas_call(functools.partial(score_kernel, size, n_pieces), out_shape...  2.39 us
  transfers between devices with their start and end apart: 11, of which 3 were waited for; matrix products, arithmetic and copies ran while one was open for 0% of the time, Pallas kernels for 29%

profile of v27, /device:TPU:0, one launch (start us, length us, event | category | flops | bytes accessed | tf_op | source)
XLA Modules:
  0.0 28.1 jit_solution(6317333086677584649)
XLA Ops:
  0.0 4.0 %collective-permute-start.1 = (bf16[8,4096]{1,0:T(8,128)(2,1)}, bf16[8,4096]{1,0:T(8,128)(2,1)S(1)}, u32[]{:S(2)}, u32[]{:S(2)}) collective-permute-start(bf16[8,4096]{1,0:T(8,128)(2,1)} %param.9), channel_id=1, source_target_pairs={{0,8},{1,9},{2,10},{3,11},{4,12},{5,13},{6,14},{7,15},{8,0},{9,1},... | collective-permute-start | bytes 196616 | tf_op jit(solution)/shard_map/ppermute | solution.py:329
  4.0 1.3 %collective-permute-start = (bf16[8,4096]{1,0:T(8,128)(2,1)}, bf16[8,4096]{1,0:T(8,128)(2,1)S(1)}, u32[]{:S(2)}, u32[]{:S(2)}) collective-permute-start(bf16[8,4096]{1,0:T(8,128)(2,1)} %param.9), channel_id=1, source_target_pairs={{0,12},{1,13},{2,14},{3,15},{4,8},{5,9},{6,10},{7,11},{8,4},{9,5},... | collective-permute-start | bytes 196616 | tf_op jit(solution)/shard_map/ppermute | solution.py:329
  5.4 0.2 collective-permute-start.2
  5.6 5.5 %project.1 = (f32[64,512]{1,0:T(8,128)S(1)}, f32[64,512]{1,0:T(8,128)S(1)}, f32[40,128]{1,0:T(8,128)S(1)}) custom-call(bf16[512,4096]{1,0:T(8,128)(2,1)} %acts.1, bf16[512,4096]{1,0:T(8,128)(2,1)} %grads.1, bf16[64,4096]{1,0:T(8,128)(2,1)} %bitcast.2, bf16[64,4096]{1,0:T(8,128)(2,1)} %bitcast.3), custom_call_target="tpu_custom_call" | custom-call | flops 536870912 | bytes 8388608 | tf_op jit(solution)/shard_map/project/pallas_call | solution.py:125
  11.1 0.0 collective-permute-done.1
  11.1 0.0 collective-permute-done
  11.2 0.0 collective-permute-done.2
  11.2 0.5 %collective-permute-start.6 = (f32[40,128]{1,0:T(8,128)S(1)}, f32[40,128]{1,0:T(8,128)S(1)}, u32[]{:S(2)}, u32[]{:S(2)}) collective-permute-start(f32[40,128]{1,0:T(8,128)S(1)} %get-tuple-element.24), channel_id=1, source_target_pairs={{0,3},{1,2},{2,1},{3,0},{4,7},{5,6},{6,5},{7,4},{8,11},{9,10},{10,... | collective-permute-start | bytes 61448 | tf_op jit(solution)/shard_map/ppermute | solution.py:329
  11.6 1.2 %collective-permute-start.5 = (f32[40,128]{1,0:T(8,128)S(1)}, f32[40,128]{1,0:T(8,128)S(1)}, u32[]{:S(2)}, u32[]{:S(2)}) collective-permute-start(f32[40,128]{1,0:T(8,128)S(1)} %get-tuple-element.24), channel_id=1, source_target_pairs={{0,2},{1,3},{2,0},{3,1},{4,6},{5,7},{6,4},{7,5},{8,10},{9,11},{10,... | collective-permute-start | bytes 61448 | tf_op jit(solution)/shard_map/ppermute | solution.py:329
  12.8 0.3 collective-permute-start.4
  13.1 1.6 %collective-permute-start.3 = (bf16[32,4096]{1,0:T(8,128)(2,1)S(1)}, bf16[32,4096]{1,0:T(8,128)(2,1)S(1)}, u32[]{:S(2)}, u32[]{:S(2)}) collective-permute-start(bf16[32,4096]{1,0:T(8,128)(2,1)S(1)} %constant_dynamic-update-slice_fusion), channel_id=1, source_target_pairs={{0,2},{1,3},{2,0},{3,1},{4,6},{5,7},{6,4},{7,5},{8,10},{9,11},{10,... | collective-permute-start | bytes 786440 | tf_op jit(solution)/shard_map/ppermute | solution.py:329
  14.7 0.0 collective-permute-done.6
  14.7 0.7 %collective-permute-done.5 = f32[40,128]{1,0:T(8,128)S(1)} collective-permute-done((f32[40,128]{1,0:T(8,128)S(1)}, f32[40,128]{1,0:T(8,128)S(1)}, u32[]{:S(2)}, u32[]{:S(2)}) %collective-permute-start.5) | collective-permute-done | bytes 20512 | tf_op jit(solution)/shard_map/ppermute | solution.py:329
  15.4 0.0 collective-permute-done.4
  15.4 2.7 %collective-permute-start.9 = (f32[40,128]{1,0:T(8,128)S(1)}, f32[40,128]{1,0:T(8,128)S(1)}, u32[]{:S(2)}, u32[]{:S(2)}) collective-permute-start(f32[40,128]{1,0:T(8,128)S(1)} %add_add_fusion.refs_0_), channel_id=1, source_target_pairs={{0,12},{1,13},{2,14},{3,15},{4,8},{5,9},{6,10},{7,11},{8,4},{9,5},... | collective-permute-start | bytes 61448 | tf_op jit(solution)/shard_map/ppermute | solution.py:329
  18.1 0.3 %collective-permute-start.8 = (f32[40,128]{1,0:T(8,128)S(1)}, f32[40,128]{1,0:T(8,128)S(1)}, u32[]{:S(2)}, u32[]{:S(2)}) collective-permute-start(f32[40,128]{1,0:T(8,128)S(1)} %add_add_fusion.refs_0_), channel_id=1, source_target_pairs={{0,8},{1,9},{2,10},{3,11},{4,12},{5,13},{6,14},{7,15},{8,0},{9,1},... | collective-permute-start | bytes 61448 | tf_op jit(solution)/shard_map/ppermute | solution.py:329
  18.5 1.4 %collective-permute-start.7 = (f32[40,128]{1,0:T(8,128)S(1)}, f32[40,128]{1,0:T(8,128)S(1)}, u32[]{:S(2)}, u32[]{:S(2)}) collective-permute-start(f32[40,128]{1,0:T(8,128)S(1)} %add_add_fusion.refs_0_), channel_id=1, source_target_pairs={{0,4},{1,5},{2,6},{3,7},{4,0},{5,1},{6,2},{7,3},{8,12},{9,13},{10,... | collective-permute-start | bytes 61448 | tf_op jit(solution)/shard_map/ppermute | solution.py:329
  19.9 1.2 %collective-permute-done.9.refs_3_ = f32[40,128]{1,0:T(8,128)S(1)} collective-permute-done((f32[40,128]{1,0:T(8,128)S(1)}, f32[40,128]{1,0:T(8,128)S(1)}, u32[]{:S(2)}, u32[]{:S(2)}) %collective-permute-start.9) | collective-permute-done | bytes 20512 | tf_op jit(solution)/shard_map/ppermute | solution.py:329
  21.1 1.9 %collective-permute-done.8.refs_2_ = f32[40,128]{1,0:T(8,128)S(1)} collective-permute-done((f32[40,128]{1,0:T(8,128)S(1)}, f32[40,128]{1,0:T(8,128)S(1)}, u32[]{:S(2)}, u32[]{:S(2)}) %collective-permute-start.8) | collective-permute-done | bytes 20512 | tf_op jit(solution)/shard_map/ppermute | solution.py:329
  22.9 0.0 collective-permute-done.3
  23.0 0.1 collective-permute-start.10
  23.1 2.7 %precondition.1.moved = f32[128,512]{1,0:T(8,128)S(1)} custom-call(f32[40,128]{1,0:T(8,128)S(1)} %add_add_fusion.refs_0_, f32[40,128]{1,0:T(8,128)S(1)} %collective-permute-done.7.refs_1_, f32[40,128]{1,0:T(8,128)S(1)} %collective-permute-done.8.refs_2_, f32[40,128]{1,0:T(8,128)S(1)} %collective-permute-done.9.refs_3_, ...), custom_call_target="tpu_custom_call" | custom-call | flops 3355443200 | bytes 524288 | tf_op jit(solution)/shard_map/precondition/pallas_call | solution.py:228
  25.8 0.0 collective-permute-done.10.refs_1_
  25.8 2.4 %score.1 = f32[512,128]{1,0:T(8,128)} custom-call(f32[128,512]{1,0:T(8,128)S(1)} %precondition.1.moved, bf16[64,4096]{1,0:T(8,128)(2,1)S(1)} %constant_dynamic-update-slice_fusion.4.refs_0_, bf16[64,4096]{1,0:T(8,128)(2,1)S(1)} %collective-permute-done.10.refs_1_), custom_call_target="tpu_custom_call" | custom-call | tf_op jit(solution)/shard_map/score/pallas_call | solution.py:289
  (10 shorter events, 0.1 us)
Async XLA Ops:
  0.0 11.1 %collective-permute-start.1 = (bf16[8,4096]{1,0:T(8,128)(2,1)}, bf16[8,4096]{1,0:T(8,128)(2,1)S(1)}, u32[]{:S(2)}, u32[]{:S(2)}) collective-permute-start(bf16[8,4096]{1,0:T(8,128)(2,1)} %param.9), channel_id=1, source_target_pairs={{0,8},{1,9},{2,10},{3,11},{4,12},{5,13},{6,14},{7,15},{8,0},{9,1},... | collective-permute-start | bytes 196616 | tf_op jit(solution)/shard_map/ppermute | solution.py:329
  4.0 7.1 %collective-permute-start = (bf16[8,4096]{1,0:T(8,128)(2,1)}, bf16[8,4096]{1,0:T(8,128)(2,1)S(1)}, u32[]{:S(2)}, u32[]{:S(2)}) collective-permute-start(bf16[8,4096]{1,0:T(8,128)(2,1)} %param.9), channel_id=1, source_target_pairs={{0,12},{1,13},{2,14},{3,15},{4,8},{5,9},{6,10},{7,11},{8,4},{9,5},... | collective-permute-start | bytes 196616 | tf_op jit(solution)/shard_map/ppermute | solution.py:329
  5.4 5.8 %collective-permute-start.2 = (bf16[8,4096]{1,0:T(8,128)(2,1)}, bf16[8,4096]{1,0:T(8,128)(2,1)S(1)}, u32[]{:S(2)}, u32[]{:S(2)}) collective-permute-start(bf16[8,4096]{1,0:T(8,128)(2,1)} %param.9), channel_id=1, source_target_pairs={{0,4},{1,5},{2,6},{3,7},{4,0},{5,1},{6,2},{7,3},{8,12},{9,13},{10,... | collective-permute-start | bytes 196616 | tf_op jit(solution)/shard_map/ppermute | solution.py:329
  5.6 7.5 %copy-start = (bf16[8,4096]{1,0:T(8,128)(2,1)S(1)}, bf16[8,4096]{1,0:T(8,128)(2,1)}, u32[]{:S(2)}) copy-start(bf16[8,4096]{1,0:T(8,128)(2,1)} %param.9) | copy-start | bytes 196612
  11.2 3.6 %collective-permute-start.6 = (f32[40,128]{1,0:T(8,128)S(1)}, f32[40,128]{1,0:T(8,128)S(1)}, u32[]{:S(2)}, u32[]{:S(2)}) collective-permute-start(f32[40,128]{1,0:T(8,128)S(1)} %get-tuple-element.24), channel_id=1, source_target_pairs={{0,3},{1,2},{2,1},{3,0},{4,7},{5,6},{6,5},{7,4},{8,11},{9,10},{10,... | collective-permute-start | bytes 61448 | tf_op jit(solution)/shard_map/ppermute | solution.py:329
  11.6 3.8 %collective-permute-start.5 = (f32[40,128]{1,0:T(8,128)S(1)}, f32[40,128]{1,0:T(8,128)S(1)}, u32[]{:S(2)}, u32[]{:S(2)}) collective-permute-start(f32[40,128]{1,0:T(8,128)S(1)} %get-tuple-element.24), channel_id=1, source_target_pairs={{0,2},{1,3},{2,0},{3,1},{4,6},{5,7},{6,4},{7,5},{8,10},{9,11},{10,... | collective-permute-start | bytes 61448 | tf_op jit(solution)/shard_map/ppermute | solution.py:329
  12.8 2.6 %collective-permute-start.4 = (f32[40,128]{1,0:T(8,128)S(1)}, f32[40,128]{1,0:T(8,128)S(1)}, u32[]{:S(2)}, u32[]{:S(2)}) collective-permute-start(f32[40,128]{1,0:T(8,128)S(1)} %get-tuple-element.24), channel_id=1, source_target_pairs={{0,1},{1,0},{2,3},{3,2},{4,5},{5,4},{6,7},{7,6},{8,9},{9,8},{10,11... | collective-permute-start | bytes 61448 | tf_op jit(solution)/shard_map/ppermute | solution.py:329
  13.1 9.8 %collective-permute-start.3 = (bf16[32,4096]{1,0:T(8,128)(2,1)S(1)}, bf16[32,4096]{1,0:T(8,128)(2,1)S(1)}, u32[]{:S(2)}, u32[]{:S(2)}) collective-permute-start(bf16[32,4096]{1,0:T(8,128)(2,1)S(1)} %constant_dynamic-update-slice_fusion), channel_id=1, source_target_pairs={{0,2},{1,3},{2,0},{3,1},{4,6},{5,7},{6,4},{7,5},{8,10},{9,11},{10,... | collective-permute-start | bytes 786440 | tf_op jit(solution)/shard_map/ppermute | solution.py:329
  15.4 5.7 %collective-permute-start.9 = (f32[40,128]{1,0:T(8,128)S(1)}, f32[40,128]{1,0:T(8,128)S(1)}, u32[]{:S(2)}, u32[]{:S(2)}) collective-permute-start(f32[40,128]{1,0:T(8,128)S(1)} %add_add_fusion.refs_0_), channel_id=1, source_target_pairs={{0,12},{1,13},{2,14},{3,15},{4,8},{5,9},{6,10},{7,11},{8,4},{9,5},... | collective-permute-start | bytes 61448 | tf_op jit(solution)/shard_map/ppermute | solution.py:329
  18.1 4.8 %collective-permute-start.8 = (f32[40,128]{1,0:T(8,128)S(1)}, f32[40,128]{1,0:T(8,128)S(1)}, u32[]{:S(2)}, u32[]{:S(2)}) collective-permute-start(f32[40,128]{1,0:T(8,128)S(1)} %add_add_fusion.refs_0_), channel_id=1, source_target_pairs={{0,8},{1,9},{2,10},{3,11},{4,12},{5,13},{6,14},{7,15},{8,0},{9,1},... | collective-permute-start | bytes 61448 | tf_op jit(solution)/shard_map/ppermute | solution.py:329
  18.5 4.5 %collective-permute-start.7 = (f32[40,128]{1,0:T(8,128)S(1)}, f32[40,128]{1,0:T(8,128)S(1)}, u32[]{:S(2)}, u32[]{:S(2)}) collective-permute-start(f32[40,128]{1,0:T(8,128)S(1)} %add_add_fusion.refs_0_), channel_id=1, source_target_pairs={{0,4},{1,5},{2,6},{3,7},{4,0},{5,1},{6,2},{7,3},{8,12},{9,13},{10,... | collective-permute-start | bytes 61448 | tf_op jit(solution)/shard_map/ppermute | solution.py:329
  23.0 2.8 %collective-permute-start.10 = (bf16[64,4096]{1,0:T(8,128)(2,1)S(1)}, bf16[64,4096]{1,0:T(8,128)(2,1)S(1)}, u32[]{:S(2)}, u32[]{:S(2)}) collective-permute-start(bf16[64,4096]{1,0:T(8,128)(2,1)S(1)} %constant_dynamic-update-slice_fusion.4.refs_0_), channel_id=1, source_target_pairs={{0,1},{1,0},{2,3},{3,2},{4,5},{5,4},{6,7},{7,6},{8,9},{9,8},{10,11... | collective-permute-start | bytes 1572872 | tf_op jit(solution)/shard_map/ppermute | solution.py:329

commit v28 on v27

--- a/solution.py
+++ b/solution.py
@@ -10,7 +10,7 @@
 DAMP = 0.1
 HIGHEST = lax.Precision.HIGHEST
 COPY_ROWS = 256
-IN_FLIGHT = 4
+IN_FLIGHT = 5
 TOKENS_AT_ONCE = 256
 
 

time: 28.4 us -> 29 us (1.021)
  Pallas kernels: 10.6 us -> 11.2 us
    pallas_call x1, Pallas kernels: 5.5 us -> 6.13 us  [project(): pl.pallas_call(project_kernel, out_shape=(jax.ShapeDtypeStruct((factor, t...]
  transfers between devices with their start and end apart: 11 -> 11, of which waited for: 3 -> 3; matrix products, arithmetic and copies ran while one was open for 0% -> 0% of each run, Pallas kernels for 29% -> 31%
where the time goes in v28:
time: 29 us; the launch traced here: 28.8 us
  starting transfers between devices  13.6 us (47%)
  Pallas kernels  11.2 us (39%)
  waiting for transfers between devices  3.75 us (13%)
    ppermute x11, starting transfers between devices, swapped(): return lax.ppermute(value, 'dp', perm)  13.6 us
    pallas_call x1, Pallas kernels, project(): pl.pallas_call(project_kernel, out_shape=(jax.ShapeDtypeStruct((factor, t...  6.13 us
    ppermute x11, waiting for transfers between devices, swapped(): return lax.ppermute(value, 'dp', perm)  3.75 us
    pallas_call x1, Pallas kernels, precondition(): pl.pallas_call(functools.partial(precondition_kernel, tok_total, n_terms)...  2.67 us
    pallas_call x1, Pallas kernels, score(): pl.pallas_call(functools.partial(score_kernel, size, n_pieces), out_shape...  2.39 us
  transfers between devices with their start and end apart: 11, of which 3 were waited for; matrix products, arithmetic and copies ran while one was open for 0% of the time, Pallas kernels for 31%

profile of v28, /device:TPU:0, one launch (start us, length us, event | category | flops | bytes accessed | tf_op | source)
XLA Modules:
  0.0 28.8 jit_solution(13444116274251794569)
XLA Ops:
  0.0 4.0 %collective-permute-start.1 = (bf16[8,4096]{1,0:T(8,128)(2,1)}, bf16[8,4096]{1,0:T(8,128)(2,1)S(1)}, u32[]{:S(2)}, u32[]{:S(2)}) collective-permute-start(bf16[8,4096]{1,0:T(8,128)(2,1)} %param.9), channel_id=1, source_target_pairs={{0,8},{1,9},{2,10},{3,11},{4,12},{5,13},{6,14},{7,15},{8,0},{9,1},... | collective-permute-start | bytes 196616 | tf_op jit(solution)/shard_map/ppermute | solution.py:329
  4.0 1.3 %collective-permute-start = (bf16[8,4096]{1,0:T(8,128)(2,1)}, bf16[8,4096]{1,0:T(8,128)(2,1)S(1)}, u32[]{:S(2)}, u32[]{:S(2)}) collective-permute-start(bf16[8,4096]{1,0:T(8,128)(2,1)} %param.9), channel_id=1, source_target_pairs={{0,12},{1,13},{2,14},{3,15},{4,8},{5,9},{6,10},{7,11},{8,4},{9,5},... | collective-permute-start | bytes 196616 | tf_op jit(solution)/shard_map/ppermute | solution.py:329
  5.4 0.2 collective-permute-start.2
  5.6 6.1 %project.1 = (f32[64,512]{1,0:T(8,128)S(1)}, f32[64,512]{1,0:T(8,128)S(1)}, f32[40,128]{1,0:T(8,128)S(1)}) custom-call(bf16[512,4096]{1,0:T(8,128)(2,1)} %acts.1, bf16[512,4096]{1,0:T(8,128)(2,1)} %grads.1, bf16[64,4096]{1,0:T(8,128)(2,1)} %bitcast.2, bf16[64,4096]{1,0:T(8,128)(2,1)} %bitcast.3), custom_call_target="tpu_custom_call" | custom-call | flops 536870912 | bytes 8388608 | tf_op jit(solution)/shard_map/project/pallas_call | solution.py:125
  11.8 0.0 collective-permute-done.1
  11.8 0.0 collective-permute-done
  11.8 0.5 %collective-permute-start.6 = (f32[40,128]{1,0:T(8,128)S(1)}, f32[40,128]{1,0:T(8,128)S(1)}, u32[]{:S(2)}, u32[]{:S(2)}) collective-permute-start(f32[40,128]{1,0:T(8,128)S(1)} %get-tuple-element.24), channel_id=1, source_target_pairs={{0,3},{1,2},{2,1},{3,0},{4,7},{5,6},{6,5},{7,4},{8,11},{9,10},{10,... | collective-permute-start | bytes 61448 | tf_op jit(solution)/shard_map/ppermute | solution.py:329
  12.2 1.2 %collective-permute-start.5 = (f32[40,128]{1,0:T(8,128)S(1)}, f32[40,128]{1,0:T(8,128)S(1)}, u32[]{:S(2)}, u32[]{:S(2)}) collective-permute-start(f32[40,128]{1,0:T(8,128)S(1)} %get-tuple-element.24), channel_id=1, source_target_pairs={{0,2},{1,3},{2,0},{3,1},{4,6},{5,7},{6,4},{7,5},{8,10},{9,11},{10,... | collective-permute-start | bytes 61448 | tf_op jit(solution)/shard_map/ppermute | solution.py:329
  13.5 0.3 collective-permute-start.4
  13.8 1.6 %collective-permute-start.3 = (bf16[32,4096]{1,0:T(8,128)(2,1)S(1)}, bf16[32,4096]{1,0:T(8,128)(2,1)S(1)}, u32[]{:S(2)}, u32[]{:S(2)}) collective-permute-start(bf16[32,4096]{1,0:T(8,128)(2,1)S(1)} %constant_dynamic-update-slice_fusion), channel_id=1, source_target_pairs={{0,2},{1,3},{2,0},{3,1},{4,6},{5,7},{6,4},{7,5},{8,10},{9,11},{10,... | collective-permute-start | bytes 786440 | tf_op jit(solution)/shard_map/ppermute | solution.py:329
  15.4 0.0 collective-permute-done.6
  15.4 0.7 %collective-permute-done.5 = f32[40,128]{1,0:T(8,128)S(1)} collective-permute-done((f32[40,128]{1,0:T(8,128)S(1)}, f32[40,128]{1,0:T(8,128)S(1)}, u32[]{:S(2)}, u32[]{:S(2)}) %collective-permute-start.5) | collective-permute-done | bytes 20512 | tf_op jit(solution)/shard_map/ppermute | solution.py:329
  16.0 0.0 collective-permute-done.4
  16.0 2.7 %collective-permute-start.9 = (f32[40,128]{1,0:T(8,128)S(1)}, f32[40,128]{1,0:T(8,128)S(1)}, u32[]{:S(2)}, u32[]{:S(2)}) collective-permute-start(f32[40,128]{1,0:T(8,128)S(1)} %add_add_fusion.refs_0_), channel_id=1, source_target_pairs={{0,12},{1,13},{2,14},{3,15},{4,8},{5,9},{6,10},{7,11},{8,4},{9,5},... | collective-permute-start | bytes 61448 | tf_op jit(solution)/shard_map/ppermute | solution.py:329
  18.8 0.3 %collective-permute-start.8 = (f32[40,128]{1,0:T(8,128)S(1)}, f32[40,128]{1,0:T(8,128)S(1)}, u32[]{:S(2)}, u32[]{:S(2)}) collective-permute-start(f32[40,128]{1,0:T(8,128)S(1)} %add_add_fusion.refs_0_), channel_id=1, source_target_pairs={{0,8},{1,9},{2,10},{3,11},{4,12},{5,13},{6,14},{7,15},{8,0},{9,1},... | collective-permute-start | bytes 61448 | tf_op jit(solution)/shard_map/ppermute | solution.py:329
  19.1 1.4 %collective-permute-start.7 = (f32[40,128]{1,0:T(8,128)S(1)}, f32[40,128]{1,0:T(8,128)S(1)}, u32[]{:S(2)}, u32[]{:S(2)}) collective-permute-start(f32[40,128]{1,0:T(8,128)S(1)} %add_add_fusion.refs_0_), channel_id=1, source_target_pairs={{0,4},{1,5},{2,6},{3,7},{4,0},{5,1},{6,2},{7,3},{8,12},{9,13},{10,... | collective-permute-start | bytes 61448 | tf_op jit(solution)/shard_map/ppermute | solution.py:329
  20.5 1.2 %collective-permute-done.9.refs_3_ = f32[40,128]{1,0:T(8,128)S(1)} collective-permute-done((f32[40,128]{1,0:T(8,128)S(1)}, f32[40,128]{1,0:T(8,128)S(1)}, u32[]{:S(2)}, u32[]{:S(2)}) %collective-permute-start.9) | collective-permute-done | bytes 20512 | tf_op jit(solution)/shard_map/ppermute | solution.py:329
  21.7 1.9 %collective-permute-done.8.refs_2_ = f32[40,128]{1,0:T(8,128)S(1)} collective-permute-done((f32[40,128]{1,0:T(8,128)S(1)}, f32[40,128]{1,0:T(8,128)S(1)}, u32[]{:S(2)}, u32[]{:S(2)}) %collective-permute-start.8) | collective-permute-done | bytes 20512 | tf_op jit(solution)/shard_map/ppermute | solution.py:329
  23.6 0.0 collective-permute-done.7.refs_1_
  23.6 0.0 collective-permute-done.3
  23.6 0.1 collective-permute-start.10
  23.7 2.7 %precondition.1.moved = f32[128,512]{1,0:T(8,128)S(1)} custom-call(f32[40,128]{1,0:T(8,128)S(1)} %add_add_fusion.refs_0_, f32[40,128]{1,0:T(8,128)S(1)} %collective-permute-done.7.refs_1_, f32[40,128]{1,0:T(8,128)S(1)} %collective-permute-done.8.refs_2_, f32[40,128]{1,0:T(8,128)S(1)} %collective-permute-done.9.refs_3_, ...), custom_call_target="tpu_custom_call" | custom-call | flops 3355443200 | bytes 524288 | tf_op jit(solution)/shard_map/precondition/pallas_call | solution.py:228
  26.4 0.0 collective-permute-done.10.refs_1_
  26.4 2.4 %score.1 = f32[512,128]{1,0:T(8,128)} custom-call(f32[128,512]{1,0:T(8,128)S(1)} %precondition.1.moved, bf16[64,4096]{1,0:T(8,128)(2,1)S(1)} %constant_dynamic-update-slice_fusion.4.refs_0_, bf16[64,4096]{1,0:T(8,128)(2,1)S(1)} %collective-permute-done.10.refs_1_), custom_call_target="tpu_custom_call" | custom-call | tf_op jit(solution)/shard_map/score/pallas_call | solution.py:289
  (10 shorter events, 0.1 us)
Async XLA Ops:
  0.0 11.8 %collective-permute-start.1 = (bf16[8,4096]{1,0:T(8,128)(2,1)}, bf16[8,4096]{1,0:T(8,128)(2,1)S(1)}, u32[]{:S(2)}, u32[]{:S(2)}) collective-permute-start(bf16[8,4096]{1,0:T(8,128)(2,1)} %param.9), channel_id=1, source_target_pairs={{0,8},{1,9},{2,10},{3,11},{4,12},{5,13},{6,14},{7,15},{8,0},{9,1},... | collective-permute-start | bytes 196616 | tf_op jit(solution)/shard_map/ppermute | solution.py:329
  4.0 7.7 %collective-permute-start = (bf16[8,4096]{1,0:T(8,128)(2,1)}, bf16[8,4096]{1,0:T(8,128)(2,1)S(1)}, u32[]{:S(2)}, u32[]{:S(2)}) collective-permute-start(bf16[8,4096]{1,0:T(8,128)(2,1)} %param.9), channel_id=1, source_target_pairs={{0,12},{1,13},{2,14},{3,15},{4,8},{5,9},{6,10},{7,11},{8,4},{9,5},... | collective-permute-start | bytes 196616 | tf_op jit(solution)/shard_map/ppermute | solution.py:329
  5.4 6.4 %collective-permute-start.2 = (bf16[8,4096]{1,0:T(8,128)(2,1)}, bf16[8,4096]{1,0:T(8,128)(2,1)S(1)}, u32[]{:S(2)}, u32[]{:S(2)}) collective-permute-start(bf16[8,4096]{1,0:T(8,128)(2,1)} %param.9), channel_id=1, source_target_pairs={{0,4},{1,5},{2,6},{3,7},{4,0},{5,1},{6,2},{7,3},{8,12},{9,13},{10,... | collective-permute-start | bytes 196616 | tf_op jit(solution)/shard_map/ppermute | solution.py:329
  5.6 8.1 %copy-start = (bf16[8,4096]{1,0:T(8,128)(2,1)S(1)}, bf16[8,4096]{1,0:T(8,128)(2,1)}, u32[]{:S(2)}) copy-start(bf16[8,4096]{1,0:T(8,128)(2,1)} %param.9) | copy-start | bytes 196612
  11.8 3.6 %collective-permute-start.6 = (f32[40,128]{1,0:T(8,128)S(1)}, f32[40,128]{1,0:T(8,128)S(1)}, u32[]{:S(2)}, u32[]{:S(2)}) collective-permute-start(f32[40,128]{1,0:T(8,128)S(1)} %get-tuple-element.24), channel_id=1, source_target_pairs={{0,3},{1,2},{2,1},{3,0},{4,7},{5,6},{6,5},{7,4},{8,11},{9,10},{10,... | collective-permute-start | bytes 61448 | tf_op jit(solution)/shard_map/ppermute | solution.py:329
  12.2 3.8 %collective-permute-start.5 = (f32[40,128]{1,0:T(8,128)S(1)}, f32[40,128]{1,0:T(8,128)S(1)}, u32[]{:S(2)}, u32[]{:S(2)}) collective-permute-start(f32[40,128]{1,0:T(8,128)S(1)} %get-tuple-element.24), channel_id=1, source_target_pairs={{0,2},{1,3},{2,0},{3,1},{4,6},{5,7},{6,4},{7,5},{8,10},{9,11},{10,... | collective-permute-start | bytes 61448 | tf_op jit(solution)/shard_map/ppermute | solution.py:329
  13.5 2.6 %collective-permute-start.4 = (f32[40,128]{1,0:T(8,128)S(1)}, f32[40,128]{1,0:T(8,128)S(1)}, u32[]{:S(2)}, u32[]{:S(2)}) collective-permute-start(f32[40,128]{1,0:T(8,128)S(1)} %get-tuple-element.24), channel_id=1, source_target_pairs={{0,1},{1,0},{2,3},{3,2},{4,5},{5,4},{6,7},{7,6},{8,9},{9,8},{10,11... | collective-permute-start | bytes 61448 | tf_op jit(solution)/shard_map/ppermute | solution.py:329
  13.8 9.8 %collective-permute-start.3 = (bf16[32,4096]{1,0:T(8,128)(2,1)S(1)}, bf16[32,4096]{1,0:T(8,128)(2,1)S(1)}, u32[]{:S(2)}, u32[]{:S(2)}) collective-permute-start(bf16[32,4096]{1,0:T(8,128)(2,1)S(1)} %constant_dynamic-update-slice_fusion), channel_id=1, source_target_pairs={{0,2},{1,3},{2,0},{3,1},{4,6},{5,7},{6,4},{7,5},{8,10},{9,11},{10,... | collective-permute-start | bytes 786440 | tf_op jit(solution)/shard_map/ppermute | solution.py:329
  16.0 5.7 %collective-permute-start.9 = (f32[40,128]{1,0:T(8,128)S(1)}, f32[40,128]{1,0:T(8,128)S(1)}, u32[]{:S(2)}, u32[]{:S(2)}) collective-permute-start(f32[40,128]{1,0:T(8,128)S(1)} %add_add_fusion.refs_0_), channel_id=1, source_target_pairs={{0,12},{1,13},{2,14},{3,15},{4,8},{5,9},{6,10},{7,11},{8,4},{9,5},... | collective-permute-start | bytes 61448 | tf_op jit(solution)/shard_map/ppermute | solution.py:329
  18.8 4.8 %collective-permute-start.8 = (f32[40,128]{1,0:T(8,128)S(1)}, f32[40,128]{1,0:T(8,128)S(1)}, u32[]{:S(2)}, u32[]{:S(2)}) collective-permute-start(f32[40,128]{1,0:T(8,128)S(1)} %add_add_fusion.refs_0_), channel_id=1, source_target_pairs={{0,8},{1,9},{2,10},{3,11},{4,12},{5,13},{6,14},{7,15},{8,0},{9,1},... | collective-permute-start | bytes 61448 | tf_op jit(solution)/shard_map/ppermute | solution.py:329
  19.1 4.5 %collective-permute-start.7 = (f32[40,128]{1,0:T(8,128)S(1)}, f32[40,128]{1,0:T(8,128)S(1)}, u32[]{:S(2)}, u32[]{:S(2)}) collective-permute-start(f32[40,128]{1,0:T(8,128)S(1)} %add_add_fusion.refs_0_), channel_id=1, source_target_pairs={{0,4},{1,5},{2,6},{3,7},{4,0},{5,1},{6,2},{7,3},{8,12},{9,13},{10,... | collective-permute-start | bytes 61448 | tf_op jit(solution)/shard_map/ppermute | solution.py:329
  23.6 2.8 %collective-permute-start.10 = (bf16[64,4096]{1,0:T(8,128)(2,1)S(1)}, bf16[64,4096]{1,0:T(8,128)(2,1)S(1)}, u32[]{:S(2)}, u32[]{:S(2)}) collective-permute-start(bf16[64,4096]{1,0:T(8,128)(2,1)S(1)} %constant_dynamic-update-slice_fusion.4.refs_0_), channel_id=1, source_target_pairs={{0,1},{1,0},{2,3},{3,2},{4,5},{5,4},{6,7},{7,6},{8,9},{9,8},{10,11... | collective-permute-start | bytes 1572872 | tf_op jit(solution)/shard_map/ppermute | solution.py:329
